TPU v7x, 128 devices: a whole 4x4x4 slice. The times are simulated.
128 devices in a mesh: row: 32 (over x, y, core), col: 4 (over z).
Axes of the slice: x: 4, y: 4, z: 4, core: 2. Of those that a mesh axis runs over, the one named last changes fastest.
Arguments:
- coeffs: bfloat16 [4096, 1024], P('row', 'col'), may hold values from -0.09375 to 0.09375
- coef_pattern: int32 [32, 8], replicated, may hold values 0 or 1
- keep_density: int32 [2, 32, 32], replicated, may hold values 0 or 1
- keep_square: int32 [2, 32, 32], replicated, may hold values 0 or 1
Outputs:
- density: float32 [4096, 4096], P('row', 'col')
All inputs are finite; a program needn't handle non-finite values.
Results may differ from a plain program's by a relative error of at most 0.0042.
Values may be sent and summed in bfloat16 or wider, within the bound.
No kernel may reach another device: no remote copies, remote signals or barrier semaphores. Data moves between devices by JAX's collectives and lax.ppermute only.
A program may use at most 64 MiB of HBM per device.

v0:
```python
import functools

import jax
import jax.numpy as jnp
from jax import lax
from jax.experimental import pallas as pl
from jax.experimental.pallas import tpu as pltpu
from jax.sharding import PartitionSpec as P

B = 128
N = 4096
K = 1024
ROWS = 256
COLS = 512
AXES = ("row", "col")
MIB = 1024 * 1024


def device(x, y, core, z):
    return (((x % 4) * 4 + y % 4) * 2 + core) * 4 + z % 4


def pairs(target):
    return [
        (device(x, y, core, z), device(*target(x, y, core, z)))
        for x in range(4) for y in range(4) for core in range(2) for z in range(4)
    ]


def other_core(a):
    return lax.ppermute(a, AXES, pairs(lambda x, y, core, z: (x, y, 1 - core, z)))


def from_z(a, d):
    return lax.ppermute(a, AXES, pairs(lambda x, y, core, z: (x, y, core, z - d)))


def from_first(a, d):
    return lax.ppermute(a, AXES, pairs(
        lambda x, y, core, z: (x - d, y, core, z) if core == 0 else (x, y - d, core, z)))


def from_second(a, d):
    return lax.ppermute(a, AXES, pairs(
        lambda x, y, core, z: (x, y - d, core, z) if core == 0 else (x - d, y, core, z)))


def gather(a, fetch):
    one, three, two = fetch(a, 1), fetch(a, 3), fetch(a, 2)
    return [a, one, two, three]


def place(x, y, kind, first, second):
    px = jnp.where(kind == 0, x + first, x + second) & 3
    py = jnp.where(kind == 0, y + second, y + first) & 3
    return px, py


def dot_t(a, b):
    return lax.dot_general(a, b, (((1,), (1,)), ((), ())), preferred_element_type=jnp.float32)


def dot(a, b):
    return jnp.dot(a, b, preferred_element_type=jnp.float32)


def aligned(block, size):
    return pl.ds(pl.multiple_of(block * size, size), size)


def block_at(x, y, kind, place_in_order):
    px, py = place(x, y, kind, place_in_order % 4, place_in_order // 4)
    return px * 8 + py * 2 + kind


def some_rows(where, keep_d, rows, half, parts, line):
    x, y, core = where[0], where[1], where[2]
    kind = core if half == 0 else 1 - core
    for n, part in parts.items():
        value = dot_t(rows[...], part[...])
        for u in range(4):
            block = block_at(x, y, kind, n * 4 + u)
            at = (half * 16 + n * 4 + u) * B
            for t in range(2):
                keep = keep_d[0, (x * 4 + y) * 2 + t, block].astype(jnp.float32)
                piece = value[t * B:(t + 1) * B, u * B:(u + 1) * B] * keep
                line[t * B:(t + 1) * B, at:at + B] = piece.astype(jnp.bfloat16)


def some_columns(where, keep_d, half, parts, columns, panel, mirrored=()):
    x, y, core = where[0], where[1], where[2]
    kind = core if half == 0 else 1 - core

    def put(value, kind, n, i, m, u, turn):
        keep = keep_d[0, block_at(x, y, kind, n * 4 + i), block_at(x, y, core, m * 4 + u)]
        piece = (value * keep.astype(jnp.float32)).astype(jnp.bfloat16)
        at, to = (half * 16 + n * 4 + i) * B, (m * 4 + u) * B
        panel[at:at + B, to:to + B] = piece.T if turn else piece

    for n, part in parts.items():
        for m, column in columns.items():
            if (n, m) in mirrored:
                continue
            value = dot_t(part[...], column[...])
            for i in range(4):
                for u in range(4):
                    piece = value[i * B:(i + 1) * B, u * B:(u + 1) * B]
                    put(piece, kind, n, i, m, u, False)
                    if (m, n) in mirrored:
                        put(piece, core, m, u, n, i, True)


EARLY = (0, 1, 3)


def density_0(where, keep_d, own0, other0, panel, line, rows):
    first = where[2] == 0
    mine, its = own0[:B, :], other0[:B, :]
    rows[:B, :] = jnp.where(first, mine, its)
    rows[B:, :] = jnp.where(first, its, mine)
    for half, part in enumerate((own0, other0)):
        some_rows(where, keep_d, rows, half, {0: part}, line)
        some_columns(where, keep_d, half, {0: part}, {0: own0}, panel)


def density_1(where, keep_d, own0, own1, own3, other0, rows, _, __, panel, line):
    own = {0: own0, 1: own1, 3: own3}
    some_rows(where, keep_d, rows, 0, {1: own1, 3: own3}, line)
    some_columns(where, keep_d, 0, {0: own0}, {1: own1, 3: own3}, panel, ((1, 0), (3, 0)))
    some_columns(where, keep_d, 0, {1: own1, 3: own3}, {1: own1, 3: own3}, panel, ((3, 1),))
    some_columns(where, keep_d, 1, {0: other0}, {1: own1, 3: own3}, panel)


def density_2(where, keep_d, own0, own1, own3, other1, other3, rows, _, __, panel, line):
    other = {1: other1, 3: other3}
    some_rows(where, keep_d, rows, 1, other, line)
    some_columns(where, keep_d, 1, other, {0: own0, 1: own1, 3: own3}, panel)


def density_3(where, keep_d, own0, own1, own2, own3, other0, other1, other3, rows, _, __, panel, line):
    some_rows(where, keep_d, rows, 0, {2: own2}, line)
    own = {0: own0, 1: own1, 2: own2, 3: own3}
    some_columns(where, keep_d, 0, {2: own2}, own, panel, ((0, 2), (1, 2), (3, 2)))
    some_columns(where, keep_d, 1, {0: other0, 1: other1, 3: other3}, {2: own2}, panel)


def first_square(where, keep_d, keep_s, own0, own1, own2, own3, other2, rows, _, __, panel, line, low, square, total):
    x, y, core, z = where[0], where[1], where[2], where[3]
    some_rows(where, keep_d, rows, 1, {2: other2}, line)
    some_columns(where, keep_d, 1, {2: other2}, {0: own0, 1: own1, 2: own2, 3: own3}, panel)

    @pl.loop(0, 2)
    def _(half):
        value = dot(line[...], panel[:, aligned(half, 1024)])
        for t in range(2):
            for u in range(8):
                block = block_at(x, y, core, half * 8 + u)
                keep = keep_s[0, (x * 4 + y) * 2 + t, block].astype(jnp.float32)
                piece = value[t * B:(t + 1) * B, u * B:(u + 1) * B] * keep
                total[t * B:(t + 1) * B, aligned(half * 8 + u, B)] = piece
                low[t * B:(t + 1) * B, aligned(half * 8 + u, B)] = piece.astype(jnp.bfloat16)

    for t in range(4):
        square[:, t * B:(t + 1) * B] = total[:, aligned(column_at(where, t), B)]


def column_at(where, t):
    x, y, core, z = where[0], where[1], where[2], where[3]
    dx, dy = (z - x) & 3, (t - y) & 3
    return jnp.where(core == 0, dy * 4 + dx, dx * 4 + dy)


def early_first_cube(where, low, panel, early, columns):
    for t in range(4):
        at = aligned(column_at(where, t), B)
        columns[:, t * B:(t + 1) * B] = panel[:, at]
    early[...] = dot(low[...], columns[:2048, :])


def first_density(where, keep_d, its, columns, early, square, out):
    x, y, core, z = where[0], where[1], where[2], where[3]
    value = 3.0 * square[...] - 2.0 * (early[...] + dot(its[...], columns[2048:, :]))
    for t in range(2):
        for u in range(4):
            keep = keep_d[1, (x * 4 + y) * 2 + t, z * 8 + u * 2 + core].astype(jnp.float32)
            piece = value[t * B:(t + 1) * B, u * B:(u + 1) * B] * keep
            out[t * B:(t + 1) * B, u * B:(u + 1) * B] = piece.astype(jnp.bfloat16)


def parts_times_panel(parts, z, panel):
    total = None
    for ref, d, kind in parts:
        rows = [panel[aligned(((z + d) & 3) * 8 + t * 2 + kind, B), :] for t in range(4)]
        term = dot(ref[...], jnp.concatenate(rows, axis=0))
        total = term if total is None else total + term
    return total


def early_cube(where, *refs):
    own, other, panel, out = refs[:4], refs[4], refs[5], refs[6]
    core, z = where[2], where[3]
    parts = [(own[d], d, core) for d in range(4)] + [(other, 0, 1 - core)]
    out[...] = parts_times_panel(parts, z, panel)


def chips_times(where, line, chips, panel, sems):
    x, y, core = where[0], where[1], where[2]
    copies, left, right = [], [], []
    for n, (ref, offset, first, second) in enumerate(chips):
        px, py = place(x, y, core, first, second)
        copies.append(pltpu.make_async_copy(
            ref.at[pl.ds(offset, ROWS)], panel.at[aligned(px * 4 + py, ROWS)], sems.at[n]))
        copies[-1].start()
        left.append(line[:, aligned(px * 4 + py, ROWS)])
        right.append(ref[offset:offset + ROWS, :])
    total = None
    for n in range(0, len(chips), 4):
        term = dot(jnp.concatenate(left[n:n + 4], axis=1), jnp.concatenate(right[n:n + 4], axis=0))
        total = term if total is None else total + term
    return total, copies


def early_square(where, *refs):
    own, other, near, far, (early, line, panel), (sems,) = (
        refs[:4], refs[4:8], refs[8], refs[9:13], refs[13:16], refs[16:])
    core, z = where[2], where[3]
    for d in range(4):
        for ref, kind in ((own[d], core), (other[d], 1 - core)):
            for t in range(4):
                line[:, aligned(((z + d) & 3) * 8 + t * 2 + kind, B)] = ref[:, t * B:(t + 1) * B]
    chips = [(near, i * ROWS, i, 0) for i in range(4)] + [(far[i], 0, i, 2) for i in range(4)]
    value, copies = chips_times(where, line, chips, panel, sems)
    early[...] = value
    for copy in copies:
        copy.wait()


def second_square(where, keep_s, one, three, early, line, _, square, low, panel, sems):
    x, y, core, z = where[0], where[1], where[2], where[3]
    chips = [(ref, i * ROWS, i, j) for ref, j in ((one, 1), (three, 3)) for i in range(4)]
    value, copies = chips_times(where, line, chips, panel, sems)
    value = early[...] + value
    for t in range(2):
        for u in range(4):
            keep = keep_s[1, (x * 4 + y) * 2 + t, z * 8 + u * 2 + core].astype(jnp.float32)
            piece = value[t * B:(t + 1) * B, u * B:(u + 1) * B] * keep
            square[t * B:(t + 1) * B, u * B:(u + 1) * B] = piece
            low[t * B:(t + 1) * B, u * B:(u + 1) * B] = piece.astype(jnp.bfloat16)
    for copy in copies:
        copy.wait()


def second_density(leave, where, *refs):
    others, (early, square, panel), (come, out) = refs[:3], refs[3:6], (refs[6:] if not leave else (None,) + refs[6:])
    core, z = where[2], where[3]
    at = aligned(1 - core if leave else core, B)
    total = early[at, :]
    for d in (1, 2, 3):
        rows = [panel[aligned(((z + d) & 3) * 8 + t * 2 + 1 - core, B), :] for t in range(4)]
        total = total + dot(others[d - 1][at, :], jnp.concatenate(rows, axis=0))
    value = 3.0 * square[at, :] - 2.0 * total
    if leave:
        out[...] = value
        return
    first = core == 0
    for t in range(4):
        mine, its = value[:, t * B:(t + 1) * B], come[:, t * B:(t + 1) * B]
        out[:, 2 * t * B:(2 * t + 1) * B] = jnp.where(first, mine, its)
        out[:, (2 * t + 1) * B:(2 * t + 2) * B] = jnp.where(first, its, mine)


SMEM = pl.BlockSpec(memory_space=pltpu.SMEM)
VMEM = pl.BlockSpec(memory_space=pltpu.VMEM)


def call(kernel, n_smem, ins, outs, scratch, flops, moved, aliases={}):
    return pl.pallas_call(
        kernel,
        in_specs=[SMEM] * n_smem + [VMEM] * (len(ins) - n_smem),
        out_specs=[VMEM] * len(outs),
        out_shape=outs,
        scratch_shapes=scratch,
        input_output_aliases=aliases,
        cost_estimate=pl.CostEstimate(flops=flops, bytes_accessed=moved, transcendentals=0),
        compiler_params=pltpu.CompilerParams(vmem_limit_bytes=12 * MIB),
    )(*ins)


def body(coeffs, coef_pattern, keep_density, keep_square):
    r, z = lax.axis_index("row"), lax.axis_index("col")
    x, y, core = r // 8, (r // 2) % 4, r % 2
    where = jnp.stack([x, y, core, z]).astype(jnp.int32)
    low_block = jax.ShapeDtypeStruct((ROWS, COLS), jnp.bfloat16)
    full_block = jax.ShapeDtypeStruct((ROWS, COLS), jnp.float32)
    panel_shape = jax.ShapeDtypeStruct((N, COLS), jnp.bfloat16)
    line_shape = jax.ShapeDtypeStruct((ROWS, N), jnp.bfloat16)
    wide_shape = jax.ShapeDtypeStruct((N, N // 2), jnp.bfloat16)
    block_flops = 2 * ROWS * N * COLS
    pair_flops = 2 * 512 * 512 * K

    kept = jnp.concatenate(gather(coeffs, from_z), axis=1)
    pattern = lax.dynamic_slice(coef_pattern, (r, 0), (1, 8)).reshape(4, 2)
    pattern = jnp.concatenate([pattern, pattern], axis=0)
    pattern = lax.dynamic_slice(pattern, (z, 0), (4, 2)).reshape(1, 8)
    kept = kept * jnp.repeat(pattern, B, 1).astype(jnp.bfloat16)
    near = jnp.concatenate(gather(kept, from_first), axis=0)
    own1, own3, other0 = from_second(near, 1), from_second(near, 3), other_core(near)
    rows_shape = jax.ShapeDtypeStruct((ROWS, K), jnp.bfloat16)
    out_shapes = [wide_shape, line_shape]
    panel, line, rows = call(
        density_0, 2, [where, keep_density, near, other0], out_shapes + [rows_shape], [], pair_flops // 8, MIB)
    panel, line, own0, own1, own3 = lax.optimization_barrier((panel, line, near, own1, own3))
    own2 = from_second(own0, 2)
    other1, other3 = other_core(own1), other_core(own3)
    panel, line = call(
        density_1, 2, [where, keep_density, own0, own1, own3, other0, rows, panel, line],
        out_shapes, [], 11 * pair_flops, 8 * MIB, {7: 0, 8: 1})
    panel, line = call(
        density_2, 2, [where, keep_density, own0, own1, own3, other1, other3, rows, panel, line],
        out_shapes, [], 7 * pair_flops, 8 * MIB, {8: 0, 9: 1})
    panel, line, own2 = lax.optimization_barrier((panel, line, own2))
    other2 = other_core(own2)
    panel, line = call(
        density_3, 2, [where, keep_density, own0, own1, own2, own3, other0, other1, other3, rows, panel, line],
        out_shapes, [], 10 * pair_flops, 8 * MIB, {10: 0, 11: 1})
    panel, line, low, square = call(
        first_square, 3,
        [where, keep_density, keep_square, own0, own1, own2, own3, other2, rows, panel, line],
        out_shapes + [jax.ShapeDtypeStruct((ROWS, N // 2), jnp.bfloat16), full_block],
        [pltpu.VMEM((ROWS, N // 2), jnp.float32)],
        4 * pair_flops + 4 * block_flops, 20 * MIB, {9: 0, 10: 1})

    its = other_core(low)
    early, columns = call(
        early_first_cube, 1, [where, low, panel], [full_block, panel_shape], [], block_flops // 2, 12 * MIB)
    (current,) = call(
        first_density, 2, [where, keep_density, its, columns, early, square], [low_block], [],
        block_flops // 2, 4 * MIB)

    own0, one, three, two, far = lax.optimization_barrier((
        current, from_first(current, 1), from_first(current, 3), from_first(current, 2), from_second(current, 2)))
    near = jnp.concatenate([own0, one, two, three], axis=0)
    one, three = from_second(near, 1), from_second(near, 3)
    far, own1, own2, own3 = lax.optimization_barrier((far, *gather(current, from_z)[1:]))
    far = gather(far, from_first)
    own = [own0, own1, own2, own3]
    other = [other_core(part) for part in own]
    early, line, panel = call(
        early_square, 1, [where, *own, *other, near, *far], [full_block, line_shape, panel_shape],
        [pltpu.SemaphoreType.DMA((8,))], block_flops // 2, 10 * MIB)
    square, low, panel = call(
        second_square, 2, [where, keep_square, one, three, early, line, panel],
        [full_block, low_block, panel_shape],
        [pltpu.SemaphoreType.DMA((8,))], block_flops // 2, 8 * MIB, {6: 2})

    own = gather(low, from_z)
    other = [other_core(part) for part in own]
    (early,) = call(
        early_cube, 1, [where, *own, other[0], panel], [full_block], [], block_flops * 5 // 8, 4 * MIB)
    last = [*other[1:], early, square, panel]
    (leave,) = call(
        functools.partial(second_density, True), 1, [where, *last],
        [jax.ShapeDtypeStruct((B, COLS), jnp.float32)], [], block_flops * 3 // 16, 3 * MIB)
    (out,) = call(
        functools.partial(second_density, False), 1, [where, *last, other_core(leave)],
        [jax.ShapeDtypeStruct((B, 2 * COLS), jnp.float32)], [], block_flops * 3 // 16, 3 * MIB)
    return out


def solution(mesh):
    placed = (P("row", "col"), P(), P(), P())
    return jax.shard_map(
        body, mesh=mesh, in_specs=placed, out_specs=P("row", "col"), check_vma=False
    )
```

profile of v0, /device:TPU:1, one launch (start us, length us, event | category | flops | bytes accessed | tf_op | source)
XLA Modules:
  0.0 141.5 jit_solution(15515252072304287219)
XLA Ops:
  0.0 4.4 %collective-permute-start.1 = (bf16[128,256]{1,0:T(8,128)(2,1)}, bf16[128,256]{1,0:T(8,128)(2,1)S(1)}, u32[]{:S(2)}, u32[]{:S(2)}) collective-permute-start(bf16[128,256]{1,0:T(8,128)(2,1)} %param.4), channel_id=1, source_target_pairs={{0,2},{1,3},{2,0},{3,1},{4,6},{5,7},{6,4},{7,5},{8,10},{9,11},{10,... | collective-permute-start | bytes 196616 | tf_op jit(solution)/shard_map/ppermute | solution.py:35
  4.9 1.0 collective-permute-start.2
  6.7 1.4 %collective-permute-done = bf16[128,256]{1,0:T(8,128)(2,1)S(1)} collective-permute-done((bf16[128,256]{1,0:T(8,128)(2,1)}, bf16[128,256]{1,0:T(8,128)(2,1)S(1)}, u32[]{:S(2)}, u32[]{:S(2)}) %collective-permute-start) | collective-permute-done | bytes 65568 | tf_op jit(solution)/shard_map/ppermute | solution.py:35
  8.1 1.3 collective-permute-done.2
  10.3 1.4 collective-permute-start.5
  11.7 2.6 %collective-permute-start.4 = (bf16[128,1024]{1,0:T(8,128)(2,1)S(1)}, bf16[128,1024]{1,0:T(8,128)(2,1)S(1)}, u32[]{:S(2)}, u32[]{:S(2)}) collective-permute-start(bf16[128,1024]{1,0:T(8,128)(2,1)S(1)} %maximum_multiply_fusion), channel_id=1, source_target_pairs={{0,64},{1,65},{2,66},{3,67},{4,20},{5,21},{6,22},{7,23},{8,72},{9,... | collective-permute-start | bytes 786440 | tf_op jit(solution)/shard_map/ppermute | solution.py:39
  14.3 1.1 collective-permute-start.3
  15.4 1.8 %collective-permute-done.5 = bf16[128,1024]{1,0:T(8,128)(2,1)S(1)} collective-permute-done((bf16[128,1024]{1,0:T(8,128)(2,1)S(1)}, bf16[128,1024]{1,0:T(8,128)(2,1)S(1)}, u32[]{:S(2)}, u32[]{:S(2)}) %collective-permute-start.5) | collective-permute-done | bytes 262176 | tf_op jit(solution)/shard_map/ppermute | solution.py:39
  17.2 4.0 %collective-permute-done.4 = bf16[128,1024]{1,0:T(8,128)(2,1)S(1)} collective-permute-done((bf16[128,1024]{1,0:T(8,128)(2,1)S(1)}, bf16[128,1024]{1,0:T(8,128)(2,1)S(1)}, u32[]{:S(2)}, u32[]{:S(2)}) %collective-permute-start.4) | collective-permute-done | bytes 262176 | tf_op jit(solution)/shard_map/ppermute | solution.py:39
  21.2 3.1 %collective-permute-start.6 = (bf16[512,1024]{1,0:T(8,128)(2,1)S(1)}, bf16[512,1024]{1,0:T(8,128)(2,1)}, u32[]{:S(2)}, u32[]{:S(2)}) collective-permute-start(bf16[512,1024]{1,0:T(8,128)(2,1)S(1)} %pad_maximum_fusion.own0), channel_id=1, source_target_pairs={{0,4},{1,5},{2,6},{3,7},{4,0},{5,1},{6,2},{7,3},{8,12},{9,13},{10,... | collective-permute-start | bytes 3145736 | tf_op jit(solution)/shard_map/ppermute | solution.py:31
  24.3 1.6 %collective-permute-start.8 = (bf16[512,1024]{1,0:T(8,128)(2,1)S(1)}, bf16[512,1024]{1,0:T(8,128)(2,1)S(1)}, u32[]{:S(2)}, u32[]{:S(2)}) collective-permute-start(bf16[512,1024]{1,0:T(8,128)(2,1)S(1)} %pad_maximum_fusion.own0), channel_id=1, source_target_pairs={{0,8},{1,9},{2,10},{3,11},{4,36},{5,37},{6,38},{7,39},{8,16},{9,17... | collective-permute-start | bytes 3145736 | tf_op jit(solution)/shard_map/ppermute | solution.py:44
  25.9 1.1 collective-permute-start.7
  27.0 3.1 %shard_map.46 = (bf16[4096,2048]{1,0:T(8,128)(2,1)S(1)}, bf16[256,4096]{1,0:T(8,128)(2,1)S(1)}, bf16[256,1024]{1,0:T(8,128)(2,1)S(1)}) custom-call(s32[4]{0:T(128)S(1)} %pad_add_fusion.1.where, s32[2,32,32]{2,1,0:T(8,128)S(1)} %copy-done.1, bf16[512,1024]{1,0:T(8,128)(2,1)S(1)} %pad_maximum_fusion.own0, bf16[512,1024]{1,0:T(8,128)(2,1)} %collective-permute-done.6.other0), custom_call_target="tpu_custom_call" | custom-call | flops 67108864 | bytes 1048576 | tf_op jit(solution)/shard_map/pallas_call | solution.py:277
  30.1 9.3 %collective-permute-done.8.own3 = bf16[512,1024]{1,0:T(8,128)(2,1)S(1)} collective-permute-done((bf16[512,1024]{1,0:T(8,128)(2,1)S(1)}, bf16[512,1024]{1,0:T(8,128)(2,1)S(1)}, u32[]{:S(2)}, u32[]{:S(2)}) %collective-permute-start.8) | collective-permute-done | bytes 1048608 | tf_op jit(solution)/shard_map/ppermute | solution.py:44
  40.7 2.7 %collective-permute-start.11 = (bf16[512,1024]{1,0:T(8,128)(2,1)S(1)}, bf16[512,1024]{1,0:T(8,128)(2,1)S(1)}, u32[]{:S(2)}, u32[]{:S(2)}) collective-permute-start(bf16[512,1024]{1,0:T(8,128)(2,1)S(1)} %pad_maximum_fusion.own0), channel_id=1, source_target_pairs={{0,16},{1,17},{2,18},{3,19},{4,68},{5,69},{6,70},{7,71},{8,24},{9,... | collective-permute-start | bytes 3145736 | tf_op jit(solution)/shard_map/ppermute | solution.py:44
  43.4 5.9 %shard_map.47 = (bf16[4096,2048]{1,0:T(8,128)(2,1)S(1)}, bf16[256,4096]{1,0:T(8,128)(2,1)S(1)}) custom-call(s32[4]{0:T(128)S(1)} %pad_add_fusion.1.where, s32[2,32,32]{2,1,0:T(8,128)S(1)} %copy-done.1, bf16[512,1024]{1,0:T(8,128)(2,1)S(1)} %pad_maximum_fusion.own0, ...), custom_call_target="tpu_custom_call", output_to_operand_aliasing={{0}: (7, {}), {1}: (8, {})} | custom-call | flops 5905580032 | bytes 8388608 | tf_op jit(solution)/shard_map/pallas_call | solution.py:277
  49.4 5.1 %shard_map.48 = (bf16[4096,2048]{1,0:T(8,128)(2,1)S(1)}, bf16[256,4096]{1,0:T(8,128)(2,1)S(1)}) custom-call(s32[4]{0:T(128)S(1)} %pad_add_fusion.1.where, s32[2,32,32]{2,1,0:T(8,128)S(1)} %copy-done.1, bf16[512,1024]{1,0:T(8,128)(2,1)S(1)} %pad_maximum_fusion.own0, ...), custom_call_target="tpu_custom_call", output_to_operand_aliasing={{0}: (8, {}), {1}: (9, {})} | custom-call | flops 3758096384 | bytes 8388608 | tf_op jit(solution)/shard_map/pallas_call | solution.py:277
  54.4 1.8 %collective-permute-done.11.own2 = bf16[512,1024]{1,0:T(8,128)(2,1)S(1)} collective-permute-done((bf16[512,1024]{1,0:T(8,128)(2,1)S(1)}, bf16[512,1024]{1,0:T(8,128)(2,1)S(1)}, u32[]{:S(2)}, u32[]{:S(2)}) %collective-permute-start.11) | collective-permute-done | bytes 1048608 | tf_op jit(solution)/shard_map/ppermute | solution.py:44
  56.2 1.4 collective-permute-start.12
  57.6 5.7 %shard_map.49 = (bf16[4096,2048]{1,0:T(8,128)(2,1)S(1)}, bf16[256,4096]{1,0:T(8,128)(2,1)S(1)}) custom-call(s32[4]{0:T(128)S(1)} %pad_add_fusion.1.where, s32[2,32,32]{2,1,0:T(8,128)S(1)} %copy-done.1, bf16[512,1024]{1,0:T(8,128)(2,1)S(1)} %pad_maximum_fusion.own0, ...), custom_call_target="tpu_custom_call", output_to_operand_aliasing={{0}: (10, {}), {1}: (11, {})} | custom-call | flops 5368709120 | bytes 8388608 | tf_op jit(solution)/shard_map/pallas_call | solution.py:277
  63.2 9.5 %shard_map.50 = (bf16[4096,2048]{1,0:T(8,128)(2,1)S(1)}, bf16[256,4096]{1,0:T(8,128)(2,1)S(1)}, bf16[256,2048]{1,0:T(8,128)(2,1)S(1)}, f32[256,512]{1,0:T(8,128)S(1)}) custom-call(s32[4]{0:T(128)S(1)} %pad_add_fusion.1.where, s32[2,32,32]{2,1,0:T(8,128)S(1)} %copy-done.1, s32[2,32,32]{2,1,0:T(8,128)S(1)} %copy-done.2, ...), custom_call_target="tpu_custom_call", output_to_operand_aliasing={{0}: (9, {}), {1}: (10, {})} | custom-call | flops 6442450944 | bytes 20971520 | tf_op jit(solution)/shard_map/pallas_call | solution.py:277
  72.8 2.3 %shard_map.51 = (f32[256,512]{1,0:T(8,128)S(1)}, bf16[4096,512]{1,0:T(8,128)(2,1)S(1)}) custom-call(s32[4]{0:T(128)S(1)} %pad_add_fusion.1.where, bf16[256,2048]{1,0:T(8,128)(2,1)S(1)} %get-tuple-element.59.low, bf16[4096,2048]{1,0:T(8,128)(2,1)S(1)} %get-tuple-element.60.panel), custom_call_target="tpu_custom_call" | custom-call | flops 536870912 | bytes 12582912 | tf_op jit(solution)/shard_map/pallas_call | solution.py:277
  75.5 1.8 %shard_map.52.refs_0_ = bf16[256,512]{1,0:T(8,128)(2,1)S(1)} custom-call(s32[4]{0:T(128)S(1)} %pad_add_fusion.1.where, s32[2,32,32]{2,1,0:T(8,128)S(1)} %copy-done.1, bf16[256,2048]{1,0:T(8,128)(2,1)S(1)} %collective-permute-done.13.its, bf16[4096,512]{1,0:T(8,128)(2,1)S(1)} %get-tuple-element.61.columns, f32[256,512]{1,0:T(8,128)S(1)} %get-tuple-element.62.early, ...), custom_call_target="tpu_custom_call" | custom-call | flops 536870912 | bytes 4194304 | tf_op jit(solution)/shard_map/pallas_call | solution.py:277
  77.3 2.7 %collective-permute-start.17 = (bf16[256,512]{1,0:T(8,128)(2,1)S(1)}, bf16[256,512]{1,0:T(8,128)(2,1)S(1)}, u32[]{:S(2)}, u32[]{:S(2)}) collective-permute-start(bf16[256,512]{1,0:T(8,128)(2,1)S(1)} %shard_map.52.refs_0_), channel_id=1, source_target_pairs={{0,16},{1,17},{2,18},{3,19},{4,68},{5,69},{6,70},{7,71},{8,24},{9,... | collective-permute-start | bytes 786440 | tf_op jit(solution)/shard_map/ppermute | solution.py:44
  80.0 2.6 %collective-permute-start.16 = (bf16[256,512]{1,0:T(8,128)(2,1)S(1)}, bf16[256,512]{1,0:T(8,128)(2,1)S(1)}, u32[]{:S(2)}, u32[]{:S(2)}) collective-permute-start(bf16[256,512]{1,0:T(8,128)(2,1)S(1)} %shard_map.52.refs_0_), channel_id=1, source_target_pairs={{0,64},{1,65},{2,66},{3,67},{4,20},{5,21},{6,22},{7,23},{8,72},{9,... | collective-permute-start | bytes 786440 | tf_op jit(solution)/shard_map/ppermute | solution.py:39
  83.2 2.1 %collective-permute-start.14 = (bf16[256,512]{1,0:T(8,128)(2,1)S(1)}, bf16[256,512]{1,0:T(8,128)(2,1)S(1)}, u32[]{:S(2)}, u32[]{:S(2)}) collective-permute-start(bf16[256,512]{1,0:T(8,128)(2,1)S(1)} %shard_map.52.refs_0_), channel_id=1, source_target_pairs={{0,96},{1,97},{2,98},{3,99},{4,28},{5,29},{6,30},{7,31},{8,104},{9... | collective-permute-start | bytes 786440 | tf_op jit(solution)/shard_map/ppermute | solution.py:39
  85.3 1.6 %collective-permute-start.21 = (bf16[256,512]{1,0:T(8,128)(2,1)S(1)}, bf16[256,512]{1,0:T(8,128)(2,1)S(1)}, u32[]{:S(2)}, u32[]{:S(2)}) collective-permute-start(bf16[256,512]{1,0:T(8,128)(2,1)S(1)} %shard_map.52.refs_0_), channel_id=1, source_target_pairs={{0,2},{1,3},{2,0},{3,1},{4,6},{5,7},{6,4},{7,5},{8,10},{9,11},{10,... | collective-permute-start | bytes 786440 | tf_op jit(solution)/shard_map/ppermute | solution.py:35
  88.3 2.3 %collective-permute-done.15 = bf16[256,512]{1,0:T(8,128)(2,1)S(1)} collective-permute-done((bf16[256,512]{1,0:T(8,128)(2,1)S(1)}, bf16[256,512]{1,0:T(8,128)(2,1)S(1)}, u32[]{:S(2)}, u32[]{:S(2)}) %collective-permute-start.15) | collective-permute-done | bytes 262176 | tf_op jit(solution)/shard_map/ppermute | solution.py:39
  90.8 1.9 %collective-permute-start.19 = (bf16[1024,512]{1,0:T(8,128)(2,1)S(1)}, bf16[1024,512]{1,0:T(8,128)(2,1)S(1)}, u32[]{:S(2)}, u32[]{:S(2)}) collective-permute-start(bf16[1024,512]{1,0:T(8,128)(2,1)S(1)} %constant_dynamic-update-slice_fusion.refs_8_), channel_id=1, source_target_pairs={{0,8},{1,9},{2,10},{3,11},{4,36},{5,37},{6,38},{7,39},{8,16},{9,17... | collective-permute-start | bytes 3145736 | tf_op jit(solution)/shard_map/ppermute | solution.py:44
  94.1 3.5 %collective-permute-done.21.refs_2_ = bf16[256,512]{1,0:T(8,128)(2,1)S(1)} collective-permute-done((bf16[256,512]{1,0:T(8,128)(2,1)S(1)}, bf16[256,512]{1,0:T(8,128)(2,1)S(1)}, u32[]{:S(2)}, u32[]{:S(2)}) %collective-permute-start.21) | collective-permute-done | bytes 262176 | tf_op jit(solution)/shard_map/ppermute | solution.py:35
  97.7 2.3 %collective-permute-done.20.refs_1_ = bf16[256,512]{1,0:T(8,128)(2,1)S(1)} collective-permute-done((bf16[256,512]{1,0:T(8,128)(2,1)S(1)}, bf16[256,512]{1,0:T(8,128)(2,1)S(1)}, u32[]{:S(2)}, u32[]{:S(2)}) %collective-permute-start.20) | collective-permute-done | bytes 262176 | tf_op jit(solution)/shard_map/ppermute | solution.py:35
  99.9 1.6 %collective-permute-start.24 = (bf16[256,512]{1,0:T(8,128)(2,1)S(1)}, bf16[256,512]{1,0:T(8,128)(2,1)S(1)}, u32[]{:S(2)}, u32[]{:S(2)}) collective-permute-start(bf16[256,512]{1,0:T(8,128)(2,1)S(1)} %collective-permute-done.20.refs_1_), channel_id=1, source_target_pairs={{0,4},{1,5},{2,6},{3,7},{4,0},{5,1},{6,2},{7,3},{8,12},{9,13},{10,... | collective-permute-start | bytes 786440 | tf_op jit(solution)/shard_map/ppermute | solution.py:31
  103.0 1.0 collective-permute-start.28
  104.1 1.6 %collective-permute-start.27 = (bf16[256,512]{1,0:T(8,128)(2,1)S(1)}, bf16[256,512]{1,0:T(8,128)(2,1)S(1)}, u32[]{:S(2)}, u32[]{:S(2)}) collective-permute-start(bf16[256,512]{1,0:T(8,128)(2,1)S(1)} %collective-permute-done.17.refs_9_), channel_id=1, source_target_pairs={{0,96},{1,97},{2,98},{3,99},{4,28},{5,29},{6,30},{7,31},{8,104},{9... | collective-permute-start | bytes 786440 | tf_op jit(solution)/shard_map/ppermute | solution.py:39
  105.7 4.0 %collective-permute-done.29.refs_12_ = bf16[256,512]{1,0:T(8,128)(2,1)S(1)} collective-permute-done((bf16[256,512]{1,0:T(8,128)(2,1)S(1)}, bf16[256,512]{1,0:T(8,128)(2,1)S(1)}, u32[]{:S(2)}, u32[]{:S(2)}) %collective-permute-start.29) | collective-permute-done | bytes 262176 | tf_op jit(solution)/shard_map/ppermute | solution.py:39
  109.7 3.7 %collective-permute-start.23 = (bf16[256,512]{1,0:T(8,128)(2,1)S(1)}, bf16[256,512]{1,0:T(8,128)(2,1)S(1)}, u32[]{:S(2)}, u32[]{:S(2)}) collective-permute-start(bf16[256,512]{1,0:T(8,128)(2,1)S(1)} %shard_map.52.refs_0_), channel_id=1, source_target_pairs={{0,4},{1,5},{2,6},{3,7},{4,0},{5,1},{6,2},{7,3},{8,12},{9,13},{10,... | collective-permute-start | bytes 786440 | tf_op jit(solution)/shard_map/ppermute | solution.py:31
  113.4 1.2 collective-permute-done.23.refs_4_
  114.6 2.3 %shard_map.53 = (f32[256,512]{1,0:T(8,128)S(1)}, bf16[256,4096]{1,0:T(8,128)(2,1)S(1)}, bf16[4096,512]{1,0:T(8,128)(2,1)S(1)}) custom-call(s32[4]{0:T(128)S(1)} %pad_add_fusion.1.where, bf16[256,512]{1,0:T(8,128)(2,1)S(1)} %shard_map.52.refs_0_, bf16[256,512]{1,0:T(8,128)(2,1)S(1)} %collective-permute-done.20.refs_1_, ...), custom_call_target="tpu_custom_call" | custom-call | flops 536870912 | bytes 10485760 | tf_op jit(solution)/shard_map/pallas_call | solution.py:277
  116.9 2.3 %shard_map.54 = (f32[256,512]{1,0:T(8,128)S(1)}, bf16[256,512]{1,0:T(8,128)(2,1)S(1)}, bf16[4096,512]{1,0:T(8,128)(2,1)S(1)}) custom-call(s32[4]{0:T(128)S(1)} %pad_add_fusion.1.where, s32[2,32,32]{2,1,0:T(8,128)S(1)} %copy-done.2, bf16[1024,512]{1,0:T(8,128)(2,1)S(1)} %collective-permute-done.18.one, ...), custom_call_target="tpu_custom_call", output_to_operand_aliasing={{2}: (6, {})} | custom-call | flops 536870912 | bytes 8388608 | tf_op jit(solution)/shard_map/pallas_call | solution.py:277
  119.5 3.3 %collective-permute-start.32 = (bf16[256,512]{1,0:T(8,128)(2,1)S(1)}, bf16[256,512]{1,0:T(8,128)(2,1)S(1)}, u32[]{:S(2)}, u32[]{:S(2)}) collective-permute-start(bf16[256,512]{1,0:T(8,128)(2,1)S(1)} %get-tuple-element.76.refs_0_), channel_id=1, source_target_pairs={{0,2},{1,3},{2,0},{3,1},{4,6},{5,7},{6,4},{7,5},{8,10},{9,11},{10,... | collective-permute-start | bytes 786440 | tf_op jit(solution)/shard_map/ppermute | solution.py:35
  122.8 1.0 collective-permute-start.36
  123.7 4.2 %collective-permute-done.34.refs_3_ = bf16[256,512]{1,0:T(8,128)(2,1)S(1)} collective-permute-done((bf16[256,512]{1,0:T(8,128)(2,1)S(1)}, bf16[256,512]{1,0:T(8,128)(2,1)S(1)}, u32[]{:S(2)}, u32[]{:S(2)}) %collective-permute-start.34) | collective-permute-done | bytes 262176 | tf_op jit(solution)/shard_map/ppermute | solution.py:35
  127.9 1.2 collective-permute-start.35
  129.2 5.2 %collective-permute-done.32.refs_2_ = bf16[256,512]{1,0:T(8,128)(2,1)S(1)} collective-permute-done((bf16[256,512]{1,0:T(8,128)(2,1)S(1)}, bf16[256,512]{1,0:T(8,128)(2,1)S(1)}, u32[]{:S(2)}, u32[]{:S(2)}) %collective-permute-start.32) | collective-permute-done | bytes 262176 | tf_op jit(solution)/shard_map/ppermute | solution.py:35
  134.4 1.2 collective-permute-start.33
  135.6 1.4 shard_map.55.refs_3_
  138.6 1.2 collective-permute-done.37.refs_6_
  139.7 1.7 %shard_map.57 = f32[128,1024]{1,0:T(8,128)} custom-call(s32[4]{0:T(128)S(1)} %pad_add_fusion.1.where, bf16[256,512]{1,0:T(8,128)(2,1)S(1)} %collective-permute-done.31.refs_0_, bf16[256,512]{1,0:T(8,128)(2,1)S(1)} %collective-permute-done.33.refs_1_, bf16[256,512]{1,0:T(8,128)(2,1)S(1)} %collective-permute-done.35.refs_2_, ...), custom_call_target="tpu_custom_call" | custom-call | flops 201326592 | bytes 3145728 | tf_op jit(solution)/shard_map/pallas_call | solution.py:277
  (61 shorter events, 11.1 us)
Async XLA Ops:
  0.0 5.9 %copy-start = (s32[32,8]{0,1:T(8,128)S(1)}, s32[32,8]{0,1:T(8,128)}, u32[]{:S(2)}) copy-start(s32[32,8]{0,1:T(8,128)} %param.5) | copy-start | bytes 3076
  0.0 27.0 %copy-start.1 = (s32[2,32,32]{2,1,0:T(8,128)S(1)}, s32[2,32,32]{2,1,0:T(8,128)}, u32[]{:S(2)}) copy-start(s32[2,32,32]{2,1,0:T(8,128)} %keep_d.11) | copy-start | bytes 24580
  0.0 6.7 %collective-permute-start.1 = (bf16[128,256]{1,0:T(8,128)(2,1)}, bf16[128,256]{1,0:T(8,128)(2,1)S(1)}, u32[]{:S(2)}, u32[]{:S(2)}) collective-permute-start(bf16[128,256]{1,0:T(8,128)(2,1)} %param.4), channel_id=1, source_target_pairs={{0,2},{1,3},{2,0},{3,1},{4,6},{5,7},{6,4},{7,5},{8,10},{9,11},{10,... | collective-permute-start | bytes 196616 | tf_op jit(solution)/shard_map/ppermute | solution.py:35
  4.4 3.7 %collective-permute-start = (bf16[128,256]{1,0:T(8,128)(2,1)}, bf16[128,256]{1,0:T(8,128)(2,1)S(1)}, u32[]{:S(2)}, u32[]{:S(2)}) collective-permute-start(bf16[128,256]{1,0:T(8,128)(2,1)} %param.4), channel_id=1, source_target_pairs={{0,3},{1,0},{2,1},{3,2},{4,7},{5,4},{6,5},{7,6},{8,11},{9,8},{10,9... | collective-permute-start | bytes 196616 | tf_op jit(solution)/shard_map/ppermute | solution.py:35
  4.9 4.5 %collective-permute-start.2 = (bf16[128,256]{1,0:T(8,128)(2,1)}, bf16[128,256]{1,0:T(8,128)(2,1)S(1)}, u32[]{:S(2)}, u32[]{:S(2)}) collective-permute-start(bf16[128,256]{1,0:T(8,128)(2,1)} %param.4), channel_id=1, source_target_pairs={{0,1},{1,2},{2,3},{3,0},{4,5},{5,6},{6,7},{7,4},{8,9},{9,10},{10,1... | collective-permute-start | bytes 196616 | tf_op jit(solution)/shard_map/ppermute | solution.py:35
  10.3 6.9 %collective-permute-start.5 = (bf16[128,1024]{1,0:T(8,128)(2,1)S(1)}, bf16[128,1024]{1,0:T(8,128)(2,1)S(1)}, u32[]{:S(2)}, u32[]{:S(2)}) collective-permute-start(bf16[128,1024]{1,0:T(8,128)(2,1)S(1)} %maximum_multiply_fusion), channel_id=1, source_target_pairs={{0,32},{1,33},{2,34},{3,35},{4,12},{5,13},{6,14},{7,15},{8,40},{9,... | collective-permute-start | bytes 786440 | tf_op jit(solution)/shard_map/ppermute | solution.py:39
  11.7 9.5 %collective-permute-start.4 = (bf16[128,1024]{1,0:T(8,128)(2,1)S(1)}, bf16[128,1024]{1,0:T(8,128)(2,1)S(1)}, u32[]{:S(2)}, u32[]{:S(2)}) collective-permute-start(bf16[128,1024]{1,0:T(8,128)(2,1)S(1)} %maximum_multiply_fusion), channel_id=1, source_target_pairs={{0,64},{1,65},{2,66},{3,67},{4,20},{5,21},{6,22},{7,23},{8,72},{9,... | collective-permute-start | bytes 786440 | tf_op jit(solution)/shard_map/ppermute | solution.py:39
  14.3 6.9 %collective-permute-start.3 = (bf16[128,1024]{1,0:T(8,128)(2,1)S(1)}, bf16[128,1024]{1,0:T(8,128)(2,1)S(1)}, u32[]{:S(2)}, u32[]{:S(2)}) collective-permute-start(bf16[128,1024]{1,0:T(8,128)(2,1)S(1)} %maximum_multiply_fusion), channel_id=1, source_target_pairs={{0,96},{1,97},{2,98},{3,99},{4,28},{5,29},{6,30},{7,31},{8,104},{9... | collective-permute-start | bytes 786440 | tf_op jit(solution)/shard_map/ppermute | solution.py:39
  21.2 5.8 %collective-permute-start.6 = (bf16[512,1024]{1,0:T(8,128)(2,1)S(1)}, bf16[512,1024]{1,0:T(8,128)(2,1)}, u32[]{:S(2)}, u32[]{:S(2)}) collective-permute-start(bf16[512,1024]{1,0:T(8,128)(2,1)S(1)} %pad_maximum_fusion.own0), channel_id=1, source_target_pairs={{0,4},{1,5},{2,6},{3,7},{4,0},{5,1},{6,2},{7,3},{8,12},{9,13},{10,... | collective-permute-start | bytes 3145736 | tf_op jit(solution)/shard_map/ppermute | solution.py:31
  24.3 15.2 %collective-permute-start.8 = (bf16[512,1024]{1,0:T(8,128)(2,1)S(1)}, bf16[512,1024]{1,0:T(8,128)(2,1)S(1)}, u32[]{:S(2)}, u32[]{:S(2)}) collective-permute-start(bf16[512,1024]{1,0:T(8,128)(2,1)S(1)} %pad_maximum_fusion.own0), channel_id=1, source_target_pairs={{0,8},{1,9},{2,10},{3,11},{4,36},{5,37},{6,38},{7,39},{8,16},{9,17... | collective-permute-start | bytes 3145736 | tf_op jit(solution)/shard_map/ppermute | solution.py:44
  25.9 13.9 %collective-permute-start.7 = (bf16[512,1024]{1,0:T(8,128)(2,1)S(1)}, bf16[512,1024]{1,0:T(8,128)(2,1)S(1)}, u32[]{:S(2)}, u32[]{:S(2)}) collective-permute-start(bf16[512,1024]{1,0:T(8,128)(2,1)S(1)} %pad_maximum_fusion.own0), channel_id=1, source_target_pairs={{0,24},{1,25},{2,26},{3,27},{4,100},{5,101},{6,102},{7,103},{8,0},... | collective-permute-start | bytes 3145736 | tf_op jit(solution)/shard_map/ppermute | solution.py:44
  39.8 9.5 %collective-permute-start.9 = (bf16[512,1024]{1,0:T(8,128)(2,1)S(1)}, bf16[512,1024]{1,0:T(8,128)(2,1)S(1)}, u32[]{:S(2)}, u32[]{:S(2)}) collective-permute-start(bf16[512,1024]{1,0:T(8,128)(2,1)S(1)} %collective-permute-done.7.own1), channel_id=1, source_target_pairs={{0,4},{1,5},{2,6},{3,7},{4,0},{5,1},{6,2},{7,3},{8,12},{9,13},{10,... | collective-permute-start | bytes 3145736 | tf_op jit(solution)/shard_map/ppermute | solution.py:31
  40.7 8.6 %collective-permute-start.10 = (bf16[512,1024]{1,0:T(8,128)(2,1)S(1)}, bf16[512,1024]{1,0:T(8,128)(2,1)S(1)}, u32[]{:S(2)}, u32[]{:S(2)}) collective-permute-start(bf16[512,1024]{1,0:T(8,128)(2,1)S(1)} %collective-permute-done.8.own3), channel_id=1, source_target_pairs={{0,4},{1,5},{2,6},{3,7},{4,0},{5,1},{6,2},{7,3},{8,12},{9,13},{10,... | collective-permute-start | bytes 3145736 | tf_op jit(solution)/shard_map/ppermute | solution.py:31
  40.7 15.4 %collective-permute-start.11 = (bf16[512,1024]{1,0:T(8,128)(2,1)S(1)}, bf16[512,1024]{1,0:T(8,128)(2,1)S(1)}, u32[]{:S(2)}, u32[]{:S(2)}) collective-permute-start(bf16[512,1024]{1,0:T(8,128)(2,1)S(1)} %pad_maximum_fusion.own0), channel_id=1, source_target_pairs={{0,16},{1,17},{2,18},{3,19},{4,68},{5,69},{6,70},{7,71},{8,24},{9,... | collective-permute-start | bytes 3145736 | tf_op jit(solution)/shard_map/ppermute | solution.py:44
  56.2 7.0 %copy-start.2 = (s32[2,32,32]{2,1,0:T(8,128)S(1)}, s32[2,32,32]{2,1,0:T(8,128)}, u32[]{:S(2)}) copy-start(s32[2,32,32]{2,1,0:T(8,128)} %keep_s.3) | copy-start | bytes 24580
  56.2 7.0 %collective-permute-start.12 = (bf16[512,1024]{1,0:T(8,128)(2,1)S(1)}, bf16[512,1024]{1,0:T(8,128)(2,1)S(1)}, u32[]{:S(2)}, u32[]{:S(2)}) collective-permute-start(bf16[512,1024]{1,0:T(8,128)(2,1)S(1)} %collective-permute-done.11.own2), channel_id=1, source_target_pairs={{0,4},{1,5},{2,6},{3,7},{4,0},{5,1},{6,2},{7,3},{8,12},{9,13},{10,... | collective-permute-start | bytes 3145736 | tf_op jit(solution)/shard_map/ppermute | solution.py:31
  72.7 2.7 %collective-permute-start.13 = (bf16[256,2048]{1,0:T(8,128)(2,1)S(1)}, bf16[256,2048]{1,0:T(8,128)(2,1)S(1)}, u32[]{:S(2)}, u32[]{:S(2)}) collective-permute-start(bf16[256,2048]{1,0:T(8,128)(2,1)S(1)} %get-tuple-element.59.low), channel_id=1, source_target_pairs={{0,4},{1,5},{2,6},{3,7},{4,0},{5,1},{6,2},{7,3},{8,12},{9,13},{10,... | collective-permute-start | bytes 3145736 | tf_op jit(solution)/shard_map/ppermute | solution.py:31
  77.3 8.0 %collective-permute-start.17 = (bf16[256,512]{1,0:T(8,128)(2,1)S(1)}, bf16[256,512]{1,0:T(8,128)(2,1)S(1)}, u32[]{:S(2)}, u32[]{:S(2)}) collective-permute-start(bf16[256,512]{1,0:T(8,128)(2,1)S(1)} %shard_map.52.refs_0_), channel_id=1, source_target_pairs={{0,16},{1,17},{2,18},{3,19},{4,68},{5,69},{6,70},{7,71},{8,24},{9,... | collective-permute-start | bytes 786440 | tf_op jit(solution)/shard_map/ppermute | solution.py:44
  80.0 7.8 %collective-permute-start.16 = (bf16[256,512]{1,0:T(8,128)(2,1)S(1)}, bf16[256,512]{1,0:T(8,128)(2,1)S(1)}, u32[]{:S(2)}, u32[]{:S(2)}) collective-permute-start(bf16[256,512]{1,0:T(8,128)(2,1)S(1)} %shard_map.52.refs_0_), channel_id=1, source_target_pairs={{0,64},{1,65},{2,66},{3,67},{4,20},{5,21},{6,22},{7,23},{8,72},{9,... | collective-permute-start | bytes 786440 | tf_op jit(solution)/shard_map/ppermute | solution.py:39
  82.6 8.0 %collective-permute-start.15 = (bf16[256,512]{1,0:T(8,128)(2,1)S(1)}, bf16[256,512]{1,0:T(8,128)(2,1)S(1)}, u32[]{:S(2)}, u32[]{:S(2)}) collective-permute-start(bf16[256,512]{1,0:T(8,128)(2,1)S(1)} %shard_map.52.refs_0_), channel_id=1, source_target_pairs={{0,32},{1,33},{2,34},{3,35},{4,12},{5,13},{6,14},{7,15},{8,40},{9,... | collective-permute-start | bytes 786440 | tf_op jit(solution)/shard_map/ppermute | solution.py:39
  83.2 7.5 %collective-permute-start.14 = (bf16[256,512]{1,0:T(8,128)(2,1)S(1)}, bf16[256,512]{1,0:T(8,128)(2,1)S(1)}, u32[]{:S(2)}, u32[]{:S(2)}) collective-permute-start(bf16[256,512]{1,0:T(8,128)(2,1)S(1)} %shard_map.52.refs_0_), channel_id=1, source_target_pairs={{0,96},{1,97},{2,98},{3,99},{4,28},{5,29},{6,30},{7,31},{8,104},{9... | collective-permute-start | bytes 786440 | tf_op jit(solution)/shard_map/ppermute | solution.py:39
  85.3 8.8 %collective-permute-start.22 = (bf16[256,512]{1,0:T(8,128)(2,1)S(1)}, bf16[256,512]{1,0:T(8,128)(2,1)S(1)}, u32[]{:S(2)}, u32[]{:S(2)}) collective-permute-start(bf16[256,512]{1,0:T(8,128)(2,1)S(1)} %shard_map.52.refs_0_), channel_id=1, source_target_pairs={{0,1},{1,2},{2,3},{3,0},{4,5},{5,6},{6,7},{7,4},{8,9},{9,10},{10,1... | collective-permute-start | bytes 786440 | tf_op jit(solution)/shard_map/ppermute | solution.py:35
  85.3 12.3 %collective-permute-start.21 = (bf16[256,512]{1,0:T(8,128)(2,1)S(1)}, bf16[256,512]{1,0:T(8,128)(2,1)S(1)}, u32[]{:S(2)}, u32[]{:S(2)}) collective-permute-start(bf16[256,512]{1,0:T(8,128)(2,1)S(1)} %shard_map.52.refs_0_), channel_id=1, source_target_pairs={{0,2},{1,3},{2,0},{3,1},{4,6},{5,7},{6,4},{7,5},{8,10},{9,11},{10,... | collective-permute-start | bytes 786440 | tf_op jit(solution)/shard_map/ppermute | solution.py:35
  87.8 12.1 %collective-permute-start.20 = (bf16[256,512]{1,0:T(8,128)(2,1)S(1)}, bf16[256,512]{1,0:T(8,128)(2,1)S(1)}, u32[]{:S(2)}, u32[]{:S(2)}) collective-permute-start(bf16[256,512]{1,0:T(8,128)(2,1)S(1)} %shard_map.52.refs_0_), channel_id=1, source_target_pairs={{0,3},{1,0},{2,1},{3,2},{4,7},{5,4},{6,5},{7,6},{8,11},{9,8},{10,9... | collective-permute-start | bytes 786440 | tf_op jit(solution)/shard_map/ppermute | solution.py:35
  90.8 26.1 %collective-permute-start.19 = (bf16[1024,512]{1,0:T(8,128)(2,1)S(1)}, bf16[1024,512]{1,0:T(8,128)(2,1)S(1)}, u32[]{:S(2)}, u32[]{:S(2)}) collective-permute-start(bf16[1024,512]{1,0:T(8,128)(2,1)S(1)} %constant_dynamic-update-slice_fusion.refs_8_), channel_id=1, source_target_pairs={{0,8},{1,9},{2,10},{3,11},{4,36},{5,37},{6,38},{7,39},{8,16},{9,17... | collective-permute-start | bytes 3145736 | tf_op jit(solution)/shard_map/ppermute | solution.py:44
  92.6 24.2 %collective-permute-start.18 = (bf16[1024,512]{1,0:T(8,128)(2,1)S(1)}, bf16[1024,512]{1,0:T(8,128)(2,1)S(1)}, u32[]{:S(2)}, u32[]{:S(2)}) collective-permute-start(bf16[1024,512]{1,0:T(8,128)(2,1)S(1)} %constant_dynamic-update-slice_fusion.refs_8_), channel_id=1, source_target_pairs={{0,24},{1,25},{2,26},{3,27},{4,100},{5,101},{6,102},{7,103},{8,0},... | collective-permute-start | bytes 3145736 | tf_op jit(solution)/shard_map/ppermute | solution.py:44
  99.9 2.7 %collective-permute-start.24 = (bf16[256,512]{1,0:T(8,128)(2,1)S(1)}, bf16[256,512]{1,0:T(8,128)(2,1)S(1)}, u32[]{:S(2)}, u32[]{:S(2)}) collective-permute-start(bf16[256,512]{1,0:T(8,128)(2,1)S(1)} %collective-permute-done.20.refs_1_), channel_id=1, source_target_pairs={{0,4},{1,5},{2,6},{3,7},{4,0},{5,1},{6,2},{7,3},{8,12},{9,13},{10,... | collective-permute-start | bytes 786440 | tf_op jit(solution)/shard_map/ppermute | solution.py:31
  101.5 1.5 %collective-permute-start.25 = (bf16[256,512]{1,0:T(8,128)(2,1)S(1)}, bf16[256,512]{1,0:T(8,128)(2,1)S(1)}, u32[]{:S(2)}, u32[]{:S(2)}) collective-permute-start(bf16[256,512]{1,0:T(8,128)(2,1)S(1)} %collective-permute-done.21.refs_2_), channel_id=1, source_target_pairs={{0,4},{1,5},{2,6},{3,7},{4,0},{5,1},{6,2},{7,3},{8,12},{9,13},{10,... | collective-permute-start | bytes 786440 | tf_op jit(solution)/shard_map/ppermute | solution.py:31
  101.5 2.6 %collective-permute-start.26 = (bf16[256,512]{1,0:T(8,128)(2,1)S(1)}, bf16[256,512]{1,0:T(8,128)(2,1)S(1)}, u32[]{:S(2)}, u32[]{:S(2)}) collective-permute-start(bf16[256,512]{1,0:T(8,128)(2,1)S(1)} %collective-permute-done.22.refs_3_), channel_id=1, source_target_pairs={{0,4},{1,5},{2,6},{3,7},{4,0},{5,1},{6,2},{7,3},{8,12},{9,13},{10,... | collective-permute-start | bytes 786440 | tf_op jit(solution)/shard_map/ppermute | solution.py:31
  102.7 7.0 %collective-permute-start.29 = (bf16[256,512]{1,0:T(8,128)(2,1)S(1)}, bf16[256,512]{1,0:T(8,128)(2,1)S(1)}, u32[]{:S(2)}, u32[]{:S(2)}) collective-permute-start(bf16[256,512]{1,0:T(8,128)(2,1)S(1)} %collective-permute-done.17.refs_9_), channel_id=1, source_target_pairs={{0,32},{1,33},{2,34},{3,35},{4,12},{5,13},{6,14},{7,15},{8,40},{9,... | collective-permute-start | bytes 786440 | tf_op jit(solution)/shard_map/ppermute | solution.py:39
  103.0 10.4 %collective-permute-start.28 = (bf16[256,512]{1,0:T(8,128)(2,1)S(1)}, bf16[256,512]{1,0:T(8,128)(2,1)S(1)}, u32[]{:S(2)}, u32[]{:S(2)}) collective-permute-start(bf16[256,512]{1,0:T(8,128)(2,1)S(1)} %collective-permute-done.17.refs_9_), channel_id=1, source_target_pairs={{0,64},{1,65},{2,66},{3,67},{4,20},{5,21},{6,22},{7,23},{8,72},{9,... | collective-permute-start | bytes 786440 | tf_op jit(solution)/shard_map/ppermute | solution.py:39
  104.1 9.4 %collective-permute-start.27 = (bf16[256,512]{1,0:T(8,128)(2,1)S(1)}, bf16[256,512]{1,0:T(8,128)(2,1)S(1)}, u32[]{:S(2)}, u32[]{:S(2)}) collective-permute-start(bf16[256,512]{1,0:T(8,128)(2,1)S(1)} %collective-permute-done.17.refs_9_), channel_id=1, source_target_pairs={{0,96},{1,97},{2,98},{3,99},{4,28},{5,29},{6,30},{7,31},{8,104},{9... | collective-permute-start | bytes 786440 | tf_op jit(solution)/shard_map/ppermute | solution.py:39
  109.7 4.9 %collective-permute-start.23 = (bf16[256,512]{1,0:T(8,128)(2,1)S(1)}, bf16[256,512]{1,0:T(8,128)(2,1)S(1)}, u32[]{:S(2)}, u32[]{:S(2)}) collective-permute-start(bf16[256,512]{1,0:T(8,128)(2,1)S(1)} %shard_map.52.refs_0_), channel_id=1, source_target_pairs={{0,4},{1,5},{2,6},{3,7},{4,0},{5,1},{6,2},{7,3},{8,12},{9,13},{10,... | collective-permute-start | bytes 786440 | tf_op jit(solution)/shard_map/ppermute | solution.py:31
  119.2 8.8 %collective-permute-start.34 = (bf16[256,512]{1,0:T(8,128)(2,1)S(1)}, bf16[256,512]{1,0:T(8,128)(2,1)S(1)}, u32[]{:S(2)}, u32[]{:S(2)}) collective-permute-start(bf16[256,512]{1,0:T(8,128)(2,1)S(1)} %get-tuple-element.76.refs_0_), channel_id=1, source_target_pairs={{0,1},{1,2},{2,3},{3,0},{4,5},{5,6},{6,7},{7,4},{8,9},{9,10},{10,1... | collective-permute-start | bytes 786440 | tf_op jit(solution)/shard_map/ppermute | solution.py:35
  119.5 14.9 %collective-permute-start.32 = (bf16[256,512]{1,0:T(8,128)(2,1)S(1)}, bf16[256,512]{1,0:T(8,128)(2,1)S(1)}, u32[]{:S(2)}, u32[]{:S(2)}) collective-permute-start(bf16[256,512]{1,0:T(8,128)(2,1)S(1)} %get-tuple-element.76.refs_0_), channel_id=1, source_target_pairs={{0,2},{1,3},{2,0},{3,1},{4,6},{5,7},{6,4},{7,5},{8,10},{9,11},{10,... | collective-permute-start | bytes 786440 | tf_op jit(solution)/shard_map/ppermute | solution.py:35
  122.8 12.9 %collective-permute-start.30 = (bf16[256,512]{1,0:T(8,128)(2,1)S(1)}, bf16[256,512]{1,0:T(8,128)(2,1)S(1)}, u32[]{:S(2)}, u32[]{:S(2)}) collective-permute-start(bf16[256,512]{1,0:T(8,128)(2,1)S(1)} %get-tuple-element.76.refs_0_), channel_id=1, source_target_pairs={{0,3},{1,0},{2,1},{3,2},{4,7},{5,4},{6,5},{7,6},{8,11},{9,8},{10,9... | collective-permute-start | bytes 786440 | tf_op jit(solution)/shard_map/ppermute | solution.py:35
  122.8 12.9 %collective-permute-start.36 = (bf16[256,512]{1,0:T(8,128)(2,1)S(1)}, bf16[256,512]{1,0:T(8,128)(2,1)S(1)}, u32[]{:S(2)}, u32[]{:S(2)}) collective-permute-start(bf16[256,512]{1,0:T(8,128)(2,1)S(1)} %get-tuple-element.76.refs_0_), channel_id=1, source_target_pairs={{0,4},{1,5},{2,6},{3,7},{4,0},{5,1},{6,2},{7,3},{8,12},{9,13},{10,... | collective-permute-start | bytes 786440 | tf_op jit(solution)/shard_map/ppermute | solution.py:31
  127.9 9.1 %collective-permute-start.35 = (bf16[256,512]{1,0:T(8,128)(2,1)S(1)}, bf16[256,512]{1,0:T(8,128)(2,1)S(1)}, u32[]{:S(2)}, u32[]{:S(2)}) collective-permute-start(bf16[256,512]{1,0:T(8,128)(2,1)S(1)} %collective-permute-done.34.refs_3_), channel_id=1, source_target_pairs={{0,4},{1,5},{2,6},{3,7},{4,0},{5,1},{6,2},{7,3},{8,12},{9,13},{10,... | collective-permute-start | bytes 786440 | tf_op jit(solution)/shard_map/ppermute | solution.py:31
  134.4 2.6 %collective-permute-start.33 = (bf16[256,512]{1,0:T(8,128)(2,1)S(1)}, bf16[256,512]{1,0:T(8,128)(2,1)S(1)}, u32[]{:S(2)}, u32[]{:S(2)}) collective-permute-start(bf16[256,512]{1,0:T(8,128)(2,1)S(1)} %collective-permute-done.32.refs_2_), channel_id=1, source_target_pairs={{0,4},{1,5},{2,6},{3,7},{4,0},{5,1},{6,2},{7,3},{8,12},{9,13},{10,... | collective-permute-start | bytes 786440 | tf_op jit(solution)/shard_map/ppermute | solution.py:31
  135.6 1.5 %collective-permute-start.31 = (bf16[256,512]{1,0:T(8,128)(2,1)S(1)}, bf16[256,512]{1,0:T(8,128)(2,1)S(1)}, u32[]{:S(2)}, u32[]{:S(2)}) collective-permute-start(bf16[256,512]{1,0:T(8,128)(2,1)S(1)} %collective-permute-done.30.refs_1_), channel_id=1, source_target_pairs={{0,4},{1,5},{2,6},{3,7},{4,0},{5,1},{6,2},{7,3},{8,12},{9,13},{10,... | collective-permute-start | bytes 786440 | tf_op jit(solution)/shard_map/ppermute | solution.py:31
  138.1 1.6 %collective-permute-start.37 = (f32[128,512]{1,0:T(8,128)S(1)}, f32[128,512]{1,0:T(8,128)S(1)}, u32[]{:S(2)}, u32[]{:S(2)}) collective-permute-start(f32[128,512]{1,0:T(8,128)S(1)} %shard_map.56), channel_id=1, source_target_pairs={{0,4},{1,5},{2,6},{3,7},{4,0},{5,1},{6,2},{7,3},{8,12},{9,13},{10,... | collective-permute-start | bytes 786440 | tf_op jit(solution)/shard_map/ppermute | solution.py:31
where the time goes:
time: 142 us; the launch traced here: 141 us
  starting transfers between devices  50.6 us (36%)
  waiting for transfers between devices  46.9 us (33%)
  Pallas kernels  41.9 us (30%)
    pallas_call x12, Pallas kernels, call(): pl.pallas_call(kernel, in_specs=[SMEM] * n_smem + [VMEM] * (len(ins) - n_...  41.9 us
    ppermute x9, waiting for transfers between devices, from_z(): lax.ppermute(a, AXES, pairs(lambda x, y, core, z: (x, y, core, z - d)))  18.6 us
    ppermute x14, starting transfers between devices, other_core(): lax.ppermute(a, AXES, pairs(lambda x, y, core, z: (x, y, 1 - core, z)))  15.1 us
    ppermute x9, starting transfers between devices, from_first(): lax.ppermute(a, AXES, pairs(lambda x, y, core, z: (x - d, y, core, z) if...  13 us
    ppermute x9, waiting for transfers between devices, from_first(): lax.ppermute(a, AXES, pairs(lambda x, y, core, z: (x - d, y, core, z) if...  13 us
    ppermute x9, starting transfers between devices, from_z(): lax.ppermute(a, AXES, pairs(lambda x, y, core, z: (x, y, core, z - d)))  11.6 us
    ppermute x6, waiting for transfers between devices, from_second(): lax.ppermute(a, AXES, pairs(lambda x, y, core, z: (x, y - d, core, z) if...  11.5 us
    ppermute x6, starting transfers between devices, from_second(): lax.ppermute(a, AXES, pairs(lambda x, y, core, z: (x, y - d, core, z) if...  10.8 us
  transfers between devices with their start and end apart: 38, of which 22 were waited for; matrix products, arithmetic and copies ran while one was open for 1% of the time, Pallas kernels for 18%

commit v1 on v0

--- a/solution.py
+++ b/solution.py
@@ -131,10 +131,18 @@
     some_columns(where, keep_d, 1, {0: other0}, {1: own1, 3: own3}, panel)
 
 
-def density_2(where, keep_d, own0, own1, own3, other1, other3, rows, _, __, panel, line):
+def density_2(where, keep_d, own0, own1, own3, other1, other3, rows, _, __, panel, line, some):
     other = {1: other1, 3: other3}
     some_rows(where, keep_d, rows, 1, other, line)
     some_columns(where, keep_d, 1, other, {0: own0, 1: own1, 3: own3}, panel)
+
+    @pl.loop(0, 3)
+    def _(part):
+        at = aligned(part + part // 2, 512)
+        some[:, at] = (
+            dot(line[:, :1024], panel[:1024, at])
+            + dot(line[:, 1536:3072], panel[1536:3072, at])
+            + dot(line[:, 3584:], panel[3584:, at]))
 
 
 def density_3(where, keep_d, own0, own1, own2, own3, other0, other1, other3, rows, _, __, panel, line):
@@ -144,22 +152,28 @@
     some_columns(where, keep_d, 1, {0: other0, 1: other1, 3: other3}, {2: own2}, panel)
 
 
-def first_square(where, keep_d, keep_s, own0, own1, own2, own3, other2, rows, _, __, panel, line, low, square, total):
+def first_square(where, keep_d, keep_s, own0, own1, own2, own3, other2, rows, some, _, __, panel, line, low, square, total):
     x, y, core, z = where[0], where[1], where[2], where[3]
     some_rows(where, keep_d, rows, 1, {2: other2}, line)
     some_columns(where, keep_d, 1, {2: other2}, {0: own0, 1: own1, 2: own2, 3: own3}, panel)
 
-    @pl.loop(0, 2)
-    def _(half):
-        value = dot(line[...], panel[:, aligned(half, 1024)])
+    def put(value, part):
         for t in range(2):
-            for u in range(8):
-                block = block_at(x, y, core, half * 8 + u)
+            for u in range(4):
+                block = block_at(x, y, core, part * 4 + u)
                 keep = keep_s[0, (x * 4 + y) * 2 + t, block].astype(jnp.float32)
                 piece = value[t * B:(t + 1) * B, u * B:(u + 1) * B] * keep
-                total[t * B:(t + 1) * B, aligned(half * 8 + u, B)] = piece
-                low[t * B:(t + 1) * B, aligned(half * 8 + u, B)] = piece.astype(jnp.bfloat16)
-
+                total[t * B:(t + 1) * B, aligned(part * 4 + u, B)] = piece
+                low[t * B:(t + 1) * B, aligned(part * 4 + u, B)] = piece.astype(jnp.bfloat16)
+
+    @pl.loop(0, 3)
+    def _(n):
+        part = n + n // 2
+        at = aligned(part, 512)
+        put(some[:, at] + dot(line[:, 1024:1536], panel[1024:1536, at])
+            + dot(line[:, 3072:3584], panel[3072:3584, at]), part)
+
+    put(dot(line[...], panel[:, 1024:1536]), 2)
     for t in range(4):
         square[:, t * B:(t + 1) * B] = total[:, aligned(column_at(where, t), B)]
 
@@ -220,24 +234,30 @@
     return total, copies
 
 
-def early_square(where, *refs):
-    own, other, near, far, (early, line, panel), (sems,) = (
-        refs[:4], refs[4:8], refs[8], refs[9:13], refs[13:16], refs[16:])
+def second_square_0(where, *refs):
+    own, other, near, (early, line, panel), (sems,) = refs[:4], refs[4:8], refs[8], refs[9:12], refs[12:]
     core, z = where[2], where[3]
     for d in range(4):
         for ref, kind in ((own[d], core), (other[d], 1 - core)):
             for t in range(4):
                 line[:, aligned(((z + d) & 3) * 8 + t * 2 + kind, B)] = ref[:, t * B:(t + 1) * B]
-    chips = [(near, i * ROWS, i, 0) for i in range(4)] + [(far[i], 0, i, 2) for i in range(4)]
-    value, copies = chips_times(where, line, chips, panel, sems)
+    value, copies = chips_times(where, line, [(near, i * ROWS, i, 0) for i in range(4)], panel, sems)
     early[...] = value
     for copy in copies:
         copy.wait()
 
 
-def second_square(where, keep_s, one, three, early, line, _, square, low, panel, sems):
+def second_square_1(where, one, three, early, line, _, out, panel, sems):
+    chips = [(ref, i * ROWS, i, j) for ref, j in ((one, 1), (three, 3)) for i in range(4)]
+    value, copies = chips_times(where, line, chips, panel, sems)
+    out[...] = early[...] + value
+    for copy in copies:
+        copy.wait()
+
+
+def second_square_2(where, keep_s, far0, far1, far2, far3, early, line, _, square, low, panel, sems):
     x, y, core, z = where[0], where[1], where[2], where[3]
-    chips = [(ref, i * ROWS, i, j) for ref, j in ((one, 1), (three, 3)) for i in range(4)]
+    chips = [(ref, 0, i, 2) for i, ref in enumerate((far0, far1, far2, far3))]
     value, copies = chips_times(where, line, chips, panel, sems)
     value = early[...] + value
     for t in range(2):
@@ -315,9 +335,9 @@
     panel, line = call(
         density_1, 2, [where, keep_density, own0, own1, own3, other0, rows, panel, line],
         out_shapes, [], 11 * pair_flops, 8 * MIB, {7: 0, 8: 1})
-    panel, line = call(
+    panel, line, some = call(
         density_2, 2, [where, keep_density, own0, own1, own3, other1, other3, rows, panel, line],
-        out_shapes, [], 7 * pair_flops, 8 * MIB, {8: 0, 9: 1})
+        out_shapes + [jax.ShapeDtypeStruct((ROWS, N // 2), jnp.float32)], [], 11 * pair_flops, 8 * MIB, {8: 0, 9: 1})
     panel, line, own2 = lax.optimization_barrier((panel, line, own2))
     other2 = other_core(own2)
     panel, line = call(
@@ -325,10 +345,10 @@
         out_shapes, [], 10 * pair_flops, 8 * MIB, {10: 0, 11: 1})
     panel, line, low, square = call(
         first_square, 3,
-        [where, keep_density, keep_square, own0, own1, own2, own3, other2, rows, panel, line],
+        [where, keep_density, keep_square, own0, own1, own2, own3, other2, rows, some, panel, line],
         out_shapes + [jax.ShapeDtypeStruct((ROWS, N // 2), jnp.bfloat16), full_block],
         [pltpu.VMEM((ROWS, N // 2), jnp.float32)],
-        4 * pair_flops + 4 * block_flops, 20 * MIB, {9: 0, 10: 1})
+        4 * pair_flops + 2 * block_flops, 20 * MIB, {10: 0, 11: 1})
 
     its = other_core(low)
     early, columns = call(
@@ -346,12 +366,15 @@
     own = [own0, own1, own2, own3]
     other = [other_core(part) for part in own]
     early, line, panel = call(
-        early_square, 1, [where, *own, *other, near, *far], [full_block, line_shape, panel_shape],
-        [pltpu.SemaphoreType.DMA((8,))], block_flops // 2, 10 * MIB)
+        second_square_0, 1, [where, *own, *other, near], [full_block, line_shape, panel_shape],
+        [pltpu.SemaphoreType.DMA((4,))], block_flops // 4, 8 * MIB)
+    early, panel = call(
+        second_square_1, 1, [where, one, three, early, line, panel], [full_block, panel_shape],
+        [pltpu.SemaphoreType.DMA((8,))], block_flops // 2, 8 * MIB, {5: 1})
     square, low, panel = call(
-        second_square, 2, [where, keep_square, one, three, early, line, panel],
+        second_square_2, 2, [where, keep_square, *far, early, line, panel],
         [full_block, low_block, panel_shape],
-        [pltpu.SemaphoreType.DMA((8,))], block_flops // 2, 8 * MIB, {6: 2})
+        [pltpu.SemaphoreType.DMA((4,))], block_flops // 4, 6 * MIB, {8: 2})
 
     own = gather(low, from_z)
     other = [other_core(part) for part in own]

time: 142 us -> 144 us (1.014)
  starting transfers between devices: 50.6 us -> 53.2 us
  waiting for transfers between devices: 46.9 us -> 45.1 us
    ppermute x6, waiting for transfers between devices: 11.5 us -> 9.73 us  [from_second(): lax.ppermute(a, AXES, pairs(lambda x, y, core, z: (x, y - d, core, z) if...]
    ppermute x14, waiting for transfers between devices: 3.85 us -> 2.33 us  [other_core(): lax.ppermute(a, AXES, pairs(lambda x, y, core, z: (x, y, 1 - core, z)))]
    pallas_call x12 -> x13, Pallas kernels: 41.9 us -> 43.1 us  [call(): pl.pallas_call(kernel, in_specs=[SMEM] * n_smem + [VMEM] * (len(ins) - n_...]
  transfers between devices with their start and end apart: 38 -> 38, of which waited for: 22 -> 19; matrix products, arithmetic and copies ran while one was open for 1% -> 1% of each run, Pallas kernels for 18% -> 21%
where the time goes in v1:
time: 144 us
  starting transfers between devices  53.2 us (37%)
  waiting for transfers between devices  45.1 us (31%)
  Pallas kernels  43.1 us (30%)
    pallas_call x13, Pallas kernels, call(): pl.pallas_call(kernel, in_specs=[SMEM] * n_smem + [VMEM] * (len(ins) - n_...  43.1 us
    ppermute x9, waiting for transfers between devices, from_z(): lax.ppermute(a, AXES, pairs(lambda x, y, core, z: (x, y, core, z - d)))  18.9 us
    ppermute x14, starting transfers between devices, other_core(): lax.ppermute(a, AXES, pairs(lambda x, y, core, z: (x, y, 1 - core, z)))  16.3 us
    ppermute x9, waiting for transfers between devices, from_first(): lax.ppermute(a, AXES, pairs(lambda x, y, core, z: (x - d, y, core, z) if...  14.1 us
    ppermute x9, starting transfers between devices, from_first(): lax.ppermute(a, AXES, pairs(lambda x, y, core, z: (x - d, y, core, z) if...  13.6 us
    ppermute x9, starting transfers between devices, from_z(): lax.ppermute(a, AXES, pairs(lambda x, y, core, z: (x, y, core, z - d)))  12.5 us
    ppermute x6, starting transfers between devices, from_second(): lax.ppermute(a, AXES, pairs(lambda x, y, core, z: (x, y - d, core, z) if...  10.8 us
    ppermute x6, waiting for transfers between devices, from_second(): lax.ppermute(a, AXES, pairs(lambda x, y, core, z: (x, y - d, core, z) if...  9.73 us
  transfers between devices with their start and end apart: 38, of which 19 were waited for; matrix products, arithmetic and copies ran while one was open for 1% of the time, Pallas kernels for 21%

profile of v1, /device:TPU:1, one launch (start us, length us, event | category | flops | bytes accessed | tf_op | source)
XLA Modules:
  0.0 143.6 jit_solution(8675227837320857092)
XLA Ops:
  0.0 4.4 %collective-permute-start.1 = (bf16[128,256]{1,0:T(8,128)(2,1)}, bf16[128,256]{1,0:T(8,128)(2,1)S(1)}, u32[]{:S(2)}, u32[]{:S(2)}) collective-permute-start(bf16[128,256]{1,0:T(8,128)(2,1)} %param.4), channel_id=1, source_target_pairs={{0,2},{1,3},{2,0},{3,1},{4,6},{5,7},{6,4},{7,5},{8,10},{9,11},{10,... | collective-permute-start | bytes 196616 | tf_op jit(solution)/shard_map/ppermute | solution.py:35
  6.7 1.4 %collective-permute-done = bf16[128,256]{1,0:T(8,128)(2,1)S(1)} collective-permute-done((bf16[128,256]{1,0:T(8,128)(2,1)}, bf16[128,256]{1,0:T(8,128)(2,1)S(1)}, u32[]{:S(2)}, u32[]{:S(2)}) %collective-permute-start) | collective-permute-done | bytes 65568 | tf_op jit(solution)/shard_map/ppermute | solution.py:35
  8.1 1.3 collective-permute-done.2
  10.3 1.4 collective-permute-start.5
  11.7 2.6 %collective-permute-start.4 = (bf16[128,1024]{1,0:T(8,128)(2,1)S(1)}, bf16[128,1024]{1,0:T(8,128)(2,1)S(1)}, u32[]{:S(2)}, u32[]{:S(2)}) collective-permute-start(bf16[128,1024]{1,0:T(8,128)(2,1)S(1)} %maximum_multiply_fusion), channel_id=1, source_target_pairs={{0,64},{1,65},{2,66},{3,67},{4,20},{5,21},{6,22},{7,23},{8,72},{9,... | collective-permute-start | bytes 786440 | tf_op jit(solution)/shard_map/ppermute | solution.py:39
  14.3 1.1 collective-permute-start.3
  15.4 1.8 %collective-permute-done.5 = bf16[128,1024]{1,0:T(8,128)(2,1)S(1)} collective-permute-done((bf16[128,1024]{1,0:T(8,128)(2,1)S(1)}, bf16[128,1024]{1,0:T(8,128)(2,1)S(1)}, u32[]{:S(2)}, u32[]{:S(2)}) %collective-permute-start.5) | collective-permute-done | bytes 262176 | tf_op jit(solution)/shard_map/ppermute | solution.py:39
  17.2 4.0 %collective-permute-done.4 = bf16[128,1024]{1,0:T(8,128)(2,1)S(1)} collective-permute-done((bf16[128,1024]{1,0:T(8,128)(2,1)S(1)}, bf16[128,1024]{1,0:T(8,128)(2,1)S(1)}, u32[]{:S(2)}, u32[]{:S(2)}) %collective-permute-start.4) | collective-permute-done | bytes 262176 | tf_op jit(solution)/shard_map/ppermute | solution.py:39
  21.2 3.1 %collective-permute-start.6 = (bf16[512,1024]{1,0:T(8,128)(2,1)S(1)}, bf16[512,1024]{1,0:T(8,128)(2,1)}, u32[]{:S(2)}, u32[]{:S(2)}) collective-permute-start(bf16[512,1024]{1,0:T(8,128)(2,1)S(1)} %pad_maximum_fusion.own0), channel_id=1, source_target_pairs={{0,4},{1,5},{2,6},{3,7},{4,0},{5,1},{6,2},{7,3},{8,12},{9,13},{10,... | collective-permute-start | bytes 3145736 | tf_op jit(solution)/shard_map/ppermute | solution.py:31
  24.3 1.6 %collective-permute-start.8 = (bf16[512,1024]{1,0:T(8,128)(2,1)S(1)}, bf16[512,1024]{1,0:T(8,128)(2,1)S(1)}, u32[]{:S(2)}, u32[]{:S(2)}) collective-permute-start(bf16[512,1024]{1,0:T(8,128)(2,1)S(1)} %pad_maximum_fusion.own0), channel_id=1, source_target_pairs={{0,8},{1,9},{2,10},{3,11},{4,36},{5,37},{6,38},{7,39},{8,16},{9,17... | collective-permute-start | bytes 3145736 | tf_op jit(solution)/shard_map/ppermute | solution.py:44
  25.9 1.1 collective-permute-start.7
  27.0 3.1 %shard_map.46 = (bf16[4096,2048]{1,0:T(8,128)(2,1)S(1)}, bf16[256,4096]{1,0:T(8,128)(2,1)S(1)}, bf16[256,1024]{1,0:T(8,128)(2,1)S(1)}) custom-call(s32[4]{0:T(128)S(1)} %pad_add_fusion.1.where, s32[2,32,32]{2,1,0:T(8,128)S(1)} %copy-done.1, bf16[512,1024]{1,0:T(8,128)(2,1)S(1)} %pad_maximum_fusion.own0, bf16[512,1024]{1,0:T(8,128)(2,1)} %collective-permute-done.6.other0), custom_call_target="tpu_custom_call" | custom-call | flops 67108864 | bytes 1048576 | tf_op jit(solution)/shard_map/pallas_call | solution.py:297
  30.1 9.3 %collective-permute-done.8.own3 = bf16[512,1024]{1,0:T(8,128)(2,1)S(1)} collective-permute-done((bf16[512,1024]{1,0:T(8,128)(2,1)S(1)}, bf16[512,1024]{1,0:T(8,128)(2,1)S(1)}, u32[]{:S(2)}, u32[]{:S(2)}) %collective-permute-start.8) | collective-permute-done | bytes 1048608 | tf_op jit(solution)/shard_map/ppermute | solution.py:44
  40.7 2.7 %collective-permute-start.11 = (bf16[512,1024]{1,0:T(8,128)(2,1)S(1)}, bf16[512,1024]{1,0:T(8,128)(2,1)S(1)}, u32[]{:S(2)}, u32[]{:S(2)}) collective-permute-start(bf16[512,1024]{1,0:T(8,128)(2,1)S(1)} %pad_maximum_fusion.own0), channel_id=1, source_target_pairs={{0,16},{1,17},{2,18},{3,19},{4,68},{5,69},{6,70},{7,71},{8,24},{9,... | collective-permute-start | bytes 3145736 | tf_op jit(solution)/shard_map/ppermute | solution.py:44
  43.4 5.9 %shard_map.47 = (bf16[4096,2048]{1,0:T(8,128)(2,1)S(1)}, bf16[256,4096]{1,0:T(8,128)(2,1)S(1)}) custom-call(s32[4]{0:T(128)S(1)} %pad_add_fusion.1.where, s32[2,32,32]{2,1,0:T(8,128)S(1)} %copy-done.1, bf16[512,1024]{1,0:T(8,128)(2,1)S(1)} %pad_maximum_fusion.own0, ...), custom_call_target="tpu_custom_call", output_to_operand_aliasing={{0}: (7, {}), {1}: (8, {})} | custom-call | flops 5905580032 | bytes 8388608 | tf_op jit(solution)/shard_map/pallas_call | solution.py:297
  49.4 8.0 %shard_map.48 = (bf16[4096,2048]{1,0:T(8,128)(2,1)S(1)}, bf16[256,4096]{1,0:T(8,128)(2,1)S(1)}, f32[256,2048]{1,0:T(8,128)S(1)}) custom-call(s32[4]{0:T(128)S(1)} %pad_add_fusion.1.where, s32[2,32,32]{2,1,0:T(8,128)S(1)} %copy-done.1, bf16[512,1024]{1,0:T(8,128)(2,1)S(1)} %pad_maximum_fusion.own0, ...), custom_call_target="tpu_custom_call", output_to_operand_aliasing={{0}: (8, {}), {1}: (9, {})} | custom-call | flops 5905580032 | bytes 8388608 | tf_op jit(solution)/shard_map/pallas_call | solution.py:297
  57.4 1.0 collective-permute-start.12
  58.5 5.7 %shard_map.49 = (bf16[4096,2048]{1,0:T(8,128)(2,1)S(1)}, bf16[256,4096]{1,0:T(8,128)(2,1)S(1)}) custom-call(s32[4]{0:T(128)S(1)} %pad_add_fusion.1.where, s32[2,32,32]{2,1,0:T(8,128)S(1)} %copy-done.1, bf16[512,1024]{1,0:T(8,128)(2,1)S(1)} %pad_maximum_fusion.own0, ...), custom_call_target="tpu_custom_call", output_to_operand_aliasing={{0}: (10, {}), {1}: (11, {})} | custom-call | flops 5368709120 | bytes 8388608 | tf_op jit(solution)/shard_map/pallas_call | solution.py:297
  64.2 7.1 %shard_map.50 = (bf16[4096,2048]{1,0:T(8,128)(2,1)S(1)}, bf16[256,4096]{1,0:T(8,128)(2,1)S(1)}, bf16[256,2048]{1,0:T(8,128)(2,1)S(1)}, f32[256,512]{1,0:T(8,128)S(1)}) custom-call(s32[4]{0:T(128)S(1)} %pad_add_fusion.1.where, s32[2,32,32]{2,1,0:T(8,128)S(1)} %copy-done.1, ...), custom_call_target="tpu_custom_call", output_to_operand_aliasing={{0}: (10, {}), {1}: (11, {})} | custom-call | flops 4294967296 | bytes 20971520 | tf_op jit(solution)/shard_map/pallas_call | solution.py:297
  71.4 2.3 %shard_map.51 = (f32[256,512]{1,0:T(8,128)S(1)}, bf16[4096,512]{1,0:T(8,128)(2,1)S(1)}) custom-call(s32[4]{0:T(128)S(1)} %pad_add_fusion.1.where, bf16[256,2048]{1,0:T(8,128)(2,1)S(1)} %get-tuple-element.63.low, bf16[4096,2048]{1,0:T(8,128)(2,1)S(1)} %get-tuple-element.64.panel), custom_call_target="tpu_custom_call" | custom-call | flops 536870912 | bytes 12582912 | tf_op jit(solution)/shard_map/pallas_call | solution.py:297
  74.0 1.8 %shard_map.52.refs_0_ = bf16[256,512]{1,0:T(8,128)(2,1)S(1)} custom-call(s32[4]{0:T(128)S(1)} %pad_add_fusion.1.where, s32[2,32,32]{2,1,0:T(8,128)S(1)} %copy-done.1, bf16[256,2048]{1,0:T(8,128)(2,1)S(1)} %collective-permute-done.13.its, bf16[4096,512]{1,0:T(8,128)(2,1)S(1)} %get-tuple-element.65.columns, f32[256,512]{1,0:T(8,128)S(1)} %get-tuple-element.66.early, ...), custom_call_target="tpu_custom_call" | custom-call | flops 536870912 | bytes 4194304 | tf_op jit(solution)/shard_map/pallas_call | solution.py:297
  75.8 2.7 %collective-permute-start.17 = (bf16[256,512]{1,0:T(8,128)(2,1)S(1)}, bf16[256,512]{1,0:T(8,128)(2,1)S(1)}, u32[]{:S(2)}, u32[]{:S(2)}) collective-permute-start(bf16[256,512]{1,0:T(8,128)(2,1)S(1)} %shard_map.52.refs_0_), channel_id=1, source_target_pairs={{0,16},{1,17},{2,18},{3,19},{4,68},{5,69},{6,70},{7,71},{8,24},{9,... | collective-permute-start | bytes 786440 | tf_op jit(solution)/shard_map/ppermute | solution.py:44
  78.6 1.7 %collective-permute-start.16 = (bf16[256,512]{1,0:T(8,128)(2,1)S(1)}, bf16[256,512]{1,0:T(8,128)(2,1)S(1)}, u32[]{:S(2)}, u32[]{:S(2)}) collective-permute-start(bf16[256,512]{1,0:T(8,128)(2,1)S(1)} %shard_map.52.refs_0_), channel_id=1, source_target_pairs={{0,64},{1,65},{2,66},{3,67},{4,20},{5,21},{6,22},{7,23},{8,72},{9,... | collective-permute-start | bytes 786440 | tf_op jit(solution)/shard_map/ppermute | solution.py:39
  80.9 2.1 %collective-permute-start.14 = (bf16[256,512]{1,0:T(8,128)(2,1)S(1)}, bf16[256,512]{1,0:T(8,128)(2,1)S(1)}, u32[]{:S(2)}, u32[]{:S(2)}) collective-permute-start(bf16[256,512]{1,0:T(8,128)(2,1)S(1)} %shard_map.52.refs_0_), channel_id=1, source_target_pairs={{0,96},{1,97},{2,98},{3,99},{4,28},{5,29},{6,30},{7,31},{8,104},{9... | collective-permute-start | bytes 786440 | tf_op jit(solution)/shard_map/ppermute | solution.py:39
  83.0 3.2 %collective-permute-done.16 = bf16[256,512]{1,0:T(8,128)(2,1)S(1)} collective-permute-done((bf16[256,512]{1,0:T(8,128)(2,1)S(1)}, bf16[256,512]{1,0:T(8,128)(2,1)S(1)}, u32[]{:S(2)}, u32[]{:S(2)}) %collective-permute-start.16) | collective-permute-done | bytes 262176 | tf_op jit(solution)/shard_map/ppermute | solution.py:39
  86.2 2.7 %collective-permute-done.15 = bf16[256,512]{1,0:T(8,128)(2,1)S(1)} collective-permute-done((bf16[256,512]{1,0:T(8,128)(2,1)S(1)}, bf16[256,512]{1,0:T(8,128)(2,1)S(1)}, u32[]{:S(2)}, u32[]{:S(2)}) %collective-permute-start.15) | collective-permute-done | bytes 262176 | tf_op jit(solution)/shard_map/ppermute | solution.py:39
  89.0 1.7 %collective-permute-start.25 = (bf16[1024,512]{1,0:T(8,128)(2,1)S(1)}, bf16[1024,512]{1,0:T(8,128)(2,1)S(1)}, u32[]{:S(2)}, u32[]{:S(2)}) collective-permute-start(bf16[1024,512]{1,0:T(8,128)(2,1)S(1)} %constant_dynamic-update-slice_fusion.refs_8_), channel_id=1, source_target_pairs={{0,8},{1,9},{2,10},{3,11},{4,36},{5,37},{6,38},{7,39},{8,16},{9,17... | collective-permute-start | bytes 3145736 | tf_op jit(solution)/shard_map/ppermute | solution.py:44
  90.7 1.1 collective-permute-start.24
  91.7 1.6 %collective-permute-start.19 = (bf16[256,512]{1,0:T(8,128)(2,1)S(1)}, bf16[256,512]{1,0:T(8,128)(2,1)S(1)}, u32[]{:S(2)}, u32[]{:S(2)}) collective-permute-start(bf16[256,512]{1,0:T(8,128)(2,1)S(1)} %shard_map.52.refs_0_), channel_id=1, source_target_pairs={{0,2},{1,3},{2,0},{3,1},{4,6},{5,7},{6,4},{7,5},{8,10},{9,11},{10,... | collective-permute-start | bytes 786440 | tf_op jit(solution)/shard_map/ppermute | solution.py:35
  93.3 1.4 collective-permute-start.18
  94.7 6.2 %collective-permute-done.20.refs_3_ = bf16[256,512]{1,0:T(8,128)(2,1)S(1)} collective-permute-done((bf16[256,512]{1,0:T(8,128)(2,1)S(1)}, bf16[256,512]{1,0:T(8,128)(2,1)S(1)}, u32[]{:S(2)}, u32[]{:S(2)}) %collective-permute-start.20) | collective-permute-done | bytes 262176 | tf_op jit(solution)/shard_map/ppermute | solution.py:35
  100.9 3.5 %collective-permute-done.19.refs_2_ = bf16[256,512]{1,0:T(8,128)(2,1)S(1)} collective-permute-done((bf16[256,512]{1,0:T(8,128)(2,1)S(1)}, bf16[256,512]{1,0:T(8,128)(2,1)S(1)}, u32[]{:S(2)}, u32[]{:S(2)}) %collective-permute-start.19) | collective-permute-done | bytes 262176 | tf_op jit(solution)/shard_map/ppermute | solution.py:35
  104.4 1.9 %collective-permute-done.18.refs_1_ = bf16[256,512]{1,0:T(8,128)(2,1)S(1)} collective-permute-done((bf16[256,512]{1,0:T(8,128)(2,1)S(1)}, bf16[256,512]{1,0:T(8,128)(2,1)S(1)}, u32[]{:S(2)}, u32[]{:S(2)}) %collective-permute-start.18) | collective-permute-done | bytes 262176 | tf_op jit(solution)/shard_map/ppermute | solution.py:35
  106.3 1.6 %collective-permute-start.27 = (bf16[256,512]{1,0:T(8,128)(2,1)S(1)}, bf16[256,512]{1,0:T(8,128)(2,1)S(1)}, u32[]{:S(2)}, u32[]{:S(2)}) collective-permute-start(bf16[256,512]{1,0:T(8,128)(2,1)S(1)} %collective-permute-done.18.refs_1_), channel_id=1, source_target_pairs={{0,4},{1,5},{2,6},{3,7},{4,0},{5,1},{6,2},{7,3},{8,12},{9,13},{10,... | collective-permute-start | bytes 786440 | tf_op jit(solution)/shard_map/ppermute | solution.py:31
  110.3 2.4 %collective-permute-start.22 = (bf16[256,512]{1,0:T(8,128)(2,1)S(1)}, bf16[256,512]{1,0:T(8,128)(2,1)S(1)}, u32[]{:S(2)}, u32[]{:S(2)}) collective-permute-start(bf16[256,512]{1,0:T(8,128)(2,1)S(1)} %collective-permute-done.17.far0), channel_id=1, source_target_pairs={{0,64},{1,65},{2,66},{3,67},{4,20},{5,21},{6,22},{7,23},{8,72},{9,... | collective-permute-start | bytes 786440 | tf_op jit(solution)/shard_map/ppermute | solution.py:39
  113.6 1.8 %shard_map.53 = (f32[256,512]{1,0:T(8,128)S(1)}, bf16[256,4096]{1,0:T(8,128)(2,1)S(1)}, bf16[4096,512]{1,0:T(8,128)(2,1)S(1)}) custom-call(s32[4]{0:T(128)S(1)} %pad_add_fusion.1.where, bf16[256,512]{1,0:T(8,128)(2,1)S(1)} %shard_map.52.refs_0_, bf16[256,512]{1,0:T(8,128)(2,1)S(1)} %collective-permute-done.18.refs_1_, ...), custom_call_target="tpu_custom_call" | custom-call | flops 268435456 | bytes 8388608 | tf_op jit(solution)/shard_map/pallas_call | solution.py:297
  115.4 1.7 %shard_map.54 = (f32[256,512]{1,0:T(8,128)S(1)}, bf16[4096,512]{1,0:T(8,128)(2,1)S(1)}) custom-call(s32[4]{0:T(128)S(1)} %pad_add_fusion.1.where, bf16[1024,512]{1,0:T(8,128)(2,1)S(1)} %collective-permute-done.24.one, bf16[1024,512]{1,0:T(8,128)(2,1)S(1)} %collective-permute-done.25.three, ...), custom_call_target="tpu_custom_call", output_to_operand_aliasing={{1}: (5, {})} | custom-call | flops 536870912 | bytes 8388608 | tf_op jit(solution)/shard_map/pallas_call | solution.py:297
  117.2 2.2 %collective-permute-done.22.far2 = bf16[256,512]{1,0:T(8,128)(2,1)S(1)} collective-permute-done((bf16[256,512]{1,0:T(8,128)(2,1)S(1)}, bf16[256,512]{1,0:T(8,128)(2,1)S(1)}, u32[]{:S(2)}, u32[]{:S(2)}) %collective-permute-start.22) | collective-permute-done | bytes 262176 | tf_op jit(solution)/shard_map/ppermute | solution.py:39
  119.6 1.7 %shard_map.55 = (f32[256,512]{1,0:T(8,128)S(1)}, bf16[256,512]{1,0:T(8,128)(2,1)S(1)}, bf16[4096,512]{1,0:T(8,128)(2,1)S(1)}) custom-call(s32[4]{0:T(128)S(1)} %pad_add_fusion.1.where, s32[2,32,32]{2,1,0:T(8,128)S(1)} %copy-done.2, bf16[256,512]{1,0:T(8,128)(2,1)S(1)} %collective-permute-done.17.far0, ...), custom_call_target="tpu_custom_call", output_to_operand_aliasing={{2}: (8, {})} | custom-call | flops 268435456 | bytes 6291456 | tf_op jit(solution)/shard_map/pallas_call | solution.py:297
  121.6 3.3 %collective-permute-start.32 = (bf16[256,512]{1,0:T(8,128)(2,1)S(1)}, bf16[256,512]{1,0:T(8,128)(2,1)S(1)}, u32[]{:S(2)}, u32[]{:S(2)}) collective-permute-start(bf16[256,512]{1,0:T(8,128)(2,1)S(1)} %get-tuple-element.82.refs_0_), channel_id=1, source_target_pairs={{0,2},{1,3},{2,0},{3,1},{4,6},{5,7},{6,4},{7,5},{8,10},{9,11},{10,... | collective-permute-start | bytes 786440 | tf_op jit(solution)/shard_map/ppermute | solution.py:35
  124.9 2.1 %collective-permute-start.36 = (bf16[256,512]{1,0:T(8,128)(2,1)S(1)}, bf16[256,512]{1,0:T(8,128)(2,1)S(1)}, u32[]{:S(2)}, u32[]{:S(2)}) collective-permute-start(bf16[256,512]{1,0:T(8,128)(2,1)S(1)} %get-tuple-element.82.refs_0_), channel_id=1, source_target_pairs={{0,4},{1,5},{2,6},{3,7},{4,0},{5,1},{6,2},{7,3},{8,12},{9,13},{10,... | collective-permute-start | bytes 786440 | tf_op jit(solution)/shard_map/ppermute | solution.py:31
  127.0 1.8 %collective-permute-done.34.refs_3_ = bf16[256,512]{1,0:T(8,128)(2,1)S(1)} collective-permute-done((bf16[256,512]{1,0:T(8,128)(2,1)S(1)}, bf16[256,512]{1,0:T(8,128)(2,1)S(1)}, u32[]{:S(2)}, u32[]{:S(2)}) %collective-permute-start.34) | collective-permute-done | bytes 262176 | tf_op jit(solution)/shard_map/ppermute | solution.py:35
  128.8 3.7 %collective-permute-start.35 = (bf16[256,512]{1,0:T(8,128)(2,1)S(1)}, bf16[256,512]{1,0:T(8,128)(2,1)S(1)}, u32[]{:S(2)}, u32[]{:S(2)}) collective-permute-start(bf16[256,512]{1,0:T(8,128)(2,1)S(1)} %collective-permute-done.34.refs_3_), channel_id=1, source_target_pairs={{0,4},{1,5},{2,6},{3,7},{4,0},{5,1},{6,2},{7,3},{8,12},{9,13},{10,... | collective-permute-start | bytes 786440 | tf_op jit(solution)/shard_map/ppermute | solution.py:31
  132.5 2.8 %collective-permute-done.32.refs_2_ = bf16[256,512]{1,0:T(8,128)(2,1)S(1)} collective-permute-done((bf16[256,512]{1,0:T(8,128)(2,1)S(1)}, bf16[256,512]{1,0:T(8,128)(2,1)S(1)}, u32[]{:S(2)}, u32[]{:S(2)}) %collective-permute-start.32) | collective-permute-done | bytes 262176 | tf_op jit(solution)/shard_map/ppermute | solution.py:35
  135.3 2.5 %collective-permute-start.33 = (bf16[256,512]{1,0:T(8,128)(2,1)S(1)}, bf16[256,512]{1,0:T(8,128)(2,1)S(1)}, u32[]{:S(2)}, u32[]{:S(2)}) collective-permute-start(bf16[256,512]{1,0:T(8,128)(2,1)S(1)} %collective-permute-done.32.refs_2_), channel_id=1, source_target_pairs={{0,4},{1,5},{2,6},{3,7},{4,0},{5,1},{6,2},{7,3},{8,12},{9,13},{10,... | collective-permute-start | bytes 786440 | tf_op jit(solution)/shard_map/ppermute | solution.py:31
  137.8 1.4 shard_map.56.refs_3_
  140.7 1.2 collective-permute-done.37.refs_6_
  141.9 1.7 %shard_map.58 = f32[128,1024]{1,0:T(8,128)} custom-call(s32[4]{0:T(128)S(1)} %pad_add_fusion.1.where, bf16[256,512]{1,0:T(8,128)(2,1)S(1)} %collective-permute-done.31.refs_0_, bf16[256,512]{1,0:T(8,128)(2,1)S(1)} %collective-permute-done.33.refs_1_, bf16[256,512]{1,0:T(8,128)(2,1)S(1)} %collective-permute-done.35.refs_2_, ...), custom_call_target="tpu_custom_call" | custom-call | flops 201326592 | bytes 3145728 | tf_op jit(solution)/shard_map/pallas_call | solution.py:297
  (62 shorter events, 11.1 us)
Async XLA Ops:
  0.0 5.9 %copy-start = (s32[32,8]{0,1:T(8,128)S(1)}, s32[32,8]{0,1:T(8,128)}, u32[]{:S(2)}) copy-start(s32[32,8]{0,1:T(8,128)} %param.5) | copy-start | bytes 3076
  0.0 27.0 %copy-start.1 = (s32[2,32,32]{2,1,0:T(8,128)S(1)}, s32[2,32,32]{2,1,0:T(8,128)}, u32[]{:S(2)}) copy-start(s32[2,32,32]{2,1,0:T(8,128)} %keep_d.11) | copy-start | bytes 24580
  0.0 6.7 %collective-permute-start.1 = (bf16[128,256]{1,0:T(8,128)(2,1)}, bf16[128,256]{1,0:T(8,128)(2,1)S(1)}, u32[]{:S(2)}, u32[]{:S(2)}) collective-permute-start(bf16[128,256]{1,0:T(8,128)(2,1)} %param.4), channel_id=1, source_target_pairs={{0,2},{1,3},{2,0},{3,1},{4,6},{5,7},{6,4},{7,5},{8,10},{9,11},{10,... | collective-permute-start | bytes 196616 | tf_op jit(solution)/shard_map/ppermute | solution.py:35
  4.4 3.7 %collective-permute-start = (bf16[128,256]{1,0:T(8,128)(2,1)}, bf16[128,256]{1,0:T(8,128)(2,1)S(1)}, u32[]{:S(2)}, u32[]{:S(2)}) collective-permute-start(bf16[128,256]{1,0:T(8,128)(2,1)} %param.4), channel_id=1, source_target_pairs={{0,3},{1,0},{2,1},{3,2},{4,7},{5,4},{6,5},{7,6},{8,11},{9,8},{10,9... | collective-permute-start | bytes 196616 | tf_op jit(solution)/shard_map/ppermute | solution.py:35
  4.9 4.5 %collective-permute-start.2 = (bf16[128,256]{1,0:T(8,128)(2,1)}, bf16[128,256]{1,0:T(8,128)(2,1)S(1)}, u32[]{:S(2)}, u32[]{:S(2)}) collective-permute-start(bf16[128,256]{1,0:T(8,128)(2,1)} %param.4), channel_id=1, source_target_pairs={{0,1},{1,2},{2,3},{3,0},{4,5},{5,6},{6,7},{7,4},{8,9},{9,10},{10,1... | collective-permute-start | bytes 196616 | tf_op jit(solution)/shard_map/ppermute | solution.py:35
  10.3 6.9 %collective-permute-start.5 = (bf16[128,1024]{1,0:T(8,128)(2,1)S(1)}, bf16[128,1024]{1,0:T(8,128)(2,1)S(1)}, u32[]{:S(2)}, u32[]{:S(2)}) collective-permute-start(bf16[128,1024]{1,0:T(8,128)(2,1)S(1)} %maximum_multiply_fusion), channel_id=1, source_target_pairs={{0,32},{1,33},{2,34},{3,35},{4,12},{5,13},{6,14},{7,15},{8,40},{9,... | collective-permute-start | bytes 786440 | tf_op jit(solution)/shard_map/ppermute | solution.py:39
  11.7 9.5 %collective-permute-start.4 = (bf16[128,1024]{1,0:T(8,128)(2,1)S(1)}, bf16[128,1024]{1,0:T(8,128)(2,1)S(1)}, u32[]{:S(2)}, u32[]{:S(2)}) collective-permute-start(bf16[128,1024]{1,0:T(8,128)(2,1)S(1)} %maximum_multiply_fusion), channel_id=1, source_target_pairs={{0,64},{1,65},{2,66},{3,67},{4,20},{5,21},{6,22},{7,23},{8,72},{9,... | collective-permute-start | bytes 786440 | tf_op jit(solution)/shard_map/ppermute | solution.py:39
  14.3 6.9 %collective-permute-start.3 = (bf16[128,1024]{1,0:T(8,128)(2,1)S(1)}, bf16[128,1024]{1,0:T(8,128)(2,1)S(1)}, u32[]{:S(2)}, u32[]{:S(2)}) collective-permute-start(bf16[128,1024]{1,0:T(8,128)(2,1)S(1)} %maximum_multiply_fusion), channel_id=1, source_target_pairs={{0,96},{1,97},{2,98},{3,99},{4,28},{5,29},{6,30},{7,31},{8,104},{9... | collective-permute-start | bytes 786440 | tf_op jit(solution)/shard_map/ppermute | solution.py:39
  21.2 5.8 %collective-permute-start.6 = (bf16[512,1024]{1,0:T(8,128)(2,1)S(1)}, bf16[512,1024]{1,0:T(8,128)(2,1)}, u32[]{:S(2)}, u32[]{:S(2)}) collective-permute-start(bf16[512,1024]{1,0:T(8,128)(2,1)S(1)} %pad_maximum_fusion.own0), channel_id=1, source_target_pairs={{0,4},{1,5},{2,6},{3,7},{4,0},{5,1},{6,2},{7,3},{8,12},{9,13},{10,... | collective-permute-start | bytes 3145736 | tf_op jit(solution)/shard_map/ppermute | solution.py:31
  24.3 15.2 %collective-permute-start.8 = (bf16[512,1024]{1,0:T(8,128)(2,1)S(1)}, bf16[512,1024]{1,0:T(8,128)(2,1)S(1)}, u32[]{:S(2)}, u32[]{:S(2)}) collective-permute-start(bf16[512,1024]{1,0:T(8,128)(2,1)S(1)} %pad_maximum_fusion.own0), channel_id=1, source_target_pairs={{0,8},{1,9},{2,10},{3,11},{4,36},{5,37},{6,38},{7,39},{8,16},{9,17... | collective-permute-start | bytes 3145736 | tf_op jit(solution)/shard_map/ppermute | solution.py:44
  25.9 13.9 %collective-permute-start.7 = (bf16[512,1024]{1,0:T(8,128)(2,1)S(1)}, bf16[512,1024]{1,0:T(8,128)(2,1)S(1)}, u32[]{:S(2)}, u32[]{:S(2)}) collective-permute-start(bf16[512,1024]{1,0:T(8,128)(2,1)S(1)} %pad_maximum_fusion.own0), channel_id=1, source_target_pairs={{0,24},{1,25},{2,26},{3,27},{4,100},{5,101},{6,102},{7,103},{8,0},... | collective-permute-start | bytes 3145736 | tf_op jit(solution)/shard_map/ppermute | solution.py:44
  39.8 9.5 %collective-permute-start.9 = (bf16[512,1024]{1,0:T(8,128)(2,1)S(1)}, bf16[512,1024]{1,0:T(8,128)(2,1)S(1)}, u32[]{:S(2)}, u32[]{:S(2)}) collective-permute-start(bf16[512,1024]{1,0:T(8,128)(2,1)S(1)} %collective-permute-done.7.own1), channel_id=1, source_target_pairs={{0,4},{1,5},{2,6},{3,7},{4,0},{5,1},{6,2},{7,3},{8,12},{9,13},{10,... | collective-permute-start | bytes 3145736 | tf_op jit(solution)/shard_map/ppermute | solution.py:31
  40.7 8.6 %collective-permute-start.10 = (bf16[512,1024]{1,0:T(8,128)(2,1)S(1)}, bf16[512,1024]{1,0:T(8,128)(2,1)S(1)}, u32[]{:S(2)}, u32[]{:S(2)}) collective-permute-start(bf16[512,1024]{1,0:T(8,128)(2,1)S(1)} %collective-permute-done.8.own3), channel_id=1, source_target_pairs={{0,4},{1,5},{2,6},{3,7},{4,0},{5,1},{6,2},{7,3},{8,12},{9,13},{10,... | collective-permute-start | bytes 3145736 | tf_op jit(solution)/shard_map/ppermute | solution.py:31
  40.7 16.7 %collective-permute-start.11 = (bf16[512,1024]{1,0:T(8,128)(2,1)S(1)}, bf16[512,1024]{1,0:T(8,128)(2,1)S(1)}, u32[]{:S(2)}, u32[]{:S(2)}) collective-permute-start(bf16[512,1024]{1,0:T(8,128)(2,1)S(1)} %pad_maximum_fusion.own0), channel_id=1, source_target_pairs={{0,16},{1,17},{2,18},{3,19},{4,68},{5,69},{6,70},{7,71},{8,24},{9,... | collective-permute-start | bytes 3145736 | tf_op jit(solution)/shard_map/ppermute | solution.py:44
  57.4 6.7 %copy-start.2 = (s32[2,32,32]{2,1,0:T(8,128)S(1)}, s32[2,32,32]{2,1,0:T(8,128)}, u32[]{:S(2)}) copy-start(s32[2,32,32]{2,1,0:T(8,128)} %keep_s.3) | copy-start | bytes 24580
  57.4 6.7 %collective-permute-start.12 = (bf16[512,1024]{1,0:T(8,128)(2,1)S(1)}, bf16[512,1024]{1,0:T(8,128)(2,1)S(1)}, u32[]{:S(2)}, u32[]{:S(2)}) collective-permute-start(bf16[512,1024]{1,0:T(8,128)(2,1)S(1)} %collective-permute-done.11.own2), channel_id=1, source_target_pairs={{0,4},{1,5},{2,6},{3,7},{4,0},{5,1},{6,2},{7,3},{8,12},{9,13},{10,... | collective-permute-start | bytes 3145736 | tf_op jit(solution)/shard_map/ppermute | solution.py:31
  71.3 2.7 %collective-permute-start.13 = (bf16[256,2048]{1,0:T(8,128)(2,1)S(1)}, bf16[256,2048]{1,0:T(8,128)(2,1)S(1)}, u32[]{:S(2)}, u32[]{:S(2)}) collective-permute-start(bf16[256,2048]{1,0:T(8,128)(2,1)S(1)} %get-tuple-element.63.low), channel_id=1, source_target_pairs={{0,4},{1,5},{2,6},{3,7},{4,0},{5,1},{6,2},{7,3},{8,12},{9,13},{10,... | collective-permute-start | bytes 3145736 | tf_op jit(solution)/shard_map/ppermute | solution.py:31
  75.8 7.1 %collective-permute-start.17 = (bf16[256,512]{1,0:T(8,128)(2,1)S(1)}, bf16[256,512]{1,0:T(8,128)(2,1)S(1)}, u32[]{:S(2)}, u32[]{:S(2)}) collective-permute-start(bf16[256,512]{1,0:T(8,128)(2,1)S(1)} %shard_map.52.refs_0_), channel_id=1, source_target_pairs={{0,16},{1,17},{2,18},{3,19},{4,68},{5,69},{6,70},{7,71},{8,24},{9,... | collective-permute-start | bytes 786440 | tf_op jit(solution)/shard_map/ppermute | solution.py:44
  78.6 7.6 %collective-permute-start.16 = (bf16[256,512]{1,0:T(8,128)(2,1)S(1)}, bf16[256,512]{1,0:T(8,128)(2,1)S(1)}, u32[]{:S(2)}, u32[]{:S(2)}) collective-permute-start(bf16[256,512]{1,0:T(8,128)(2,1)S(1)} %shard_map.52.refs_0_), channel_id=1, source_target_pairs={{0,64},{1,65},{2,66},{3,67},{4,20},{5,21},{6,22},{7,23},{8,72},{9,... | collective-permute-start | bytes 786440 | tf_op jit(solution)/shard_map/ppermute | solution.py:39
  80.3 8.6 %collective-permute-start.15 = (bf16[256,512]{1,0:T(8,128)(2,1)S(1)}, bf16[256,512]{1,0:T(8,128)(2,1)S(1)}, u32[]{:S(2)}, u32[]{:S(2)}) collective-permute-start(bf16[256,512]{1,0:T(8,128)(2,1)S(1)} %shard_map.52.refs_0_), channel_id=1, source_target_pairs={{0,32},{1,33},{2,34},{3,35},{4,12},{5,13},{6,14},{7,15},{8,40},{9,... | collective-permute-start | bytes 786440 | tf_op jit(solution)/shard_map/ppermute | solution.py:39
  80.9 8.0 %collective-permute-start.14 = (bf16[256,512]{1,0:T(8,128)(2,1)S(1)}, bf16[256,512]{1,0:T(8,128)(2,1)S(1)}, u32[]{:S(2)}, u32[]{:S(2)}) collective-permute-start(bf16[256,512]{1,0:T(8,128)(2,1)S(1)} %shard_map.52.refs_0_), channel_id=1, source_target_pairs={{0,96},{1,97},{2,98},{3,99},{4,28},{5,29},{6,30},{7,31},{8,104},{9... | collective-permute-start | bytes 786440 | tf_op jit(solution)/shard_map/ppermute | solution.py:39
  89.0 26.4 %collective-permute-start.25 = (bf16[1024,512]{1,0:T(8,128)(2,1)S(1)}, bf16[1024,512]{1,0:T(8,128)(2,1)S(1)}, u32[]{:S(2)}, u32[]{:S(2)}) collective-permute-start(bf16[1024,512]{1,0:T(8,128)(2,1)S(1)} %constant_dynamic-update-slice_fusion.refs_8_), channel_id=1, source_target_pairs={{0,8},{1,9},{2,10},{3,11},{4,36},{5,37},{6,38},{7,39},{8,16},{9,17... | collective-permute-start | bytes 3145736 | tf_op jit(solution)/shard_map/ppermute | solution.py:44
  90.7 24.8 %collective-permute-start.24 = (bf16[1024,512]{1,0:T(8,128)(2,1)S(1)}, bf16[1024,512]{1,0:T(8,128)(2,1)S(1)}, u32[]{:S(2)}, u32[]{:S(2)}) collective-permute-start(bf16[1024,512]{1,0:T(8,128)(2,1)S(1)} %constant_dynamic-update-slice_fusion.refs_8_), channel_id=1, source_target_pairs={{0,24},{1,25},{2,26},{3,27},{4,100},{5,101},{6,102},{7,103},{8,0},... | collective-permute-start | bytes 3145736 | tf_op jit(solution)/shard_map/ppermute | solution.py:44
  91.7 9.1 %collective-permute-start.20 = (bf16[256,512]{1,0:T(8,128)(2,1)S(1)}, bf16[256,512]{1,0:T(8,128)(2,1)S(1)}, u32[]{:S(2)}, u32[]{:S(2)}) collective-permute-start(bf16[256,512]{1,0:T(8,128)(2,1)S(1)} %shard_map.52.refs_0_), channel_id=1, source_target_pairs={{0,1},{1,2},{2,3},{3,0},{4,5},{5,6},{6,7},{7,4},{8,9},{9,10},{10,1... | collective-permute-start | bytes 786440 | tf_op jit(solution)/shard_map/ppermute | solution.py:35
  91.7 12.7 %collective-permute-start.19 = (bf16[256,512]{1,0:T(8,128)(2,1)S(1)}, bf16[256,512]{1,0:T(8,128)(2,1)S(1)}, u32[]{:S(2)}, u32[]{:S(2)}) collective-permute-start(bf16[256,512]{1,0:T(8,128)(2,1)S(1)} %shard_map.52.refs_0_), channel_id=1, source_target_pairs={{0,2},{1,3},{2,0},{3,1},{4,6},{5,7},{6,4},{7,5},{8,10},{9,11},{10,... | collective-permute-start | bytes 786440 | tf_op jit(solution)/shard_map/ppermute | solution.py:35
  93.3 13.0 %collective-permute-start.18 = (bf16[256,512]{1,0:T(8,128)(2,1)S(1)}, bf16[256,512]{1,0:T(8,128)(2,1)S(1)}, u32[]{:S(2)}, u32[]{:S(2)}) collective-permute-start(bf16[256,512]{1,0:T(8,128)(2,1)S(1)} %shard_map.52.refs_0_), channel_id=1, source_target_pairs={{0,3},{1,0},{2,1},{3,2},{4,7},{5,4},{6,5},{7,6},{8,11},{9,8},{10,9... | collective-permute-start | bytes 786440 | tf_op jit(solution)/shard_map/ppermute | solution.py:35
  106.3 2.7 %collective-permute-start.27 = (bf16[256,512]{1,0:T(8,128)(2,1)S(1)}, bf16[256,512]{1,0:T(8,128)(2,1)S(1)}, u32[]{:S(2)}, u32[]{:S(2)}) collective-permute-start(bf16[256,512]{1,0:T(8,128)(2,1)S(1)} %collective-permute-done.18.refs_1_), channel_id=1, source_target_pairs={{0,4},{1,5},{2,6},{3,7},{4,0},{5,1},{6,2},{7,3},{8,12},{9,13},{10,... | collective-permute-start | bytes 786440 | tf_op jit(solution)/shard_map/ppermute | solution.py:31
  107.9 1.5 %collective-permute-start.28 = (bf16[256,512]{1,0:T(8,128)(2,1)S(1)}, bf16[256,512]{1,0:T(8,128)(2,1)S(1)}, u32[]{:S(2)}, u32[]{:S(2)}) collective-permute-start(bf16[256,512]{1,0:T(8,128)(2,1)S(1)} %collective-permute-done.19.refs_2_), channel_id=1, source_target_pairs={{0,4},{1,5},{2,6},{3,7},{4,0},{5,1},{6,2},{7,3},{8,12},{9,13},{10,... | collective-permute-start | bytes 786440 | tf_op jit(solution)/shard_map/ppermute | solution.py:31
  107.9 2.4 %collective-permute-start.29 = (bf16[256,512]{1,0:T(8,128)(2,1)S(1)}, bf16[256,512]{1,0:T(8,128)(2,1)S(1)}, u32[]{:S(2)}, u32[]{:S(2)}) collective-permute-start(bf16[256,512]{1,0:T(8,128)(2,1)S(1)} %collective-permute-done.20.refs_3_), channel_id=1, source_target_pairs={{0,4},{1,5},{2,6},{3,7},{4,0},{5,1},{6,2},{7,3},{8,12},{9,13},{10,... | collective-permute-start | bytes 786440 | tf_op jit(solution)/shard_map/ppermute | solution.py:31
  109.1 3.7 %collective-permute-start.26 = (bf16[256,512]{1,0:T(8,128)(2,1)S(1)}, bf16[256,512]{1,0:T(8,128)(2,1)S(1)}, u32[]{:S(2)}, u32[]{:S(2)}) collective-permute-start(bf16[256,512]{1,0:T(8,128)(2,1)S(1)} %shard_map.52.refs_0_), channel_id=1, source_target_pairs={{0,4},{1,5},{2,6},{3,7},{4,0},{5,1},{6,2},{7,3},{8,12},{9,13},{10,... | collective-permute-start | bytes 786440 | tf_op jit(solution)/shard_map/ppermute | solution.py:31
  109.4 7.7 %collective-permute-start.23 = (bf16[256,512]{1,0:T(8,128)(2,1)S(1)}, bf16[256,512]{1,0:T(8,128)(2,1)S(1)}, u32[]{:S(2)}, u32[]{:S(2)}) collective-permute-start(bf16[256,512]{1,0:T(8,128)(2,1)S(1)} %collective-permute-done.17.far0), channel_id=1, source_target_pairs={{0,32},{1,33},{2,34},{3,35},{4,12},{5,13},{6,14},{7,15},{8,40},{9,... | collective-permute-start | bytes 786440 | tf_op jit(solution)/shard_map/ppermute | solution.py:39
  110.3 9.1 %collective-permute-start.22 = (bf16[256,512]{1,0:T(8,128)(2,1)S(1)}, bf16[256,512]{1,0:T(8,128)(2,1)S(1)}, u32[]{:S(2)}, u32[]{:S(2)}) collective-permute-start(bf16[256,512]{1,0:T(8,128)(2,1)S(1)} %collective-permute-done.17.far0), channel_id=1, source_target_pairs={{0,64},{1,65},{2,66},{3,67},{4,20},{5,21},{6,22},{7,23},{8,72},{9,... | collective-permute-start | bytes 786440 | tf_op jit(solution)/shard_map/ppermute | solution.py:39
  112.7 6.8 %collective-permute-start.21 = (bf16[256,512]{1,0:T(8,128)(2,1)S(1)}, bf16[256,512]{1,0:T(8,128)(2,1)S(1)}, u32[]{:S(2)}, u32[]{:S(2)}) collective-permute-start(bf16[256,512]{1,0:T(8,128)(2,1)S(1)} %collective-permute-done.17.far0), channel_id=1, source_target_pairs={{0,96},{1,97},{2,98},{3,99},{4,28},{5,29},{6,30},{7,31},{8,104},{9... | collective-permute-start | bytes 786440 | tf_op jit(solution)/shard_map/ppermute | solution.py:39
  121.3 7.5 %collective-permute-start.34 = (bf16[256,512]{1,0:T(8,128)(2,1)S(1)}, bf16[256,512]{1,0:T(8,128)(2,1)S(1)}, u32[]{:S(2)}, u32[]{:S(2)}) collective-permute-start(bf16[256,512]{1,0:T(8,128)(2,1)S(1)} %get-tuple-element.82.refs_0_), channel_id=1, source_target_pairs={{0,1},{1,2},{2,3},{3,0},{4,5},{5,6},{6,7},{7,4},{8,9},{9,10},{10,1... | collective-permute-start | bytes 786440 | tf_op jit(solution)/shard_map/ppermute | solution.py:35
  121.6 13.7 %collective-permute-start.32 = (bf16[256,512]{1,0:T(8,128)(2,1)S(1)}, bf16[256,512]{1,0:T(8,128)(2,1)S(1)}, u32[]{:S(2)}, u32[]{:S(2)}) collective-permute-start(bf16[256,512]{1,0:T(8,128)(2,1)S(1)} %get-tuple-element.82.refs_0_), channel_id=1, source_target_pairs={{0,2},{1,3},{2,0},{3,1},{4,6},{5,7},{6,4},{7,5},{8,10},{9,11},{10,... | collective-permute-start | bytes 786440 | tf_op jit(solution)/shard_map/ppermute | solution.py:35
  124.9 12.9 %collective-permute-start.30 = (bf16[256,512]{1,0:T(8,128)(2,1)S(1)}, bf16[256,512]{1,0:T(8,128)(2,1)S(1)}, u32[]{:S(2)}, u32[]{:S(2)}) collective-permute-start(bf16[256,512]{1,0:T(8,128)(2,1)S(1)} %get-tuple-element.82.refs_0_), channel_id=1, source_target_pairs={{0,3},{1,0},{2,1},{3,2},{4,7},{5,4},{6,5},{7,6},{8,11},{9,8},{10,9... | collective-permute-start | bytes 786440 | tf_op jit(solution)/shard_map/ppermute | solution.py:35
  124.9 12.9 %collective-permute-start.36 = (bf16[256,512]{1,0:T(8,128)(2,1)S(1)}, bf16[256,512]{1,0:T(8,128)(2,1)S(1)}, u32[]{:S(2)}, u32[]{:S(2)}) collective-permute-start(bf16[256,512]{1,0:T(8,128)(2,1)S(1)} %get-tuple-element.82.refs_0_), channel_id=1, source_target_pairs={{0,4},{1,5},{2,6},{3,7},{4,0},{5,1},{6,2},{7,3},{8,12},{9,13},{10,... | collective-permute-start | bytes 786440 | tf_op jit(solution)/shard_map/ppermute | solution.py:31
  128.8 10.3 %collective-permute-start.35 = (bf16[256,512]{1,0:T(8,128)(2,1)S(1)}, bf16[256,512]{1,0:T(8,128)(2,1)S(1)}, u32[]{:S(2)}, u32[]{:S(2)}) collective-permute-start(bf16[256,512]{1,0:T(8,128)(2,1)S(1)} %collective-permute-done.34.refs_3_), channel_id=1, source_target_pairs={{0,4},{1,5},{2,6},{3,7},{4,0},{5,1},{6,2},{7,3},{8,12},{9,13},{10,... | collective-permute-start | bytes 786440 | tf_op jit(solution)/shard_map/ppermute | solution.py:31
  135.3 3.9 %collective-permute-start.33 = (bf16[256,512]{1,0:T(8,128)(2,1)S(1)}, bf16[256,512]{1,0:T(8,128)(2,1)S(1)}, u32[]{:S(2)}, u32[]{:S(2)}) collective-permute-start(bf16[256,512]{1,0:T(8,128)(2,1)S(1)} %collective-permute-done.32.refs_2_), channel_id=1, source_target_pairs={{0,4},{1,5},{2,6},{3,7},{4,0},{5,1},{6,2},{7,3},{8,12},{9,13},{10,... | collective-permute-start | bytes 786440 | tf_op jit(solution)/shard_map/ppermute | solution.py:31
  137.8 1.5 %collective-permute-start.31 = (bf16[256,512]{1,0:T(8,128)(2,1)S(1)}, bf16[256,512]{1,0:T(8,128)(2,1)S(1)}, u32[]{:S(2)}, u32[]{:S(2)}) collective-permute-start(bf16[256,512]{1,0:T(8,128)(2,1)S(1)} %collective-permute-done.30.refs_1_), channel_id=1, source_target_pairs={{0,4},{1,5},{2,6},{3,7},{4,0},{5,1},{6,2},{7,3},{8,12},{9,13},{10,... | collective-permute-start | bytes 786440 | tf_op jit(solution)/shard_map/ppermute | solution.py:31
  140.2 1.6 %collective-permute-start.37 = (f32[128,512]{1,0:T(8,128)S(1)}, f32[128,512]{1,0:T(8,128)S(1)}, u32[]{:S(2)}, u32[]{:S(2)}) collective-permute-start(f32[128,512]{1,0:T(8,128)S(1)} %shard_map.57), channel_id=1, source_target_pairs={{0,4},{1,5},{2,6},{3,7},{4,0},{5,1},{6,2},{7,3},{8,12},{9,13},{10,... | collective-permute-start | bytes 786440 | tf_op jit(solution)/shard_map/ppermute | solution.py:31

commit v2 on v1

--- a/solution.py
+++ b/solution.py
@@ -1,5 +1,3 @@
-import functools
-
 import jax
 import jax.numpy as jnp
 from jax import lax
@@ -201,31 +199,17 @@
             out[t * B:(t + 1) * B, u * B:(u + 1) * B] = piece.astype(jnp.bfloat16)
 
 
-def parts_times_panel(parts, z, panel):
-    total = None
-    for ref, d, kind in parts:
-        rows = [panel[aligned(((z + d) & 3) * 8 + t * 2 + kind, B), :] for t in range(4)]
-        term = dot(ref[...], jnp.concatenate(rows, axis=0))
-        total = term if total is None else total + term
-    return total
-
-
-def early_cube(where, *refs):
-    own, other, panel, out = refs[:4], refs[4], refs[5], refs[6]
-    core, z = where[2], where[3]
-    parts = [(own[d], d, core) for d in range(4)] + [(other, 0, 1 - core)]
-    out[...] = parts_times_panel(parts, z, panel)
-
-
-def chips_times(where, line, chips, panel, sems):
+def chips_times(where, line, chips, mine, its, sems):
     x, y, core = where[0], where[1], where[2]
     copies, left, right = [], [], []
     for n, (ref, offset, first, second) in enumerate(chips):
         px, py = place(x, y, core, first, second)
-        copies.append(pltpu.make_async_copy(
-            ref.at[pl.ds(offset, ROWS)], panel.at[aligned(px * 4 + py, ROWS)], sems.at[n]))
-        copies[-1].start()
-        left.append(line[:, aligned(px * 4 + py, ROWS)])
+        chip = px * 4 + py
+        for m, (panel, kind) in enumerate(((mine, core), (its, 1 - core))):
+            copies.append(pltpu.make_async_copy(
+                ref.at[pl.ds(pl.multiple_of(offset + kind * B, B), B)], panel.at[aligned(chip, B)], sems.at[n, m]))
+            copies[-1].start()
+        left.append(line[:, aligned(chip, ROWS)])
         right.append(ref[offset:offset + ROWS, :])
     total = None
     for n in range(0, len(chips), 4):
@@ -234,31 +218,25 @@
     return total, copies
 
 
-def second_square_0(where, *refs):
-    own, other, near, (early, line, panel), (sems,) = refs[:4], refs[4:8], refs[8], refs[9:12], refs[12:]
+def early_square(where, *refs):
+    own, other, near, far, (early, line, mine, its), (sems,) = (
+        refs[:4], refs[4:8], refs[8], refs[9:13], refs[13:17], refs[17:])
     core, z = where[2], where[3]
     for d in range(4):
         for ref, kind in ((own[d], core), (other[d], 1 - core)):
             for t in range(4):
                 line[:, aligned(((z + d) & 3) * 8 + t * 2 + kind, B)] = ref[:, t * B:(t + 1) * B]
-    value, copies = chips_times(where, line, [(near, i * ROWS, i, 0) for i in range(4)], panel, sems)
+    chips = [(near, i * ROWS, i, 0) for i in range(4)] + [(far[i], 0, i, 2) for i in range(4)]
+    value, copies = chips_times(where, line, chips, mine, its, sems)
     early[...] = value
     for copy in copies:
         copy.wait()
 
 
-def second_square_1(where, one, three, early, line, _, out, panel, sems):
+def second_square(where, keep_s, one, three, early, line, _, __, square, low, mine, its, sems):
+    x, y, core, z = where[0], where[1], where[2], where[3]
     chips = [(ref, i * ROWS, i, j) for ref, j in ((one, 1), (three, 3)) for i in range(4)]
-    value, copies = chips_times(where, line, chips, panel, sems)
-    out[...] = early[...] + value
-    for copy in copies:
-        copy.wait()
-
-
-def second_square_2(where, keep_s, far0, far1, far2, far3, early, line, _, square, low, panel, sems):
-    x, y, core, z = where[0], where[1], where[2], where[3]
-    chips = [(ref, 0, i, 2) for i, ref in enumerate((far0, far1, far2, far3))]
-    value, copies = chips_times(where, line, chips, panel, sems)
+    value, copies = chips_times(where, line, chips, mine, its, sems)
     value = early[...] + value
     for t in range(2):
         for u in range(4):
@@ -270,23 +248,38 @@
         copy.wait()
 
 
-def second_density(leave, where, *refs):
-    others, (early, square, panel), (come, out) = refs[:3], refs[3:6], (refs[6:] if not leave else (None,) + refs[6:])
-    core, z = where[2], where[3]
-    at = aligned(1 - core if leave else core, B)
-    total = early[at, :]
-    for d in (1, 2, 3):
-        rows = [panel[aligned(((z + d) & 3) * 8 + t * 2 + 1 - core, B), :] for t in range(4)]
-        total = total + dot(others[d - 1][at, :], jnp.concatenate(rows, axis=0))
-    value = 3.0 * square[at, :] - 2.0 * total
-    if leave:
-        out[...] = value
-        return
-    first = core == 0
+def parts_times_panel(parts, z, mine, come):
+    total = [None, None]
+    for value, d in parts:
+        for n, panel in enumerate((mine, come)):
+            term = dot(value, panel[aligned((z + d) & 3, 512), :])
+            total[n] = term if total[n] is None else total[n] + term
+    return total
+
+
+def early_cube(where, own0, own1, own3, mine, come, out):
+    parts = [(own0[...], 0), (own1[...], 1), (own3[...], 3)]
+    out[:, :COLS], out[:, COLS:] = parts_times_panel(parts, where[3], mine, come)
+
+
+def density_share(where, at, own2, early, square, mine, come):
+    first, second = parts_times_panel([(own2[at, :], 2)], where[3], mine, come)
+    return 3.0 * square[at, :] - 2.0 * (early[at, :COLS] + first), -2.0 * (early[at, COLS:] + second)
+
+
+def leaving_density(where, own2, early, square, mine, come, out):
+    at = aligned(1 - where[2], B)
+    out[:, :COLS], out[:, COLS:] = density_share(where, at, own2, early, square, mine, come)
+
+
+def second_density(where, own2, early, square, mine, come, share, out):
+    own, other = density_share(where, aligned(where[2], B), own2, early, square, mine, come)
+    own, other = own + share[:, COLS:], other + share[:, :COLS]
+    first = where[2] == 0
     for t in range(4):
-        mine, its = value[:, t * B:(t + 1) * B], come[:, t * B:(t + 1) * B]
-        out[:, 2 * t * B:(2 * t + 1) * B] = jnp.where(first, mine, its)
-        out[:, (2 * t + 1) * B:(2 * t + 2) * B] = jnp.where(first, its, mine)
+        one, two = own[:, t * B:(t + 1) * B], other[:, t * B:(t + 1) * B]
+        out[:, 2 * t * B:(2 * t + 1) * B] = jnp.where(first, one, two)
+        out[:, (2 * t + 1) * B:(2 * t + 2) * B] = jnp.where(first, two, one)
 
 
 SMEM = pl.BlockSpec(memory_space=pltpu.SMEM)
@@ -361,32 +354,32 @@
         current, from_first(current, 1), from_first(current, 3), from_first(current, 2), from_second(current, 2)))
     near = jnp.concatenate([own0, one, two, three], axis=0)
     one, three = from_second(near, 1), from_second(near, 3)
-    far, own1, own2, own3 = lax.optimization_barrier((far, *gather(current, from_z)[1:]))
+    far, *own = lax.optimization_barrier((far, *gather(current, from_z)[1:]))
     far = gather(far, from_first)
-    own = [own0, own1, own2, own3]
+    own0, *both = lax.optimization_barrier((own0, *own, *far))
+    own, far = [own0, *both[:3]], both[3:]
     other = [other_core(part) for part in own]
-    early, line, panel = call(
-        second_square_0, 1, [where, *own, *other, near], [full_block, line_shape, panel_shape],
-        [pltpu.SemaphoreType.DMA((4,))], block_flops // 4, 8 * MIB)
-    early, panel = call(
-        second_square_1, 1, [where, one, three, early, line, panel], [full_block, panel_shape],
-        [pltpu.SemaphoreType.DMA((8,))], block_flops // 2, 8 * MIB, {5: 1})
-    square, low, panel = call(
-        second_square_2, 2, [where, keep_square, *far, early, line, panel],
-        [full_block, low_block, panel_shape],
-        [pltpu.SemaphoreType.DMA((4,))], block_flops // 4, 6 * MIB, {8: 2})
-
-    own = gather(low, from_z)
-    other = [other_core(part) for part in own]
+    half_shape = jax.ShapeDtypeStruct((N // 2, COLS), jnp.bfloat16)
+    early, line, mine, its = call(
+        early_square, 1, [where, *own, *other, near, *far], [full_block, line_shape, half_shape, half_shape],
+        [pltpu.SemaphoreType.DMA((8, 2))], block_flops // 2, 10 * MIB)
+    square, low, mine, its = call(
+        second_square, 2, [where, keep_square, one, three, early, line, mine, its],
+        [full_block, low_block, half_shape, half_shape],
+        [pltpu.SemaphoreType.DMA((8, 2))], block_flops // 2, 8 * MIB, {6: 2, 7: 3})
+
+    own0, own1, own2, own3 = gather(low, from_z)
+    come = other_core(its)
     (early,) = call(
-        early_cube, 1, [where, *own, other[0], panel], [full_block], [], block_flops * 5 // 8, 4 * MIB)
-    last = [*other[1:], early, square, panel]
+        early_cube, 1, [where, own0, own1, own3, mine, come],
+        [jax.ShapeDtypeStruct((ROWS, 2 * COLS), jnp.float32)], [], block_flops * 3 // 4, 4 * MIB)
+    early, own2 = lax.optimization_barrier((early, own2))
+    half = jax.ShapeDtypeStruct((B, 2 * COLS), jnp.float32)
     (leave,) = call(
-        functools.partial(second_density, True), 1, [where, *last],
-        [jax.ShapeDtypeStruct((B, COLS), jnp.float32)], [], block_flops * 3 // 16, 3 * MIB)
+        leaving_density, 1, [where, own2, early, square, mine, come], [half], [], block_flops // 8, 3 * MIB)
     (out,) = call(
-        functools.partial(second_density, False), 1, [where, *last, other_core(leave)],
-        [jax.ShapeDtypeStruct((B, 2 * COLS), jnp.float32)], [], block_flops * 3 // 16, 3 * MIB)
+        second_density, 1, [where, own2, early, square, mine, come, other_core(leave)], [half], [],
+        block_flops // 8, 3 * MIB)
     return out
 
 

time: 144 us -> 146 us (1.014)
  starting transfers between devices: 53.2 us -> 43.1 us
  waiting for transfers between devices: 45.1 us -> 52.8 us
  Pallas kernels: 43.1 us -> 47.7 us
    ppermute x14 -> x11, starting transfers between devices: 16.3 us -> 9.28 us  [other_core(): lax.ppermute(a, AXES, pairs(lambda x, y, core, z: (x, y, 1 - core, z)))]
    ppermute x9, waiting for transfers between devices: 14.1 us -> 20.6 us  [from_first(): lax.ppermute(a, AXES, pairs(lambda x, y, core, z: (x - d, y, core, z) if...]
    pallas_call x13 -> x12, Pallas kernels: 43.1 us -> 47.7 us  [call(): pl.pallas_call(kernel, in_specs=[SMEM] * n_smem + [VMEM] * (len(ins) - n_...]
    ppermute x9, starting transfers between devices: 12.5 us -> 10.6 us  [from_z(): lax.ppermute(a, AXES, pairs(lambda x, y, core, z: (x, y, core, z - d)))]
    ppermute x9, starting transfers between devices: 13.6 us -> 12.1 us  [from_first(): lax.ppermute(a, AXES, pairs(lambda x, y, core, z: (x - d, y, core, z) if...]
    ppermute x14 -> x11, waiting for transfers between devices: 2.33 us -> 3.73 us  [other_core(): lax.ppermute(a, AXES, pairs(lambda x, y, core, z: (x, y, 1 - core, z)))]
  transfers between devices with their start and end apart: 38 -> 35, of which waited for: 19 -> 19; matrix products, arithmetic and copies ran while one was open for 1% -> 1% of each run, Pallas kernels for 21% -> 22%
where the time goes in v2:
time: 146 us
  waiting for transfers between devices  52.8 us (36%)
  Pallas kernels  47.7 us (33%)
  starting transfers between devices  43.1 us (30%)
    pallas_call x12, Pallas kernels, call(): pl.pallas_call(kernel, in_specs=[SMEM] * n_smem + [VMEM] * (len(ins) - n_...  47.7 us
    ppermute x9, waiting for transfers between devices, from_first(): lax.ppermute(a, AXES, pairs(lambda x, y, core, z: (x - d, y, core, z) if...  20.6 us
    ppermute x9, waiting for transfers between devices, from_z(): lax.ppermute(a, AXES, pairs(lambda x, y, core, z: (x, y, core, z - d)))  18.7 us
    ppermute x9, starting transfers between devices, from_first(): lax.ppermute(a, AXES, pairs(lambda x, y, core, z: (x - d, y, core, z) if...  12.1 us
    ppermute x6, starting transfers between devices, from_second(): lax.ppermute(a, AXES, pairs(lambda x, y, core, z: (x, y - d, core, z) if...  11.1 us
    ppermute x9, starting transfers between devices, from_z(): lax.ppermute(a, AXES, pairs(lambda x, y, core, z: (x, y, core, z - d)))  10.6 us
    ppermute x6, waiting for transfers between devices, from_second(): lax.ppermute(a, AXES, pairs(lambda x, y, core, z: (x, y - d, core, z) if...  9.73 us
    ppermute x11, starting transfers between devices, other_core(): lax.ppermute(a, AXES, pairs(lambda x, y, core, z: (x, y, 1 - core, z)))  9.28 us
  transfers between devices with their start and end apart: 35, of which 19 were waited for; matrix products, arithmetic and copies ran while one was open for 1% of the time, Pallas kernels for 22%

profile of v2, /device:TPU:1, one launch (start us, length us, event | category | flops | bytes accessed | tf_op | source)
XLA Modules:
  0.0 145.8 jit_solution(8279545147580830304)
XLA Ops:
  0.0 4.4 %collective-permute-start.1 = (bf16[128,256]{1,0:T(8,128)(2,1)}, bf16[128,256]{1,0:T(8,128)(2,1)S(1)}, u32[]{:S(2)}, u32[]{:S(2)}) collective-permute-start(bf16[128,256]{1,0:T(8,128)(2,1)} %param.4), channel_id=1, source_target_pairs={{0,2},{1,3},{2,0},{3,1},{4,6},{5,7},{6,4},{7,5},{8,10},{9,11},{10,... | collective-permute-start | bytes 196616 | tf_op jit(solution)/shard_map/ppermute | solution.py:33
  4.9 1.0 collective-permute-start.2
  6.7 1.4 collective-permute-done
  8.1 1.3 collective-permute-done.2
  9.4 0.9 maximum_multiply_fusion
  10.3 1.4 collective-permute-start.5
  11.7 2.6 %collective-permute-start.4 = (bf16[128,1024]{1,0:T(8,128)(2,1)S(1)}, bf16[128,1024]{1,0:T(8,128)(2,1)S(1)}, u32[]{:S(2)}, u32[]{:S(2)}) collective-permute-start(bf16[128,1024]{1,0:T(8,128)(2,1)S(1)} %maximum_multiply_fusion), channel_id=1, source_target_pairs={{0,64},{1,65},{2,66},{3,67},{4,20},{5,21},{6,22},{7,23},{8,72},{9,... | collective-permute-start | bytes 786440 | tf_op jit(solution)/shard_map/ppermute | solution.py:37
  14.3 1.1 collective-permute-start.3
  15.4 1.8 %collective-permute-done.5 = bf16[128,1024]{1,0:T(8,128)(2,1)S(1)} collective-permute-done((bf16[128,1024]{1,0:T(8,128)(2,1)S(1)}, bf16[128,1024]{1,0:T(8,128)(2,1)S(1)}, u32[]{:S(2)}, u32[]{:S(2)}) %collective-permute-start.5) | collective-permute-done | bytes 262176 | tf_op jit(solution)/shard_map/ppermute | solution.py:37
  17.2 4.0 %collective-permute-done.4 = bf16[128,1024]{1,0:T(8,128)(2,1)S(1)} collective-permute-done((bf16[128,1024]{1,0:T(8,128)(2,1)S(1)}, bf16[128,1024]{1,0:T(8,128)(2,1)S(1)}, u32[]{:S(2)}, u32[]{:S(2)}) %collective-permute-start.4) | collective-permute-done | bytes 262176 | tf_op jit(solution)/shard_map/ppermute | solution.py:37
  21.2 3.1 %collective-permute-start.6 = (bf16[512,1024]{1,0:T(8,128)(2,1)S(1)}, bf16[512,1024]{1,0:T(8,128)(2,1)}, u32[]{:S(2)}, u32[]{:S(2)}) collective-permute-start(bf16[512,1024]{1,0:T(8,128)(2,1)S(1)} %pad_maximum_fusion.own0), channel_id=1, source_target_pairs={{0,4},{1,5},{2,6},{3,7},{4,0},{5,1},{6,2},{7,3},{8,12},{9,13},{10,... | collective-permute-start | bytes 3145736 | tf_op jit(solution)/shard_map/ppermute | solution.py:29
  24.3 1.6 %collective-permute-start.8 = (bf16[512,1024]{1,0:T(8,128)(2,1)S(1)}, bf16[512,1024]{1,0:T(8,128)(2,1)S(1)}, u32[]{:S(2)}, u32[]{:S(2)}) collective-permute-start(bf16[512,1024]{1,0:T(8,128)(2,1)S(1)} %pad_maximum_fusion.own0), channel_id=1, source_target_pairs={{0,8},{1,9},{2,10},{3,11},{4,36},{5,37},{6,38},{7,39},{8,16},{9,17... | collective-permute-start | bytes 3145736 | tf_op jit(solution)/shard_map/ppermute | solution.py:42
  25.9 1.1 collective-permute-start.7
  27.0 3.1 %shard_map.46 = (bf16[4096,2048]{1,0:T(8,128)(2,1)S(1)}, bf16[256,4096]{1,0:T(8,128)(2,1)S(1)}, bf16[256,1024]{1,0:T(8,128)(2,1)S(1)}) custom-call(s32[4]{0:T(128)S(1)} %pad_add_fusion.1.where, s32[2,32,32]{2,1,0:T(8,128)S(1)} %copy-done.1, bf16[512,1024]{1,0:T(8,128)(2,1)S(1)} %pad_maximum_fusion.own0, bf16[512,1024]{1,0:T(8,128)(2,1)} %collective-permute-done.6.other0), custom_call_target="tpu_custom_call" | custom-call | flops 67108864 | bytes 1048576 | tf_op jit(solution)/shard_map/pallas_call | solution.py:290
  30.1 9.3 %collective-permute-done.8.own3 = bf16[512,1024]{1,0:T(8,128)(2,1)S(1)} collective-permute-done((bf16[512,1024]{1,0:T(8,128)(2,1)S(1)}, bf16[512,1024]{1,0:T(8,128)(2,1)S(1)}, u32[]{:S(2)}, u32[]{:S(2)}) %collective-permute-start.8) | collective-permute-done | bytes 1048608 | tf_op jit(solution)/shard_map/ppermute | solution.py:42
  39.8 0.9 collective-permute-start.9
  40.7 2.7 %collective-permute-start.11 = (bf16[512,1024]{1,0:T(8,128)(2,1)S(1)}, bf16[512,1024]{1,0:T(8,128)(2,1)S(1)}, u32[]{:S(2)}, u32[]{:S(2)}) collective-permute-start(bf16[512,1024]{1,0:T(8,128)(2,1)S(1)} %pad_maximum_fusion.own0), channel_id=1, source_target_pairs={{0,16},{1,17},{2,18},{3,19},{4,68},{5,69},{6,70},{7,71},{8,24},{9,... | collective-permute-start | bytes 3145736 | tf_op jit(solution)/shard_map/ppermute | solution.py:42
  43.4 5.9 %shard_map.47 = (bf16[4096,2048]{1,0:T(8,128)(2,1)S(1)}, bf16[256,4096]{1,0:T(8,128)(2,1)S(1)}) custom-call(s32[4]{0:T(128)S(1)} %pad_add_fusion.1.where, s32[2,32,32]{2,1,0:T(8,128)S(1)} %copy-done.1, bf16[512,1024]{1,0:T(8,128)(2,1)S(1)} %pad_maximum_fusion.own0, ...), custom_call_target="tpu_custom_call", output_to_operand_aliasing={{0}: (7, {}), {1}: (8, {})} | custom-call | flops 5905580032 | bytes 8388608 | tf_op jit(solution)/shard_map/pallas_call | solution.py:290
  49.4 8.0 %shard_map.48 = (bf16[4096,2048]{1,0:T(8,128)(2,1)S(1)}, bf16[256,4096]{1,0:T(8,128)(2,1)S(1)}, f32[256,2048]{1,0:T(8,128)S(1)}) custom-call(s32[4]{0:T(128)S(1)} %pad_add_fusion.1.where, s32[2,32,32]{2,1,0:T(8,128)S(1)} %copy-done.1, bf16[512,1024]{1,0:T(8,128)(2,1)S(1)} %pad_maximum_fusion.own0, ...), custom_call_target="tpu_custom_call", output_to_operand_aliasing={{0}: (8, {}), {1}: (9, {})} | custom-call | flops 5905580032 | bytes 8388608 | tf_op jit(solution)/shard_map/pallas_call | solution.py:290
  57.4 1.0 collective-permute-start.12
  58.5 5.7 %shard_map.49 = (bf16[4096,2048]{1,0:T(8,128)(2,1)S(1)}, bf16[256,4096]{1,0:T(8,128)(2,1)S(1)}) custom-call(s32[4]{0:T(128)S(1)} %pad_add_fusion.1.where, s32[2,32,32]{2,1,0:T(8,128)S(1)} %copy-done.1, bf16[512,1024]{1,0:T(8,128)(2,1)S(1)} %pad_maximum_fusion.own0, ...), custom_call_target="tpu_custom_call", output_to_operand_aliasing={{0}: (10, {}), {1}: (11, {})} | custom-call | flops 5368709120 | bytes 8388608 | tf_op jit(solution)/shard_map/pallas_call | solution.py:290
  64.2 7.1 %shard_map.50 = (bf16[4096,2048]{1,0:T(8,128)(2,1)S(1)}, bf16[256,4096]{1,0:T(8,128)(2,1)S(1)}, bf16[256,2048]{1,0:T(8,128)(2,1)S(1)}, f32[256,512]{1,0:T(8,128)S(1)}) custom-call(s32[4]{0:T(128)S(1)} %pad_add_fusion.1.where, s32[2,32,32]{2,1,0:T(8,128)S(1)} %copy-done.1, ...), custom_call_target="tpu_custom_call", output_to_operand_aliasing={{0}: (10, {}), {1}: (11, {})} | custom-call | flops 4294967296 | bytes 20971520 | tf_op jit(solution)/shard_map/pallas_call | solution.py:290
  71.4 2.3 %shard_map.51 = (f32[256,512]{1,0:T(8,128)S(1)}, bf16[4096,512]{1,0:T(8,128)(2,1)S(1)}) custom-call(s32[4]{0:T(128)S(1)} %pad_add_fusion.1.where, bf16[256,2048]{1,0:T(8,128)(2,1)S(1)} %get-tuple-element.73.low, bf16[4096,2048]{1,0:T(8,128)(2,1)S(1)} %get-tuple-element.74.panel), custom_call_target="tpu_custom_call" | custom-call | flops 536870912 | bytes 12582912 | tf_op jit(solution)/shard_map/pallas_call | solution.py:290
  74.0 1.8 %shard_map.52.refs_0_ = bf16[256,512]{1,0:T(8,128)(2,1)S(1)} custom-call(s32[4]{0:T(128)S(1)} %pad_add_fusion.1.where, s32[2,32,32]{2,1,0:T(8,128)S(1)} %copy-done.1, bf16[256,2048]{1,0:T(8,128)(2,1)S(1)} %collective-permute-done.13.its, bf16[4096,512]{1,0:T(8,128)(2,1)S(1)} %get-tuple-element.75.columns, f32[256,512]{1,0:T(8,128)S(1)} %get-tuple-element.76.early, ...), custom_call_target="tpu_custom_call" | custom-call | flops 536870912 | bytes 4194304 | tf_op jit(solution)/shard_map/pallas_call | solution.py:290
  75.8 2.7 %collective-permute-start.17 = (bf16[256,512]{1,0:T(8,128)(2,1)S(1)}, bf16[256,512]{1,0:T(8,128)(2,1)S(1)}, u32[]{:S(2)}, u32[]{:S(2)}) collective-permute-start(bf16[256,512]{1,0:T(8,128)(2,1)S(1)} %shard_map.52.refs_0_), channel_id=1, source_target_pairs={{0,16},{1,17},{2,18},{3,19},{4,68},{5,69},{6,70},{7,71},{8,24},{9,... | collective-permute-start | bytes 786440 | tf_op jit(solution)/shard_map/ppermute | solution.py:42
  78.6 1.7 %collective-permute-start.16 = (bf16[256,512]{1,0:T(8,128)(2,1)S(1)}, bf16[256,512]{1,0:T(8,128)(2,1)S(1)}, u32[]{:S(2)}, u32[]{:S(2)}) collective-permute-start(bf16[256,512]{1,0:T(8,128)(2,1)S(1)} %shard_map.52.refs_0_), channel_id=1, source_target_pairs={{0,64},{1,65},{2,66},{3,67},{4,20},{5,21},{6,22},{7,23},{8,72},{9,... | collective-permute-start | bytes 786440 | tf_op jit(solution)/shard_map/ppermute | solution.py:37
  80.9 2.1 %collective-permute-start.14 = (bf16[256,512]{1,0:T(8,128)(2,1)S(1)}, bf16[256,512]{1,0:T(8,128)(2,1)S(1)}, u32[]{:S(2)}, u32[]{:S(2)}) collective-permute-start(bf16[256,512]{1,0:T(8,128)(2,1)S(1)} %shard_map.52.refs_0_), channel_id=1, source_target_pairs={{0,96},{1,97},{2,98},{3,99},{4,28},{5,29},{6,30},{7,31},{8,104},{9... | collective-permute-start | bytes 786440 | tf_op jit(solution)/shard_map/ppermute | solution.py:37
  83.0 1.6 %collective-permute-start.21 = (bf16[256,512]{1,0:T(8,128)(2,1)S(1)}, bf16[256,512]{1,0:T(8,128)(2,1)S(1)}, u32[]{:S(2)}, u32[]{:S(2)}) collective-permute-start(bf16[256,512]{1,0:T(8,128)(2,1)S(1)} %shard_map.52.refs_0_), channel_id=1, source_target_pairs={{0,2},{1,3},{2,0},{3,1},{4,6},{5,7},{6,4},{7,5},{8,10},{9,11},{10,... | collective-permute-start | bytes 786440 | tf_op jit(solution)/shard_map/ppermute | solution.py:33
  84.6 1.6 %collective-permute-done.16 = bf16[256,512]{1,0:T(8,128)(2,1)S(1)} collective-permute-done((bf16[256,512]{1,0:T(8,128)(2,1)S(1)}, bf16[256,512]{1,0:T(8,128)(2,1)S(1)}, u32[]{:S(2)}, u32[]{:S(2)}) %collective-permute-start.16) | collective-permute-done | bytes 262176 | tf_op jit(solution)/shard_map/ppermute | solution.py:37
  86.6 2.6 %collective-permute-done.15 = bf16[256,512]{1,0:T(8,128)(2,1)S(1)} collective-permute-done((bf16[256,512]{1,0:T(8,128)(2,1)S(1)}, bf16[256,512]{1,0:T(8,128)(2,1)S(1)}, u32[]{:S(2)}, u32[]{:S(2)}) %collective-permute-start.15) | collective-permute-done | bytes 262176 | tf_op jit(solution)/shard_map/ppermute | solution.py:37
  89.3 2.0 %collective-permute-start.19 = (bf16[1024,512]{1,0:T(8,128)(2,1)S(1)}, bf16[1024,512]{1,0:T(8,128)(2,1)S(1)}, u32[]{:S(2)}, u32[]{:S(2)}) collective-permute-start(bf16[1024,512]{1,0:T(8,128)(2,1)S(1)} %constant_dynamic-update-slice_fusion.refs_8_), channel_id=1, source_target_pairs={{0,8},{1,9},{2,10},{3,11},{4,36},{5,37},{6,38},{7,39},{8,16},{9,17... | collective-permute-start | bytes 3145736 | tf_op jit(solution)/shard_map/ppermute | solution.py:42
  91.2 1.1 collective-permute-start.18
  92.3 3.0 %collective-permute-done.21.refs_2_ = bf16[256,512]{1,0:T(8,128)(2,1)S(1)} collective-permute-done((bf16[256,512]{1,0:T(8,128)(2,1)S(1)}, bf16[256,512]{1,0:T(8,128)(2,1)S(1)}, u32[]{:S(2)}, u32[]{:S(2)}) %collective-permute-start.21) | collective-permute-done | bytes 262176 | tf_op jit(solution)/shard_map/ppermute | solution.py:33
  95.3 2.3 %collective-permute-done.20.refs_1_ = bf16[256,512]{1,0:T(8,128)(2,1)S(1)} collective-permute-done((bf16[256,512]{1,0:T(8,128)(2,1)S(1)}, bf16[256,512]{1,0:T(8,128)(2,1)S(1)}, u32[]{:S(2)}, u32[]{:S(2)}) %collective-permute-start.20) | collective-permute-done | bytes 262176 | tf_op jit(solution)/shard_map/ppermute | solution.py:33
  97.6 0.8 collective-permute-start.24
  98.4 1.9 %collective-permute-start.23 = (bf16[256,512]{1,0:T(8,128)(2,1)S(1)}, bf16[256,512]{1,0:T(8,128)(2,1)S(1)}, u32[]{:S(2)}, u32[]{:S(2)}) collective-permute-start(bf16[256,512]{1,0:T(8,128)(2,1)S(1)} %collective-permute-done.17.refs_9_), channel_id=1, source_target_pairs={{0,96},{1,97},{2,98},{3,99},{4,28},{5,29},{6,30},{7,31},{8,104},{9... | collective-permute-start | bytes 786440 | tf_op jit(solution)/shard_map/ppermute | solution.py:37
  100.3 8.8 %collective-permute-done.25.refs_12_ = bf16[256,512]{1,0:T(8,128)(2,1)S(1)} collective-permute-done((bf16[256,512]{1,0:T(8,128)(2,1)S(1)}, bf16[256,512]{1,0:T(8,128)(2,1)S(1)}, u32[]{:S(2)}, u32[]{:S(2)}) %collective-permute-start.25) | collective-permute-done | bytes 262176 | tf_op jit(solution)/shard_map/ppermute | solution.py:37
  109.1 1.9 %collective-permute-done.24.refs_11_ = bf16[256,512]{1,0:T(8,128)(2,1)S(1)} collective-permute-done((bf16[256,512]{1,0:T(8,128)(2,1)S(1)}, bf16[256,512]{1,0:T(8,128)(2,1)S(1)}, u32[]{:S(2)}, u32[]{:S(2)}) %collective-permute-start.24) | collective-permute-done | bytes 262176 | tf_op jit(solution)/shard_map/ppermute | solution.py:37
  114.2 4.9 %shard_map.53 = (f32[256,512]{1,0:T(8,128)S(1)}, bf16[256,4096]{1,0:T(8,128)(2,1)S(1)}, bf16[2048,512]{1,0:T(8,128)(2,1)S(1)}, bf16[2048,512]{1,0:T(8,128)(2,1)S(1)}) custom-call(s32[4]{0:T(128)S(1)} %pad_add_fusion.1.where, bf16[256,512]{1,0:T(8,128)(2,1)S(1)} %shard_map.52.refs_0_, bf16[256,512]{1,0:T(8,128)(2,1)S(1)} %collective-permute-done.20.refs_1_, ...), custom_call_target="tpu_custom_call" | custom-call | flops 536870912 | bytes 10485760 | tf_op jit(solution)/shard_map/pallas_call | solution.py:290
  119.2 4.9 %shard_map.54 = (f32[256,512]{1,0:T(8,128)S(1)}, bf16[256,512]{1,0:T(8,128)(2,1)S(1)}, bf16[2048,512]{1,0:T(8,128)(2,1)S(1)}, bf16[2048,512]{1,0:T(8,128)(2,1)S(1)}) custom-call(s32[4]{0:T(128)S(1)} %pad_add_fusion.1.where, s32[2,32,32]{2,1,0:T(8,128)S(1)} %copy-done.2, ...), custom_call_target="tpu_custom_call", output_to_operand_aliasing={{2}: (6, {}), {3}: (7, {})} | custom-call | flops 536870912 | bytes 8388608 | tf_op jit(solution)/shard_map/pallas_call | solution.py:290
  124.5 2.7 %collective-permute-start.30 = (bf16[256,512]{1,0:T(8,128)(2,1)S(1)}, bf16[256,512]{1,0:T(8,128)(2,1)S(1)}, u32[]{:S(2)}, u32[]{:S(2)}) collective-permute-start(bf16[256,512]{1,0:T(8,128)(2,1)S(1)} %get-tuple-element.99.own0), channel_id=1, source_target_pairs={{0,3},{1,0},{2,1},{3,2},{4,7},{5,4},{6,5},{7,6},{8,11},{9,8},{10,9... | collective-permute-start | bytes 786440 | tf_op jit(solution)/shard_map/ppermute | solution.py:33
  127.2 6.5 %collective-permute-done.31.own3 = bf16[256,512]{1,0:T(8,128)(2,1)S(1)} collective-permute-done((bf16[256,512]{1,0:T(8,128)(2,1)S(1)}, bf16[256,512]{1,0:T(8,128)(2,1)S(1)}, u32[]{:S(2)}, u32[]{:S(2)}) %collective-permute-start.31) | collective-permute-done | bytes 262176 | tf_op jit(solution)/shard_map/ppermute | solution.py:33
  133.7 4.2 %collective-permute-done.30.own1 = bf16[256,512]{1,0:T(8,128)(2,1)S(1)} collective-permute-done((bf16[256,512]{1,0:T(8,128)(2,1)S(1)}, bf16[256,512]{1,0:T(8,128)(2,1)S(1)}, u32[]{:S(2)}, u32[]{:S(2)}) %collective-permute-start.30) | collective-permute-done | bytes 262176 | tf_op jit(solution)/shard_map/ppermute | solution.py:33
  137.9 1.5 %shard_map.55.early = f32[256,1024]{1,0:T(8,128)S(1)} custom-call(s32[4]{0:T(128)S(1)} %pad_add_fusion.1.where, bf16[256,512]{1,0:T(8,128)(2,1)S(1)} %get-tuple-element.99.own0, bf16[256,512]{1,0:T(8,128)(2,1)S(1)} %collective-permute-done.30.own1, bf16[256,512]{1,0:T(8,128)(2,1)S(1)} %collective-permute-done.31.own3, ...), custom_call_target="tpu_custom_call" | custom-call | flops 805306368 | bytes 4194304 | tf_op jit(solution)/shard_map/pallas_call | solution.py:290
  139.5 0.9 shard_map.56
  140.3 2.2 %collective-permute-start.34 = (f32[128,1024]{1,0:T(8,128)S(1)}, f32[128,1024]{1,0:T(8,128)S(1)}, u32[]{:S(2)}, u32[]{:S(2)}) collective-permute-start(f32[128,1024]{1,0:T(8,128)S(1)} %shard_map.56), channel_id=1, source_target_pairs={{0,4},{1,5},{2,6},{3,7},{4,0},{5,1},{6,2},{7,3},{8,12},{9,13},{10,... | collective-permute-start | bytes 1572872 | tf_op jit(solution)/shard_map/ppermute | solution.py:29
  142.6 1.5 %collective-permute-done.34.share = f32[128,1024]{1,0:T(8,128)S(1)} collective-permute-done((f32[128,1024]{1,0:T(8,128)S(1)}, f32[128,1024]{1,0:T(8,128)S(1)}, u32[]{:S(2)}, u32[]{:S(2)}) %collective-permute-start.34) | collective-permute-done | bytes 524320 | tf_op jit(solution)/shard_map/ppermute | solution.py:29
  144.1 1.7 %shard_map.57 = f32[128,1024]{1,0:T(8,128)} custom-call(s32[4]{0:T(128)S(1)} %pad_add_fusion.1.where, bf16[256,512]{1,0:T(8,128)(2,1)S(1)} %collective-permute-done.33.own2, f32[256,1024]{1,0:T(8,128)S(1)} %shard_map.55.early, f32[256,512]{1,0:T(8,128)S(1)} %get-tuple-element.104.square, bf16[2048,512]{1,0:T(8,128)(2,1)S(1)} %get-tuple-element.100.mine, ...), custom_call_target="tpu_custom_call" | custom-call | flops 134217728 | bytes 3145728 | tf_op jit(solution)/shard_map/pallas_call | solution.py:290
  (55 shorter events, 7.1 us)
Async XLA Ops:
  0.0 5.9 %copy-start = (s32[32,8]{0,1:T(8,128)S(1)}, s32[32,8]{0,1:T(8,128)}, u32[]{:S(2)}) copy-start(s32[32,8]{0,1:T(8,128)} %param.5) | copy-start | bytes 3076
  0.0 27.0 %copy-start.1 = (s32[2,32,32]{2,1,0:T(8,128)S(1)}, s32[2,32,32]{2,1,0:T(8,128)}, u32[]{:S(2)}) copy-start(s32[2,32,32]{2,1,0:T(8,128)} %keep_d.11) | copy-start | bytes 24580
  0.0 6.7 %collective-permute-start.1 = (bf16[128,256]{1,0:T(8,128)(2,1)}, bf16[128,256]{1,0:T(8,128)(2,1)S(1)}, u32[]{:S(2)}, u32[]{:S(2)}) collective-permute-start(bf16[128,256]{1,0:T(8,128)(2,1)} %param.4), channel_id=1, source_target_pairs={{0,2},{1,3},{2,0},{3,1},{4,6},{5,7},{6,4},{7,5},{8,10},{9,11},{10,... | collective-permute-start | bytes 196616 | tf_op jit(solution)/shard_map/ppermute | solution.py:33
  4.4 3.7 %collective-permute-start = (bf16[128,256]{1,0:T(8,128)(2,1)}, bf16[128,256]{1,0:T(8,128)(2,1)S(1)}, u32[]{:S(2)}, u32[]{:S(2)}) collective-permute-start(bf16[128,256]{1,0:T(8,128)(2,1)} %param.4), channel_id=1, source_target_pairs={{0,3},{1,0},{2,1},{3,2},{4,7},{5,4},{6,5},{7,6},{8,11},{9,8},{10,9... | collective-permute-start | bytes 196616 | tf_op jit(solution)/shard_map/ppermute | solution.py:33
  4.9 4.5 %collective-permute-start.2 = (bf16[128,256]{1,0:T(8,128)(2,1)}, bf16[128,256]{1,0:T(8,128)(2,1)S(1)}, u32[]{:S(2)}, u32[]{:S(2)}) collective-permute-start(bf16[128,256]{1,0:T(8,128)(2,1)} %param.4), channel_id=1, source_target_pairs={{0,1},{1,2},{2,3},{3,0},{4,5},{5,6},{6,7},{7,4},{8,9},{9,10},{10,1... | collective-permute-start | bytes 196616 | tf_op jit(solution)/shard_map/ppermute | solution.py:33
  10.3 6.9 %collective-permute-start.5 = (bf16[128,1024]{1,0:T(8,128)(2,1)S(1)}, bf16[128,1024]{1,0:T(8,128)(2,1)S(1)}, u32[]{:S(2)}, u32[]{:S(2)}) collective-permute-start(bf16[128,1024]{1,0:T(8,128)(2,1)S(1)} %maximum_multiply_fusion), channel_id=1, source_target_pairs={{0,32},{1,33},{2,34},{3,35},{4,12},{5,13},{6,14},{7,15},{8,40},{9,... | collective-permute-start | bytes 786440 | tf_op jit(solution)/shard_map/ppermute | solution.py:37
  11.7 9.5 %collective-permute-start.4 = (bf16[128,1024]{1,0:T(8,128)(2,1)S(1)}, bf16[128,1024]{1,0:T(8,128)(2,1)S(1)}, u32[]{:S(2)}, u32[]{:S(2)}) collective-permute-start(bf16[128,1024]{1,0:T(8,128)(2,1)S(1)} %maximum_multiply_fusion), channel_id=1, source_target_pairs={{0,64},{1,65},{2,66},{3,67},{4,20},{5,21},{6,22},{7,23},{8,72},{9,... | collective-permute-start | bytes 786440 | tf_op jit(solution)/shard_map/ppermute | solution.py:37
  14.3 6.9 %collective-permute-start.3 = (bf16[128,1024]{1,0:T(8,128)(2,1)S(1)}, bf16[128,1024]{1,0:T(8,128)(2,1)S(1)}, u32[]{:S(2)}, u32[]{:S(2)}) collective-permute-start(bf16[128,1024]{1,0:T(8,128)(2,1)S(1)} %maximum_multiply_fusion), channel_id=1, source_target_pairs={{0,96},{1,97},{2,98},{3,99},{4,28},{5,29},{6,30},{7,31},{8,104},{9... | collective-permute-start | bytes 786440 | tf_op jit(solution)/shard_map/ppermute | solution.py:37
  21.2 5.8 %collective-permute-start.6 = (bf16[512,1024]{1,0:T(8,128)(2,1)S(1)}, bf16[512,1024]{1,0:T(8,128)(2,1)}, u32[]{:S(2)}, u32[]{:S(2)}) collective-permute-start(bf16[512,1024]{1,0:T(8,128)(2,1)S(1)} %pad_maximum_fusion.own0), channel_id=1, source_target_pairs={{0,4},{1,5},{2,6},{3,7},{4,0},{5,1},{6,2},{7,3},{8,12},{9,13},{10,... | collective-permute-start | bytes 3145736 | tf_op jit(solution)/shard_map/ppermute | solution.py:29
  24.3 15.2 %collective-permute-start.8 = (bf16[512,1024]{1,0:T(8,128)(2,1)S(1)}, bf16[512,1024]{1,0:T(8,128)(2,1)S(1)}, u32[]{:S(2)}, u32[]{:S(2)}) collective-permute-start(bf16[512,1024]{1,0:T(8,128)(2,1)S(1)} %pad_maximum_fusion.own0), channel_id=1, source_target_pairs={{0,8},{1,9},{2,10},{3,11},{4,36},{5,37},{6,38},{7,39},{8,16},{9,17... | collective-permute-start | bytes 3145736 | tf_op jit(solution)/shard_map/ppermute | solution.py:42
  25.9 13.9 %collective-permute-start.7 = (bf16[512,1024]{1,0:T(8,128)(2,1)S(1)}, bf16[512,1024]{1,0:T(8,128)(2,1)S(1)}, u32[]{:S(2)}, u32[]{:S(2)}) collective-permute-start(bf16[512,1024]{1,0:T(8,128)(2,1)S(1)} %pad_maximum_fusion.own0), channel_id=1, source_target_pairs={{0,24},{1,25},{2,26},{3,27},{4,100},{5,101},{6,102},{7,103},{8,0},... | collective-permute-start | bytes 3145736 | tf_op jit(solution)/shard_map/ppermute | solution.py:42
  39.8 9.5 %collective-permute-start.9 = (bf16[512,1024]{1,0:T(8,128)(2,1)S(1)}, bf16[512,1024]{1,0:T(8,128)(2,1)S(1)}, u32[]{:S(2)}, u32[]{:S(2)}) collective-permute-start(bf16[512,1024]{1,0:T(8,128)(2,1)S(1)} %collective-permute-done.7.own1), channel_id=1, source_target_pairs={{0,4},{1,5},{2,6},{3,7},{4,0},{5,1},{6,2},{7,3},{8,12},{9,13},{10,... | collective-permute-start | bytes 3145736 | tf_op jit(solution)/shard_map/ppermute | solution.py:29
  40.7 8.6 %collective-permute-start.10 = (bf16[512,1024]{1,0:T(8,128)(2,1)S(1)}, bf16[512,1024]{1,0:T(8,128)(2,1)S(1)}, u32[]{:S(2)}, u32[]{:S(2)}) collective-permute-start(bf16[512,1024]{1,0:T(8,128)(2,1)S(1)} %collective-permute-done.8.own3), channel_id=1, source_target_pairs={{0,4},{1,5},{2,6},{3,7},{4,0},{5,1},{6,2},{7,3},{8,12},{9,13},{10,... | collective-permute-start | bytes 3145736 | tf_op jit(solution)/shard_map/ppermute | solution.py:29
  40.7 16.7 %collective-permute-start.11 = (bf16[512,1024]{1,0:T(8,128)(2,1)S(1)}, bf16[512,1024]{1,0:T(8,128)(2,1)S(1)}, u32[]{:S(2)}, u32[]{:S(2)}) collective-permute-start(bf16[512,1024]{1,0:T(8,128)(2,1)S(1)} %pad_maximum_fusion.own0), channel_id=1, source_target_pairs={{0,16},{1,17},{2,18},{3,19},{4,68},{5,69},{6,70},{7,71},{8,24},{9,... | collective-permute-start | bytes 3145736 | tf_op jit(solution)/shard_map/ppermute | solution.py:42
  57.4 6.7 %copy-start.2 = (s32[2,32,32]{2,1,0:T(8,128)S(1)}, s32[2,32,32]{2,1,0:T(8,128)}, u32[]{:S(2)}) copy-start(s32[2,32,32]{2,1,0:T(8,128)} %keep_s.3) | copy-start | bytes 24580
  57.4 6.7 %collective-permute-start.12 = (bf16[512,1024]{1,0:T(8,128)(2,1)S(1)}, bf16[512,1024]{1,0:T(8,128)(2,1)S(1)}, u32[]{:S(2)}, u32[]{:S(2)}) collective-permute-start(bf16[512,1024]{1,0:T(8,128)(2,1)S(1)} %collective-permute-done.11.own2), channel_id=1, source_target_pairs={{0,4},{1,5},{2,6},{3,7},{4,0},{5,1},{6,2},{7,3},{8,12},{9,13},{10,... | collective-permute-start | bytes 3145736 | tf_op jit(solution)/shard_map/ppermute | solution.py:29
  71.3 2.7 %collective-permute-start.13 = (bf16[256,2048]{1,0:T(8,128)(2,1)S(1)}, bf16[256,2048]{1,0:T(8,128)(2,1)S(1)}, u32[]{:S(2)}, u32[]{:S(2)}) collective-permute-start(bf16[256,2048]{1,0:T(8,128)(2,1)S(1)} %get-tuple-element.73.low), channel_id=1, source_target_pairs={{0,4},{1,5},{2,6},{3,7},{4,0},{5,1},{6,2},{7,3},{8,12},{9,13},{10,... | collective-permute-start | bytes 3145736 | tf_op jit(solution)/shard_map/ppermute | solution.py:29
  75.8 7.1 %collective-permute-start.17 = (bf16[256,512]{1,0:T(8,128)(2,1)S(1)}, bf16[256,512]{1,0:T(8,128)(2,1)S(1)}, u32[]{:S(2)}, u32[]{:S(2)}) collective-permute-start(bf16[256,512]{1,0:T(8,128)(2,1)S(1)} %shard_map.52.refs_0_), channel_id=1, source_target_pairs={{0,16},{1,17},{2,18},{3,19},{4,68},{5,69},{6,70},{7,71},{8,24},{9,... | collective-permute-start | bytes 786440 | tf_op jit(solution)/shard_map/ppermute | solution.py:42
  78.6 7.6 %collective-permute-start.16 = (bf16[256,512]{1,0:T(8,128)(2,1)S(1)}, bf16[256,512]{1,0:T(8,128)(2,1)S(1)}, u32[]{:S(2)}, u32[]{:S(2)}) collective-permute-start(bf16[256,512]{1,0:T(8,128)(2,1)S(1)} %shard_map.52.refs_0_), channel_id=1, source_target_pairs={{0,64},{1,65},{2,66},{3,67},{4,20},{5,21},{6,22},{7,23},{8,72},{9,... | collective-permute-start | bytes 786440 | tf_op jit(solution)/shard_map/ppermute | solution.py:37
  80.3 8.9 %collective-permute-start.15 = (bf16[256,512]{1,0:T(8,128)(2,1)S(1)}, bf16[256,512]{1,0:T(8,128)(2,1)S(1)}, u32[]{:S(2)}, u32[]{:S(2)}) collective-permute-start(bf16[256,512]{1,0:T(8,128)(2,1)S(1)} %shard_map.52.refs_0_), channel_id=1, source_target_pairs={{0,32},{1,33},{2,34},{3,35},{4,12},{5,13},{6,14},{7,15},{8,40},{9,... | collective-permute-start | bytes 786440 | tf_op jit(solution)/shard_map/ppermute | solution.py:37
  80.9 8.3 %collective-permute-start.14 = (bf16[256,512]{1,0:T(8,128)(2,1)S(1)}, bf16[256,512]{1,0:T(8,128)(2,1)S(1)}, u32[]{:S(2)}, u32[]{:S(2)}) collective-permute-start(bf16[256,512]{1,0:T(8,128)(2,1)S(1)} %shard_map.52.refs_0_), channel_id=1, source_target_pairs={{0,96},{1,97},{2,98},{3,99},{4,28},{5,29},{6,30},{7,31},{8,104},{9... | collective-permute-start | bytes 786440 | tf_op jit(solution)/shard_map/ppermute | solution.py:37
  83.0 9.3 %collective-permute-start.22 = (bf16[256,512]{1,0:T(8,128)(2,1)S(1)}, bf16[256,512]{1,0:T(8,128)(2,1)S(1)}, u32[]{:S(2)}, u32[]{:S(2)}) collective-permute-start(bf16[256,512]{1,0:T(8,128)(2,1)S(1)} %shard_map.52.refs_0_), channel_id=1, source_target_pairs={{0,1},{1,2},{2,3},{3,0},{4,5},{5,6},{6,7},{7,4},{8,9},{9,10},{10,1... | collective-permute-start | bytes 786440 | tf_op jit(solution)/shard_map/ppermute | solution.py:33
  83.0 12.3 %collective-permute-start.21 = (bf16[256,512]{1,0:T(8,128)(2,1)S(1)}, bf16[256,512]{1,0:T(8,128)(2,1)S(1)}, u32[]{:S(2)}, u32[]{:S(2)}) collective-permute-start(bf16[256,512]{1,0:T(8,128)(2,1)S(1)} %shard_map.52.refs_0_), channel_id=1, source_target_pairs={{0,2},{1,3},{2,0},{3,1},{4,6},{5,7},{6,4},{7,5},{8,10},{9,11},{10,... | collective-permute-start | bytes 786440 | tf_op jit(solution)/shard_map/ppermute | solution.py:33
  86.2 11.4 %collective-permute-start.20 = (bf16[256,512]{1,0:T(8,128)(2,1)S(1)}, bf16[256,512]{1,0:T(8,128)(2,1)S(1)}, u32[]{:S(2)}, u32[]{:S(2)}) collective-permute-start(bf16[256,512]{1,0:T(8,128)(2,1)S(1)} %shard_map.52.refs_0_), channel_id=1, source_target_pairs={{0,3},{1,0},{2,1},{3,2},{4,7},{5,4},{6,5},{7,6},{8,11},{9,8},{10,9... | collective-permute-start | bytes 786440 | tf_op jit(solution)/shard_map/ppermute | solution.py:33
  89.3 29.9 %collective-permute-start.19 = (bf16[1024,512]{1,0:T(8,128)(2,1)S(1)}, bf16[1024,512]{1,0:T(8,128)(2,1)S(1)}, u32[]{:S(2)}, u32[]{:S(2)}) collective-permute-start(bf16[1024,512]{1,0:T(8,128)(2,1)S(1)} %constant_dynamic-update-slice_fusion.refs_8_), channel_id=1, source_target_pairs={{0,8},{1,9},{2,10},{3,11},{4,36},{5,37},{6,38},{7,39},{8,16},{9,17... | collective-permute-start | bytes 3145736 | tf_op jit(solution)/shard_map/ppermute | solution.py:42
  91.2 28.0 %collective-permute-start.18 = (bf16[1024,512]{1,0:T(8,128)(2,1)S(1)}, bf16[1024,512]{1,0:T(8,128)(2,1)S(1)}, u32[]{:S(2)}, u32[]{:S(2)}) collective-permute-start(bf16[1024,512]{1,0:T(8,128)(2,1)S(1)} %constant_dynamic-update-slice_fusion.refs_8_), channel_id=1, source_target_pairs={{0,24},{1,25},{2,26},{3,27},{4,100},{5,101},{6,102},{7,103},{8,0},... | collective-permute-start | bytes 3145736 | tf_op jit(solution)/shard_map/ppermute | solution.py:42
  97.6 11.5 %collective-permute-start.25 = (bf16[256,512]{1,0:T(8,128)(2,1)S(1)}, bf16[256,512]{1,0:T(8,128)(2,1)S(1)}, u32[]{:S(2)}, u32[]{:S(2)}) collective-permute-start(bf16[256,512]{1,0:T(8,128)(2,1)S(1)} %collective-permute-done.17.refs_9_), channel_id=1, source_target_pairs={{0,32},{1,33},{2,34},{3,35},{4,12},{5,13},{6,14},{7,15},{8,40},{9,... | collective-permute-start | bytes 786440 | tf_op jit(solution)/shard_map/ppermute | solution.py:37
  97.6 13.3 %collective-permute-start.24 = (bf16[256,512]{1,0:T(8,128)(2,1)S(1)}, bf16[256,512]{1,0:T(8,128)(2,1)S(1)}, u32[]{:S(2)}, u32[]{:S(2)}) collective-permute-start(bf16[256,512]{1,0:T(8,128)(2,1)S(1)} %collective-permute-done.17.refs_9_), channel_id=1, source_target_pairs={{0,64},{1,65},{2,66},{3,67},{4,20},{5,21},{6,22},{7,23},{8,72},{9,... | collective-permute-start | bytes 786440 | tf_op jit(solution)/shard_map/ppermute | solution.py:37
  98.4 12.5 %collective-permute-start.23 = (bf16[256,512]{1,0:T(8,128)(2,1)S(1)}, bf16[256,512]{1,0:T(8,128)(2,1)S(1)}, u32[]{:S(2)}, u32[]{:S(2)}) collective-permute-start(bf16[256,512]{1,0:T(8,128)(2,1)S(1)} %collective-permute-done.17.refs_9_), channel_id=1, source_target_pairs={{0,96},{1,97},{2,98},{3,99},{4,28},{5,29},{6,30},{7,31},{8,104},{9... | collective-permute-start | bytes 786440 | tf_op jit(solution)/shard_map/ppermute | solution.py:37
  110.9 1.8 %collective-permute-start.26 = (bf16[256,512]{1,0:T(8,128)(2,1)S(1)}, bf16[256,512]{1,0:T(8,128)(2,1)S(1)}, u32[]{:S(2)}, u32[]{:S(2)}) collective-permute-start(bf16[256,512]{1,0:T(8,128)(2,1)S(1)} %shard_map.52.refs_0_), channel_id=1, source_target_pairs={{0,4},{1,5},{2,6},{3,7},{4,0},{5,1},{6,2},{7,3},{8,12},{9,13},{10,... | collective-permute-start | bytes 786440 | tf_op jit(solution)/shard_map/ppermute | solution.py:29
  111.5 1.5 %collective-permute-start.27 = (bf16[256,512]{1,0:T(8,128)(2,1)S(1)}, bf16[256,512]{1,0:T(8,128)(2,1)S(1)}, u32[]{:S(2)}, u32[]{:S(2)}) collective-permute-start(bf16[256,512]{1,0:T(8,128)(2,1)S(1)} %collective-permute-done.20.refs_1_), channel_id=1, source_target_pairs={{0,4},{1,5},{2,6},{3,7},{4,0},{5,1},{6,2},{7,3},{8,12},{9,13},{10,... | collective-permute-start | bytes 786440 | tf_op jit(solution)/shard_map/ppermute | solution.py:29
  111.5 1.9 %collective-permute-start.28 = (bf16[256,512]{1,0:T(8,128)(2,1)S(1)}, bf16[256,512]{1,0:T(8,128)(2,1)S(1)}, u32[]{:S(2)}, u32[]{:S(2)}) collective-permute-start(bf16[256,512]{1,0:T(8,128)(2,1)S(1)} %collective-permute-done.21.refs_2_), channel_id=1, source_target_pairs={{0,4},{1,5},{2,6},{3,7},{4,0},{5,1},{6,2},{7,3},{8,12},{9,13},{10,... | collective-permute-start | bytes 786440 | tf_op jit(solution)/shard_map/ppermute | solution.py:29
  112.7 1.5 %collective-permute-start.29 = (bf16[256,512]{1,0:T(8,128)(2,1)S(1)}, bf16[256,512]{1,0:T(8,128)(2,1)S(1)}, u32[]{:S(2)}, u32[]{:S(2)}) collective-permute-start(bf16[256,512]{1,0:T(8,128)(2,1)S(1)} %collective-permute-done.22.refs_3_), channel_id=1, source_target_pairs={{0,4},{1,5},{2,6},{3,7},{4,0},{5,1},{6,2},{7,3},{8,12},{9,13},{10,... | collective-permute-start | bytes 786440 | tf_op jit(solution)/shard_map/ppermute | solution.py:29
  124.1 13.9 %collective-permute-start.32 = (bf16[2048,512]{1,0:T(8,128)(2,1)S(1)}, bf16[2048,512]{1,0:T(8,128)(2,1)S(1)}, u32[]{:S(2)}, u32[]{:S(2)}) collective-permute-start(bf16[2048,512]{1,0:T(8,128)(2,1)S(1)} %get-tuple-element.101), channel_id=1, source_target_pairs={{0,4},{1,5},{2,6},{3,7},{4,0},{5,1},{6,2},{7,3},{8,12},{9,13},{10,... | collective-permute-start | bytes 6291464 | tf_op jit(solution)/shard_map/ppermute | solution.py:29
  124.5 9.2 %collective-permute-start.31 = (bf16[256,512]{1,0:T(8,128)(2,1)S(1)}, bf16[256,512]{1,0:T(8,128)(2,1)S(1)}, u32[]{:S(2)}, u32[]{:S(2)}) collective-permute-start(bf16[256,512]{1,0:T(8,128)(2,1)S(1)} %get-tuple-element.99.own0), channel_id=1, source_target_pairs={{0,1},{1,2},{2,3},{3,0},{4,5},{5,6},{6,7},{7,4},{8,9},{9,10},{10,1... | collective-permute-start | bytes 786440 | tf_op jit(solution)/shard_map/ppermute | solution.py:33
  124.5 13.4 %collective-permute-start.30 = (bf16[256,512]{1,0:T(8,128)(2,1)S(1)}, bf16[256,512]{1,0:T(8,128)(2,1)S(1)}, u32[]{:S(2)}, u32[]{:S(2)}) collective-permute-start(bf16[256,512]{1,0:T(8,128)(2,1)S(1)} %get-tuple-element.99.own0), channel_id=1, source_target_pairs={{0,3},{1,0},{2,1},{3,2},{4,7},{5,4},{6,5},{7,6},{8,11},{9,8},{10,9... | collective-permute-start | bytes 786440 | tf_op jit(solution)/shard_map/ppermute | solution.py:33
  127.2 12.3 %collective-permute-start.33 = (bf16[256,512]{1,0:T(8,128)(2,1)S(1)}, bf16[256,512]{1,0:T(8,128)(2,1)S(1)}, u32[]{:S(2)}, u32[]{:S(2)}) collective-permute-start(bf16[256,512]{1,0:T(8,128)(2,1)S(1)} %get-tuple-element.99.own0), channel_id=1, source_target_pairs={{0,2},{1,3},{2,0},{3,1},{4,6},{5,7},{6,4},{7,5},{8,10},{9,11},{10,... | collective-permute-start | bytes 786440 | tf_op jit(solution)/shard_map/ppermute | solution.py:33
  140.3 3.8 %collective-permute-start.34 = (f32[128,1024]{1,0:T(8,128)S(1)}, f32[128,1024]{1,0:T(8,128)S(1)}, u32[]{:S(2)}, u32[]{:S(2)}) collective-permute-start(f32[128,1024]{1,0:T(8,128)S(1)} %shard_map.56), channel_id=1, source_target_pairs={{0,4},{1,5},{2,6},{3,7},{4,0},{5,1},{6,2},{7,3},{8,12},{9,13},{10,... | collective-permute-start | bytes 1572872 | tf_op jit(solution)/shard_map/ppermute | solution.py:29

commit v3 on v2

--- a/solution.py
+++ b/solution.py
@@ -199,53 +199,44 @@
             out[t * B:(t + 1) * B, u * B:(u + 1) * B] = piece.astype(jnp.bfloat16)
 
 
-def chips_times(where, line, chips, mine, its, sems):
+def chips_times(where, line, chips, mine, its):
     x, y, core = where[0], where[1], where[2]
-    copies, left, right = [], [], []
-    for n, (ref, offset, first, second) in enumerate(chips):
+    left, right = [], []
+    for ref, offset, first, second in chips:
         px, py = place(x, y, core, first, second)
         chip = px * 4 + py
-        for m, (panel, kind) in enumerate(((mine, core), (its, 1 - core))):
-            copies.append(pltpu.make_async_copy(
-                ref.at[pl.ds(pl.multiple_of(offset + kind * B, B), B)], panel.at[aligned(chip, B)], sems.at[n, m]))
-            copies[-1].start()
+        mine[aligned(chip, B), :] = ref[pl.ds(pl.multiple_of(offset + core * B, B), B), :]
+        its[aligned(chip, B), :] = ref[pl.ds(pl.multiple_of(offset + (1 - core) * B, B), B), :]
         left.append(line[:, aligned(chip, ROWS)])
         right.append(ref[offset:offset + ROWS, :])
     total = None
     for n in range(0, len(chips), 4):
         term = dot(jnp.concatenate(left[n:n + 4], axis=1), jnp.concatenate(right[n:n + 4], axis=0))
         total = term if total is None else total + term
-    return total, copies
+    return total
 
 
 def early_square(where, *refs):
-    own, other, near, far, (early, line, mine, its), (sems,) = (
-        refs[:4], refs[4:8], refs[8], refs[9:13], refs[13:17], refs[17:])
+    own, other, near, far, (early, line, mine, its) = refs[:4], refs[4:8], refs[8], refs[9:13], refs[13:]
     core, z = where[2], where[3]
     for d in range(4):
         for ref, kind in ((own[d], core), (other[d], 1 - core)):
             for t in range(4):
                 line[:, aligned(((z + d) & 3) * 8 + t * 2 + kind, B)] = ref[:, t * B:(t + 1) * B]
     chips = [(near, i * ROWS, i, 0) for i in range(4)] + [(far[i], 0, i, 2) for i in range(4)]
-    value, copies = chips_times(where, line, chips, mine, its, sems)
-    early[...] = value
-    for copy in copies:
-        copy.wait()
-
-
-def second_square(where, keep_s, one, three, early, line, _, __, square, low, mine, its, sems):
+    early[...] = chips_times(where, line, chips, mine, its)
+
+
+def second_square(where, keep_s, one, three, early, line, _, __, square, low, mine, its):
     x, y, core, z = where[0], where[1], where[2], where[3]
     chips = [(ref, i * ROWS, i, j) for ref, j in ((one, 1), (three, 3)) for i in range(4)]
-    value, copies = chips_times(where, line, chips, mine, its, sems)
-    value = early[...] + value
+    value = early[...] + chips_times(where, line, chips, mine, its)
     for t in range(2):
         for u in range(4):
             keep = keep_s[1, (x * 4 + y) * 2 + t, z * 8 + u * 2 + core].astype(jnp.float32)
             piece = value[t * B:(t + 1) * B, u * B:(u + 1) * B] * keep
             square[t * B:(t + 1) * B, u * B:(u + 1) * B] = piece
             low[t * B:(t + 1) * B, u * B:(u + 1) * B] = piece.astype(jnp.bfloat16)
-    for copy in copies:
-        copy.wait()
 
 
 def parts_times_panel(parts, z, mine, come):
@@ -355,18 +346,16 @@
     near = jnp.concatenate([own0, one, two, three], axis=0)
     one, three = from_second(near, 1), from_second(near, 3)
     far, *own = lax.optimization_barrier((far, *gather(current, from_z)[1:]))
-    far = gather(far, from_first)
-    own0, *both = lax.optimization_barrier((own0, *own, *far))
-    own, far = [own0, *both[:3]], both[3:]
+    far, own = gather(far, from_first), [own0, *own]
     other = [other_core(part) for part in own]
     half_shape = jax.ShapeDtypeStruct((N // 2, COLS), jnp.bfloat16)
     early, line, mine, its = call(
         early_square, 1, [where, *own, *other, near, *far], [full_block, line_shape, half_shape, half_shape],
-        [pltpu.SemaphoreType.DMA((8, 2))], block_flops // 2, 10 * MIB)
+        [], block_flops // 2, 10 * MIB)
     square, low, mine, its = call(
         second_square, 2, [where, keep_square, one, three, early, line, mine, its],
         [full_block, low_block, half_shape, half_shape],
-        [pltpu.SemaphoreType.DMA((8, 2))], block_flops // 2, 8 * MIB, {6: 2, 7: 3})
+        [], block_flops // 2, 8 * MIB, {6: 2, 7: 3})
 
     own0, own1, own2, own3 = gather(low, from_z)
     come = other_core(its)

time: 146 us -> 137 us (0.938)
  Pallas kernels: 47.7 us -> 41.8 us
  waiting for transfers between devices: 52.8 us -> 48.7 us
    pallas_call x12, Pallas kernels: 47.7 us -> 41.8 us  [call(): pl.pallas_call(kernel, in_specs=[SMEM] * n_smem + [VMEM] * (len(ins) - n_...]
    ppermute x9, waiting for transfers between devices: 20.6 us -> 17.6 us  [from_first(): lax.ppermute(a, AXES, pairs(lambda x, y, core, z: (x - d, y, core, z) if...]
    ppermute x9, starting transfers between devices: 10.6 us -> 12.1 us  [from_z(): lax.ppermute(a, AXES, pairs(lambda x, y, core, z: (x, y, core, z - d)))]
  transfers between devices with their start and end apart: 35 -> 35, of which waited for: 19 -> 19; matrix products, arithmetic and copies ran while one was open for 1% -> 1% of each run, Pallas kernels for 22% -> 21%
where the time goes in v3:
time: 137 us
  waiting for transfers between devices  48.7 us (36%)
  starting transfers between devices  44.5 us (32%)
  Pallas kernels  41.8 us (31%)
    pallas_call x12, Pallas kernels, call(): pl.pallas_call(kernel, in_specs=[SMEM] * n_smem + [VMEM] * (len(ins) - n_...  41.8 us
    ppermute x9, waiting for transfers between devices, from_z(): lax.ppermute(a, AXES, pairs(lambda x, y, core, z: (x, y, core, z - d)))  18.4 us
    ppermute x9, waiting for transfers between devices, from_first(): lax.ppermute(a, AXES, pairs(lambda x, y, core, z: (x - d, y, core, z) if...  17.6 us
    ppermute x9, starting transfers between devices, from_z(): lax.ppermute(a, AXES, pairs(lambda x, y, core, z: (x, y, core, z - d)))  12.1 us
    ppermute x9, starting transfers between devices, from_first(): lax.ppermute(a, AXES, pairs(lambda x, y, core, z: (x - d, y, core, z) if...  11.8 us
    ppermute x6, starting transfers between devices, from_second(): lax.ppermute(a, AXES, pairs(lambda x, y, core, z: (x, y - d, core, z) if...  11.1 us
    ppermute x6, waiting for transfers between devices, from_second(): lax.ppermute(a, AXES, pairs(lambda x, y, core, z: (x, y - d, core, z) if...  9.73 us
    ppermute x11, starting transfers between devices, other_core(): lax.ppermute(a, AXES, pairs(lambda x, y, core, z: (x, y, 1 - core, z)))  9.54 us
  transfers between devices with their start and end apart: 35, of which 19 were waited for; matrix products, arithmetic and copies ran while one was open for 1% of the time, Pallas kernels for 21%

profile of v3, /device:TPU:1, one launch (start us, length us, event | category | flops | bytes accessed | tf_op | source)
XLA Modules:
  0.0 137.2 jit_solution(6567905399682329812)
XLA Ops:
  0.0 4.4 %collective-permute-start.1 = (bf16[128,256]{1,0:T(8,128)(2,1)}, bf16[128,256]{1,0:T(8,128)(2,1)S(1)}, u32[]{:S(2)}, u32[]{:S(2)}) collective-permute-start(bf16[128,256]{1,0:T(8,128)(2,1)} %param.4), channel_id=1, source_target_pairs={{0,2},{1,3},{2,0},{3,1},{4,6},{5,7},{6,4},{7,5},{8,10},{9,11},{10,... | collective-permute-start | bytes 196616 | tf_op jit(solution)/shard_map/ppermute | solution.py:33
  4.9 1.0 collective-permute-start.2
  6.7 1.4 %collective-permute-done = bf16[128,256]{1,0:T(8,128)(2,1)S(1)} collective-permute-done((bf16[128,256]{1,0:T(8,128)(2,1)}, bf16[128,256]{1,0:T(8,128)(2,1)S(1)}, u32[]{:S(2)}, u32[]{:S(2)}) %collective-permute-start) | collective-permute-done | bytes 65568 | tf_op jit(solution)/shard_map/ppermute | solution.py:33
  8.1 1.3 collective-permute-done.2
  10.3 1.4 collective-permute-start.5
  11.7 2.6 %collective-permute-start.4 = (bf16[128,1024]{1,0:T(8,128)(2,1)S(1)}, bf16[128,1024]{1,0:T(8,128)(2,1)S(1)}, u32[]{:S(2)}, u32[]{:S(2)}) collective-permute-start(bf16[128,1024]{1,0:T(8,128)(2,1)S(1)} %maximum_multiply_fusion), channel_id=1, source_target_pairs={{0,64},{1,65},{2,66},{3,67},{4,20},{5,21},{6,22},{7,23},{8,72},{9,... | collective-permute-start | bytes 786440 | tf_op jit(solution)/shard_map/ppermute | solution.py:37
  14.3 1.1 collective-permute-start.3
  15.4 1.8 %collective-permute-done.5 = bf16[128,1024]{1,0:T(8,128)(2,1)S(1)} collective-permute-done((bf16[128,1024]{1,0:T(8,128)(2,1)S(1)}, bf16[128,1024]{1,0:T(8,128)(2,1)S(1)}, u32[]{:S(2)}, u32[]{:S(2)}) %collective-permute-start.5) | collective-permute-done | bytes 262176 | tf_op jit(solution)/shard_map/ppermute | solution.py:37
  17.2 4.0 %collective-permute-done.4 = bf16[128,1024]{1,0:T(8,128)(2,1)S(1)} collective-permute-done((bf16[128,1024]{1,0:T(8,128)(2,1)S(1)}, bf16[128,1024]{1,0:T(8,128)(2,1)S(1)}, u32[]{:S(2)}, u32[]{:S(2)}) %collective-permute-start.4) | collective-permute-done | bytes 262176 | tf_op jit(solution)/shard_map/ppermute | solution.py:37
  21.2 3.1 %collective-permute-start.6 = (bf16[512,1024]{1,0:T(8,128)(2,1)S(1)}, bf16[512,1024]{1,0:T(8,128)(2,1)}, u32[]{:S(2)}, u32[]{:S(2)}) collective-permute-start(bf16[512,1024]{1,0:T(8,128)(2,1)S(1)} %pad_maximum_fusion.own0), channel_id=1, source_target_pairs={{0,4},{1,5},{2,6},{3,7},{4,0},{5,1},{6,2},{7,3},{8,12},{9,13},{10,... | collective-permute-start | bytes 3145736 | tf_op jit(solution)/shard_map/ppermute | solution.py:29
  24.3 1.6 %collective-permute-start.8 = (bf16[512,1024]{1,0:T(8,128)(2,1)S(1)}, bf16[512,1024]{1,0:T(8,128)(2,1)S(1)}, u32[]{:S(2)}, u32[]{:S(2)}) collective-permute-start(bf16[512,1024]{1,0:T(8,128)(2,1)S(1)} %pad_maximum_fusion.own0), channel_id=1, source_target_pairs={{0,8},{1,9},{2,10},{3,11},{4,36},{5,37},{6,38},{7,39},{8,16},{9,17... | collective-permute-start | bytes 3145736 | tf_op jit(solution)/shard_map/ppermute | solution.py:42
  25.9 1.1 collective-permute-start.7
  27.0 3.1 %shard_map.46 = (bf16[4096,2048]{1,0:T(8,128)(2,1)S(1)}, bf16[256,4096]{1,0:T(8,128)(2,1)S(1)}, bf16[256,1024]{1,0:T(8,128)(2,1)S(1)}) custom-call(s32[4]{0:T(128)S(1)} %pad_add_fusion.1.where, s32[2,32,32]{2,1,0:T(8,128)S(1)} %copy-done.1, bf16[512,1024]{1,0:T(8,128)(2,1)S(1)} %pad_maximum_fusion.own0, bf16[512,1024]{1,0:T(8,128)(2,1)} %collective-permute-done.6.other0), custom_call_target="tpu_custom_call" | custom-call | flops 67108864 | bytes 1048576 | tf_op jit(solution)/shard_map/pallas_call | solution.py:281
  30.1 9.3 %collective-permute-done.8.own3 = bf16[512,1024]{1,0:T(8,128)(2,1)S(1)} collective-permute-done((bf16[512,1024]{1,0:T(8,128)(2,1)S(1)}, bf16[512,1024]{1,0:T(8,128)(2,1)S(1)}, u32[]{:S(2)}, u32[]{:S(2)}) %collective-permute-start.8) | collective-permute-done | bytes 1048608 | tf_op jit(solution)/shard_map/ppermute | solution.py:42
  40.7 2.7 %collective-permute-start.11 = (bf16[512,1024]{1,0:T(8,128)(2,1)S(1)}, bf16[512,1024]{1,0:T(8,128)(2,1)S(1)}, u32[]{:S(2)}, u32[]{:S(2)}) collective-permute-start(bf16[512,1024]{1,0:T(8,128)(2,1)S(1)} %pad_maximum_fusion.own0), channel_id=1, source_target_pairs={{0,16},{1,17},{2,18},{3,19},{4,68},{5,69},{6,70},{7,71},{8,24},{9,... | collective-permute-start | bytes 3145736 | tf_op jit(solution)/shard_map/ppermute | solution.py:42
  43.4 5.9 %shard_map.47 = (bf16[4096,2048]{1,0:T(8,128)(2,1)S(1)}, bf16[256,4096]{1,0:T(8,128)(2,1)S(1)}) custom-call(s32[4]{0:T(128)S(1)} %pad_add_fusion.1.where, s32[2,32,32]{2,1,0:T(8,128)S(1)} %copy-done.1, bf16[512,1024]{1,0:T(8,128)(2,1)S(1)} %pad_maximum_fusion.own0, ...), custom_call_target="tpu_custom_call", output_to_operand_aliasing={{0}: (7, {}), {1}: (8, {})} | custom-call | flops 5905580032 | bytes 8388608 | tf_op jit(solution)/shard_map/pallas_call | solution.py:281
  49.4 8.0 %shard_map.48 = (bf16[4096,2048]{1,0:T(8,128)(2,1)S(1)}, bf16[256,4096]{1,0:T(8,128)(2,1)S(1)}, f32[256,2048]{1,0:T(8,128)S(1)}) custom-call(s32[4]{0:T(128)S(1)} %pad_add_fusion.1.where, s32[2,32,32]{2,1,0:T(8,128)S(1)} %copy-done.1, bf16[512,1024]{1,0:T(8,128)(2,1)S(1)} %pad_maximum_fusion.own0, ...), custom_call_target="tpu_custom_call", output_to_operand_aliasing={{0}: (8, {}), {1}: (9, {})} | custom-call | flops 5905580032 | bytes 8388608 | tf_op jit(solution)/shard_map/pallas_call | solution.py:281
  57.4 1.0 collective-permute-start.12
  58.5 5.7 %shard_map.49 = (bf16[4096,2048]{1,0:T(8,128)(2,1)S(1)}, bf16[256,4096]{1,0:T(8,128)(2,1)S(1)}) custom-call(s32[4]{0:T(128)S(1)} %pad_add_fusion.1.where, s32[2,32,32]{2,1,0:T(8,128)S(1)} %copy-done.1, bf16[512,1024]{1,0:T(8,128)(2,1)S(1)} %pad_maximum_fusion.own0, ...), custom_call_target="tpu_custom_call", output_to_operand_aliasing={{0}: (10, {}), {1}: (11, {})} | custom-call | flops 5368709120 | bytes 8388608 | tf_op jit(solution)/shard_map/pallas_call | solution.py:281
  64.2 7.1 %shard_map.50 = (bf16[4096,2048]{1,0:T(8,128)(2,1)S(1)}, bf16[256,4096]{1,0:T(8,128)(2,1)S(1)}, bf16[256,2048]{1,0:T(8,128)(2,1)S(1)}, f32[256,512]{1,0:T(8,128)S(1)}) custom-call(s32[4]{0:T(128)S(1)} %pad_add_fusion.1.where, s32[2,32,32]{2,1,0:T(8,128)S(1)} %copy-done.1, ...), custom_call_target="tpu_custom_call", output_to_operand_aliasing={{0}: (10, {}), {1}: (11, {})} | custom-call | flops 4294967296 | bytes 20971520 | tf_op jit(solution)/shard_map/pallas_call | solution.py:281
  71.4 2.3 %shard_map.51 = (f32[256,512]{1,0:T(8,128)S(1)}, bf16[4096,512]{1,0:T(8,128)(2,1)S(1)}) custom-call(s32[4]{0:T(128)S(1)} %pad_add_fusion.1.where, bf16[256,2048]{1,0:T(8,128)(2,1)S(1)} %get-tuple-element.65.low, bf16[4096,2048]{1,0:T(8,128)(2,1)S(1)} %get-tuple-element.66.panel), custom_call_target="tpu_custom_call" | custom-call | flops 536870912 | bytes 12582912 | tf_op jit(solution)/shard_map/pallas_call | solution.py:281
  74.0 1.8 %shard_map.52.refs_0_ = bf16[256,512]{1,0:T(8,128)(2,1)S(1)} custom-call(s32[4]{0:T(128)S(1)} %pad_add_fusion.1.where, s32[2,32,32]{2,1,0:T(8,128)S(1)} %copy-done.1, bf16[256,2048]{1,0:T(8,128)(2,1)S(1)} %collective-permute-done.13.its, bf16[4096,512]{1,0:T(8,128)(2,1)S(1)} %get-tuple-element.67.columns, f32[256,512]{1,0:T(8,128)S(1)} %get-tuple-element.68.early, ...), custom_call_target="tpu_custom_call" | custom-call | flops 536870912 | bytes 4194304 | tf_op jit(solution)/shard_map/pallas_call | solution.py:281
  75.8 2.7 %collective-permute-start.17 = (bf16[256,512]{1,0:T(8,128)(2,1)S(1)}, bf16[256,512]{1,0:T(8,128)(2,1)S(1)}, u32[]{:S(2)}, u32[]{:S(2)}) collective-permute-start(bf16[256,512]{1,0:T(8,128)(2,1)S(1)} %shard_map.52.refs_0_), channel_id=1, source_target_pairs={{0,16},{1,17},{2,18},{3,19},{4,68},{5,69},{6,70},{7,71},{8,24},{9,... | collective-permute-start | bytes 786440 | tf_op jit(solution)/shard_map/ppermute | solution.py:42
  78.6 1.7 %collective-permute-start.16 = (bf16[256,512]{1,0:T(8,128)(2,1)S(1)}, bf16[256,512]{1,0:T(8,128)(2,1)S(1)}, u32[]{:S(2)}, u32[]{:S(2)}) collective-permute-start(bf16[256,512]{1,0:T(8,128)(2,1)S(1)} %shard_map.52.refs_0_), channel_id=1, source_target_pairs={{0,64},{1,65},{2,66},{3,67},{4,20},{5,21},{6,22},{7,23},{8,72},{9,... | collective-permute-start | bytes 786440 | tf_op jit(solution)/shard_map/ppermute | solution.py:37
  80.9 2.1 %collective-permute-start.14 = (bf16[256,512]{1,0:T(8,128)(2,1)S(1)}, bf16[256,512]{1,0:T(8,128)(2,1)S(1)}, u32[]{:S(2)}, u32[]{:S(2)}) collective-permute-start(bf16[256,512]{1,0:T(8,128)(2,1)S(1)} %shard_map.52.refs_0_), channel_id=1, source_target_pairs={{0,96},{1,97},{2,98},{3,99},{4,28},{5,29},{6,30},{7,31},{8,104},{9... | collective-permute-start | bytes 786440 | tf_op jit(solution)/shard_map/ppermute | solution.py:37
  83.0 1.6 %collective-permute-start.21 = (bf16[256,512]{1,0:T(8,128)(2,1)S(1)}, bf16[256,512]{1,0:T(8,128)(2,1)S(1)}, u32[]{:S(2)}, u32[]{:S(2)}) collective-permute-start(bf16[256,512]{1,0:T(8,128)(2,1)S(1)} %shard_map.52.refs_0_), channel_id=1, source_target_pairs={{0,2},{1,3},{2,0},{3,1},{4,6},{5,7},{6,4},{7,5},{8,10},{9,11},{10,... | collective-permute-start | bytes 786440 | tf_op jit(solution)/shard_map/ppermute | solution.py:33
  84.6 1.6 %collective-permute-done.16 = bf16[256,512]{1,0:T(8,128)(2,1)S(1)} collective-permute-done((bf16[256,512]{1,0:T(8,128)(2,1)S(1)}, bf16[256,512]{1,0:T(8,128)(2,1)S(1)}, u32[]{:S(2)}, u32[]{:S(2)}) %collective-permute-start.16) | collective-permute-done | bytes 262176 | tf_op jit(solution)/shard_map/ppermute | solution.py:37
  86.6 2.6 %collective-permute-done.15 = bf16[256,512]{1,0:T(8,128)(2,1)S(1)} collective-permute-done((bf16[256,512]{1,0:T(8,128)(2,1)S(1)}, bf16[256,512]{1,0:T(8,128)(2,1)S(1)}, u32[]{:S(2)}, u32[]{:S(2)}) %collective-permute-start.15) | collective-permute-done | bytes 262176 | tf_op jit(solution)/shard_map/ppermute | solution.py:37
  89.3 2.0 %collective-permute-start.19 = (bf16[1024,512]{1,0:T(8,128)(2,1)S(1)}, bf16[1024,512]{1,0:T(8,128)(2,1)S(1)}, u32[]{:S(2)}, u32[]{:S(2)}) collective-permute-start(bf16[1024,512]{1,0:T(8,128)(2,1)S(1)} %constant_dynamic-update-slice_fusion.refs_8_), channel_id=1, source_target_pairs={{0,8},{1,9},{2,10},{3,11},{4,36},{5,37},{6,38},{7,39},{8,16},{9,17... | collective-permute-start | bytes 3145736 | tf_op jit(solution)/shard_map/ppermute | solution.py:42
  91.2 1.1 collective-permute-start.18
  92.3 3.0 %collective-permute-done.21.refs_2_ = bf16[256,512]{1,0:T(8,128)(2,1)S(1)} collective-permute-done((bf16[256,512]{1,0:T(8,128)(2,1)S(1)}, bf16[256,512]{1,0:T(8,128)(2,1)S(1)}, u32[]{:S(2)}, u32[]{:S(2)}) %collective-permute-start.21) | collective-permute-done | bytes 262176 | tf_op jit(solution)/shard_map/ppermute | solution.py:33
  95.3 2.3 %collective-permute-done.20.refs_1_ = bf16[256,512]{1,0:T(8,128)(2,1)S(1)} collective-permute-done((bf16[256,512]{1,0:T(8,128)(2,1)S(1)}, bf16[256,512]{1,0:T(8,128)(2,1)S(1)}, u32[]{:S(2)}, u32[]{:S(2)}) %collective-permute-start.20) | collective-permute-done | bytes 262176 | tf_op jit(solution)/shard_map/ppermute | solution.py:33
  97.6 1.6 %collective-permute-start.24 = (bf16[256,512]{1,0:T(8,128)(2,1)S(1)}, bf16[256,512]{1,0:T(8,128)(2,1)S(1)}, u32[]{:S(2)}, u32[]{:S(2)}) collective-permute-start(bf16[256,512]{1,0:T(8,128)(2,1)S(1)} %collective-permute-done.20.refs_1_), channel_id=1, source_target_pairs={{0,4},{1,5},{2,6},{3,7},{4,0},{5,1},{6,2},{7,3},{8,12},{9,13},{10,... | collective-permute-start | bytes 786440 | tf_op jit(solution)/shard_map/ppermute | solution.py:29
  100.7 1.2 collective-permute-start.28
  101.9 1.2 collective-permute-start.27
  103.1 4.8 %collective-permute-done.29.refs_12_ = bf16[256,512]{1,0:T(8,128)(2,1)S(1)} collective-permute-done((bf16[256,512]{1,0:T(8,128)(2,1)S(1)}, bf16[256,512]{1,0:T(8,128)(2,1)S(1)}, u32[]{:S(2)}, u32[]{:S(2)}) %collective-permute-start.29) | collective-permute-done | bytes 262176 | tf_op jit(solution)/shard_map/ppermute | solution.py:37
  108.3 2.9 %collective-permute-done.28.refs_11_ = bf16[256,512]{1,0:T(8,128)(2,1)S(1)} collective-permute-done((bf16[256,512]{1,0:T(8,128)(2,1)S(1)}, bf16[256,512]{1,0:T(8,128)(2,1)S(1)}, u32[]{:S(2)}, u32[]{:S(2)}) %collective-permute-start.28) | collective-permute-done | bytes 262176 | tf_op jit(solution)/shard_map/ppermute | solution.py:37
  111.1 2.0 %shard_map.53 = (f32[256,512]{1,0:T(8,128)S(1)}, bf16[256,4096]{1,0:T(8,128)(2,1)S(1)}, bf16[2048,512]{1,0:T(8,128)(2,1)S(1)}, bf16[2048,512]{1,0:T(8,128)(2,1)S(1)}) custom-call(s32[4]{0:T(128)S(1)} %pad_add_fusion.1.where, bf16[256,512]{1,0:T(8,128)(2,1)S(1)} %shard_map.52.refs_0_, bf16[256,512]{1,0:T(8,128)(2,1)S(1)} %collective-permute-done.20.refs_1_, ...), custom_call_target="tpu_custom_call" | custom-call | flops 536870912 | bytes 10485760 | tf_op jit(solution)/shard_map/pallas_call | solution.py:281
  113.1 1.9 %shard_map.54 = (f32[256,512]{1,0:T(8,128)S(1)}, bf16[256,512]{1,0:T(8,128)(2,1)S(1)}, bf16[2048,512]{1,0:T(8,128)(2,1)S(1)}, bf16[2048,512]{1,0:T(8,128)(2,1)S(1)}) custom-call(s32[4]{0:T(128)S(1)} %pad_add_fusion.1.where, s32[2,32,32]{2,1,0:T(8,128)S(1)} %copy-done.2, ...), custom_call_target="tpu_custom_call", output_to_operand_aliasing={{2}: (6, {}), {3}: (7, {})} | custom-call | flops 536870912 | bytes 8388608 | tf_op jit(solution)/shard_map/pallas_call | solution.py:281
  115.1 0.9 collective-permute-start.32
  116.2 2.8 %collective-permute-start.30 = (bf16[256,512]{1,0:T(8,128)(2,1)S(1)}, bf16[256,512]{1,0:T(8,128)(2,1)S(1)}, u32[]{:S(2)}, u32[]{:S(2)}) collective-permute-start(bf16[256,512]{1,0:T(8,128)(2,1)S(1)} %get-tuple-element.83.own0), channel_id=1, source_target_pairs={{0,3},{1,0},{2,1},{3,2},{4,7},{5,4},{6,5},{7,6},{8,11},{9,8},{10,9... | collective-permute-start | bytes 786440 | tf_op jit(solution)/shard_map/ppermute | solution.py:33
  119.0 1.2 collective-permute-start.33
  120.2 5.4 %collective-permute-done.31.own3 = bf16[256,512]{1,0:T(8,128)(2,1)S(1)} collective-permute-done((bf16[256,512]{1,0:T(8,128)(2,1)S(1)}, bf16[256,512]{1,0:T(8,128)(2,1)S(1)}, u32[]{:S(2)}, u32[]{:S(2)}) %collective-permute-start.31) | collective-permute-done | bytes 262176 | tf_op jit(solution)/shard_map/ppermute | solution.py:33
  125.5 4.5 %collective-permute-done.30.own1 = bf16[256,512]{1,0:T(8,128)(2,1)S(1)} collective-permute-done((bf16[256,512]{1,0:T(8,128)(2,1)S(1)}, bf16[256,512]{1,0:T(8,128)(2,1)S(1)}, u32[]{:S(2)}, u32[]{:S(2)}) %collective-permute-start.30) | collective-permute-done | bytes 262176 | tf_op jit(solution)/shard_map/ppermute | solution.py:33
  130.0 1.5 %shard_map.55.early = f32[256,1024]{1,0:T(8,128)S(1)} custom-call(s32[4]{0:T(128)S(1)} %pad_add_fusion.1.where, bf16[256,512]{1,0:T(8,128)(2,1)S(1)} %get-tuple-element.83.own0, bf16[256,512]{1,0:T(8,128)(2,1)S(1)} %collective-permute-done.30.own1, bf16[256,512]{1,0:T(8,128)(2,1)S(1)} %collective-permute-done.31.own3, ...), custom_call_target="tpu_custom_call" | custom-call | flops 805306368 | bytes 4194304 | tf_op jit(solution)/shard_map/pallas_call | solution.py:281
  132.9 1.0 collective-permute-start.34
  134.0 1.5 %collective-permute-done.34.share = f32[128,1024]{1,0:T(8,128)S(1)} collective-permute-done((f32[128,1024]{1,0:T(8,128)S(1)}, f32[128,1024]{1,0:T(8,128)S(1)}, u32[]{:S(2)}, u32[]{:S(2)}) %collective-permute-start.34) | collective-permute-done | bytes 524320 | tf_op jit(solution)/shard_map/ppermute | solution.py:29
  135.5 1.7 %shard_map.57 = f32[128,1024]{1,0:T(8,128)} custom-call(s32[4]{0:T(128)S(1)} %pad_add_fusion.1.where, bf16[256,512]{1,0:T(8,128)(2,1)S(1)} %collective-permute-done.33.own2, f32[256,1024]{1,0:T(8,128)S(1)} %shard_map.55.early, f32[256,512]{1,0:T(8,128)S(1)} %get-tuple-element.88.square, bf16[2048,512]{1,0:T(8,128)(2,1)S(1)} %get-tuple-element.84.mine, ...), custom_call_target="tpu_custom_call" | custom-call | flops 134217728 | bytes 3145728 | tf_op jit(solution)/shard_map/pallas_call | solution.py:281
  (55 shorter events, 8.7 us)
Async XLA Ops:
  0.0 5.9 %copy-start = (s32[32,8]{0,1:T(8,128)S(1)}, s32[32,8]{0,1:T(8,128)}, u32[]{:S(2)}) copy-start(s32[32,8]{0,1:T(8,128)} %param.5) | copy-start | bytes 3076
  0.0 27.0 %copy-start.1 = (s32[2,32,32]{2,1,0:T(8,128)S(1)}, s32[2,32,32]{2,1,0:T(8,128)}, u32[]{:S(2)}) copy-start(s32[2,32,32]{2,1,0:T(8,128)} %keep_d.11) | copy-start | bytes 24580
  0.0 6.7 %collective-permute-start.1 = (bf16[128,256]{1,0:T(8,128)(2,1)}, bf16[128,256]{1,0:T(8,128)(2,1)S(1)}, u32[]{:S(2)}, u32[]{:S(2)}) collective-permute-start(bf16[128,256]{1,0:T(8,128)(2,1)} %param.4), channel_id=1, source_target_pairs={{0,2},{1,3},{2,0},{3,1},{4,6},{5,7},{6,4},{7,5},{8,10},{9,11},{10,... | collective-permute-start | bytes 196616 | tf_op jit(solution)/shard_map/ppermute | solution.py:33
  4.4 3.7 %collective-permute-start = (bf16[128,256]{1,0:T(8,128)(2,1)}, bf16[128,256]{1,0:T(8,128)(2,1)S(1)}, u32[]{:S(2)}, u32[]{:S(2)}) collective-permute-start(bf16[128,256]{1,0:T(8,128)(2,1)} %param.4), channel_id=1, source_target_pairs={{0,3},{1,0},{2,1},{3,2},{4,7},{5,4},{6,5},{7,6},{8,11},{9,8},{10,9... | collective-permute-start | bytes 196616 | tf_op jit(solution)/shard_map/ppermute | solution.py:33
  4.9 4.5 %collective-permute-start.2 = (bf16[128,256]{1,0:T(8,128)(2,1)}, bf16[128,256]{1,0:T(8,128)(2,1)S(1)}, u32[]{:S(2)}, u32[]{:S(2)}) collective-permute-start(bf16[128,256]{1,0:T(8,128)(2,1)} %param.4), channel_id=1, source_target_pairs={{0,1},{1,2},{2,3},{3,0},{4,5},{5,6},{6,7},{7,4},{8,9},{9,10},{10,1... | collective-permute-start | bytes 196616 | tf_op jit(solution)/shard_map/ppermute | solution.py:33
  10.3 6.9 %collective-permute-start.5 = (bf16[128,1024]{1,0:T(8,128)(2,1)S(1)}, bf16[128,1024]{1,0:T(8,128)(2,1)S(1)}, u32[]{:S(2)}, u32[]{:S(2)}) collective-permute-start(bf16[128,1024]{1,0:T(8,128)(2,1)S(1)} %maximum_multiply_fusion), channel_id=1, source_target_pairs={{0,32},{1,33},{2,34},{3,35},{4,12},{5,13},{6,14},{7,15},{8,40},{9,... | collective-permute-start | bytes 786440 | tf_op jit(solution)/shard_map/ppermute | solution.py:37
  11.7 9.5 %collective-permute-start.4 = (bf16[128,1024]{1,0:T(8,128)(2,1)S(1)}, bf16[128,1024]{1,0:T(8,128)(2,1)S(1)}, u32[]{:S(2)}, u32[]{:S(2)}) collective-permute-start(bf16[128,1024]{1,0:T(8,128)(2,1)S(1)} %maximum_multiply_fusion), channel_id=1, source_target_pairs={{0,64},{1,65},{2,66},{3,67},{4,20},{5,21},{6,22},{7,23},{8,72},{9,... | collective-permute-start | bytes 786440 | tf_op jit(solution)/shard_map/ppermute | solution.py:37
  14.3 6.9 %collective-permute-start.3 = (bf16[128,1024]{1,0:T(8,128)(2,1)S(1)}, bf16[128,1024]{1,0:T(8,128)(2,1)S(1)}, u32[]{:S(2)}, u32[]{:S(2)}) collective-permute-start(bf16[128,1024]{1,0:T(8,128)(2,1)S(1)} %maximum_multiply_fusion), channel_id=1, source_target_pairs={{0,96},{1,97},{2,98},{3,99},{4,28},{5,29},{6,30},{7,31},{8,104},{9... | collective-permute-start | bytes 786440 | tf_op jit(solution)/shard_map/ppermute | solution.py:37
  21.2 5.8 %collective-permute-start.6 = (bf16[512,1024]{1,0:T(8,128)(2,1)S(1)}, bf16[512,1024]{1,0:T(8,128)(2,1)}, u32[]{:S(2)}, u32[]{:S(2)}) collective-permute-start(bf16[512,1024]{1,0:T(8,128)(2,1)S(1)} %pad_maximum_fusion.own0), channel_id=1, source_target_pairs={{0,4},{1,5},{2,6},{3,7},{4,0},{5,1},{6,2},{7,3},{8,12},{9,13},{10,... | collective-permute-start | bytes 3145736 | tf_op jit(solution)/shard_map/ppermute | solution.py:29
  24.3 15.2 %collective-permute-start.8 = (bf16[512,1024]{1,0:T(8,128)(2,1)S(1)}, bf16[512,1024]{1,0:T(8,128)(2,1)S(1)}, u32[]{:S(2)}, u32[]{:S(2)}) collective-permute-start(bf16[512,1024]{1,0:T(8,128)(2,1)S(1)} %pad_maximum_fusion.own0), channel_id=1, source_target_pairs={{0,8},{1,9},{2,10},{3,11},{4,36},{5,37},{6,38},{7,39},{8,16},{9,17... | collective-permute-start | bytes 3145736 | tf_op jit(solution)/shard_map/ppermute | solution.py:42
  25.9 13.9 %collective-permute-start.7 = (bf16[512,1024]{1,0:T(8,128)(2,1)S(1)}, bf16[512,1024]{1,0:T(8,128)(2,1)S(1)}, u32[]{:S(2)}, u32[]{:S(2)}) collective-permute-start(bf16[512,1024]{1,0:T(8,128)(2,1)S(1)} %pad_maximum_fusion.own0), channel_id=1, source_target_pairs={{0,24},{1,25},{2,26},{3,27},{4,100},{5,101},{6,102},{7,103},{8,0},... | collective-permute-start | bytes 3145736 | tf_op jit(solution)/shard_map/ppermute | solution.py:42
  39.8 9.5 %collective-permute-start.9 = (bf16[512,1024]{1,0:T(8,128)(2,1)S(1)}, bf16[512,1024]{1,0:T(8,128)(2,1)S(1)}, u32[]{:S(2)}, u32[]{:S(2)}) collective-permute-start(bf16[512,1024]{1,0:T(8,128)(2,1)S(1)} %collective-permute-done.7.own1), channel_id=1, source_target_pairs={{0,4},{1,5},{2,6},{3,7},{4,0},{5,1},{6,2},{7,3},{8,12},{9,13},{10,... | collective-permute-start | bytes 3145736 | tf_op jit(solution)/shard_map/ppermute | solution.py:29
  40.7 8.6 %collective-permute-start.10 = (bf16[512,1024]{1,0:T(8,128)(2,1)S(1)}, bf16[512,1024]{1,0:T(8,128)(2,1)S(1)}, u32[]{:S(2)}, u32[]{:S(2)}) collective-permute-start(bf16[512,1024]{1,0:T(8,128)(2,1)S(1)} %collective-permute-done.8.own3), channel_id=1, source_target_pairs={{0,4},{1,5},{2,6},{3,7},{4,0},{5,1},{6,2},{7,3},{8,12},{9,13},{10,... | collective-permute-start | bytes 3145736 | tf_op jit(solution)/shard_map/ppermute | solution.py:29
  40.7 16.7 %collective-permute-start.11 = (bf16[512,1024]{1,0:T(8,128)(2,1)S(1)}, bf16[512,1024]{1,0:T(8,128)(2,1)S(1)}, u32[]{:S(2)}, u32[]{:S(2)}) collective-permute-start(bf16[512,1024]{1,0:T(8,128)(2,1)S(1)} %pad_maximum_fusion.own0), channel_id=1, source_target_pairs={{0,16},{1,17},{2,18},{3,19},{4,68},{5,69},{6,70},{7,71},{8,24},{9,... | collective-permute-start | bytes 3145736 | tf_op jit(solution)/shard_map/ppermute | solution.py:42
  57.4 6.7 %copy-start.2 = (s32[2,32,32]{2,1,0:T(8,128)S(1)}, s32[2,32,32]{2,1,0:T(8,128)}, u32[]{:S(2)}) copy-start(s32[2,32,32]{2,1,0:T(8,128)} %keep_s.3) | copy-start | bytes 24580
  57.4 6.7 %collective-permute-start.12 = (bf16[512,1024]{1,0:T(8,128)(2,1)S(1)}, bf16[512,1024]{1,0:T(8,128)(2,1)S(1)}, u32[]{:S(2)}, u32[]{:S(2)}) collective-permute-start(bf16[512,1024]{1,0:T(8,128)(2,1)S(1)} %collective-permute-done.11.own2), channel_id=1, source_target_pairs={{0,4},{1,5},{2,6},{3,7},{4,0},{5,1},{6,2},{7,3},{8,12},{9,13},{10,... | collective-permute-start | bytes 3145736 | tf_op jit(solution)/shard_map/ppermute | solution.py:29
  71.3 2.7 %collective-permute-start.13 = (bf16[256,2048]{1,0:T(8,128)(2,1)S(1)}, bf16[256,2048]{1,0:T(8,128)(2,1)S(1)}, u32[]{:S(2)}, u32[]{:S(2)}) collective-permute-start(bf16[256,2048]{1,0:T(8,128)(2,1)S(1)} %get-tuple-element.65.low), channel_id=1, source_target_pairs={{0,4},{1,5},{2,6},{3,7},{4,0},{5,1},{6,2},{7,3},{8,12},{9,13},{10,... | collective-permute-start | bytes 3145736 | tf_op jit(solution)/shard_map/ppermute | solution.py:29
  75.8 7.1 %collective-permute-start.17 = (bf16[256,512]{1,0:T(8,128)(2,1)S(1)}, bf16[256,512]{1,0:T(8,128)(2,1)S(1)}, u32[]{:S(2)}, u32[]{:S(2)}) collective-permute-start(bf16[256,512]{1,0:T(8,128)(2,1)S(1)} %shard_map.52.refs_0_), channel_id=1, source_target_pairs={{0,16},{1,17},{2,18},{3,19},{4,68},{5,69},{6,70},{7,71},{8,24},{9,... | collective-permute-start | bytes 786440 | tf_op jit(solution)/shard_map/ppermute | solution.py:42
  78.6 7.6 %collective-permute-start.16 = (bf16[256,512]{1,0:T(8,128)(2,1)S(1)}, bf16[256,512]{1,0:T(8,128)(2,1)S(1)}, u32[]{:S(2)}, u32[]{:S(2)}) collective-permute-start(bf16[256,512]{1,0:T(8,128)(2,1)S(1)} %shard_map.52.refs_0_), channel_id=1, source_target_pairs={{0,64},{1,65},{2,66},{3,67},{4,20},{5,21},{6,22},{7,23},{8,72},{9,... | collective-permute-start | bytes 786440 | tf_op jit(solution)/shard_map/ppermute | solution.py:37
  80.3 8.9 %collective-permute-start.15 = (bf16[256,512]{1,0:T(8,128)(2,1)S(1)}, bf16[256,512]{1,0:T(8,128)(2,1)S(1)}, u32[]{:S(2)}, u32[]{:S(2)}) collective-permute-start(bf16[256,512]{1,0:T(8,128)(2,1)S(1)} %shard_map.52.refs_0_), channel_id=1, source_target_pairs={{0,32},{1,33},{2,34},{3,35},{4,12},{5,13},{6,14},{7,15},{8,40},{9,... | collective-permute-start | bytes 786440 | tf_op jit(solution)/shard_map/ppermute | solution.py:37
  80.9 8.3 %collective-permute-start.14 = (bf16[256,512]{1,0:T(8,128)(2,1)S(1)}, bf16[256,512]{1,0:T(8,128)(2,1)S(1)}, u32[]{:S(2)}, u32[]{:S(2)}) collective-permute-start(bf16[256,512]{1,0:T(8,128)(2,1)S(1)} %shard_map.52.refs_0_), channel_id=1, source_target_pairs={{0,96},{1,97},{2,98},{3,99},{4,28},{5,29},{6,30},{7,31},{8,104},{9... | collective-permute-start | bytes 786440 | tf_op jit(solution)/shard_map/ppermute | solution.py:37
  83.0 9.3 %collective-permute-start.22 = (bf16[256,512]{1,0:T(8,128)(2,1)S(1)}, bf16[256,512]{1,0:T(8,128)(2,1)S(1)}, u32[]{:S(2)}, u32[]{:S(2)}) collective-permute-start(bf16[256,512]{1,0:T(8,128)(2,1)S(1)} %shard_map.52.refs_0_), channel_id=1, source_target_pairs={{0,1},{1,2},{2,3},{3,0},{4,5},{5,6},{6,7},{7,4},{8,9},{9,10},{10,1... | collective-permute-start | bytes 786440 | tf_op jit(solution)/shard_map/ppermute | solution.py:33
  83.0 12.3 %collective-permute-start.21 = (bf16[256,512]{1,0:T(8,128)(2,1)S(1)}, bf16[256,512]{1,0:T(8,128)(2,1)S(1)}, u32[]{:S(2)}, u32[]{:S(2)}) collective-permute-start(bf16[256,512]{1,0:T(8,128)(2,1)S(1)} %shard_map.52.refs_0_), channel_id=1, source_target_pairs={{0,2},{1,3},{2,0},{3,1},{4,6},{5,7},{6,4},{7,5},{8,10},{9,11},{10,... | collective-permute-start | bytes 786440 | tf_op jit(solution)/shard_map/ppermute | solution.py:33
  86.2 11.4 %collective-permute-start.20 = (bf16[256,512]{1,0:T(8,128)(2,1)S(1)}, bf16[256,512]{1,0:T(8,128)(2,1)S(1)}, u32[]{:S(2)}, u32[]{:S(2)}) collective-permute-start(bf16[256,512]{1,0:T(8,128)(2,1)S(1)} %shard_map.52.refs_0_), channel_id=1, source_target_pairs={{0,3},{1,0},{2,1},{3,2},{4,7},{5,4},{6,5},{7,6},{8,11},{9,8},{10,9... | collective-permute-start | bytes 786440 | tf_op jit(solution)/shard_map/ppermute | solution.py:33
  89.3 23.9 %collective-permute-start.19 = (bf16[1024,512]{1,0:T(8,128)(2,1)S(1)}, bf16[1024,512]{1,0:T(8,128)(2,1)S(1)}, u32[]{:S(2)}, u32[]{:S(2)}) collective-permute-start(bf16[1024,512]{1,0:T(8,128)(2,1)S(1)} %constant_dynamic-update-slice_fusion.refs_8_), channel_id=1, source_target_pairs={{0,8},{1,9},{2,10},{3,11},{4,36},{5,37},{6,38},{7,39},{8,16},{9,17... | collective-permute-start | bytes 3145736 | tf_op jit(solution)/shard_map/ppermute | solution.py:42
  91.2 21.9 %collective-permute-start.18 = (bf16[1024,512]{1,0:T(8,128)(2,1)S(1)}, bf16[1024,512]{1,0:T(8,128)(2,1)S(1)}, u32[]{:S(2)}, u32[]{:S(2)}) collective-permute-start(bf16[1024,512]{1,0:T(8,128)(2,1)S(1)} %constant_dynamic-update-slice_fusion.refs_8_), channel_id=1, source_target_pairs={{0,24},{1,25},{2,26},{3,27},{4,100},{5,101},{6,102},{7,103},{8,0},... | collective-permute-start | bytes 3145736 | tf_op jit(solution)/shard_map/ppermute | solution.py:42
  97.6 2.7 %collective-permute-start.24 = (bf16[256,512]{1,0:T(8,128)(2,1)S(1)}, bf16[256,512]{1,0:T(8,128)(2,1)S(1)}, u32[]{:S(2)}, u32[]{:S(2)}) collective-permute-start(bf16[256,512]{1,0:T(8,128)(2,1)S(1)} %collective-permute-done.20.refs_1_), channel_id=1, source_target_pairs={{0,4},{1,5},{2,6},{3,7},{4,0},{5,1},{6,2},{7,3},{8,12},{9,13},{10,... | collective-permute-start | bytes 786440 | tf_op jit(solution)/shard_map/ppermute | solution.py:29
  99.1 1.5 %collective-permute-start.25 = (bf16[256,512]{1,0:T(8,128)(2,1)S(1)}, bf16[256,512]{1,0:T(8,128)(2,1)S(1)}, u32[]{:S(2)}, u32[]{:S(2)}) collective-permute-start(bf16[256,512]{1,0:T(8,128)(2,1)S(1)} %collective-permute-done.21.refs_2_), channel_id=1, source_target_pairs={{0,4},{1,5},{2,6},{3,7},{4,0},{5,1},{6,2},{7,3},{8,12},{9,13},{10,... | collective-permute-start | bytes 786440 | tf_op jit(solution)/shard_map/ppermute | solution.py:29
  99.1 2.7 %collective-permute-start.26 = (bf16[256,512]{1,0:T(8,128)(2,1)S(1)}, bf16[256,512]{1,0:T(8,128)(2,1)S(1)}, u32[]{:S(2)}, u32[]{:S(2)}) collective-permute-start(bf16[256,512]{1,0:T(8,128)(2,1)S(1)} %collective-permute-done.22.refs_3_), channel_id=1, source_target_pairs={{0,4},{1,5},{2,6},{3,7},{4,0},{5,1},{6,2},{7,3},{8,12},{9,13},{10,... | collective-permute-start | bytes 786440 | tf_op jit(solution)/shard_map/ppermute | solution.py:29
  100.3 7.6 %collective-permute-start.29 = (bf16[256,512]{1,0:T(8,128)(2,1)S(1)}, bf16[256,512]{1,0:T(8,128)(2,1)S(1)}, u32[]{:S(2)}, u32[]{:S(2)}) collective-permute-start(bf16[256,512]{1,0:T(8,128)(2,1)S(1)} %collective-permute-done.17.refs_9_), channel_id=1, source_target_pairs={{0,32},{1,33},{2,34},{3,35},{4,12},{5,13},{6,14},{7,15},{8,40},{9,... | collective-permute-start | bytes 786440 | tf_op jit(solution)/shard_map/ppermute | solution.py:37
  100.7 10.4 %collective-permute-start.28 = (bf16[256,512]{1,0:T(8,128)(2,1)S(1)}, bf16[256,512]{1,0:T(8,128)(2,1)S(1)}, u32[]{:S(2)}, u32[]{:S(2)}) collective-permute-start(bf16[256,512]{1,0:T(8,128)(2,1)S(1)} %collective-permute-done.17.refs_9_), channel_id=1, source_target_pairs={{0,64},{1,65},{2,66},{3,67},{4,20},{5,21},{6,22},{7,23},{8,72},{9,... | collective-permute-start | bytes 786440 | tf_op jit(solution)/shard_map/ppermute | solution.py:37
  101.9 9.3 %collective-permute-start.27 = (bf16[256,512]{1,0:T(8,128)(2,1)S(1)}, bf16[256,512]{1,0:T(8,128)(2,1)S(1)}, u32[]{:S(2)}, u32[]{:S(2)}) collective-permute-start(bf16[256,512]{1,0:T(8,128)(2,1)S(1)} %collective-permute-done.17.refs_9_), channel_id=1, source_target_pairs={{0,96},{1,97},{2,98},{3,99},{4,28},{5,29},{6,30},{7,31},{8,104},{9... | collective-permute-start | bytes 786440 | tf_op jit(solution)/shard_map/ppermute | solution.py:37
  107.9 3.3 %collective-permute-start.23 = (bf16[256,512]{1,0:T(8,128)(2,1)S(1)}, bf16[256,512]{1,0:T(8,128)(2,1)S(1)}, u32[]{:S(2)}, u32[]{:S(2)}) collective-permute-start(bf16[256,512]{1,0:T(8,128)(2,1)S(1)} %shard_map.52.refs_0_), channel_id=1, source_target_pairs={{0,4},{1,5},{2,6},{3,7},{4,0},{5,1},{6,2},{7,3},{8,12},{9,13},{10,... | collective-permute-start | bytes 786440 | tf_op jit(solution)/shard_map/ppermute | solution.py:29
  115.1 14.9 %collective-permute-start.32 = (bf16[2048,512]{1,0:T(8,128)(2,1)S(1)}, bf16[2048,512]{1,0:T(8,128)(2,1)S(1)}, u32[]{:S(2)}, u32[]{:S(2)}) collective-permute-start(bf16[2048,512]{1,0:T(8,128)(2,1)S(1)} %get-tuple-element.85), channel_id=1, source_target_pairs={{0,4},{1,5},{2,6},{3,7},{4,0},{5,1},{6,2},{7,3},{8,12},{9,13},{10,... | collective-permute-start | bytes 6291464 | tf_op jit(solution)/shard_map/ppermute | solution.py:29
  116.0 9.5 %collective-permute-start.31 = (bf16[256,512]{1,0:T(8,128)(2,1)S(1)}, bf16[256,512]{1,0:T(8,128)(2,1)S(1)}, u32[]{:S(2)}, u32[]{:S(2)}) collective-permute-start(bf16[256,512]{1,0:T(8,128)(2,1)S(1)} %get-tuple-element.83.own0), channel_id=1, source_target_pairs={{0,1},{1,2},{2,3},{3,0},{4,5},{5,6},{6,7},{7,4},{8,9},{9,10},{10,1... | collective-permute-start | bytes 786440 | tf_op jit(solution)/shard_map/ppermute | solution.py:33
  116.2 13.8 %collective-permute-start.30 = (bf16[256,512]{1,0:T(8,128)(2,1)S(1)}, bf16[256,512]{1,0:T(8,128)(2,1)S(1)}, u32[]{:S(2)}, u32[]{:S(2)}) collective-permute-start(bf16[256,512]{1,0:T(8,128)(2,1)S(1)} %get-tuple-element.83.own0), channel_id=1, source_target_pairs={{0,3},{1,0},{2,1},{3,2},{4,7},{5,4},{6,5},{7,6},{8,11},{9,8},{10,9... | collective-permute-start | bytes 786440 | tf_op jit(solution)/shard_map/ppermute | solution.py:33
  119.0 13.1 %collective-permute-start.33 = (bf16[256,512]{1,0:T(8,128)(2,1)S(1)}, bf16[256,512]{1,0:T(8,128)(2,1)S(1)}, u32[]{:S(2)}, u32[]{:S(2)}) collective-permute-start(bf16[256,512]{1,0:T(8,128)(2,1)S(1)} %get-tuple-element.83.own0), channel_id=1, source_target_pairs={{0,2},{1,3},{2,0},{3,1},{4,6},{5,7},{6,4},{7,5},{8,10},{9,11},{10,... | collective-permute-start | bytes 786440 | tf_op jit(solution)/shard_map/ppermute | solution.py:33
  132.9 2.6 %collective-permute-start.34 = (f32[128,1024]{1,0:T(8,128)S(1)}, f32[128,1024]{1,0:T(8,128)S(1)}, u32[]{:S(2)}, u32[]{:S(2)}) collective-permute-start(f32[128,1024]{1,0:T(8,128)S(1)} %shard_map.56), channel_id=1, source_target_pairs={{0,4},{1,5},{2,6},{3,7},{4,0},{5,1},{6,2},{7,3},{8,12},{9,13},{10,... | collective-permute-start | bytes 1572872 | tf_op jit(solution)/shard_map/ppermute | solution.py:29

commit v4 on v3

--- a/solution.py
+++ b/solution.py
@@ -1,3 +1,5 @@
+import functools
+
 import jax
 import jax.numpy as jnp
 from jax import lax
@@ -239,38 +241,33 @@
             low[t * B:(t + 1) * B, u * B:(u + 1) * B] = piece.astype(jnp.bfloat16)
 
 
-def parts_times_panel(parts, z, mine, come):
-    total = [None, None]
+def parts_times_panel(parts, z, panel):
+    total = None
     for value, d in parts:
-        for n, panel in enumerate((mine, come)):
-            term = dot(value, panel[aligned((z + d) & 3, 512), :])
-            total[n] = term if total[n] is None else total[n] + term
+        term = dot(value, panel[aligned((z + d) & 3, 512), :])
+        total = term if total is None else total + term
     return total
 
 
-def early_cube(where, own0, own1, own3, mine, come, out):
-    parts = [(own0[...], 0), (own1[...], 1), (own3[...], 3)]
-    out[:, :COLS], out[:, COLS:] = parts_times_panel(parts, where[3], mine, come)
-
-
-def density_share(where, at, own2, early, square, mine, come):
-    first, second = parts_times_panel([(own2[at, :], 2)], where[3], mine, come)
-    return 3.0 * square[at, :] - 2.0 * (early[at, :COLS] + first), -2.0 * (early[at, COLS:] + second)
-
-
-def leaving_density(where, own2, early, square, mine, come, out):
-    at = aligned(1 - where[2], B)
-    out[:, :COLS], out[:, COLS:] = density_share(where, at, own2, early, square, mine, come)
-
-
-def second_density(where, own2, early, square, mine, come, share, out):
-    own, other = density_share(where, aligned(where[2], B), own2, early, square, mine, come)
-    own, other = own + share[:, COLS:], other + share[:, :COLS]
+def early_cube(where, own0, mine, out):
+    out[...] = parts_times_panel([(own0[...], 0)], where[3], mine)
+
+
+def density_share(leave, where, own0, own1, own2, own3, early, square, mine, come, out):
+    core, z = where[2], where[3]
+    at = aligned(1 - core if leave else core, B)
+    parts = [(own1[at, :], 1), (own3[at, :], 3), (own2[at, :], 2)]
+    out[:, :COLS] = 3.0 * square[at, :] - 2.0 * (early[at, :] + parts_times_panel(parts, z, mine))
+    out[:, COLS:] = -2.0 * parts_times_panel([(own0[at, :], 0)] + parts, z, come)
+
+
+def join(where, stay, share, out):
     first = where[2] == 0
     for t in range(4):
-        one, two = own[:, t * B:(t + 1) * B], other[:, t * B:(t + 1) * B]
-        out[:, 2 * t * B:(2 * t + 1) * B] = jnp.where(first, one, two)
-        out[:, (2 * t + 1) * B:(2 * t + 2) * B] = jnp.where(first, two, one)
+        at, far = slice(t * B, (t + 1) * B), slice(COLS + t * B, COLS + (t + 1) * B)
+        own, other = stay[:, at] + share[:, far], stay[:, far] + share[:, at]
+        out[:, 2 * t * B:(2 * t + 1) * B] = jnp.where(first, own, other)
+        out[:, (2 * t + 1) * B:(2 * t + 2) * B] = jnp.where(first, other, own)
 
 
 SMEM = pl.BlockSpec(memory_space=pltpu.SMEM)
@@ -360,15 +357,13 @@
     own0, own1, own2, own3 = gather(low, from_z)
     come = other_core(its)
     (early,) = call(
-        early_cube, 1, [where, own0, own1, own3, mine, come],
-        [jax.ShapeDtypeStruct((ROWS, 2 * COLS), jnp.float32)], [], block_flops * 3 // 4, 4 * MIB)
-    early, own2 = lax.optimization_barrier((early, own2))
+        early_cube, 1, [where, own0, mine], [full_block], [], block_flops // 8, 2 * MIB)
     half = jax.ShapeDtypeStruct((B, 2 * COLS), jnp.float32)
-    (leave,) = call(
-        leaving_density, 1, [where, own2, early, square, mine, come], [half], [], block_flops // 8, 3 * MIB)
-    (out,) = call(
-        second_density, 1, [where, own2, early, square, mine, come, other_core(leave)], [half], [],
-        block_flops // 8, 3 * MIB)
+    last = [where, own0, own1, own2, own3, early, square, mine, come]
+    (leave,) = call(functools.partial(density_share, True), 1, last, [half], [], block_flops * 3 // 8, 5 * MIB)
+    share = other_core(leave)
+    (stay,) = call(functools.partial(density_share, False), 1, last, [half], [], block_flops * 3 // 8, 5 * MIB)
+    (out,) = call(join, 1, [where, stay, share], [half], [], 0, 2 * MIB)
     return out
 
 

time: 137 us -> 138 us (level)
    pallas_call x12 -> x13, Pallas kernels: 41.8 us -> 42.5 us  [call(): pl.pallas_call(kernel, in_specs=[SMEM] * n_smem + [VMEM] * (len(ins) - n_...]
  transfers between devices with their start and end apart: 35 -> 35, of which waited for: 19 -> 18; matrix products, arithmetic and copies ran while one was open for 1% -> 1% of each run, Pallas kernels for 21% -> 21%
where the time goes in v4:
time: 138 us; the launch traced here: 137 us
  waiting for transfers between devices  48.2 us (35%)
  starting transfers between devices  44.5 us (32%)
  Pallas kernels  42.5 us (31%)
    pallas_call x13, Pallas kernels, call(): pl.pallas_call(kernel, in_specs=[SMEM] * n_smem + [VMEM] * (len(ins) - n_...  42.5 us
    ppermute x9, waiting for transfers between devices, from_z(): lax.ppermute(a, AXES, pairs(lambda x, y, core, z: (x, y, core, z - d)))  19.1 us
    ppermute x9, waiting for transfers between devices, from_first(): lax.ppermute(a, AXES, pairs(lambda x, y, core, z: (x - d, y, core, z) if...  17.6 us
    ppermute x9, starting transfers between devices, from_z(): lax.ppermute(a, AXES, pairs(lambda x, y, core, z: (x, y, core, z - d)))  12.1 us
    ppermute x9, starting transfers between devices, from_first(): lax.ppermute(a, AXES, pairs(lambda x, y, core, z: (x - d, y, core, z) if...  11.8 us
    ppermute x6, starting transfers between devices, from_second(): lax.ppermute(a, AXES, pairs(lambda x, y, core, z: (x, y - d, core, z) if...  11.1 us
    ppermute x6, waiting for transfers between devices, from_second(): lax.ppermute(a, AXES, pairs(lambda x, y, core, z: (x, y - d, core, z) if...  9.73 us
    ppermute x11, starting transfers between devices, other_core(): lax.ppermute(a, AXES, pairs(lambda x, y, core, z: (x, y, 1 - core, z)))  9.55 us
  transfers between devices with their start and end apart: 35, of which 18 were waited for; matrix products, arithmetic and copies ran while one was open for 1% of the time, Pallas kernels for 21%

profile of v4, /device:TPU:1, one launch (start us, length us, event | category | flops | bytes accessed | tf_op | source)
XLA Modules:
  0.0 137.3 jit_solution(5778924964053198948)
XLA Ops:
  0.0 4.4 %collective-permute-start.1 = (bf16[128,256]{1,0:T(8,128)(2,1)}, bf16[128,256]{1,0:T(8,128)(2,1)S(1)}, u32[]{:S(2)}, u32[]{:S(2)}) collective-permute-start(bf16[128,256]{1,0:T(8,128)(2,1)} %param.4), channel_id=1, source_target_pairs={{0,2},{1,3},{2,0},{3,1},{4,6},{5,7},{6,4},{7,5},{8,10},{9,11},{10,... | collective-permute-start | bytes 196616 | tf_op jit(solution)/shard_map/ppermute | solution.py:35
  4.9 1.0 collective-permute-start.2
  6.7 1.4 %collective-permute-done = bf16[128,256]{1,0:T(8,128)(2,1)S(1)} collective-permute-done((bf16[128,256]{1,0:T(8,128)(2,1)}, bf16[128,256]{1,0:T(8,128)(2,1)S(1)}, u32[]{:S(2)}, u32[]{:S(2)}) %collective-permute-start) | collective-permute-done | bytes 65568 | tf_op jit(solution)/shard_map/ppermute | solution.py:35
  8.1 1.3 collective-permute-done.2
  10.3 1.4 collective-permute-start.5
  11.7 2.6 %collective-permute-start.4 = (bf16[128,1024]{1,0:T(8,128)(2,1)S(1)}, bf16[128,1024]{1,0:T(8,128)(2,1)S(1)}, u32[]{:S(2)}, u32[]{:S(2)}) collective-permute-start(bf16[128,1024]{1,0:T(8,128)(2,1)S(1)} %maximum_multiply_fusion), channel_id=1, source_target_pairs={{0,64},{1,65},{2,66},{3,67},{4,20},{5,21},{6,22},{7,23},{8,72},{9,... | collective-permute-start | bytes 786440 | tf_op jit(solution)/shard_map/ppermute | solution.py:39
  14.3 1.1 collective-permute-start.3
  15.4 1.8 %collective-permute-done.5 = bf16[128,1024]{1,0:T(8,128)(2,1)S(1)} collective-permute-done((bf16[128,1024]{1,0:T(8,128)(2,1)S(1)}, bf16[128,1024]{1,0:T(8,128)(2,1)S(1)}, u32[]{:S(2)}, u32[]{:S(2)}) %collective-permute-start.5) | collective-permute-done | bytes 262176 | tf_op jit(solution)/shard_map/ppermute | solution.py:39
  17.2 4.0 %collective-permute-done.4 = bf16[128,1024]{1,0:T(8,128)(2,1)S(1)} collective-permute-done((bf16[128,1024]{1,0:T(8,128)(2,1)S(1)}, bf16[128,1024]{1,0:T(8,128)(2,1)S(1)}, u32[]{:S(2)}, u32[]{:S(2)}) %collective-permute-start.4) | collective-permute-done | bytes 262176 | tf_op jit(solution)/shard_map/ppermute | solution.py:39
  21.2 3.1 %collective-permute-start.6 = (bf16[512,1024]{1,0:T(8,128)(2,1)S(1)}, bf16[512,1024]{1,0:T(8,128)(2,1)}, u32[]{:S(2)}, u32[]{:S(2)}) collective-permute-start(bf16[512,1024]{1,0:T(8,128)(2,1)S(1)} %pad_maximum_fusion.own0), channel_id=1, source_target_pairs={{0,4},{1,5},{2,6},{3,7},{4,0},{5,1},{6,2},{7,3},{8,12},{9,13},{10,... | collective-permute-start | bytes 3145736 | tf_op jit(solution)/shard_map/ppermute | solution.py:31
  24.3 1.6 %collective-permute-start.8 = (bf16[512,1024]{1,0:T(8,128)(2,1)S(1)}, bf16[512,1024]{1,0:T(8,128)(2,1)S(1)}, u32[]{:S(2)}, u32[]{:S(2)}) collective-permute-start(bf16[512,1024]{1,0:T(8,128)(2,1)S(1)} %pad_maximum_fusion.own0), channel_id=1, source_target_pairs={{0,8},{1,9},{2,10},{3,11},{4,36},{5,37},{6,38},{7,39},{8,16},{9,17... | collective-permute-start | bytes 3145736 | tf_op jit(solution)/shard_map/ppermute | solution.py:44
  25.9 1.1 collective-permute-start.7
  27.0 3.1 %shard_map.46 = (bf16[4096,2048]{1,0:T(8,128)(2,1)S(1)}, bf16[256,4096]{1,0:T(8,128)(2,1)S(1)}, bf16[256,1024]{1,0:T(8,128)(2,1)S(1)}) custom-call(s32[4]{0:T(128)S(1)} %pad_add_fusion.1.where, s32[2,32,32]{2,1,0:T(8,128)S(1)} %copy-done.1, bf16[512,1024]{1,0:T(8,128)(2,1)S(1)} %pad_maximum_fusion.own0, bf16[512,1024]{1,0:T(8,128)(2,1)} %collective-permute-done.6.other0), custom_call_target="tpu_custom_call" | custom-call | flops 67108864 | bytes 1048576 | tf_op jit(solution)/shard_map/pallas_call | solution.py:278
  30.1 9.3 %collective-permute-done.8.own3 = bf16[512,1024]{1,0:T(8,128)(2,1)S(1)} collective-permute-done((bf16[512,1024]{1,0:T(8,128)(2,1)S(1)}, bf16[512,1024]{1,0:T(8,128)(2,1)S(1)}, u32[]{:S(2)}, u32[]{:S(2)}) %collective-permute-start.8) | collective-permute-done | bytes 1048608 | tf_op jit(solution)/shard_map/ppermute | solution.py:44
  39.8 0.9 collective-permute-start.9
  40.7 2.7 %collective-permute-start.11 = (bf16[512,1024]{1,0:T(8,128)(2,1)S(1)}, bf16[512,1024]{1,0:T(8,128)(2,1)S(1)}, u32[]{:S(2)}, u32[]{:S(2)}) collective-permute-start(bf16[512,1024]{1,0:T(8,128)(2,1)S(1)} %pad_maximum_fusion.own0), channel_id=1, source_target_pairs={{0,16},{1,17},{2,18},{3,19},{4,68},{5,69},{6,70},{7,71},{8,24},{9,... | collective-permute-start | bytes 3145736 | tf_op jit(solution)/shard_map/ppermute | solution.py:44
  43.4 5.9 %shard_map.47 = (bf16[4096,2048]{1,0:T(8,128)(2,1)S(1)}, bf16[256,4096]{1,0:T(8,128)(2,1)S(1)}) custom-call(s32[4]{0:T(128)S(1)} %pad_add_fusion.1.where, s32[2,32,32]{2,1,0:T(8,128)S(1)} %copy-done.1, bf16[512,1024]{1,0:T(8,128)(2,1)S(1)} %pad_maximum_fusion.own0, ...), custom_call_target="tpu_custom_call", output_to_operand_aliasing={{0}: (7, {}), {1}: (8, {})} | custom-call | flops 5905580032 | bytes 8388608 | tf_op jit(solution)/shard_map/pallas_call | solution.py:278
  49.4 8.0 %shard_map.48 = (bf16[4096,2048]{1,0:T(8,128)(2,1)S(1)}, bf16[256,4096]{1,0:T(8,128)(2,1)S(1)}, f32[256,2048]{1,0:T(8,128)S(1)}) custom-call(s32[4]{0:T(128)S(1)} %pad_add_fusion.1.where, s32[2,32,32]{2,1,0:T(8,128)S(1)} %copy-done.1, bf16[512,1024]{1,0:T(8,128)(2,1)S(1)} %pad_maximum_fusion.own0, ...), custom_call_target="tpu_custom_call", output_to_operand_aliasing={{0}: (8, {}), {1}: (9, {})} | custom-call | flops 5905580032 | bytes 8388608 | tf_op jit(solution)/shard_map/pallas_call | solution.py:278
  57.4 1.0 collective-permute-start.12
  58.5 5.7 %shard_map.49 = (bf16[4096,2048]{1,0:T(8,128)(2,1)S(1)}, bf16[256,4096]{1,0:T(8,128)(2,1)S(1)}) custom-call(s32[4]{0:T(128)S(1)} %pad_add_fusion.1.where, s32[2,32,32]{2,1,0:T(8,128)S(1)} %copy-done.1, bf16[512,1024]{1,0:T(8,128)(2,1)S(1)} %pad_maximum_fusion.own0, ...), custom_call_target="tpu_custom_call", output_to_operand_aliasing={{0}: (10, {}), {1}: (11, {})} | custom-call | flops 5368709120 | bytes 8388608 | tf_op jit(solution)/shard_map/pallas_call | solution.py:278
  64.2 7.1 %shard_map.50 = (bf16[4096,2048]{1,0:T(8,128)(2,1)S(1)}, bf16[256,4096]{1,0:T(8,128)(2,1)S(1)}, bf16[256,2048]{1,0:T(8,128)(2,1)S(1)}, f32[256,512]{1,0:T(8,128)S(1)}) custom-call(s32[4]{0:T(128)S(1)} %pad_add_fusion.1.where, s32[2,32,32]{2,1,0:T(8,128)S(1)} %copy-done.1, ...), custom_call_target="tpu_custom_call", output_to_operand_aliasing={{0}: (10, {}), {1}: (11, {})} | custom-call | flops 4294967296 | bytes 20971520 | tf_op jit(solution)/shard_map/pallas_call | solution.py:278
  71.4 2.3 %shard_map.51 = (f32[256,512]{1,0:T(8,128)S(1)}, bf16[4096,512]{1,0:T(8,128)(2,1)S(1)}) custom-call(s32[4]{0:T(128)S(1)} %pad_add_fusion.1.where, bf16[256,2048]{1,0:T(8,128)(2,1)S(1)} %get-tuple-element.63.low, bf16[4096,2048]{1,0:T(8,128)(2,1)S(1)} %get-tuple-element.64.panel), custom_call_target="tpu_custom_call" | custom-call | flops 536870912 | bytes 12582912 | tf_op jit(solution)/shard_map/pallas_call | solution.py:278
  74.0 1.8 %shard_map.52.refs_0_ = bf16[256,512]{1,0:T(8,128)(2,1)S(1)} custom-call(s32[4]{0:T(128)S(1)} %pad_add_fusion.1.where, s32[2,32,32]{2,1,0:T(8,128)S(1)} %copy-done.1, bf16[256,2048]{1,0:T(8,128)(2,1)S(1)} %collective-permute-done.13.its, bf16[4096,512]{1,0:T(8,128)(2,1)S(1)} %get-tuple-element.65.columns, f32[256,512]{1,0:T(8,128)S(1)} %get-tuple-element.66.early, ...), custom_call_target="tpu_custom_call" | custom-call | flops 536870912 | bytes 4194304 | tf_op jit(solution)/shard_map/pallas_call | solution.py:278
  75.8 2.7 %collective-permute-start.17 = (bf16[256,512]{1,0:T(8,128)(2,1)S(1)}, bf16[256,512]{1,0:T(8,128)(2,1)S(1)}, u32[]{:S(2)}, u32[]{:S(2)}) collective-permute-start(bf16[256,512]{1,0:T(8,128)(2,1)S(1)} %shard_map.52.refs_0_), channel_id=1, source_target_pairs={{0,16},{1,17},{2,18},{3,19},{4,68},{5,69},{6,70},{7,71},{8,24},{9,... | collective-permute-start | bytes 786440 | tf_op jit(solution)/shard_map/ppermute | solution.py:44
  78.6 1.7 %collective-permute-start.16 = (bf16[256,512]{1,0:T(8,128)(2,1)S(1)}, bf16[256,512]{1,0:T(8,128)(2,1)S(1)}, u32[]{:S(2)}, u32[]{:S(2)}) collective-permute-start(bf16[256,512]{1,0:T(8,128)(2,1)S(1)} %shard_map.52.refs_0_), channel_id=1, source_target_pairs={{0,64},{1,65},{2,66},{3,67},{4,20},{5,21},{6,22},{7,23},{8,72},{9,... | collective-permute-start | bytes 786440 | tf_op jit(solution)/shard_map/ppermute | solution.py:39
  80.9 2.1 %collective-permute-start.14 = (bf16[256,512]{1,0:T(8,128)(2,1)S(1)}, bf16[256,512]{1,0:T(8,128)(2,1)S(1)}, u32[]{:S(2)}, u32[]{:S(2)}) collective-permute-start(bf16[256,512]{1,0:T(8,128)(2,1)S(1)} %shard_map.52.refs_0_), channel_id=1, source_target_pairs={{0,96},{1,97},{2,98},{3,99},{4,28},{5,29},{6,30},{7,31},{8,104},{9... | collective-permute-start | bytes 786440 | tf_op jit(solution)/shard_map/ppermute | solution.py:39
  83.0 1.6 %collective-permute-start.21 = (bf16[256,512]{1,0:T(8,128)(2,1)S(1)}, bf16[256,512]{1,0:T(8,128)(2,1)S(1)}, u32[]{:S(2)}, u32[]{:S(2)}) collective-permute-start(bf16[256,512]{1,0:T(8,128)(2,1)S(1)} %shard_map.52.refs_0_), channel_id=1, source_target_pairs={{0,2},{1,3},{2,0},{3,1},{4,6},{5,7},{6,4},{7,5},{8,10},{9,11},{10,... | collective-permute-start | bytes 786440 | tf_op jit(solution)/shard_map/ppermute | solution.py:35
  84.6 1.6 %collective-permute-done.16 = bf16[256,512]{1,0:T(8,128)(2,1)S(1)} collective-permute-done((bf16[256,512]{1,0:T(8,128)(2,1)S(1)}, bf16[256,512]{1,0:T(8,128)(2,1)S(1)}, u32[]{:S(2)}, u32[]{:S(2)}) %collective-permute-start.16) | collective-permute-done | bytes 262176 | tf_op jit(solution)/shard_map/ppermute | solution.py:39
  86.6 2.6 %collective-permute-done.15 = bf16[256,512]{1,0:T(8,128)(2,1)S(1)} collective-permute-done((bf16[256,512]{1,0:T(8,128)(2,1)S(1)}, bf16[256,512]{1,0:T(8,128)(2,1)S(1)}, u32[]{:S(2)}, u32[]{:S(2)}) %collective-permute-start.15) | collective-permute-done | bytes 262176 | tf_op jit(solution)/shard_map/ppermute | solution.py:39
  89.3 2.0 %collective-permute-start.19 = (bf16[1024,512]{1,0:T(8,128)(2,1)S(1)}, bf16[1024,512]{1,0:T(8,128)(2,1)S(1)}, u32[]{:S(2)}, u32[]{:S(2)}) collective-permute-start(bf16[1024,512]{1,0:T(8,128)(2,1)S(1)} %constant_dynamic-update-slice_fusion.refs_8_), channel_id=1, source_target_pairs={{0,8},{1,9},{2,10},{3,11},{4,36},{5,37},{6,38},{7,39},{8,16},{9,17... | collective-permute-start | bytes 3145736 | tf_op jit(solution)/shard_map/ppermute | solution.py:44
  91.2 1.1 collective-permute-start.18
  92.3 3.0 %collective-permute-done.21.refs_2_ = bf16[256,512]{1,0:T(8,128)(2,1)S(1)} collective-permute-done((bf16[256,512]{1,0:T(8,128)(2,1)S(1)}, bf16[256,512]{1,0:T(8,128)(2,1)S(1)}, u32[]{:S(2)}, u32[]{:S(2)}) %collective-permute-start.21) | collective-permute-done | bytes 262176 | tf_op jit(solution)/shard_map/ppermute | solution.py:35
  95.3 2.3 %collective-permute-done.20.refs_1_ = bf16[256,512]{1,0:T(8,128)(2,1)S(1)} collective-permute-done((bf16[256,512]{1,0:T(8,128)(2,1)S(1)}, bf16[256,512]{1,0:T(8,128)(2,1)S(1)}, u32[]{:S(2)}, u32[]{:S(2)}) %collective-permute-start.20) | collective-permute-done | bytes 262176 | tf_op jit(solution)/shard_map/ppermute | solution.py:35
  97.6 1.6 %collective-permute-start.24 = (bf16[256,512]{1,0:T(8,128)(2,1)S(1)}, bf16[256,512]{1,0:T(8,128)(2,1)S(1)}, u32[]{:S(2)}, u32[]{:S(2)}) collective-permute-start(bf16[256,512]{1,0:T(8,128)(2,1)S(1)} %collective-permute-done.20.refs_1_), channel_id=1, source_target_pairs={{0,4},{1,5},{2,6},{3,7},{4,0},{5,1},{6,2},{7,3},{8,12},{9,13},{10,... | collective-permute-start | bytes 786440 | tf_op jit(solution)/shard_map/ppermute | solution.py:31
  100.7 1.2 collective-permute-start.28
  101.9 1.2 collective-permute-start.27
  103.1 4.8 %collective-permute-done.29.refs_12_ = bf16[256,512]{1,0:T(8,128)(2,1)S(1)} collective-permute-done((bf16[256,512]{1,0:T(8,128)(2,1)S(1)}, bf16[256,512]{1,0:T(8,128)(2,1)S(1)}, u32[]{:S(2)}, u32[]{:S(2)}) %collective-permute-start.29) | collective-permute-done | bytes 262176 | tf_op jit(solution)/shard_map/ppermute | solution.py:39
  108.3 2.9 %collective-permute-done.28.refs_11_ = bf16[256,512]{1,0:T(8,128)(2,1)S(1)} collective-permute-done((bf16[256,512]{1,0:T(8,128)(2,1)S(1)}, bf16[256,512]{1,0:T(8,128)(2,1)S(1)}, u32[]{:S(2)}, u32[]{:S(2)}) %collective-permute-start.28) | collective-permute-done | bytes 262176 | tf_op jit(solution)/shard_map/ppermute | solution.py:39
  111.1 2.0 %shard_map.53 = (f32[256,512]{1,0:T(8,128)S(1)}, bf16[256,4096]{1,0:T(8,128)(2,1)S(1)}, bf16[2048,512]{1,0:T(8,128)(2,1)S(1)}, bf16[2048,512]{1,0:T(8,128)(2,1)S(1)}) custom-call(s32[4]{0:T(128)S(1)} %pad_add_fusion.1.where, bf16[256,512]{1,0:T(8,128)(2,1)S(1)} %shard_map.52.refs_0_, bf16[256,512]{1,0:T(8,128)(2,1)S(1)} %collective-permute-done.20.refs_1_, ...), custom_call_target="tpu_custom_call" | custom-call | flops 536870912 | bytes 10485760 | tf_op jit(solution)/shard_map/pallas_call | solution.py:278
  113.1 1.9 %shard_map.54 = (f32[256,512]{1,0:T(8,128)S(1)}, bf16[256,512]{1,0:T(8,128)(2,1)S(1)}, bf16[2048,512]{1,0:T(8,128)(2,1)S(1)}, bf16[2048,512]{1,0:T(8,128)(2,1)S(1)}) custom-call(s32[4]{0:T(128)S(1)} %pad_add_fusion.1.where, s32[2,32,32]{2,1,0:T(8,128)S(1)} %copy-done.2, ...), custom_call_target="tpu_custom_call", output_to_operand_aliasing={{2}: (6, {}), {3}: (7, {})} | custom-call | flops 536870912 | bytes 8388608 | tf_op jit(solution)/shard_map/pallas_call | solution.py:278
  115.1 0.9 collective-permute-start.33
  116.2 4.0 %collective-permute-start.31 = (bf16[256,512]{1,0:T(8,128)(2,1)S(1)}, bf16[256,512]{1,0:T(8,128)(2,1)S(1)}, u32[]{:S(2)}, u32[]{:S(2)}) collective-permute-start(bf16[256,512]{1,0:T(8,128)(2,1)S(1)} %get-tuple-element.81.own0), channel_id=1, source_target_pairs={{0,2},{1,3},{2,0},{3,1},{4,6},{5,7},{6,4},{7,5},{8,10},{9,11},{10,... | collective-permute-start | bytes 786440 | tf_op jit(solution)/shard_map/ppermute | solution.py:35
  121.0 4.5 %collective-permute-done.32.own3 = bf16[256,512]{1,0:T(8,128)(2,1)S(1)} collective-permute-done((bf16[256,512]{1,0:T(8,128)(2,1)S(1)}, bf16[256,512]{1,0:T(8,128)(2,1)S(1)}, u32[]{:S(2)}, u32[]{:S(2)}) %collective-permute-start.32) | collective-permute-done | bytes 262176 | tf_op jit(solution)/shard_map/ppermute | solution.py:35
  125.5 6.6 %collective-permute-done.31.own2 = bf16[256,512]{1,0:T(8,128)(2,1)S(1)} collective-permute-done((bf16[256,512]{1,0:T(8,128)(2,1)S(1)}, bf16[256,512]{1,0:T(8,128)(2,1)S(1)}, u32[]{:S(2)}, u32[]{:S(2)}) %collective-permute-start.31) | collective-permute-done | bytes 262176 | tf_op jit(solution)/shard_map/ppermute | solution.py:35
  132.1 1.2 shard_map.57
  133.3 1.0 collective-permute-start.34
  134.3 1.2 shard_map.56.stay
  135.9 1.4 %shard_map.58 = f32[128,1024]{1,0:T(8,128)} custom-call(s32[4]{0:T(128)S(1)} %pad_add_fusion.1.where, f32[128,1024]{1,0:T(8,128)S(1)} %shard_map.56.stay, f32[128,1024]{1,0:T(8,128)S(1)} %collective-permute-done.34.share), custom_call_target="tpu_custom_call" | custom-call | bytes 2097152 | tf_op jit(solution)/shard_map/pallas_call | solution.py:278
  (56 shorter events, 7.6 us)
Async XLA Ops:
  0.0 5.9 %copy-start = (s32[32,8]{0,1:T(8,128)S(1)}, s32[32,8]{0,1:T(8,128)}, u32[]{:S(2)}) copy-start(s32[32,8]{0,1:T(8,128)} %param.5) | copy-start | bytes 3076
  0.0 27.0 %copy-start.1 = (s32[2,32,32]{2,1,0:T(8,128)S(1)}, s32[2,32,32]{2,1,0:T(8,128)}, u32[]{:S(2)}) copy-start(s32[2,32,32]{2,1,0:T(8,128)} %keep_d.11) | copy-start | bytes 24580
  0.0 6.7 %collective-permute-start.1 = (bf16[128,256]{1,0:T(8,128)(2,1)}, bf16[128,256]{1,0:T(8,128)(2,1)S(1)}, u32[]{:S(2)}, u32[]{:S(2)}) collective-permute-start(bf16[128,256]{1,0:T(8,128)(2,1)} %param.4), channel_id=1, source_target_pairs={{0,2},{1,3},{2,0},{3,1},{4,6},{5,7},{6,4},{7,5},{8,10},{9,11},{10,... | collective-permute-start | bytes 196616 | tf_op jit(solution)/shard_map/ppermute | solution.py:35
  4.4 3.7 %collective-permute-start = (bf16[128,256]{1,0:T(8,128)(2,1)}, bf16[128,256]{1,0:T(8,128)(2,1)S(1)}, u32[]{:S(2)}, u32[]{:S(2)}) collective-permute-start(bf16[128,256]{1,0:T(8,128)(2,1)} %param.4), channel_id=1, source_target_pairs={{0,3},{1,0},{2,1},{3,2},{4,7},{5,4},{6,5},{7,6},{8,11},{9,8},{10,9... | collective-permute-start | bytes 196616 | tf_op jit(solution)/shard_map/ppermute | solution.py:35
  4.9 4.5 %collective-permute-start.2 = (bf16[128,256]{1,0:T(8,128)(2,1)}, bf16[128,256]{1,0:T(8,128)(2,1)S(1)}, u32[]{:S(2)}, u32[]{:S(2)}) collective-permute-start(bf16[128,256]{1,0:T(8,128)(2,1)} %param.4), channel_id=1, source_target_pairs={{0,1},{1,2},{2,3},{3,0},{4,5},{5,6},{6,7},{7,4},{8,9},{9,10},{10,1... | collective-permute-start | bytes 196616 | tf_op jit(solution)/shard_map/ppermute | solution.py:35
  10.3 6.9 %collective-permute-start.5 = (bf16[128,1024]{1,0:T(8,128)(2,1)S(1)}, bf16[128,1024]{1,0:T(8,128)(2,1)S(1)}, u32[]{:S(2)}, u32[]{:S(2)}) collective-permute-start(bf16[128,1024]{1,0:T(8,128)(2,1)S(1)} %maximum_multiply_fusion), channel_id=1, source_target_pairs={{0,32},{1,33},{2,34},{3,35},{4,12},{5,13},{6,14},{7,15},{8,40},{9,... | collective-permute-start | bytes 786440 | tf_op jit(solution)/shard_map/ppermute | solution.py:39
  11.7 9.5 %collective-permute-start.4 = (bf16[128,1024]{1,0:T(8,128)(2,1)S(1)}, bf16[128,1024]{1,0:T(8,128)(2,1)S(1)}, u32[]{:S(2)}, u32[]{:S(2)}) collective-permute-start(bf16[128,1024]{1,0:T(8,128)(2,1)S(1)} %maximum_multiply_fusion), channel_id=1, source_target_pairs={{0,64},{1,65},{2,66},{3,67},{4,20},{5,21},{6,22},{7,23},{8,72},{9,... | collective-permute-start | bytes 786440 | tf_op jit(solution)/shard_map/ppermute | solution.py:39
  14.3 6.9 %collective-permute-start.3 = (bf16[128,1024]{1,0:T(8,128)(2,1)S(1)}, bf16[128,1024]{1,0:T(8,128)(2,1)S(1)}, u32[]{:S(2)}, u32[]{:S(2)}) collective-permute-start(bf16[128,1024]{1,0:T(8,128)(2,1)S(1)} %maximum_multiply_fusion), channel_id=1, source_target_pairs={{0,96},{1,97},{2,98},{3,99},{4,28},{5,29},{6,30},{7,31},{8,104},{9... | collective-permute-start | bytes 786440 | tf_op jit(solution)/shard_map/ppermute | solution.py:39
  21.2 5.8 %collective-permute-start.6 = (bf16[512,1024]{1,0:T(8,128)(2,1)S(1)}, bf16[512,1024]{1,0:T(8,128)(2,1)}, u32[]{:S(2)}, u32[]{:S(2)}) collective-permute-start(bf16[512,1024]{1,0:T(8,128)(2,1)S(1)} %pad_maximum_fusion.own0), channel_id=1, source_target_pairs={{0,4},{1,5},{2,6},{3,7},{4,0},{5,1},{6,2},{7,3},{8,12},{9,13},{10,... | collective-permute-start | bytes 3145736 | tf_op jit(solution)/shard_map/ppermute | solution.py:31
  24.3 15.2 %collective-permute-start.8 = (bf16[512,1024]{1,0:T(8,128)(2,1)S(1)}, bf16[512,1024]{1,0:T(8,128)(2,1)S(1)}, u32[]{:S(2)}, u32[]{:S(2)}) collective-permute-start(bf16[512,1024]{1,0:T(8,128)(2,1)S(1)} %pad_maximum_fusion.own0), channel_id=1, source_target_pairs={{0,8},{1,9},{2,10},{3,11},{4,36},{5,37},{6,38},{7,39},{8,16},{9,17... | collective-permute-start | bytes 3145736 | tf_op jit(solution)/shard_map/ppermute | solution.py:44
  25.9 13.9 %collective-permute-start.7 = (bf16[512,1024]{1,0:T(8,128)(2,1)S(1)}, bf16[512,1024]{1,0:T(8,128)(2,1)S(1)}, u32[]{:S(2)}, u32[]{:S(2)}) collective-permute-start(bf16[512,1024]{1,0:T(8,128)(2,1)S(1)} %pad_maximum_fusion.own0), channel_id=1, source_target_pairs={{0,24},{1,25},{2,26},{3,27},{4,100},{5,101},{6,102},{7,103},{8,0},... | collective-permute-start | bytes 3145736 | tf_op jit(solution)/shard_map/ppermute | solution.py:44
  39.8 9.5 %collective-permute-start.9 = (bf16[512,1024]{1,0:T(8,128)(2,1)S(1)}, bf16[512,1024]{1,0:T(8,128)(2,1)S(1)}, u32[]{:S(2)}, u32[]{:S(2)}) collective-permute-start(bf16[512,1024]{1,0:T(8,128)(2,1)S(1)} %collective-permute-done.7.own1), channel_id=1, source_target_pairs={{0,4},{1,5},{2,6},{3,7},{4,0},{5,1},{6,2},{7,3},{8,12},{9,13},{10,... | collective-permute-start | bytes 3145736 | tf_op jit(solution)/shard_map/ppermute | solution.py:31
  40.7 8.6 %collective-permute-start.10 = (bf16[512,1024]{1,0:T(8,128)(2,1)S(1)}, bf16[512,1024]{1,0:T(8,128)(2,1)S(1)}, u32[]{:S(2)}, u32[]{:S(2)}) collective-permute-start(bf16[512,1024]{1,0:T(8,128)(2,1)S(1)} %collective-permute-done.8.own3), channel_id=1, source_target_pairs={{0,4},{1,5},{2,6},{3,7},{4,0},{5,1},{6,2},{7,3},{8,12},{9,13},{10,... | collective-permute-start | bytes 3145736 | tf_op jit(solution)/shard_map/ppermute | solution.py:31
  40.7 16.7 %collective-permute-start.11 = (bf16[512,1024]{1,0:T(8,128)(2,1)S(1)}, bf16[512,1024]{1,0:T(8,128)(2,1)S(1)}, u32[]{:S(2)}, u32[]{:S(2)}) collective-permute-start(bf16[512,1024]{1,0:T(8,128)(2,1)S(1)} %pad_maximum_fusion.own0), channel_id=1, source_target_pairs={{0,16},{1,17},{2,18},{3,19},{4,68},{5,69},{6,70},{7,71},{8,24},{9,... | collective-permute-start | bytes 3145736 | tf_op jit(solution)/shard_map/ppermute | solution.py:44
  57.4 6.7 %copy-start.2 = (s32[2,32,32]{2,1,0:T(8,128)S(1)}, s32[2,32,32]{2,1,0:T(8,128)}, u32[]{:S(2)}) copy-start(s32[2,32,32]{2,1,0:T(8,128)} %keep_s.3) | copy-start | bytes 24580
  57.4 6.7 %collective-permute-start.12 = (bf16[512,1024]{1,0:T(8,128)(2,1)S(1)}, bf16[512,1024]{1,0:T(8,128)(2,1)S(1)}, u32[]{:S(2)}, u32[]{:S(2)}) collective-permute-start(bf16[512,1024]{1,0:T(8,128)(2,1)S(1)} %collective-permute-done.11.own2), channel_id=1, source_target_pairs={{0,4},{1,5},{2,6},{3,7},{4,0},{5,1},{6,2},{7,3},{8,12},{9,13},{10,... | collective-permute-start | bytes 3145736 | tf_op jit(solution)/shard_map/ppermute | solution.py:31
  71.3 2.7 %collective-permute-start.13 = (bf16[256,2048]{1,0:T(8,128)(2,1)S(1)}, bf16[256,2048]{1,0:T(8,128)(2,1)S(1)}, u32[]{:S(2)}, u32[]{:S(2)}) collective-permute-start(bf16[256,2048]{1,0:T(8,128)(2,1)S(1)} %get-tuple-element.63.low), channel_id=1, source_target_pairs={{0,4},{1,5},{2,6},{3,7},{4,0},{5,1},{6,2},{7,3},{8,12},{9,13},{10,... | collective-permute-start | bytes 3145736 | tf_op jit(solution)/shard_map/ppermute | solution.py:31
  75.8 7.1 %collective-permute-start.17 = (bf16[256,512]{1,0:T(8,128)(2,1)S(1)}, bf16[256,512]{1,0:T(8,128)(2,1)S(1)}, u32[]{:S(2)}, u32[]{:S(2)}) collective-permute-start(bf16[256,512]{1,0:T(8,128)(2,1)S(1)} %shard_map.52.refs_0_), channel_id=1, source_target_pairs={{0,16},{1,17},{2,18},{3,19},{4,68},{5,69},{6,70},{7,71},{8,24},{9,... | collective-permute-start | bytes 786440 | tf_op jit(solution)/shard_map/ppermute | solution.py:44
  78.6 7.6 %collective-permute-start.16 = (bf16[256,512]{1,0:T(8,128)(2,1)S(1)}, bf16[256,512]{1,0:T(8,128)(2,1)S(1)}, u32[]{:S(2)}, u32[]{:S(2)}) collective-permute-start(bf16[256,512]{1,0:T(8,128)(2,1)S(1)} %shard_map.52.refs_0_), channel_id=1, source_target_pairs={{0,64},{1,65},{2,66},{3,67},{4,20},{5,21},{6,22},{7,23},{8,72},{9,... | collective-permute-start | bytes 786440 | tf_op jit(solution)/shard_map/ppermute | solution.py:39
  80.3 8.9 %collective-permute-start.15 = (bf16[256,512]{1,0:T(8,128)(2,1)S(1)}, bf16[256,512]{1,0:T(8,128)(2,1)S(1)}, u32[]{:S(2)}, u32[]{:S(2)}) collective-permute-start(bf16[256,512]{1,0:T(8,128)(2,1)S(1)} %shard_map.52.refs_0_), channel_id=1, source_target_pairs={{0,32},{1,33},{2,34},{3,35},{4,12},{5,13},{6,14},{7,15},{8,40},{9,... | collective-permute-start | bytes 786440 | tf_op jit(solution)/shard_map/ppermute | solution.py:39
  80.9 8.3 %collective-permute-start.14 = (bf16[256,512]{1,0:T(8,128)(2,1)S(1)}, bf16[256,512]{1,0:T(8,128)(2,1)S(1)}, u32[]{:S(2)}, u32[]{:S(2)}) collective-permute-start(bf16[256,512]{1,0:T(8,128)(2,1)S(1)} %shard_map.52.refs_0_), channel_id=1, source_target_pairs={{0,96},{1,97},{2,98},{3,99},{4,28},{5,29},{6,30},{7,31},{8,104},{9... | collective-permute-start | bytes 786440 | tf_op jit(solution)/shard_map/ppermute | solution.py:39
  83.0 9.3 %collective-permute-start.22 = (bf16[256,512]{1,0:T(8,128)(2,1)S(1)}, bf16[256,512]{1,0:T(8,128)(2,1)S(1)}, u32[]{:S(2)}, u32[]{:S(2)}) collective-permute-start(bf16[256,512]{1,0:T(8,128)(2,1)S(1)} %shard_map.52.refs_0_), channel_id=1, source_target_pairs={{0,1},{1,2},{2,3},{3,0},{4,5},{5,6},{6,7},{7,4},{8,9},{9,10},{10,1... | collective-permute-start | bytes 786440 | tf_op jit(solution)/shard_map/ppermute | solution.py:35
  83.0 12.3 %collective-permute-start.21 = (bf16[256,512]{1,0:T(8,128)(2,1)S(1)}, bf16[256,512]{1,0:T(8,128)(2,1)S(1)}, u32[]{:S(2)}, u32[]{:S(2)}) collective-permute-start(bf16[256,512]{1,0:T(8,128)(2,1)S(1)} %shard_map.52.refs_0_), channel_id=1, source_target_pairs={{0,2},{1,3},{2,0},{3,1},{4,6},{5,7},{6,4},{7,5},{8,10},{9,11},{10,... | collective-permute-start | bytes 786440 | tf_op jit(solution)/shard_map/ppermute | solution.py:35
  86.2 11.4 %collective-permute-start.20 = (bf16[256,512]{1,0:T(8,128)(2,1)S(1)}, bf16[256,512]{1,0:T(8,128)(2,1)S(1)}, u32[]{:S(2)}, u32[]{:S(2)}) collective-permute-start(bf16[256,512]{1,0:T(8,128)(2,1)S(1)} %shard_map.52.refs_0_), channel_id=1, source_target_pairs={{0,3},{1,0},{2,1},{3,2},{4,7},{5,4},{6,5},{7,6},{8,11},{9,8},{10,9... | collective-permute-start | bytes 786440 | tf_op jit(solution)/shard_map/ppermute | solution.py:35
  89.3 23.9 %collective-permute-start.19 = (bf16[1024,512]{1,0:T(8,128)(2,1)S(1)}, bf16[1024,512]{1,0:T(8,128)(2,1)S(1)}, u32[]{:S(2)}, u32[]{:S(2)}) collective-permute-start(bf16[1024,512]{1,0:T(8,128)(2,1)S(1)} %constant_dynamic-update-slice_fusion.refs_8_), channel_id=1, source_target_pairs={{0,8},{1,9},{2,10},{3,11},{4,36},{5,37},{6,38},{7,39},{8,16},{9,17... | collective-permute-start | bytes 3145736 | tf_op jit(solution)/shard_map/ppermute | solution.py:44
  91.2 21.9 %collective-permute-start.18 = (bf16[1024,512]{1,0:T(8,128)(2,1)S(1)}, bf16[1024,512]{1,0:T(8,128)(2,1)S(1)}, u32[]{:S(2)}, u32[]{:S(2)}) collective-permute-start(bf16[1024,512]{1,0:T(8,128)(2,1)S(1)} %constant_dynamic-update-slice_fusion.refs_8_), channel_id=1, source_target_pairs={{0,24},{1,25},{2,26},{3,27},{4,100},{5,101},{6,102},{7,103},{8,0},... | collective-permute-start | bytes 3145736 | tf_op jit(solution)/shard_map/ppermute | solution.py:44
  97.6 2.7 %collective-permute-start.24 = (bf16[256,512]{1,0:T(8,128)(2,1)S(1)}, bf16[256,512]{1,0:T(8,128)(2,1)S(1)}, u32[]{:S(2)}, u32[]{:S(2)}) collective-permute-start(bf16[256,512]{1,0:T(8,128)(2,1)S(1)} %collective-permute-done.20.refs_1_), channel_id=1, source_target_pairs={{0,4},{1,5},{2,6},{3,7},{4,0},{5,1},{6,2},{7,3},{8,12},{9,13},{10,... | collective-permute-start | bytes 786440 | tf_op jit(solution)/shard_map/ppermute | solution.py:31
  99.1 1.5 %collective-permute-start.25 = (bf16[256,512]{1,0:T(8,128)(2,1)S(1)}, bf16[256,512]{1,0:T(8,128)(2,1)S(1)}, u32[]{:S(2)}, u32[]{:S(2)}) collective-permute-start(bf16[256,512]{1,0:T(8,128)(2,1)S(1)} %collective-permute-done.21.refs_2_), channel_id=1, source_target_pairs={{0,4},{1,5},{2,6},{3,7},{4,0},{5,1},{6,2},{7,3},{8,12},{9,13},{10,... | collective-permute-start | bytes 786440 | tf_op jit(solution)/shard_map/ppermute | solution.py:31
  99.1 2.7 %collective-permute-start.26 = (bf16[256,512]{1,0:T(8,128)(2,1)S(1)}, bf16[256,512]{1,0:T(8,128)(2,1)S(1)}, u32[]{:S(2)}, u32[]{:S(2)}) collective-permute-start(bf16[256,512]{1,0:T(8,128)(2,1)S(1)} %collective-permute-done.22.refs_3_), channel_id=1, source_target_pairs={{0,4},{1,5},{2,6},{3,7},{4,0},{5,1},{6,2},{7,3},{8,12},{9,13},{10,... | collective-permute-start | bytes 786440 | tf_op jit(solution)/shard_map/ppermute | solution.py:31
  100.3 7.6 %collective-permute-start.29 = (bf16[256,512]{1,0:T(8,128)(2,1)S(1)}, bf16[256,512]{1,0:T(8,128)(2,1)S(1)}, u32[]{:S(2)}, u32[]{:S(2)}) collective-permute-start(bf16[256,512]{1,0:T(8,128)(2,1)S(1)} %collective-permute-done.17.refs_9_), channel_id=1, source_target_pairs={{0,32},{1,33},{2,34},{3,35},{4,12},{5,13},{6,14},{7,15},{8,40},{9,... | collective-permute-start | bytes 786440 | tf_op jit(solution)/shard_map/ppermute | solution.py:39
  100.7 10.4 %collective-permute-start.28 = (bf16[256,512]{1,0:T(8,128)(2,1)S(1)}, bf16[256,512]{1,0:T(8,128)(2,1)S(1)}, u32[]{:S(2)}, u32[]{:S(2)}) collective-permute-start(bf16[256,512]{1,0:T(8,128)(2,1)S(1)} %collective-permute-done.17.refs_9_), channel_id=1, source_target_pairs={{0,64},{1,65},{2,66},{3,67},{4,20},{5,21},{6,22},{7,23},{8,72},{9,... | collective-permute-start | bytes 786440 | tf_op jit(solution)/shard_map/ppermute | solution.py:39
  101.9 9.3 %collective-permute-start.27 = (bf16[256,512]{1,0:T(8,128)(2,1)S(1)}, bf16[256,512]{1,0:T(8,128)(2,1)S(1)}, u32[]{:S(2)}, u32[]{:S(2)}) collective-permute-start(bf16[256,512]{1,0:T(8,128)(2,1)S(1)} %collective-permute-done.17.refs_9_), channel_id=1, source_target_pairs={{0,96},{1,97},{2,98},{3,99},{4,28},{5,29},{6,30},{7,31},{8,104},{9... | collective-permute-start | bytes 786440 | tf_op jit(solution)/shard_map/ppermute | solution.py:39
  107.9 3.3 %collective-permute-start.23 = (bf16[256,512]{1,0:T(8,128)(2,1)S(1)}, bf16[256,512]{1,0:T(8,128)(2,1)S(1)}, u32[]{:S(2)}, u32[]{:S(2)}) collective-permute-start(bf16[256,512]{1,0:T(8,128)(2,1)S(1)} %shard_map.52.refs_0_), channel_id=1, source_target_pairs={{0,4},{1,5},{2,6},{3,7},{4,0},{5,1},{6,2},{7,3},{8,12},{9,13},{10,... | collective-permute-start | bytes 786440 | tf_op jit(solution)/shard_map/ppermute | solution.py:31
  115.1 17.0 %collective-permute-start.33 = (bf16[2048,512]{1,0:T(8,128)(2,1)S(1)}, bf16[2048,512]{1,0:T(8,128)(2,1)S(1)}, u32[]{:S(2)}, u32[]{:S(2)}) collective-permute-start(bf16[2048,512]{1,0:T(8,128)(2,1)S(1)} %get-tuple-element.84), channel_id=1, source_target_pairs={{0,4},{1,5},{2,6},{3,7},{4,0},{5,1},{6,2},{7,3},{8,12},{9,13},{10,... | collective-permute-start | bytes 6291464 | tf_op jit(solution)/shard_map/ppermute | solution.py:31
  116.0 9.5 %collective-permute-start.32 = (bf16[256,512]{1,0:T(8,128)(2,1)S(1)}, bf16[256,512]{1,0:T(8,128)(2,1)S(1)}, u32[]{:S(2)}, u32[]{:S(2)}) collective-permute-start(bf16[256,512]{1,0:T(8,128)(2,1)S(1)} %get-tuple-element.81.own0), channel_id=1, source_target_pairs={{0,1},{1,2},{2,3},{3,0},{4,5},{5,6},{6,7},{7,4},{8,9},{9,10},{10,1... | collective-permute-start | bytes 786440 | tf_op jit(solution)/shard_map/ppermute | solution.py:35
  116.2 15.9 %collective-permute-start.31 = (bf16[256,512]{1,0:T(8,128)(2,1)S(1)}, bf16[256,512]{1,0:T(8,128)(2,1)S(1)}, u32[]{:S(2)}, u32[]{:S(2)}) collective-permute-start(bf16[256,512]{1,0:T(8,128)(2,1)S(1)} %get-tuple-element.81.own0), channel_id=1, source_target_pairs={{0,2},{1,3},{2,0},{3,1},{4,6},{5,7},{6,4},{7,5},{8,10},{9,11},{10,... | collective-permute-start | bytes 786440 | tf_op jit(solution)/shard_map/ppermute | solution.py:35
  120.2 11.9 %collective-permute-start.30 = (bf16[256,512]{1,0:T(8,128)(2,1)S(1)}, bf16[256,512]{1,0:T(8,128)(2,1)S(1)}, u32[]{:S(2)}, u32[]{:S(2)}) collective-permute-start(bf16[256,512]{1,0:T(8,128)(2,1)S(1)} %get-tuple-element.81.own0), channel_id=1, source_target_pairs={{0,3},{1,0},{2,1},{3,2},{4,7},{5,4},{6,5},{7,6},{8,11},{9,8},{10,9... | collective-permute-start | bytes 786440 | tf_op jit(solution)/shard_map/ppermute | solution.py:35
  133.3 2.6 %collective-permute-start.34 = (f32[128,1024]{1,0:T(8,128)S(1)}, f32[128,1024]{1,0:T(8,128)S(1)}, u32[]{:S(2)}, u32[]{:S(2)}) collective-permute-start(f32[128,1024]{1,0:T(8,128)S(1)} %shard_map.57), channel_id=1, source_target_pairs={{0,4},{1,5},{2,6},{3,7},{4,0},{5,1},{6,2},{7,3},{8,12},{9,13},{10,... | collective-permute-start | bytes 1572872 | tf_op jit(solution)/shard_map/ppermute | solution.py:31

commit v5 on v3

--- a/solution.py
+++ b/solution.py
@@ -150,7 +150,7 @@
     some_columns(where, keep_d, 1, {0: other0, 1: other1, 3: other3}, {2: own2}, panel)
 
 
-def first_square(where, keep_d, keep_s, own0, own1, own2, own3, other2, rows, some, _, __, panel, line, low, square, total):
+def first_square(where, keep_d, keep_s, own0, own1, own2, own3, other2, rows, some, _, __, panel, line, low, total):
     x, y, core, z = where[0], where[1], where[2], where[3]
     some_rows(where, keep_d, rows, 1, {2: other2}, line)
     some_columns(where, keep_d, 1, {2: other2}, {0: own0, 1: own1, 2: own2, 3: own3}, panel)
@@ -172,8 +172,6 @@
             + dot(line[:, 3072:3584], panel[3072:3584, at]), part)
 
     put(dot(line[...], panel[:, 1024:1536]), 2)
-    for t in range(4):
-        square[:, t * B:(t + 1) * B] = total[:, aligned(column_at(where, t), B)]
 
 
 def column_at(where, t):
@@ -191,46 +189,58 @@
 
 def first_density(where, keep_d, its, columns, early, square, out):
     x, y, core, z = where[0], where[1], where[2], where[3]
-    value = 3.0 * square[...] - 2.0 * (early[...] + dot(its[...], columns[2048:, :]))
-    for t in range(2):
-        for u in range(4):
+    cube = early[...] + dot(its[...], columns[2048:, :])
+    for u in range(4):
+        value = 3.0 * square[:, aligned(column_at(where, u), B)] - 2.0 * cube[:, u * B:(u + 1) * B]
+        for t in range(2):
             keep = keep_d[1, (x * 4 + y) * 2 + t, z * 8 + u * 2 + core].astype(jnp.float32)
-            piece = value[t * B:(t + 1) * B, u * B:(u + 1) * B] * keep
+            piece = value[t * B:(t + 1) * B, :] * keep
             out[t * B:(t + 1) * B, u * B:(u + 1) * B] = piece.astype(jnp.bfloat16)
 
 
-def chips_times(where, line, chips, mine, its):
+def density_rows(where, keep_d, low, its, panel, square, out):
+    x, y, core = where[0], where[1], where[2]
+
+    @pl.loop(0, 4)
+    def _(part):
+        at = aligned(part, 512)
+        cube = dot(low[...], panel[:2048, at]) + dot(its[...], panel[2048:, at])
+        value = 3.0 * square[:, at] - 2.0 * cube
+        for t in range(2):
+            for u in range(4):
+                keep = keep_d[1, (x * 4 + y) * 2 + t, block_at(x, y, core, part * 4 + u)].astype(jnp.float32)
+                piece = value[t * B:(t + 1) * B, u * B:(u + 1) * B] * keep
+                out[t * B:(t + 1) * B, aligned(part * 4 + u, B)] = piece.astype(jnp.bfloat16)
+
+
+def chips_times(where, own, other, chips, mine, its):
     x, y, core = where[0], where[1], where[2]
     left, right = [], []
     for ref, offset, first, second in chips:
         px, py = place(x, y, core, first, second)
         chip = px * 4 + py
-        mine[aligned(chip, B), :] = ref[pl.ds(pl.multiple_of(offset + core * B, B), B), :]
-        its[aligned(chip, B), :] = ref[pl.ds(pl.multiple_of(offset + (1 - core) * B, B), B), :]
-        left.append(line[:, aligned(chip, ROWS)])
-        right.append(ref[offset:offset + ROWS, :])
+        for kind, line, at, to in ((core, own, second * 4 + first, mine), (1 - core, other, first * 4 + second, its)):
+            block = ref[pl.ds(pl.multiple_of(offset + kind * B, B), B), :]
+            to[aligned(chip, B), :] = block
+            left.append(line[:, at * B:(at + 1) * B])
+            right.append(block)
     total = None
-    for n in range(0, len(chips), 4):
-        term = dot(jnp.concatenate(left[n:n + 4], axis=1), jnp.concatenate(right[n:n + 4], axis=0))
+    for n in range(0, len(left), 8):
+        term = dot(jnp.concatenate(left[n:n + 8], axis=1), jnp.concatenate(right[n:n + 8], axis=0))
         total = term if total is None else total + term
     return total
 
 
-def early_square(where, *refs):
-    own, other, near, far, (early, line, mine, its) = refs[:4], refs[4:8], refs[8], refs[9:13], refs[13:]
-    core, z = where[2], where[3]
-    for d in range(4):
-        for ref, kind in ((own[d], core), (other[d], 1 - core)):
-            for t in range(4):
-                line[:, aligned(((z + d) & 3) * 8 + t * 2 + kind, B)] = ref[:, t * B:(t + 1) * B]
-    chips = [(near, i * ROWS, i, 0) for i in range(4)] + [(far[i], 0, i, 2) for i in range(4)]
-    early[...] = chips_times(where, line, chips, mine, its)
-
-
-def second_square(where, keep_s, one, three, early, line, _, __, square, low, mine, its):
+def early_square(where, own, other, near, far0, far1, far2, far3, early, mine, its):
+    chips = [(near, i * ROWS, i, 0) for i in range(4)]
+    chips += [(ref, 0, i, 2) for i, ref in enumerate((far0, far1, far2, far3))]
+    early[...] = chips_times(where, own, other, chips, mine, its)
+
+
+def second_square(where, keep_s, own, other, one, three, early, _, __, square, low, mine, its):
     x, y, core, z = where[0], where[1], where[2], where[3]
     chips = [(ref, i * ROWS, i, j) for ref, j in ((one, 1), (three, 3)) for i in range(4)]
-    value = early[...] + chips_times(where, line, chips, mine, its)
+    value = early[...] + chips_times(where, own, other, chips, mine, its)
     for t in range(2):
         for u in range(4):
             keep = keep_s[1, (x * 4 + y) * 2 + t, z * 8 + u * 2 + core].astype(jnp.float32)
@@ -330,8 +340,8 @@
     panel, line, low, square = call(
         first_square, 3,
         [where, keep_density, keep_square, own0, own1, own2, own3, other2, rows, some, panel, line],
-        out_shapes + [jax.ShapeDtypeStruct((ROWS, N // 2), jnp.bfloat16), full_block],
-        [pltpu.VMEM((ROWS, N // 2), jnp.float32)],
+        out_shapes + [jax.ShapeDtypeStruct((ROWS, N // 2), jnp.bfloat16), jax.ShapeDtypeStruct((ROWS, N // 2), jnp.float32)],
+        [],
         4 * pair_flops + 2 * block_flops, 20 * MIB, {10: 0, 11: 1})
 
     its = other_core(low)
@@ -341,21 +351,23 @@
         first_density, 2, [where, keep_density, its, columns, early, square], [low_block], [],
         block_flops // 2, 4 * MIB)
 
-    own0, one, three, two, far = lax.optimization_barrier((
-        current, from_first(current, 1), from_first(current, 3), from_first(current, 2), from_second(current, 2)))
-    near = jnp.concatenate([own0, one, two, three], axis=0)
+    (own,) = call(
+        density_rows, 2, [where, keep_density, low, its, panel, square],
+        [jax.ShapeDtypeStruct((ROWS, N // 2), jnp.bfloat16)], [], 4 * block_flops, 22 * MIB)
+    start, one, three, two, far, other = lax.optimization_barrier((
+        current, from_first(current, 1), from_first(current, 3), from_first(current, 2), from_second(current, 2),
+        other_core(own)))
+    near = jnp.concatenate([start, one, two, three], axis=0)
     one, three = from_second(near, 1), from_second(near, 3)
-    far, *own = lax.optimization_barrier((far, *gather(current, from_z)[1:]))
-    far, own = gather(far, from_first), [own0, *own]
-    other = [other_core(part) for part in own]
+    far = gather(far, from_first)
     half_shape = jax.ShapeDtypeStruct((N // 2, COLS), jnp.bfloat16)
-    early, line, mine, its = call(
-        early_square, 1, [where, *own, *other, near, *far], [full_block, line_shape, half_shape, half_shape],
+    early, mine, its = call(
+        early_square, 1, [where, own, other, near, *far], [full_block, half_shape, half_shape],
         [], block_flops // 2, 10 * MIB)
     square, low, mine, its = call(
-        second_square, 2, [where, keep_square, one, three, early, line, mine, its],
+        second_square, 2, [where, keep_square, own, other, one, three, early, mine, its],
         [full_block, low_block, half_shape, half_shape],
-        [], block_flops // 2, 8 * MIB, {6: 2, 7: 3})
+        [], block_flops // 2, 8 * MIB, {7: 2, 8: 3})
 
     own0, own1, own2, own3 = gather(low, from_z)
     come = other_core(its)

time: 137 us -> 144 us (1.051)
  Pallas kernels: 41.8 us -> 47.4 us
  waiting for transfers between devices: 48.7 us -> 53.7 us
  starting transfers between devices: 44.5 us -> 40.1 us
    ppermute x9, waiting for transfers between devices: 17.6 us -> 23.5 us  [from_first(): lax.ppermute(a, AXES, pairs(lambda x, y, core, z: (x - d, y, core, z) if...]
    pallas_call x12 -> x13, Pallas kernels: 41.8 us -> 47.4 us  [call(): pl.pallas_call(kernel, in_specs=[SMEM] * n_smem + [VMEM] * (len(ins) - n_...]
    ppermute x9 -> x6, waiting for transfers between devices: 18.4 us -> 14.7 us  [from_z(): lax.ppermute(a, AXES, pairs(lambda x, y, core, z: (x, y, core, z - d)))]
    ppermute x9 -> x6, starting transfers between devices: 12.1 us -> 8.58 us  [from_z(): lax.ppermute(a, AXES, pairs(lambda x, y, core, z: (x, y, core, z - d)))]
    ppermute x11 -> x8, starting transfers between devices: 9.54 us -> 7.04 us  [other_core(): lax.ppermute(a, AXES, pairs(lambda x, y, core, z: (x, y, 1 - core, z)))]
    ppermute x9, starting transfers between devices: 11.8 us -> 13.4 us  [from_first(): lax.ppermute(a, AXES, pairs(lambda x, y, core, z: (x - d, y, core, z) if...]
    ppermute x6, waiting for transfers between devices: 9.73 us -> 11.2 us  [from_second(): lax.ppermute(a, AXES, pairs(lambda x, y, core, z: (x, y - d, core, z) if...]
    ppermute x11 -> x8, waiting for transfers between devices: 2.95 us -> 4.19 us  [other_core(): lax.ppermute(a, AXES, pairs(lambda x, y, core, z: (x, y, 1 - core, z)))]
  transfers between devices with their start and end apart: 35 -> 29, of which waited for: 19 -> 17; matrix products, arithmetic and copies ran while one was open for 1% -> 1% of each run, Pallas kernels for 21% -> 21%
where the time goes in v5:
time: 144 us; the launch traced here: 143 us
  waiting for transfers between devices  53.7 us (37%)
  Pallas kernels  47.4 us (33%)
  starting transfers between devices  40.1 us (28%)
    pallas_call x13, Pallas kernels, call(): pl.pallas_call(kernel, in_specs=[SMEM] * n_smem + [VMEM] * (len(ins) - n_...  47.4 us
    ppermute x9, waiting for transfers between devices, from_first(): lax.ppermute(a, AXES, pairs(lambda x, y, core, z: (x - d, y, core, z) if...  23.5 us
    ppermute x6, waiting for transfers between devices, from_z(): lax.ppermute(a, AXES, pairs(lambda x, y, core, z: (x, y, core, z - d)))  14.7 us
    ppermute x9, starting transfers between devices, from_first(): lax.ppermute(a, AXES, pairs(lambda x, y, core, z: (x - d, y, core, z) if...  13.4 us
    ppermute x6, waiting for transfers between devices, from_second(): lax.ppermute(a, AXES, pairs(lambda x, y, core, z: (x, y - d, core, z) if...  11.2 us
    ppermute x6, starting transfers between devices, from_second(): lax.ppermute(a, AXES, pairs(lambda x, y, core, z: (x, y - d, core, z) if...  11.1 us
    ppermute x6, starting transfers between devices, from_z(): lax.ppermute(a, AXES, pairs(lambda x, y, core, z: (x, y, core, z - d)))  8.58 us
    ppermute x8, starting transfers between devices, other_core(): lax.ppermute(a, AXES, pairs(lambda x, y, core, z: (x, y, 1 - core, z)))  7.04 us
  transfers between devices with their start and end apart: 29, of which 17 were waited for; matrix products, arithmetic and copies ran while one was open for 1% of the time, Pallas kernels for 21%

profile of v5, /device:TPU:1, one launch (start us, length us, event | category | flops | bytes accessed | tf_op | source)
XLA Modules:
  0.0 143.3 jit_solution(9184795029651805886)
XLA Ops:
  0.0 4.4 %collective-permute-start.1 = (bf16[128,256]{1,0:T(8,128)(2,1)}, bf16[128,256]{1,0:T(8,128)(2,1)S(1)}, u32[]{:S(2)}, u32[]{:S(2)}) collective-permute-start(bf16[128,256]{1,0:T(8,128)(2,1)} %param.4), channel_id=1, source_target_pairs={{0,2},{1,3},{2,0},{3,1},{4,6},{5,7},{6,4},{7,5},{8,10},{9,11},{10,... | collective-permute-start | bytes 196616 | tf_op jit(solution)/shard_map/ppermute | solution.py:33
  4.9 1.0 collective-permute-start.2
  6.7 1.4 %collective-permute-done = bf16[128,256]{1,0:T(8,128)(2,1)S(1)} collective-permute-done((bf16[128,256]{1,0:T(8,128)(2,1)}, bf16[128,256]{1,0:T(8,128)(2,1)S(1)}, u32[]{:S(2)}, u32[]{:S(2)}) %collective-permute-start) | collective-permute-done | bytes 65568 | tf_op jit(solution)/shard_map/ppermute | solution.py:33
  8.1 1.3 collective-permute-done.2
  9.4 0.9 maximum_multiply_fusion
  10.3 1.4 collective-permute-start.5
  11.7 2.6 %collective-permute-start.4 = (bf16[128,1024]{1,0:T(8,128)(2,1)S(1)}, bf16[128,1024]{1,0:T(8,128)(2,1)S(1)}, u32[]{:S(2)}, u32[]{:S(2)}) collective-permute-start(bf16[128,1024]{1,0:T(8,128)(2,1)S(1)} %maximum_multiply_fusion), channel_id=1, source_target_pairs={{0,64},{1,65},{2,66},{3,67},{4,20},{5,21},{6,22},{7,23},{8,72},{9,... | collective-permute-start | bytes 786440 | tf_op jit(solution)/shard_map/ppermute | solution.py:37
  14.3 1.1 collective-permute-start.3
  15.4 1.8 %collective-permute-done.5 = bf16[128,1024]{1,0:T(8,128)(2,1)S(1)} collective-permute-done((bf16[128,1024]{1,0:T(8,128)(2,1)S(1)}, bf16[128,1024]{1,0:T(8,128)(2,1)S(1)}, u32[]{:S(2)}, u32[]{:S(2)}) %collective-permute-start.5) | collective-permute-done | bytes 262176 | tf_op jit(solution)/shard_map/ppermute | solution.py:37
  17.2 4.0 %collective-permute-done.4 = bf16[128,1024]{1,0:T(8,128)(2,1)S(1)} collective-permute-done((bf16[128,1024]{1,0:T(8,128)(2,1)S(1)}, bf16[128,1024]{1,0:T(8,128)(2,1)S(1)}, u32[]{:S(2)}, u32[]{:S(2)}) %collective-permute-start.4) | collective-permute-done | bytes 262176 | tf_op jit(solution)/shard_map/ppermute | solution.py:37
  21.2 3.1 %collective-permute-start.6 = (bf16[512,1024]{1,0:T(8,128)(2,1)S(1)}, bf16[512,1024]{1,0:T(8,128)(2,1)}, u32[]{:S(2)}, u32[]{:S(2)}) collective-permute-start(bf16[512,1024]{1,0:T(8,128)(2,1)S(1)} %pad_maximum_fusion.own0), channel_id=1, source_target_pairs={{0,4},{1,5},{2,6},{3,7},{4,0},{5,1},{6,2},{7,3},{8,12},{9,13},{10,... | collective-permute-start | bytes 3145736 | tf_op jit(solution)/shard_map/ppermute | solution.py:29
  24.3 1.6 %collective-permute-start.8 = (bf16[512,1024]{1,0:T(8,128)(2,1)S(1)}, bf16[512,1024]{1,0:T(8,128)(2,1)S(1)}, u32[]{:S(2)}, u32[]{:S(2)}) collective-permute-start(bf16[512,1024]{1,0:T(8,128)(2,1)S(1)} %pad_maximum_fusion.own0), channel_id=1, source_target_pairs={{0,8},{1,9},{2,10},{3,11},{4,36},{5,37},{6,38},{7,39},{8,16},{9,17... | collective-permute-start | bytes 3145736 | tf_op jit(solution)/shard_map/ppermute | solution.py:42
  25.9 1.1 collective-permute-start.7
  27.0 3.1 %shard_map.46 = (bf16[4096,2048]{1,0:T(8,128)(2,1)S(1)}, bf16[256,4096]{1,0:T(8,128)(2,1)S(1)}, bf16[256,1024]{1,0:T(8,128)(2,1)S(1)}) custom-call(s32[4]{0:T(128)S(1)} %pad_add_fusion.1.where, s32[2,32,32]{2,1,0:T(8,128)S(1)} %copy-done.1, bf16[512,1024]{1,0:T(8,128)(2,1)S(1)} %pad_maximum_fusion.own0, bf16[512,1024]{1,0:T(8,128)(2,1)} %collective-permute-done.6.other0), custom_call_target="tpu_custom_call" | custom-call | flops 67108864 | bytes 1048576 | tf_op jit(solution)/shard_map/pallas_call | solution.py:291
  30.1 9.3 %collective-permute-done.8.own3 = bf16[512,1024]{1,0:T(8,128)(2,1)S(1)} collective-permute-done((bf16[512,1024]{1,0:T(8,128)(2,1)S(1)}, bf16[512,1024]{1,0:T(8,128)(2,1)S(1)}, u32[]{:S(2)}, u32[]{:S(2)}) %collective-permute-start.8) | collective-permute-done | bytes 1048608 | tf_op jit(solution)/shard_map/ppermute | solution.py:42
  39.8 0.9 collective-permute-start.9
  40.7 2.7 %collective-permute-start.11 = (bf16[512,1024]{1,0:T(8,128)(2,1)S(1)}, bf16[512,1024]{1,0:T(8,128)(2,1)S(1)}, u32[]{:S(2)}, u32[]{:S(2)}) collective-permute-start(bf16[512,1024]{1,0:T(8,128)(2,1)S(1)} %pad_maximum_fusion.own0), channel_id=1, source_target_pairs={{0,16},{1,17},{2,18},{3,19},{4,68},{5,69},{6,70},{7,71},{8,24},{9,... | collective-permute-start | bytes 3145736 | tf_op jit(solution)/shard_map/ppermute | solution.py:42
  43.4 5.9 %shard_map.47 = (bf16[4096,2048]{1,0:T(8,128)(2,1)S(1)}, bf16[256,4096]{1,0:T(8,128)(2,1)S(1)}) custom-call(s32[4]{0:T(128)S(1)} %pad_add_fusion.1.where, s32[2,32,32]{2,1,0:T(8,128)S(1)} %copy-done.1, bf16[512,1024]{1,0:T(8,128)(2,1)S(1)} %pad_maximum_fusion.own0, ...), custom_call_target="tpu_custom_call", output_to_operand_aliasing={{0}: (7, {}), {1}: (8, {})} | custom-call | flops 5905580032 | bytes 8388608 | tf_op jit(solution)/shard_map/pallas_call | solution.py:291
  49.4 8.0 %shard_map.48 = (bf16[4096,2048]{1,0:T(8,128)(2,1)S(1)}, bf16[256,4096]{1,0:T(8,128)(2,1)S(1)}, f32[256,2048]{1,0:T(8,128)S(1)}) custom-call(s32[4]{0:T(128)S(1)} %pad_add_fusion.1.where, s32[2,32,32]{2,1,0:T(8,128)S(1)} %copy-done.1, bf16[512,1024]{1,0:T(8,128)(2,1)S(1)} %pad_maximum_fusion.own0, ...), custom_call_target="tpu_custom_call", output_to_operand_aliasing={{0}: (8, {}), {1}: (9, {})} | custom-call | flops 5905580032 | bytes 8388608 | tf_op jit(solution)/shard_map/pallas_call | solution.py:291
  57.4 1.0 collective-permute-start.12
  58.5 5.7 %shard_map.49 = (bf16[4096,2048]{1,0:T(8,128)(2,1)S(1)}, bf16[256,4096]{1,0:T(8,128)(2,1)S(1)}) custom-call(s32[4]{0:T(128)S(1)} %pad_add_fusion.1.where, s32[2,32,32]{2,1,0:T(8,128)S(1)} %copy-done.1, bf16[512,1024]{1,0:T(8,128)(2,1)S(1)} %pad_maximum_fusion.own0, ...), custom_call_target="tpu_custom_call", output_to_operand_aliasing={{0}: (10, {}), {1}: (11, {})} | custom-call | flops 5368709120 | bytes 8388608 | tf_op jit(solution)/shard_map/pallas_call | solution.py:291
  64.2 7.0 %shard_map.50 = (bf16[4096,2048]{1,0:T(8,128)(2,1)S(1)}, bf16[256,4096]{1,0:T(8,128)(2,1)S(1)}, bf16[256,2048]{1,0:T(8,128)(2,1)S(1)}, f32[256,2048]{1,0:T(8,128)S(1)}) custom-call(s32[4]{0:T(128)S(1)} %pad_add_fusion.1.where, s32[2,32,32]{2,1,0:T(8,128)S(1)} %copy-done.1, ...), custom_call_target="tpu_custom_call", output_to_operand_aliasing={{0}: (10, {}), {1}: (11, {})} | custom-call | flops 4294967296 | bytes 20971520 | tf_op jit(solution)/shard_map/pallas_call | solution.py:291
  71.3 2.6 %collective-permute-done.13.its = bf16[256,2048]{1,0:T(8,128)(2,1)S(1)} collective-permute-done((bf16[256,2048]{1,0:T(8,128)(2,1)S(1)}, bf16[256,2048]{1,0:T(8,128)(2,1)S(1)}, u32[]{:S(2)}, u32[]{:S(2)}) %collective-permute-start.13) | collective-permute-done | bytes 1048608 | tf_op jit(solution)/shard_map/ppermute | solution.py:29
  74.0 6.3 %shard_map.51.own = bf16[256,2048]{1,0:T(8,128)(2,1)S(1)} custom-call(s32[4]{0:T(128)S(1)} %pad_add_fusion.1.where, s32[2,32,32]{2,1,0:T(8,128)S(1)} %copy-done.1, bf16[256,2048]{1,0:T(8,128)(2,1)S(1)} %get-tuple-element.61.low, bf16[256,2048]{1,0:T(8,128)(2,1)S(1)} %collective-permute-done.13.its, bf16[4096,2048]{1,0:T(8,128)(2,1)S(1)} %get-tuple-element.62.panel, ...), custom_call_target="tpu_custom_call" | custom-call | flops 4294967296 | bytes 23068672 | tf_op jit(solution)/shard_map/pallas_call | solution.py:291
  80.5 2.3 %shard_map.52 = (f32[256,512]{1,0:T(8,128)S(1)}, bf16[4096,512]{1,0:T(8,128)(2,1)S(1)}) custom-call(s32[4]{0:T(128)S(1)} %pad_add_fusion.1.where, bf16[256,2048]{1,0:T(8,128)(2,1)S(1)} %get-tuple-element.61.low, bf16[4096,2048]{1,0:T(8,128)(2,1)S(1)} %get-tuple-element.62.panel), custom_call_target="tpu_custom_call" | custom-call | flops 536870912 | bytes 12582912 | tf_op jit(solution)/shard_map/pallas_call | solution.py:291
  82.7 1.8 %shard_map.53 = bf16[256,512]{1,0:T(8,128)(2,1)S(1)} custom-call(s32[4]{0:T(128)S(1)} %pad_add_fusion.1.where, s32[2,32,32]{2,1,0:T(8,128)S(1)} %copy-done.1, bf16[256,2048]{1,0:T(8,128)(2,1)S(1)} %collective-permute-done.13.its, bf16[4096,512]{1,0:T(8,128)(2,1)S(1)} %get-tuple-element.64.columns, f32[256,512]{1,0:T(8,128)S(1)} %get-tuple-element.65.early, ...), custom_call_target="tpu_custom_call" | custom-call | flops 536870912 | bytes 4194304 | tf_op jit(solution)/shard_map/pallas_call | solution.py:291
  84.6 2.7 %collective-permute-start.17 = (bf16[256,512]{1,0:T(8,128)(2,1)S(1)}, bf16[256,512]{1,0:T(8,128)(2,1)S(1)}, u32[]{:S(2)}, u32[]{:S(2)}) collective-permute-start(bf16[256,512]{1,0:T(8,128)(2,1)S(1)} %shard_map.53), channel_id=1, source_target_pairs={{0,16},{1,17},{2,18},{3,19},{4,68},{5,69},{6,70},{7,71},{8,24},{9,... | collective-permute-start | bytes 786440 | tf_op jit(solution)/shard_map/ppermute | solution.py:42
  87.3 1.6 %collective-permute-start.16 = (bf16[256,512]{1,0:T(8,128)(2,1)S(1)}, bf16[256,512]{1,0:T(8,128)(2,1)S(1)}, u32[]{:S(2)}, u32[]{:S(2)}) collective-permute-start(bf16[256,512]{1,0:T(8,128)(2,1)S(1)} %shard_map.53), channel_id=1, source_target_pairs={{0,64},{1,65},{2,66},{3,67},{4,20},{5,21},{6,22},{7,23},{8,72},{9,... | collective-permute-start | bytes 786440 | tf_op jit(solution)/shard_map/ppermute | solution.py:37
  89.5 2.1 %collective-permute-start.14 = (bf16[256,512]{1,0:T(8,128)(2,1)S(1)}, bf16[256,512]{1,0:T(8,128)(2,1)S(1)}, u32[]{:S(2)}, u32[]{:S(2)}) collective-permute-start(bf16[256,512]{1,0:T(8,128)(2,1)S(1)} %shard_map.53), channel_id=1, source_target_pairs={{0,96},{1,97},{2,98},{3,99},{4,28},{5,29},{6,30},{7,31},{8,104},{9... | collective-permute-start | bytes 786440 | tf_op jit(solution)/shard_map/ppermute | solution.py:37
  91.7 3.3 %collective-permute-done.16 = bf16[256,512]{1,0:T(8,128)(2,1)S(1)} collective-permute-done((bf16[256,512]{1,0:T(8,128)(2,1)S(1)}, bf16[256,512]{1,0:T(8,128)(2,1)S(1)}, u32[]{:S(2)}, u32[]{:S(2)}) %collective-permute-start.16) | collective-permute-done | bytes 262176 | tf_op jit(solution)/shard_map/ppermute | solution.py:37
  95.0 2.7 %collective-permute-done.15 = bf16[256,512]{1,0:T(8,128)(2,1)S(1)} collective-permute-done((bf16[256,512]{1,0:T(8,128)(2,1)S(1)}, bf16[256,512]{1,0:T(8,128)(2,1)S(1)}, u32[]{:S(2)}, u32[]{:S(2)}) %collective-permute-start.15) | collective-permute-done | bytes 262176 | tf_op jit(solution)/shard_map/ppermute | solution.py:37
  97.8 2.0 %collective-permute-start.20 = (bf16[1024,512]{1,0:T(8,128)(2,1)S(1)}, bf16[1024,512]{1,0:T(8,128)(2,1)S(1)}, u32[]{:S(2)}, u32[]{:S(2)}) collective-permute-start(bf16[1024,512]{1,0:T(8,128)(2,1)S(1)} %constant_dynamic-update-slice_fusion.near), channel_id=1, source_target_pairs={{0,8},{1,9},{2,10},{3,11},{4,36},{5,37},{6,38},{7,39},{8,16},{9,17... | collective-permute-start | bytes 3145736 | tf_op jit(solution)/shard_map/ppermute | solution.py:42
  99.8 1.0 collective-permute-start.19
  101.5 2.5 %collective-permute-start.22 = (bf16[256,512]{1,0:T(8,128)(2,1)S(1)}, bf16[256,512]{1,0:T(8,128)(2,1)S(1)}, u32[]{:S(2)}, u32[]{:S(2)}) collective-permute-start(bf16[256,512]{1,0:T(8,128)(2,1)S(1)} %collective-permute-done.17.far0), channel_id=1, source_target_pairs={{0,64},{1,65},{2,66},{3,67},{4,20},{5,21},{6,22},{7,23},{8,72},{9,... | collective-permute-start | bytes 786440 | tf_op jit(solution)/shard_map/ppermute | solution.py:37
  104.0 0.9 collective-permute-start.21
  104.9 5.5 %collective-permute-done.23.far3 = bf16[256,512]{1,0:T(8,128)(2,1)S(1)} collective-permute-done((bf16[256,512]{1,0:T(8,128)(2,1)S(1)}, bf16[256,512]{1,0:T(8,128)(2,1)S(1)}, u32[]{:S(2)}, u32[]{:S(2)}) %collective-permute-start.23) | collective-permute-done | bytes 262176 | tf_op jit(solution)/shard_map/ppermute | solution.py:37
  110.4 6.1 %collective-permute-done.22.far2 = bf16[256,512]{1,0:T(8,128)(2,1)S(1)} collective-permute-done((bf16[256,512]{1,0:T(8,128)(2,1)S(1)}, bf16[256,512]{1,0:T(8,128)(2,1)S(1)}, u32[]{:S(2)}, u32[]{:S(2)}) %collective-permute-start.22) | collective-permute-done | bytes 262176 | tf_op jit(solution)/shard_map/ppermute | solution.py:37
  116.6 1.4 shard_map.54
  118.0 0.9 collective-permute-done.20.three
  119.4 1.9 %shard_map.55 = (f32[256,512]{1,0:T(8,128)S(1)}, bf16[256,512]{1,0:T(8,128)(2,1)S(1)}, bf16[2048,512]{1,0:T(8,128)(2,1)S(1)}, bf16[2048,512]{1,0:T(8,128)(2,1)S(1)}) custom-call(s32[4]{0:T(128)S(1)} %pad_add_fusion.1.where, s32[2,32,32]{2,1,0:T(8,128)S(1)} %copy-done.2, ...), custom_call_target="tpu_custom_call", output_to_operand_aliasing={{2}: (7, {}), {3}: (8, {})} | custom-call | flops 536870912 | bytes 8388608 | tf_op jit(solution)/shard_map/pallas_call | solution.py:291
  121.3 0.8 collective-permute-start.26
  122.1 2.7 %collective-permute-start.24 = (bf16[256,512]{1,0:T(8,128)(2,1)S(1)}, bf16[256,512]{1,0:T(8,128)(2,1)S(1)}, u32[]{:S(2)}, u32[]{:S(2)}) collective-permute-start(bf16[256,512]{1,0:T(8,128)(2,1)S(1)} %get-tuple-element.75.own0), channel_id=1, source_target_pairs={{0,3},{1,0},{2,1},{3,2},{4,7},{5,4},{6,5},{7,6},{8,11},{9,8},{10,9... | collective-permute-start | bytes 786440 | tf_op jit(solution)/shard_map/ppermute | solution.py:33
  124.8 12.0 %collective-permute-done.25.own3 = bf16[256,512]{1,0:T(8,128)(2,1)S(1)} collective-permute-done((bf16[256,512]{1,0:T(8,128)(2,1)S(1)}, bf16[256,512]{1,0:T(8,128)(2,1)S(1)}, u32[]{:S(2)}, u32[]{:S(2)}) %collective-permute-start.25) | collective-permute-done | bytes 262176 | tf_op jit(solution)/shard_map/ppermute | solution.py:33
  136.8 1.5 %shard_map.56.early = f32[256,1024]{1,0:T(8,128)S(1)} custom-call(s32[4]{0:T(128)S(1)} %pad_add_fusion.1.where, bf16[256,512]{1,0:T(8,128)(2,1)S(1)} %get-tuple-element.75.own0, bf16[256,512]{1,0:T(8,128)(2,1)S(1)} %collective-permute-done.24.own1, bf16[256,512]{1,0:T(8,128)(2,1)S(1)} %collective-permute-done.25.own3, ...), custom_call_target="tpu_custom_call" | custom-call | flops 805306368 | bytes 4194304 | tf_op jit(solution)/shard_map/pallas_call | solution.py:291
  138.3 0.9 shard_map.57
  139.2 0.9 collective-permute-start.28
  140.1 1.5 %collective-permute-done.28.share = f32[128,1024]{1,0:T(8,128)S(1)} collective-permute-done((f32[128,1024]{1,0:T(8,128)S(1)}, f32[128,1024]{1,0:T(8,128)S(1)}, u32[]{:S(2)}, u32[]{:S(2)}) %collective-permute-start.28) | collective-permute-done | bytes 524320 | tf_op jit(solution)/shard_map/ppermute | solution.py:29
  141.6 1.7 %shard_map.58 = f32[128,1024]{1,0:T(8,128)} custom-call(s32[4]{0:T(128)S(1)} %pad_add_fusion.1.where, bf16[256,512]{1,0:T(8,128)(2,1)S(1)} %collective-permute-done.27.own2, f32[256,1024]{1,0:T(8,128)S(1)} %shard_map.56.early, f32[256,512]{1,0:T(8,128)S(1)} %get-tuple-element.80.square, bf16[2048,512]{1,0:T(8,128)(2,1)S(1)} %get-tuple-element.76.mine, ...), custom_call_target="tpu_custom_call" | custom-call | flops 134217728 | bytes 3145728 | tf_op jit(solution)/shard_map/pallas_call | solution.py:291
  (44 shorter events, 4.1 us)
Async XLA Ops:
  0.0 5.9 %copy-start = (s32[32,8]{0,1:T(8,128)S(1)}, s32[32,8]{0,1:T(8,128)}, u32[]{:S(2)}) copy-start(s32[32,8]{0,1:T(8,128)} %param.5) | copy-start | bytes 3076
  0.0 27.0 %copy-start.1 = (s32[2,32,32]{2,1,0:T(8,128)S(1)}, s32[2,32,32]{2,1,0:T(8,128)}, u32[]{:S(2)}) copy-start(s32[2,32,32]{2,1,0:T(8,128)} %keep_d.13) | copy-start | bytes 24580
  0.0 6.7 %collective-permute-start.1 = (bf16[128,256]{1,0:T(8,128)(2,1)}, bf16[128,256]{1,0:T(8,128)(2,1)S(1)}, u32[]{:S(2)}, u32[]{:S(2)}) collective-permute-start(bf16[128,256]{1,0:T(8,128)(2,1)} %param.4), channel_id=1, source_target_pairs={{0,2},{1,3},{2,0},{3,1},{4,6},{5,7},{6,4},{7,5},{8,10},{9,11},{10,... | collective-permute-start | bytes 196616 | tf_op jit(solution)/shard_map/ppermute | solution.py:33
  4.4 3.7 %collective-permute-start = (bf16[128,256]{1,0:T(8,128)(2,1)}, bf16[128,256]{1,0:T(8,128)(2,1)S(1)}, u32[]{:S(2)}, u32[]{:S(2)}) collective-permute-start(bf16[128,256]{1,0:T(8,128)(2,1)} %param.4), channel_id=1, source_target_pairs={{0,3},{1,0},{2,1},{3,2},{4,7},{5,4},{6,5},{7,6},{8,11},{9,8},{10,9... | collective-permute-start | bytes 196616 | tf_op jit(solution)/shard_map/ppermute | solution.py:33
  4.9 4.5 %collective-permute-start.2 = (bf16[128,256]{1,0:T(8,128)(2,1)}, bf16[128,256]{1,0:T(8,128)(2,1)S(1)}, u32[]{:S(2)}, u32[]{:S(2)}) collective-permute-start(bf16[128,256]{1,0:T(8,128)(2,1)} %param.4), channel_id=1, source_target_pairs={{0,1},{1,2},{2,3},{3,0},{4,5},{5,6},{6,7},{7,4},{8,9},{9,10},{10,1... | collective-permute-start | bytes 196616 | tf_op jit(solution)/shard_map/ppermute | solution.py:33
  10.3 6.9 %collective-permute-start.5 = (bf16[128,1024]{1,0:T(8,128)(2,1)S(1)}, bf16[128,1024]{1,0:T(8,128)(2,1)S(1)}, u32[]{:S(2)}, u32[]{:S(2)}) collective-permute-start(bf16[128,1024]{1,0:T(8,128)(2,1)S(1)} %maximum_multiply_fusion), channel_id=1, source_target_pairs={{0,32},{1,33},{2,34},{3,35},{4,12},{5,13},{6,14},{7,15},{8,40},{9,... | collective-permute-start | bytes 786440 | tf_op jit(solution)/shard_map/ppermute | solution.py:37
  11.7 9.5 %collective-permute-start.4 = (bf16[128,1024]{1,0:T(8,128)(2,1)S(1)}, bf16[128,1024]{1,0:T(8,128)(2,1)S(1)}, u32[]{:S(2)}, u32[]{:S(2)}) collective-permute-start(bf16[128,1024]{1,0:T(8,128)(2,1)S(1)} %maximum_multiply_fusion), channel_id=1, source_target_pairs={{0,64},{1,65},{2,66},{3,67},{4,20},{5,21},{6,22},{7,23},{8,72},{9,... | collective-permute-start | bytes 786440 | tf_op jit(solution)/shard_map/ppermute | solution.py:37
  14.3 6.9 %collective-permute-start.3 = (bf16[128,1024]{1,0:T(8,128)(2,1)S(1)}, bf16[128,1024]{1,0:T(8,128)(2,1)S(1)}, u32[]{:S(2)}, u32[]{:S(2)}) collective-permute-start(bf16[128,1024]{1,0:T(8,128)(2,1)S(1)} %maximum_multiply_fusion), channel_id=1, source_target_pairs={{0,96},{1,97},{2,98},{3,99},{4,28},{5,29},{6,30},{7,31},{8,104},{9... | collective-permute-start | bytes 786440 | tf_op jit(solution)/shard_map/ppermute | solution.py:37
  21.2 5.8 %collective-permute-start.6 = (bf16[512,1024]{1,0:T(8,128)(2,1)S(1)}, bf16[512,1024]{1,0:T(8,128)(2,1)}, u32[]{:S(2)}, u32[]{:S(2)}) collective-permute-start(bf16[512,1024]{1,0:T(8,128)(2,1)S(1)} %pad_maximum_fusion.own0), channel_id=1, source_target_pairs={{0,4},{1,5},{2,6},{3,7},{4,0},{5,1},{6,2},{7,3},{8,12},{9,13},{10,... | collective-permute-start | bytes 3145736 | tf_op jit(solution)/shard_map/ppermute | solution.py:29
  24.3 15.2 %collective-permute-start.8 = (bf16[512,1024]{1,0:T(8,128)(2,1)S(1)}, bf16[512,1024]{1,0:T(8,128)(2,1)S(1)}, u32[]{:S(2)}, u32[]{:S(2)}) collective-permute-start(bf16[512,1024]{1,0:T(8,128)(2,1)S(1)} %pad_maximum_fusion.own0), channel_id=1, source_target_pairs={{0,8},{1,9},{2,10},{3,11},{4,36},{5,37},{6,38},{7,39},{8,16},{9,17... | collective-permute-start | bytes 3145736 | tf_op jit(solution)/shard_map/ppermute | solution.py:42
  25.9 13.9 %collective-permute-start.7 = (bf16[512,1024]{1,0:T(8,128)(2,1)S(1)}, bf16[512,1024]{1,0:T(8,128)(2,1)S(1)}, u32[]{:S(2)}, u32[]{:S(2)}) collective-permute-start(bf16[512,1024]{1,0:T(8,128)(2,1)S(1)} %pad_maximum_fusion.own0), channel_id=1, source_target_pairs={{0,24},{1,25},{2,26},{3,27},{4,100},{5,101},{6,102},{7,103},{8,0},... | collective-permute-start | bytes 3145736 | tf_op jit(solution)/shard_map/ppermute | solution.py:42
  39.8 9.5 %collective-permute-start.9 = (bf16[512,1024]{1,0:T(8,128)(2,1)S(1)}, bf16[512,1024]{1,0:T(8,128)(2,1)S(1)}, u32[]{:S(2)}, u32[]{:S(2)}) collective-permute-start(bf16[512,1024]{1,0:T(8,128)(2,1)S(1)} %collective-permute-done.7.own1), channel_id=1, source_target_pairs={{0,4},{1,5},{2,6},{3,7},{4,0},{5,1},{6,2},{7,3},{8,12},{9,13},{10,... | collective-permute-start | bytes 3145736 | tf_op jit(solution)/shard_map/ppermute | solution.py:29
  40.7 8.6 %collective-permute-start.10 = (bf16[512,1024]{1,0:T(8,128)(2,1)S(1)}, bf16[512,1024]{1,0:T(8,128)(2,1)S(1)}, u32[]{:S(2)}, u32[]{:S(2)}) collective-permute-start(bf16[512,1024]{1,0:T(8,128)(2,1)S(1)} %collective-permute-done.8.own3), channel_id=1, source_target_pairs={{0,4},{1,5},{2,6},{3,7},{4,0},{5,1},{6,2},{7,3},{8,12},{9,13},{10,... | collective-permute-start | bytes 3145736 | tf_op jit(solution)/shard_map/ppermute | solution.py:29
  40.7 16.7 %collective-permute-start.11 = (bf16[512,1024]{1,0:T(8,128)(2,1)S(1)}, bf16[512,1024]{1,0:T(8,128)(2,1)S(1)}, u32[]{:S(2)}, u32[]{:S(2)}) collective-permute-start(bf16[512,1024]{1,0:T(8,128)(2,1)S(1)} %pad_maximum_fusion.own0), channel_id=1, source_target_pairs={{0,16},{1,17},{2,18},{3,19},{4,68},{5,69},{6,70},{7,71},{8,24},{9,... | collective-permute-start | bytes 3145736 | tf_op jit(solution)/shard_map/ppermute | solution.py:42
  57.4 6.7 %copy-start.2 = (s32[2,32,32]{2,1,0:T(8,128)S(1)}, s32[2,32,32]{2,1,0:T(8,128)}, u32[]{:S(2)}) copy-start(s32[2,32,32]{2,1,0:T(8,128)} %keep_s.3) | copy-start | bytes 24580
  57.4 6.7 %collective-permute-start.12 = (bf16[512,1024]{1,0:T(8,128)(2,1)S(1)}, bf16[512,1024]{1,0:T(8,128)(2,1)S(1)}, u32[]{:S(2)}, u32[]{:S(2)}) collective-permute-start(bf16[512,1024]{1,0:T(8,128)(2,1)S(1)} %collective-permute-done.11.own2), channel_id=1, source_target_pairs={{0,4},{1,5},{2,6},{3,7},{4,0},{5,1},{6,2},{7,3},{8,12},{9,13},{10,... | collective-permute-start | bytes 3145736 | tf_op jit(solution)/shard_map/ppermute | solution.py:29
  71.2 2.7 %collective-permute-start.13 = (bf16[256,2048]{1,0:T(8,128)(2,1)S(1)}, bf16[256,2048]{1,0:T(8,128)(2,1)S(1)}, u32[]{:S(2)}, u32[]{:S(2)}) collective-permute-start(bf16[256,2048]{1,0:T(8,128)(2,1)S(1)} %get-tuple-element.61.low), channel_id=1, source_target_pairs={{0,4},{1,5},{2,6},{3,7},{4,0},{5,1},{6,2},{7,3},{8,12},{9,13},{10,... | collective-permute-start | bytes 3145736 | tf_op jit(solution)/shard_map/ppermute | solution.py:29
  80.3 17.5 %collective-permute-start.18 = (bf16[256,2048]{1,0:T(8,128)(2,1)S(1)}, bf16[256,2048]{1,0:T(8,128)(2,1)S(1)}, u32[]{:S(2)}, u32[]{:S(2)}) collective-permute-start(bf16[256,2048]{1,0:T(8,128)(2,1)S(1)} %shard_map.51.own), channel_id=1, source_target_pairs={{0,4},{1,5},{2,6},{3,7},{4,0},{5,1},{6,2},{7,3},{8,12},{9,13},{10,... | collective-permute-start | bytes 3145736 | tf_op jit(solution)/shard_map/ppermute | solution.py:29
  84.6 7.1 %collective-permute-start.17 = (bf16[256,512]{1,0:T(8,128)(2,1)S(1)}, bf16[256,512]{1,0:T(8,128)(2,1)S(1)}, u32[]{:S(2)}, u32[]{:S(2)}) collective-permute-start(bf16[256,512]{1,0:T(8,128)(2,1)S(1)} %shard_map.53), channel_id=1, source_target_pairs={{0,16},{1,17},{2,18},{3,19},{4,68},{5,69},{6,70},{7,71},{8,24},{9,... | collective-permute-start | bytes 786440 | tf_op jit(solution)/shard_map/ppermute | solution.py:42
  87.3 7.7 %collective-permute-start.16 = (bf16[256,512]{1,0:T(8,128)(2,1)S(1)}, bf16[256,512]{1,0:T(8,128)(2,1)S(1)}, u32[]{:S(2)}, u32[]{:S(2)}) collective-permute-start(bf16[256,512]{1,0:T(8,128)(2,1)S(1)} %shard_map.53), channel_id=1, source_target_pairs={{0,64},{1,65},{2,66},{3,67},{4,20},{5,21},{6,22},{7,23},{8,72},{9,... | collective-permute-start | bytes 786440 | tf_op jit(solution)/shard_map/ppermute | solution.py:37
  88.9 8.8 %collective-permute-start.15 = (bf16[256,512]{1,0:T(8,128)(2,1)S(1)}, bf16[256,512]{1,0:T(8,128)(2,1)S(1)}, u32[]{:S(2)}, u32[]{:S(2)}) collective-permute-start(bf16[256,512]{1,0:T(8,128)(2,1)S(1)} %shard_map.53), channel_id=1, source_target_pairs={{0,32},{1,33},{2,34},{3,35},{4,12},{5,13},{6,14},{7,15},{8,40},{9,... | collective-permute-start | bytes 786440 | tf_op jit(solution)/shard_map/ppermute | solution.py:37
  89.5 8.3 %collective-permute-start.14 = (bf16[256,512]{1,0:T(8,128)(2,1)S(1)}, bf16[256,512]{1,0:T(8,128)(2,1)S(1)}, u32[]{:S(2)}, u32[]{:S(2)}) collective-permute-start(bf16[256,512]{1,0:T(8,128)(2,1)S(1)} %shard_map.53), channel_id=1, source_target_pairs={{0,96},{1,97},{2,98},{3,99},{4,28},{5,29},{6,30},{7,31},{8,104},{9... | collective-permute-start | bytes 786440 | tf_op jit(solution)/shard_map/ppermute | solution.py:37
  97.8 21.1 %collective-permute-start.20 = (bf16[1024,512]{1,0:T(8,128)(2,1)S(1)}, bf16[1024,512]{1,0:T(8,128)(2,1)S(1)}, u32[]{:S(2)}, u32[]{:S(2)}) collective-permute-start(bf16[1024,512]{1,0:T(8,128)(2,1)S(1)} %constant_dynamic-update-slice_fusion.near), channel_id=1, source_target_pairs={{0,8},{1,9},{2,10},{3,11},{4,36},{5,37},{6,38},{7,39},{8,16},{9,17... | collective-permute-start | bytes 3145736 | tf_op jit(solution)/shard_map/ppermute | solution.py:42
  99.8 19.6 %collective-permute-start.19 = (bf16[1024,512]{1,0:T(8,128)(2,1)S(1)}, bf16[1024,512]{1,0:T(8,128)(2,1)S(1)}, u32[]{:S(2)}, u32[]{:S(2)}) collective-permute-start(bf16[1024,512]{1,0:T(8,128)(2,1)S(1)} %constant_dynamic-update-slice_fusion.near), channel_id=1, source_target_pairs={{0,24},{1,25},{2,26},{3,27},{4,100},{5,101},{6,102},{7,103},{8,0},... | collective-permute-start | bytes 3145736 | tf_op jit(solution)/shard_map/ppermute | solution.py:42
  100.8 9.6 %collective-permute-start.23 = (bf16[256,512]{1,0:T(8,128)(2,1)S(1)}, bf16[256,512]{1,0:T(8,128)(2,1)S(1)}, u32[]{:S(2)}, u32[]{:S(2)}) collective-permute-start(bf16[256,512]{1,0:T(8,128)(2,1)S(1)} %collective-permute-done.17.far0), channel_id=1, source_target_pairs={{0,32},{1,33},{2,34},{3,35},{4,12},{5,13},{6,14},{7,15},{8,40},{9,... | collective-permute-start | bytes 786440 | tf_op jit(solution)/shard_map/ppermute | solution.py:37
  101.5 15.0 %collective-permute-start.22 = (bf16[256,512]{1,0:T(8,128)(2,1)S(1)}, bf16[256,512]{1,0:T(8,128)(2,1)S(1)}, u32[]{:S(2)}, u32[]{:S(2)}) collective-permute-start(bf16[256,512]{1,0:T(8,128)(2,1)S(1)} %collective-permute-done.17.far0), channel_id=1, source_target_pairs={{0,64},{1,65},{2,66},{3,67},{4,20},{5,21},{6,22},{7,23},{8,72},{9,... | collective-permute-start | bytes 786440 | tf_op jit(solution)/shard_map/ppermute | solution.py:37
  104.0 12.6 %collective-permute-start.21 = (bf16[256,512]{1,0:T(8,128)(2,1)S(1)}, bf16[256,512]{1,0:T(8,128)(2,1)S(1)}, u32[]{:S(2)}, u32[]{:S(2)}) collective-permute-start(bf16[256,512]{1,0:T(8,128)(2,1)S(1)} %collective-permute-done.17.far0), channel_id=1, source_target_pairs={{0,96},{1,97},{2,98},{3,99},{4,28},{5,29},{6,30},{7,31},{8,104},{9... | collective-permute-start | bytes 786440 | tf_op jit(solution)/shard_map/ppermute | solution.py:37
  121.3 15.5 %collective-permute-start.26 = (bf16[2048,512]{1,0:T(8,128)(2,1)S(1)}, bf16[2048,512]{1,0:T(8,128)(2,1)S(1)}, u32[]{:S(2)}, u32[]{:S(2)}) collective-permute-start(bf16[2048,512]{1,0:T(8,128)(2,1)S(1)} %get-tuple-element.77), channel_id=1, source_target_pairs={{0,4},{1,5},{2,6},{3,7},{4,0},{5,1},{6,2},{7,3},{8,12},{9,13},{10,... | collective-permute-start | bytes 6291464 | tf_op jit(solution)/shard_map/ppermute | solution.py:29
  122.1 14.7 %collective-permute-start.25 = (bf16[256,512]{1,0:T(8,128)(2,1)S(1)}, bf16[256,512]{1,0:T(8,128)(2,1)S(1)}, u32[]{:S(2)}, u32[]{:S(2)}) collective-permute-start(bf16[256,512]{1,0:T(8,128)(2,1)S(1)} %get-tuple-element.75.own0), channel_id=1, source_target_pairs={{0,1},{1,2},{2,3},{3,0},{4,5},{5,6},{6,7},{7,4},{8,9},{9,10},{10,1... | collective-permute-start | bytes 786440 | tf_op jit(solution)/shard_map/ppermute | solution.py:33
  122.1 14.7 %collective-permute-start.24 = (bf16[256,512]{1,0:T(8,128)(2,1)S(1)}, bf16[256,512]{1,0:T(8,128)(2,1)S(1)}, u32[]{:S(2)}, u32[]{:S(2)}) collective-permute-start(bf16[256,512]{1,0:T(8,128)(2,1)S(1)} %get-tuple-element.75.own0), channel_id=1, source_target_pairs={{0,3},{1,0},{2,1},{3,2},{4,7},{5,4},{6,5},{7,6},{8,11},{9,8},{10,9... | collective-permute-start | bytes 786440 | tf_op jit(solution)/shard_map/ppermute | solution.py:33
  124.8 13.5 %collective-permute-start.27 = (bf16[256,512]{1,0:T(8,128)(2,1)S(1)}, bf16[256,512]{1,0:T(8,128)(2,1)S(1)}, u32[]{:S(2)}, u32[]{:S(2)}) collective-permute-start(bf16[256,512]{1,0:T(8,128)(2,1)S(1)} %get-tuple-element.75.own0), channel_id=1, source_target_pairs={{0,2},{1,3},{2,0},{3,1},{4,6},{5,7},{6,4},{7,5},{8,10},{9,11},{10,... | collective-permute-start | bytes 786440 | tf_op jit(solution)/shard_map/ppermute | solution.py:33
  139.2 2.5 %collective-permute-start.28 = (f32[128,1024]{1,0:T(8,128)S(1)}, f32[128,1024]{1,0:T(8,128)S(1)}, u32[]{:S(2)}, u32[]{:S(2)}) collective-permute-start(f32[128,1024]{1,0:T(8,128)S(1)} %shard_map.57), channel_id=1, source_target_pairs={{0,4},{1,5},{2,6},{3,7},{4,0},{5,1},{6,2},{7,3},{8,12},{9,13},{10,... | collective-permute-start | bytes 1572872 | tf_op jit(solution)/shard_map/ppermute | solution.py:29

commit v6 on v5

--- a/solution.py
+++ b/solution.py
@@ -351,12 +351,12 @@
         first_density, 2, [where, keep_density, its, columns, early, square], [low_block], [],
         block_flops // 2, 4 * MIB)
 
+    start, one, three, two, far = lax.optimization_barrier((
+        current, from_first(current, 1), from_first(current, 3), from_first(current, 2), from_second(current, 2)))
     (own,) = call(
         density_rows, 2, [where, keep_density, low, its, panel, square],
         [jax.ShapeDtypeStruct((ROWS, N // 2), jnp.bfloat16)], [], 4 * block_flops, 22 * MIB)
-    start, one, three, two, far, other = lax.optimization_barrier((
-        current, from_first(current, 1), from_first(current, 3), from_first(current, 2), from_second(current, 2),
-        other_core(own)))
+    other = other_core(own)
     near = jnp.concatenate([start, one, two, three], axis=0)
     one, three = from_second(near, 1), from_second(near, 3)
     far = gather(far, from_first)

time: 144 us -> 137 us (0.951)
  waiting for transfers between devices: 53.7 us -> 47.5 us
    ppermute x8, waiting for transfers between devices: 4.19 us -> 1.93 us  [other_core(): lax.ppermute(a, AXES, pairs(lambda x, y, core, z: (x, y, 1 - core, z)))]
    ppermute x9, waiting for transfers between devices: 23.5 us -> 21.6 us  [from_first(): lax.ppermute(a, AXES, pairs(lambda x, y, core, z: (x - d, y, core, z) if...]
    ppermute x9, starting transfers between devices: 13.4 us -> 11.9 us  [from_first(): lax.ppermute(a, AXES, pairs(lambda x, y, core, z: (x - d, y, core, z) if...]
    ppermute x6, waiting for transfers between devices: 11.2 us -> 9.73 us  [from_second(): lax.ppermute(a, AXES, pairs(lambda x, y, core, z: (x, y - d, core, z) if...]
  transfers between devices with their start and end apart: 29 -> 29, of which waited for: 17 -> 12; matrix products, arithmetic and copies ran while one was open for 1% -> 1% of each run, Pallas kernels for 21% -> 25%
where the time goes in v6:
time: 137 us
  waiting for transfers between devices  47.5 us (35%)
  Pallas kernels  47.4 us (35%)
  starting transfers between devices  39.4 us (29%)
    pallas_call x13, Pallas kernels, call(): pl.pallas_call(kernel, in_specs=[SMEM] * n_smem + [VMEM] * (len(ins) - n_...  47.4 us
    ppermute x9, waiting for transfers between devices, from_first(): lax.ppermute(a, AXES, pairs(lambda x, y, core, z: (x - d, y, core, z) if...  21.6 us
    ppermute x6, waiting for transfers between devices, from_z(): lax.ppermute(a, AXES, pairs(lambda x, y, core, z: (x, y, core, z - d)))  14.3 us
    ppermute x9, starting transfers between devices, from_first(): lax.ppermute(a, AXES, pairs(lambda x, y, core, z: (x - d, y, core, z) if...  11.9 us
    ppermute x6, starting transfers between devices, from_second(): lax.ppermute(a, AXES, pairs(lambda x, y, core, z: (x, y - d, core, z) if...  11.1 us
    ppermute x6, waiting for transfers between devices, from_second(): lax.ppermute(a, AXES, pairs(lambda x, y, core, z: (x, y - d, core, z) if...  9.73 us
    ppermute x6, starting transfers between devices, from_z(): lax.ppermute(a, AXES, pairs(lambda x, y, core, z: (x, y, core, z - d)))  8.63 us
    ppermute x8, starting transfers between devices, other_core(): lax.ppermute(a, AXES, pairs(lambda x, y, core, z: (x, y, 1 - core, z)))  7.88 us
  transfers between devices with their start and end apart: 29, of which 12 were waited for; matrix products, arithmetic and copies ran while one was open for 1% of the time, Pallas kernels for 25%

profile of v6, /device:TPU:1, one launch (start us, length us, event | category | flops | bytes accessed | tf_op | source)
XLA Modules:
  0.0 136.6 jit_solution(2865136734880979633)
XLA Ops:
  0.0 4.4 %collective-permute-start.1 = (bf16[128,256]{1,0:T(8,128)(2,1)}, bf16[128,256]{1,0:T(8,128)(2,1)S(1)}, u32[]{:S(2)}, u32[]{:S(2)}) collective-permute-start(bf16[128,256]{1,0:T(8,128)(2,1)} %param.4), channel_id=1, source_target_pairs={{0,2},{1,3},{2,0},{3,1},{4,6},{5,7},{6,4},{7,5},{8,10},{9,11},{10,... | collective-permute-start | bytes 196616 | tf_op jit(solution)/shard_map/ppermute | solution.py:33
  4.4 0.4 collective-permute-start
  4.9 1.0 collective-permute-start.2
  6.7 1.4 %collective-permute-done = bf16[128,256]{1,0:T(8,128)(2,1)S(1)} collective-permute-done((bf16[128,256]{1,0:T(8,128)(2,1)}, bf16[128,256]{1,0:T(8,128)(2,1)S(1)}, u32[]{:S(2)}, u32[]{:S(2)}) %collective-permute-start) | collective-permute-done | bytes 65568 | tf_op jit(solution)/shard_map/ppermute | solution.py:33
  8.1 1.3 collective-permute-done.2
  9.4 0.9 maximum_multiply_fusion
  10.3 1.4 collective-permute-start.5
  11.7 2.6 %collective-permute-start.4 = (bf16[128,1024]{1,0:T(8,128)(2,1)S(1)}, bf16[128,1024]{1,0:T(8,128)(2,1)S(1)}, u32[]{:S(2)}, u32[]{:S(2)}) collective-permute-start(bf16[128,1024]{1,0:T(8,128)(2,1)S(1)} %maximum_multiply_fusion), channel_id=1, source_target_pairs={{0,64},{1,65},{2,66},{3,67},{4,20},{5,21},{6,22},{7,23},{8,72},{9,... | collective-permute-start | bytes 786440 | tf_op jit(solution)/shard_map/ppermute | solution.py:37
  14.3 1.1 collective-permute-start.3
  15.4 1.8 %collective-permute-done.5 = bf16[128,1024]{1,0:T(8,128)(2,1)S(1)} collective-permute-done((bf16[128,1024]{1,0:T(8,128)(2,1)S(1)}, bf16[128,1024]{1,0:T(8,128)(2,1)S(1)}, u32[]{:S(2)}, u32[]{:S(2)}) %collective-permute-start.5) | collective-permute-done | bytes 262176 | tf_op jit(solution)/shard_map/ppermute | solution.py:37
  17.2 4.0 %collective-permute-done.4 = bf16[128,1024]{1,0:T(8,128)(2,1)S(1)} collective-permute-done((bf16[128,1024]{1,0:T(8,128)(2,1)S(1)}, bf16[128,1024]{1,0:T(8,128)(2,1)S(1)}, u32[]{:S(2)}, u32[]{:S(2)}) %collective-permute-start.4) | collective-permute-done | bytes 262176 | tf_op jit(solution)/shard_map/ppermute | solution.py:37
  21.2 3.1 %collective-permute-start.6 = (bf16[512,1024]{1,0:T(8,128)(2,1)S(1)}, bf16[512,1024]{1,0:T(8,128)(2,1)}, u32[]{:S(2)}, u32[]{:S(2)}) collective-permute-start(bf16[512,1024]{1,0:T(8,128)(2,1)S(1)} %pad_maximum_fusion.own0), channel_id=1, source_target_pairs={{0,4},{1,5},{2,6},{3,7},{4,0},{5,1},{6,2},{7,3},{8,12},{9,13},{10,... | collective-permute-start | bytes 3145736 | tf_op jit(solution)/shard_map/ppermute | solution.py:29
  24.3 1.6 %collective-permute-start.8 = (bf16[512,1024]{1,0:T(8,128)(2,1)S(1)}, bf16[512,1024]{1,0:T(8,128)(2,1)S(1)}, u32[]{:S(2)}, u32[]{:S(2)}) collective-permute-start(bf16[512,1024]{1,0:T(8,128)(2,1)S(1)} %pad_maximum_fusion.own0), channel_id=1, source_target_pairs={{0,8},{1,9},{2,10},{3,11},{4,36},{5,37},{6,38},{7,39},{8,16},{9,17... | collective-permute-start | bytes 3145736 | tf_op jit(solution)/shard_map/ppermute | solution.py:42
  25.9 1.1 collective-permute-start.7
  27.0 3.1 %shard_map.46 = (bf16[4096,2048]{1,0:T(8,128)(2,1)S(1)}, bf16[256,4096]{1,0:T(8,128)(2,1)S(1)}, bf16[256,1024]{1,0:T(8,128)(2,1)S(1)}) custom-call(s32[4]{0:T(128)S(1)} %pad_add_fusion.1.where, s32[2,32,32]{2,1,0:T(8,128)S(1)} %copy-done.1, bf16[512,1024]{1,0:T(8,128)(2,1)S(1)} %pad_maximum_fusion.own0, bf16[512,1024]{1,0:T(8,128)(2,1)} %collective-permute-done.6.other0), custom_call_target="tpu_custom_call" | custom-call | flops 67108864 | bytes 1048576 | tf_op jit(solution)/shard_map/pallas_call | solution.py:291
  30.1 9.3 %collective-permute-done.8.own3 = bf16[512,1024]{1,0:T(8,128)(2,1)S(1)} collective-permute-done((bf16[512,1024]{1,0:T(8,128)(2,1)S(1)}, bf16[512,1024]{1,0:T(8,128)(2,1)S(1)}, u32[]{:S(2)}, u32[]{:S(2)}) %collective-permute-start.8) | collective-permute-done | bytes 1048608 | tf_op jit(solution)/shard_map/ppermute | solution.py:42
  39.4 0.4 collective-permute-done.7.own1
  39.8 0.9 collective-permute-start.9
  40.7 2.7 %collective-permute-start.11 = (bf16[512,1024]{1,0:T(8,128)(2,1)S(1)}, bf16[512,1024]{1,0:T(8,128)(2,1)S(1)}, u32[]{:S(2)}, u32[]{:S(2)}) collective-permute-start(bf16[512,1024]{1,0:T(8,128)(2,1)S(1)} %pad_maximum_fusion.own0), channel_id=1, source_target_pairs={{0,16},{1,17},{2,18},{3,19},{4,68},{5,69},{6,70},{7,71},{8,24},{9,... | collective-permute-start | bytes 3145736 | tf_op jit(solution)/shard_map/ppermute | solution.py:42
  43.4 5.9 %shard_map.47 = (bf16[4096,2048]{1,0:T(8,128)(2,1)S(1)}, bf16[256,4096]{1,0:T(8,128)(2,1)S(1)}) custom-call(s32[4]{0:T(128)S(1)} %pad_add_fusion.1.where, s32[2,32,32]{2,1,0:T(8,128)S(1)} %copy-done.1, bf16[512,1024]{1,0:T(8,128)(2,1)S(1)} %pad_maximum_fusion.own0, ...), custom_call_target="tpu_custom_call", output_to_operand_aliasing={{0}: (7, {}), {1}: (8, {})} | custom-call | flops 5905580032 | bytes 8388608 | tf_op jit(solution)/shard_map/pallas_call | solution.py:291
  49.4 8.0 %shard_map.48 = (bf16[4096,2048]{1,0:T(8,128)(2,1)S(1)}, bf16[256,4096]{1,0:T(8,128)(2,1)S(1)}, f32[256,2048]{1,0:T(8,128)S(1)}) custom-call(s32[4]{0:T(128)S(1)} %pad_add_fusion.1.where, s32[2,32,32]{2,1,0:T(8,128)S(1)} %copy-done.1, bf16[512,1024]{1,0:T(8,128)(2,1)S(1)} %pad_maximum_fusion.own0, ...), custom_call_target="tpu_custom_call", output_to_operand_aliasing={{0}: (8, {}), {1}: (9, {})} | custom-call | flops 5905580032 | bytes 8388608 | tf_op jit(solution)/shard_map/pallas_call | solution.py:291
  57.4 1.0 collective-permute-start.12
  58.5 5.7 %shard_map.49 = (bf16[4096,2048]{1,0:T(8,128)(2,1)S(1)}, bf16[256,4096]{1,0:T(8,128)(2,1)S(1)}) custom-call(s32[4]{0:T(128)S(1)} %pad_add_fusion.1.where, s32[2,32,32]{2,1,0:T(8,128)S(1)} %copy-done.1, bf16[512,1024]{1,0:T(8,128)(2,1)S(1)} %pad_maximum_fusion.own0, ...), custom_call_target="tpu_custom_call", output_to_operand_aliasing={{0}: (10, {}), {1}: (11, {})} | custom-call | flops 5368709120 | bytes 8388608 | tf_op jit(solution)/shard_map/pallas_call | solution.py:291
  64.2 7.0 %shard_map.50 = (bf16[4096,2048]{1,0:T(8,128)(2,1)S(1)}, bf16[256,4096]{1,0:T(8,128)(2,1)S(1)}, bf16[256,2048]{1,0:T(8,128)(2,1)S(1)}, f32[256,2048]{1,0:T(8,128)S(1)}) custom-call(s32[4]{0:T(128)S(1)} %pad_add_fusion.1.where, s32[2,32,32]{2,1,0:T(8,128)S(1)} %copy-done.1, ...), custom_call_target="tpu_custom_call", output_to_operand_aliasing={{0}: (10, {}), {1}: (11, {})} | custom-call | flops 4294967296 | bytes 20971520 | tf_op jit(solution)/shard_map/pallas_call | solution.py:291
  71.3 2.3 %shard_map.52 = (f32[256,512]{1,0:T(8,128)S(1)}, bf16[4096,512]{1,0:T(8,128)(2,1)S(1)}) custom-call(s32[4]{0:T(128)S(1)} %pad_add_fusion.1.where, bf16[256,2048]{1,0:T(8,128)(2,1)S(1)} %get-tuple-element.60.low, bf16[4096,2048]{1,0:T(8,128)(2,1)S(1)} %get-tuple-element.61.panel), custom_call_target="tpu_custom_call" | custom-call | flops 536870912 | bytes 12582912 | tf_op jit(solution)/shard_map/pallas_call | solution.py:291
  73.6 0.4 collective-permute-done.13.its
  74.0 1.8 %shard_map.53 = bf16[256,512]{1,0:T(8,128)(2,1)S(1)} custom-call(s32[4]{0:T(128)S(1)} %pad_add_fusion.1.where, s32[2,32,32]{2,1,0:T(8,128)S(1)} %copy-done.1, bf16[256,2048]{1,0:T(8,128)(2,1)S(1)} %collective-permute-done.13.its, bf16[4096,512]{1,0:T(8,128)(2,1)S(1)} %get-tuple-element.63.columns, f32[256,512]{1,0:T(8,128)S(1)} %get-tuple-element.64.early, ...), custom_call_target="tpu_custom_call" | custom-call | flops 536870912 | bytes 4194304 | tf_op jit(solution)/shard_map/pallas_call | solution.py:291
  75.8 2.7 %collective-permute-start.18 = (bf16[256,512]{1,0:T(8,128)(2,1)S(1)}, bf16[256,512]{1,0:T(8,128)(2,1)S(1)}, u32[]{:S(2)}, u32[]{:S(2)}) collective-permute-start(bf16[256,512]{1,0:T(8,128)(2,1)S(1)} %shard_map.53), channel_id=1, source_target_pairs={{0,16},{1,17},{2,18},{3,19},{4,68},{5,69},{6,70},{7,71},{8,24},{9,... | collective-permute-start | bytes 786440 | tf_op jit(solution)/shard_map/ppermute | solution.py:42
  78.5 1.7 %collective-permute-start.17 = (bf16[256,512]{1,0:T(8,128)(2,1)S(1)}, bf16[256,512]{1,0:T(8,128)(2,1)S(1)}, u32[]{:S(2)}, u32[]{:S(2)}) collective-permute-start(bf16[256,512]{1,0:T(8,128)(2,1)S(1)} %shard_map.53), channel_id=1, source_target_pairs={{0,64},{1,65},{2,66},{3,67},{4,20},{5,21},{6,22},{7,23},{8,72},{9,... | collective-permute-start | bytes 786440 | tf_op jit(solution)/shard_map/ppermute | solution.py:37
  80.2 0.5 collective-permute-start.16
  80.8 2.1 %collective-permute-start.15 = (bf16[256,512]{1,0:T(8,128)(2,1)S(1)}, bf16[256,512]{1,0:T(8,128)(2,1)S(1)}, u32[]{:S(2)}, u32[]{:S(2)}) collective-permute-start(bf16[256,512]{1,0:T(8,128)(2,1)S(1)} %shard_map.53), channel_id=1, source_target_pairs={{0,96},{1,97},{2,98},{3,99},{4,28},{5,29},{6,30},{7,31},{8,104},{9... | collective-permute-start | bytes 786440 | tf_op jit(solution)/shard_map/ppermute | solution.py:37
  82.9 6.3 %shard_map.51.own = bf16[256,2048]{1,0:T(8,128)(2,1)S(1)} custom-call(s32[4]{0:T(128)S(1)} %pad_add_fusion.1.where, s32[2,32,32]{2,1,0:T(8,128)S(1)} %copy-done.1, bf16[256,2048]{1,0:T(8,128)(2,1)S(1)} %get-tuple-element.60.low, bf16[256,2048]{1,0:T(8,128)(2,1)S(1)} %collective-permute-done.13.its, bf16[4096,2048]{1,0:T(8,128)(2,1)S(1)} %get-tuple-element.61.panel, ...), custom_call_target="tpu_custom_call" | custom-call | flops 4294967296 | bytes 23068672 | tf_op jit(solution)/shard_map/pallas_call | solution.py:291
  89.2 1.3 collective-permute-start.14
  91.0 2.7 %collective-permute-start.19 = (bf16[1024,512]{1,0:T(8,128)(2,1)S(1)}, bf16[1024,512]{1,0:T(8,128)(2,1)S(1)}, u32[]{:S(2)}, u32[]{:S(2)}) collective-permute-start(bf16[1024,512]{1,0:T(8,128)(2,1)S(1)} %constant_dynamic-update-slice_fusion.near), channel_id=1, source_target_pairs={{0,24},{1,25},{2,26},{3,27},{4,100},{5,101},{6,102},{7,103},{8,0},... | collective-permute-start | bytes 3145736 | tf_op jit(solution)/shard_map/ppermute | solution.py:42
  93.7 0.5 collective-permute-start.23
  94.2 1.9 %collective-permute-start.22 = (bf16[256,512]{1,0:T(8,128)(2,1)S(1)}, bf16[256,512]{1,0:T(8,128)(2,1)S(1)}, u32[]{:S(2)}, u32[]{:S(2)}) collective-permute-start(bf16[256,512]{1,0:T(8,128)(2,1)S(1)} %collective-permute-done.18.far0), channel_id=1, source_target_pairs={{0,64},{1,65},{2,66},{3,67},{4,20},{5,21},{6,22},{7,23},{8,72},{9,... | collective-permute-start | bytes 786440 | tf_op jit(solution)/shard_map/ppermute | solution.py:37
  96.1 7.4 %collective-permute-done.23.far3 = bf16[256,512]{1,0:T(8,128)(2,1)S(1)} collective-permute-done((bf16[256,512]{1,0:T(8,128)(2,1)S(1)}, bf16[256,512]{1,0:T(8,128)(2,1)S(1)}, u32[]{:S(2)}, u32[]{:S(2)}) %collective-permute-start.23) | collective-permute-done | bytes 262176 | tf_op jit(solution)/shard_map/ppermute | solution.py:37
  103.5 5.1 %collective-permute-done.22.far2 = bf16[256,512]{1,0:T(8,128)(2,1)S(1)} collective-permute-done((bf16[256,512]{1,0:T(8,128)(2,1)S(1)}, bf16[256,512]{1,0:T(8,128)(2,1)S(1)}, u32[]{:S(2)}, u32[]{:S(2)}) %collective-permute-start.22) | collective-permute-done | bytes 262176 | tf_op jit(solution)/shard_map/ppermute | solution.py:37
  108.6 3.2 %collective-permute-done.21.far1 = bf16[256,512]{1,0:T(8,128)(2,1)S(1)} collective-permute-done((bf16[256,512]{1,0:T(8,128)(2,1)S(1)}, bf16[256,512]{1,0:T(8,128)(2,1)S(1)}, u32[]{:S(2)}, u32[]{:S(2)}) %collective-permute-start.21) | collective-permute-done | bytes 262176 | tf_op jit(solution)/shard_map/ppermute | solution.py:37
  111.9 1.4 shard_map.54
  113.3 1.9 %shard_map.55 = (f32[256,512]{1,0:T(8,128)S(1)}, bf16[256,512]{1,0:T(8,128)(2,1)S(1)}, bf16[2048,512]{1,0:T(8,128)(2,1)S(1)}, bf16[2048,512]{1,0:T(8,128)(2,1)S(1)}) custom-call(s32[4]{0:T(128)S(1)} %pad_add_fusion.1.where, s32[2,32,32]{2,1,0:T(8,128)S(1)} %copy-done.2, ...), custom_call_target="tpu_custom_call", output_to_operand_aliasing={{2}: (7, {}), {3}: (8, {})} | custom-call | flops 536870912 | bytes 8388608 | tf_op jit(solution)/shard_map/pallas_call | solution.py:291
  115.4 2.7 %collective-permute-start.24 = (bf16[256,512]{1,0:T(8,128)(2,1)S(1)}, bf16[256,512]{1,0:T(8,128)(2,1)S(1)}, u32[]{:S(2)}, u32[]{:S(2)}) collective-permute-start(bf16[256,512]{1,0:T(8,128)(2,1)S(1)} %get-tuple-element.73.own0), channel_id=1, source_target_pairs={{0,3},{1,0},{2,1},{3,2},{4,7},{5,4},{6,5},{7,6},{8,11},{9,8},{10,9... | collective-permute-start | bytes 786440 | tf_op jit(solution)/shard_map/ppermute | solution.py:33
  118.0 11.6 %collective-permute-done.25.own3 = bf16[256,512]{1,0:T(8,128)(2,1)S(1)} collective-permute-done((bf16[256,512]{1,0:T(8,128)(2,1)S(1)}, bf16[256,512]{1,0:T(8,128)(2,1)S(1)}, u32[]{:S(2)}, u32[]{:S(2)}) %collective-permute-start.25) | collective-permute-done | bytes 262176 | tf_op jit(solution)/shard_map/ppermute | solution.py:33
  129.6 1.5 %shard_map.56.early = f32[256,1024]{1,0:T(8,128)S(1)} custom-call(s32[4]{0:T(128)S(1)} %pad_add_fusion.1.where, bf16[256,512]{1,0:T(8,128)(2,1)S(1)} %get-tuple-element.73.own0, bf16[256,512]{1,0:T(8,128)(2,1)S(1)} %collective-permute-done.24.own1, bf16[256,512]{1,0:T(8,128)(2,1)S(1)} %collective-permute-done.25.own3, ...), custom_call_target="tpu_custom_call" | custom-call | flops 805306368 | bytes 4194304 | tf_op jit(solution)/shard_map/pallas_call | solution.py:291
  131.2 0.9 shard_map.57
  132.0 1.3 collective-permute-start.28
  133.4 1.5 %collective-permute-done.28.share = f32[128,1024]{1,0:T(8,128)S(1)} collective-permute-done((f32[128,1024]{1,0:T(8,128)S(1)}, f32[128,1024]{1,0:T(8,128)S(1)}, u32[]{:S(2)}, u32[]{:S(2)}) %collective-permute-start.28) | collective-permute-done | bytes 524320 | tf_op jit(solution)/shard_map/ppermute | solution.py:29
  134.9 1.7 %shard_map.58 = f32[128,1024]{1,0:T(8,128)} custom-call(s32[4]{0:T(128)S(1)} %pad_add_fusion.1.where, bf16[256,512]{1,0:T(8,128)(2,1)S(1)} %collective-permute-done.27.own2, f32[256,1024]{1,0:T(8,128)S(1)} %shard_map.56.early, f32[256,512]{1,0:T(8,128)S(1)} %get-tuple-element.78.square, bf16[2048,512]{1,0:T(8,128)(2,1)S(1)} %get-tuple-element.74.mine, ...), custom_call_target="tpu_custom_call" | custom-call | flops 134217728 | bytes 3145728 | tf_op jit(solution)/shard_map/pallas_call | solution.py:291
  (44 shorter events, 1.7 us)
Async XLA Ops:
  0.0 5.9 %copy-start = (s32[32,8]{0,1:T(8,128)S(1)}, s32[32,8]{0,1:T(8,128)}, u32[]{:S(2)}) copy-start(s32[32,8]{0,1:T(8,128)} %param.5) | copy-start | bytes 3076
  0.0 27.0 %copy-start.1 = (s32[2,32,32]{2,1,0:T(8,128)S(1)}, s32[2,32,32]{2,1,0:T(8,128)}, u32[]{:S(2)}) copy-start(s32[2,32,32]{2,1,0:T(8,128)} %keep_d.13) | copy-start | bytes 24580
  0.0 6.7 %collective-permute-start.1 = (bf16[128,256]{1,0:T(8,128)(2,1)}, bf16[128,256]{1,0:T(8,128)(2,1)S(1)}, u32[]{:S(2)}, u32[]{:S(2)}) collective-permute-start(bf16[128,256]{1,0:T(8,128)(2,1)} %param.4), channel_id=1, source_target_pairs={{0,2},{1,3},{2,0},{3,1},{4,6},{5,7},{6,4},{7,5},{8,10},{9,11},{10,... | collective-permute-start | bytes 196616 | tf_op jit(solution)/shard_map/ppermute | solution.py:33
  4.4 3.7 %collective-permute-start = (bf16[128,256]{1,0:T(8,128)(2,1)}, bf16[128,256]{1,0:T(8,128)(2,1)S(1)}, u32[]{:S(2)}, u32[]{:S(2)}) collective-permute-start(bf16[128,256]{1,0:T(8,128)(2,1)} %param.4), channel_id=1, source_target_pairs={{0,3},{1,0},{2,1},{3,2},{4,7},{5,4},{6,5},{7,6},{8,11},{9,8},{10,9... | collective-permute-start | bytes 196616 | tf_op jit(solution)/shard_map/ppermute | solution.py:33
  4.9 4.5 %collective-permute-start.2 = (bf16[128,256]{1,0:T(8,128)(2,1)}, bf16[128,256]{1,0:T(8,128)(2,1)S(1)}, u32[]{:S(2)}, u32[]{:S(2)}) collective-permute-start(bf16[128,256]{1,0:T(8,128)(2,1)} %param.4), channel_id=1, source_target_pairs={{0,1},{1,2},{2,3},{3,0},{4,5},{5,6},{6,7},{7,4},{8,9},{9,10},{10,1... | collective-permute-start | bytes 196616 | tf_op jit(solution)/shard_map/ppermute | solution.py:33
  10.3 6.9 %collective-permute-start.5 = (bf16[128,1024]{1,0:T(8,128)(2,1)S(1)}, bf16[128,1024]{1,0:T(8,128)(2,1)S(1)}, u32[]{:S(2)}, u32[]{:S(2)}) collective-permute-start(bf16[128,1024]{1,0:T(8,128)(2,1)S(1)} %maximum_multiply_fusion), channel_id=1, source_target_pairs={{0,32},{1,33},{2,34},{3,35},{4,12},{5,13},{6,14},{7,15},{8,40},{9,... | collective-permute-start | bytes 786440 | tf_op jit(solution)/shard_map/ppermute | solution.py:37
  11.7 9.5 %collective-permute-start.4 = (bf16[128,1024]{1,0:T(8,128)(2,1)S(1)}, bf16[128,1024]{1,0:T(8,128)(2,1)S(1)}, u32[]{:S(2)}, u32[]{:S(2)}) collective-permute-start(bf16[128,1024]{1,0:T(8,128)(2,1)S(1)} %maximum_multiply_fusion), channel_id=1, source_target_pairs={{0,64},{1,65},{2,66},{3,67},{4,20},{5,21},{6,22},{7,23},{8,72},{9,... | collective-permute-start | bytes 786440 | tf_op jit(solution)/shard_map/ppermute | solution.py:37
  14.3 6.9 %collective-permute-start.3 = (bf16[128,1024]{1,0:T(8,128)(2,1)S(1)}, bf16[128,1024]{1,0:T(8,128)(2,1)S(1)}, u32[]{:S(2)}, u32[]{:S(2)}) collective-permute-start(bf16[128,1024]{1,0:T(8,128)(2,1)S(1)} %maximum_multiply_fusion), channel_id=1, source_target_pairs={{0,96},{1,97},{2,98},{3,99},{4,28},{5,29},{6,30},{7,31},{8,104},{9... | collective-permute-start | bytes 786440 | tf_op jit(solution)/shard_map/ppermute | solution.py:37
  21.2 5.8 %collective-permute-start.6 = (bf16[512,1024]{1,0:T(8,128)(2,1)S(1)}, bf16[512,1024]{1,0:T(8,128)(2,1)}, u32[]{:S(2)}, u32[]{:S(2)}) collective-permute-start(bf16[512,1024]{1,0:T(8,128)(2,1)S(1)} %pad_maximum_fusion.own0), channel_id=1, source_target_pairs={{0,4},{1,5},{2,6},{3,7},{4,0},{5,1},{6,2},{7,3},{8,12},{9,13},{10,... | collective-permute-start | bytes 3145736 | tf_op jit(solution)/shard_map/ppermute | solution.py:29
  24.3 15.2 %collective-permute-start.8 = (bf16[512,1024]{1,0:T(8,128)(2,1)S(1)}, bf16[512,1024]{1,0:T(8,128)(2,1)S(1)}, u32[]{:S(2)}, u32[]{:S(2)}) collective-permute-start(bf16[512,1024]{1,0:T(8,128)(2,1)S(1)} %pad_maximum_fusion.own0), channel_id=1, source_target_pairs={{0,8},{1,9},{2,10},{3,11},{4,36},{5,37},{6,38},{7,39},{8,16},{9,17... | collective-permute-start | bytes 3145736 | tf_op jit(solution)/shard_map/ppermute | solution.py:42
  25.9 13.9 %collective-permute-start.7 = (bf16[512,1024]{1,0:T(8,128)(2,1)S(1)}, bf16[512,1024]{1,0:T(8,128)(2,1)S(1)}, u32[]{:S(2)}, u32[]{:S(2)}) collective-permute-start(bf16[512,1024]{1,0:T(8,128)(2,1)S(1)} %pad_maximum_fusion.own0), channel_id=1, source_target_pairs={{0,24},{1,25},{2,26},{3,27},{4,100},{5,101},{6,102},{7,103},{8,0},... | collective-permute-start | bytes 3145736 | tf_op jit(solution)/shard_map/ppermute | solution.py:42
  39.8 9.5 %collective-permute-start.9 = (bf16[512,1024]{1,0:T(8,128)(2,1)S(1)}, bf16[512,1024]{1,0:T(8,128)(2,1)S(1)}, u32[]{:S(2)}, u32[]{:S(2)}) collective-permute-start(bf16[512,1024]{1,0:T(8,128)(2,1)S(1)} %collective-permute-done.7.own1), channel_id=1, source_target_pairs={{0,4},{1,5},{2,6},{3,7},{4,0},{5,1},{6,2},{7,3},{8,12},{9,13},{10,... | collective-permute-start | bytes 3145736 | tf_op jit(solution)/shard_map/ppermute | solution.py:29
  40.7 8.6 %collective-permute-start.10 = (bf16[512,1024]{1,0:T(8,128)(2,1)S(1)}, bf16[512,1024]{1,0:T(8,128)(2,1)S(1)}, u32[]{:S(2)}, u32[]{:S(2)}) collective-permute-start(bf16[512,1024]{1,0:T(8,128)(2,1)S(1)} %collective-permute-done.8.own3), channel_id=1, source_target_pairs={{0,4},{1,5},{2,6},{3,7},{4,0},{5,1},{6,2},{7,3},{8,12},{9,13},{10,... | collective-permute-start | bytes 3145736 | tf_op jit(solution)/shard_map/ppermute | solution.py:29
  40.7 16.7 %collective-permute-start.11 = (bf16[512,1024]{1,0:T(8,128)(2,1)S(1)}, bf16[512,1024]{1,0:T(8,128)(2,1)S(1)}, u32[]{:S(2)}, u32[]{:S(2)}) collective-permute-start(bf16[512,1024]{1,0:T(8,128)(2,1)S(1)} %pad_maximum_fusion.own0), channel_id=1, source_target_pairs={{0,16},{1,17},{2,18},{3,19},{4,68},{5,69},{6,70},{7,71},{8,24},{9,... | collective-permute-start | bytes 3145736 | tf_op jit(solution)/shard_map/ppermute | solution.py:42
  57.4 6.7 %copy-start.2 = (s32[2,32,32]{2,1,0:T(8,128)S(1)}, s32[2,32,32]{2,1,0:T(8,128)}, u32[]{:S(2)}) copy-start(s32[2,32,32]{2,1,0:T(8,128)} %keep_s.3) | copy-start | bytes 24580
  57.4 6.7 %collective-permute-start.12 = (bf16[512,1024]{1,0:T(8,128)(2,1)S(1)}, bf16[512,1024]{1,0:T(8,128)(2,1)S(1)}, u32[]{:S(2)}, u32[]{:S(2)}) collective-permute-start(bf16[512,1024]{1,0:T(8,128)(2,1)S(1)} %collective-permute-done.11.own2), channel_id=1, source_target_pairs={{0,4},{1,5},{2,6},{3,7},{4,0},{5,1},{6,2},{7,3},{8,12},{9,13},{10,... | collective-permute-start | bytes 3145736 | tf_op jit(solution)/shard_map/ppermute | solution.py:29
  71.2 2.7 %collective-permute-start.13 = (bf16[256,2048]{1,0:T(8,128)(2,1)S(1)}, bf16[256,2048]{1,0:T(8,128)(2,1)S(1)}, u32[]{:S(2)}, u32[]{:S(2)}) collective-permute-start(bf16[256,2048]{1,0:T(8,128)(2,1)S(1)} %get-tuple-element.60.low), channel_id=1, source_target_pairs={{0,4},{1,5},{2,6},{3,7},{4,0},{5,1},{6,2},{7,3},{8,12},{9,13},{10,... | collective-permute-start | bytes 3145736 | tf_op jit(solution)/shard_map/ppermute | solution.py:29
  75.8 14.8 %collective-permute-start.18 = (bf16[256,512]{1,0:T(8,128)(2,1)S(1)}, bf16[256,512]{1,0:T(8,128)(2,1)S(1)}, u32[]{:S(2)}, u32[]{:S(2)}) collective-permute-start(bf16[256,512]{1,0:T(8,128)(2,1)S(1)} %shard_map.53), channel_id=1, source_target_pairs={{0,16},{1,17},{2,18},{3,19},{4,68},{5,69},{6,70},{7,71},{8,24},{9,... | collective-permute-start | bytes 786440 | tf_op jit(solution)/shard_map/ppermute | solution.py:42
  78.5 12.0 %collective-permute-start.17 = (bf16[256,512]{1,0:T(8,128)(2,1)S(1)}, bf16[256,512]{1,0:T(8,128)(2,1)S(1)}, u32[]{:S(2)}, u32[]{:S(2)}) collective-permute-start(bf16[256,512]{1,0:T(8,128)(2,1)S(1)} %shard_map.53), channel_id=1, source_target_pairs={{0,64},{1,65},{2,66},{3,67},{4,20},{5,21},{6,22},{7,23},{8,72},{9,... | collective-permute-start | bytes 786440 | tf_op jit(solution)/shard_map/ppermute | solution.py:37
  80.2 10.3 %collective-permute-start.16 = (bf16[256,512]{1,0:T(8,128)(2,1)S(1)}, bf16[256,512]{1,0:T(8,128)(2,1)S(1)}, u32[]{:S(2)}, u32[]{:S(2)}) collective-permute-start(bf16[256,512]{1,0:T(8,128)(2,1)S(1)} %shard_map.53), channel_id=1, source_target_pairs={{0,32},{1,33},{2,34},{3,35},{4,12},{5,13},{6,14},{7,15},{8,40},{9,... | collective-permute-start | bytes 786440 | tf_op jit(solution)/shard_map/ppermute | solution.py:37
  80.8 9.8 %collective-permute-start.15 = (bf16[256,512]{1,0:T(8,128)(2,1)S(1)}, bf16[256,512]{1,0:T(8,128)(2,1)S(1)}, u32[]{:S(2)}, u32[]{:S(2)}) collective-permute-start(bf16[256,512]{1,0:T(8,128)(2,1)S(1)} %shard_map.53), channel_id=1, source_target_pairs={{0,96},{1,97},{2,98},{3,99},{4,28},{5,29},{6,30},{7,31},{8,104},{9... | collective-permute-start | bytes 786440 | tf_op jit(solution)/shard_map/ppermute | solution.py:37
  89.2 22.7 %collective-permute-start.14 = (bf16[256,2048]{1,0:T(8,128)(2,1)S(1)}, bf16[256,2048]{1,0:T(8,128)(2,1)S(1)}, u32[]{:S(2)}, u32[]{:S(2)}) collective-permute-start(bf16[256,2048]{1,0:T(8,128)(2,1)S(1)} %shard_map.51.own), channel_id=1, source_target_pairs={{0,4},{1,5},{2,6},{3,7},{4,0},{5,1},{6,2},{7,3},{8,12},{9,13},{10,... | collective-permute-start | bytes 3145736 | tf_op jit(solution)/shard_map/ppermute | solution.py:29
  90.7 22.6 %collective-permute-start.20 = (bf16[1024,512]{1,0:T(8,128)(2,1)S(1)}, bf16[1024,512]{1,0:T(8,128)(2,1)S(1)}, u32[]{:S(2)}, u32[]{:S(2)}) collective-permute-start(bf16[1024,512]{1,0:T(8,128)(2,1)S(1)} %constant_dynamic-update-slice_fusion.near), channel_id=1, source_target_pairs={{0,8},{1,9},{2,10},{3,11},{4,36},{5,37},{6,38},{7,39},{8,16},{9,17... | collective-permute-start | bytes 3145736 | tf_op jit(solution)/shard_map/ppermute | solution.py:42
  91.0 22.2 %collective-permute-start.19 = (bf16[1024,512]{1,0:T(8,128)(2,1)S(1)}, bf16[1024,512]{1,0:T(8,128)(2,1)S(1)}, u32[]{:S(2)}, u32[]{:S(2)}) collective-permute-start(bf16[1024,512]{1,0:T(8,128)(2,1)S(1)} %constant_dynamic-update-slice_fusion.near), channel_id=1, source_target_pairs={{0,24},{1,25},{2,26},{3,27},{4,100},{5,101},{6,102},{7,103},{8,0},... | collective-permute-start | bytes 3145736 | tf_op jit(solution)/shard_map/ppermute | solution.py:42
  93.7 9.9 %collective-permute-start.23 = (bf16[256,512]{1,0:T(8,128)(2,1)S(1)}, bf16[256,512]{1,0:T(8,128)(2,1)S(1)}, u32[]{:S(2)}, u32[]{:S(2)}) collective-permute-start(bf16[256,512]{1,0:T(8,128)(2,1)S(1)} %collective-permute-done.18.far0), channel_id=1, source_target_pairs={{0,32},{1,33},{2,34},{3,35},{4,12},{5,13},{6,14},{7,15},{8,40},{9,... | collective-permute-start | bytes 786440 | tf_op jit(solution)/shard_map/ppermute | solution.py:37
  94.2 14.4 %collective-permute-start.22 = (bf16[256,512]{1,0:T(8,128)(2,1)S(1)}, bf16[256,512]{1,0:T(8,128)(2,1)S(1)}, u32[]{:S(2)}, u32[]{:S(2)}) collective-permute-start(bf16[256,512]{1,0:T(8,128)(2,1)S(1)} %collective-permute-done.18.far0), channel_id=1, source_target_pairs={{0,64},{1,65},{2,66},{3,67},{4,20},{5,21},{6,22},{7,23},{8,72},{9,... | collective-permute-start | bytes 786440 | tf_op jit(solution)/shard_map/ppermute | solution.py:37
  103.5 8.3 %collective-permute-start.21 = (bf16[256,512]{1,0:T(8,128)(2,1)S(1)}, bf16[256,512]{1,0:T(8,128)(2,1)S(1)}, u32[]{:S(2)}, u32[]{:S(2)}) collective-permute-start(bf16[256,512]{1,0:T(8,128)(2,1)S(1)} %collective-permute-done.18.far0), channel_id=1, source_target_pairs={{0,96},{1,97},{2,98},{3,99},{4,28},{5,29},{6,30},{7,31},{8,104},{9... | collective-permute-start | bytes 786440 | tf_op jit(solution)/shard_map/ppermute | solution.py:37
  115.2 14.5 %collective-permute-start.26 = (bf16[2048,512]{1,0:T(8,128)(2,1)S(1)}, bf16[2048,512]{1,0:T(8,128)(2,1)S(1)}, u32[]{:S(2)}, u32[]{:S(2)}) collective-permute-start(bf16[2048,512]{1,0:T(8,128)(2,1)S(1)} %get-tuple-element.75), channel_id=1, source_target_pairs={{0,4},{1,5},{2,6},{3,7},{4,0},{5,1},{6,2},{7,3},{8,12},{9,13},{10,... | collective-permute-start | bytes 6291464 | tf_op jit(solution)/shard_map/ppermute | solution.py:29
  115.3 14.4 %collective-permute-start.25 = (bf16[256,512]{1,0:T(8,128)(2,1)S(1)}, bf16[256,512]{1,0:T(8,128)(2,1)S(1)}, u32[]{:S(2)}, u32[]{:S(2)}) collective-permute-start(bf16[256,512]{1,0:T(8,128)(2,1)S(1)} %get-tuple-element.73.own0), channel_id=1, source_target_pairs={{0,1},{1,2},{2,3},{3,0},{4,5},{5,6},{6,7},{7,4},{8,9},{9,10},{10,1... | collective-permute-start | bytes 786440 | tf_op jit(solution)/shard_map/ppermute | solution.py:33
  115.4 14.3 %collective-permute-start.24 = (bf16[256,512]{1,0:T(8,128)(2,1)S(1)}, bf16[256,512]{1,0:T(8,128)(2,1)S(1)}, u32[]{:S(2)}, u32[]{:S(2)}) collective-permute-start(bf16[256,512]{1,0:T(8,128)(2,1)S(1)} %get-tuple-element.73.own0), channel_id=1, source_target_pairs={{0,3},{1,0},{2,1},{3,2},{4,7},{5,4},{6,5},{7,6},{8,11},{9,8},{10,9... | collective-permute-start | bytes 786440 | tf_op jit(solution)/shard_map/ppermute | solution.py:33
  118.0 13.1 %collective-permute-start.27 = (bf16[256,512]{1,0:T(8,128)(2,1)S(1)}, bf16[256,512]{1,0:T(8,128)(2,1)S(1)}, u32[]{:S(2)}, u32[]{:S(2)}) collective-permute-start(bf16[256,512]{1,0:T(8,128)(2,1)S(1)} %get-tuple-element.73.own0), channel_id=1, source_target_pairs={{0,2},{1,3},{2,0},{3,1},{4,6},{5,7},{6,4},{7,5},{8,10},{9,11},{10,... | collective-permute-start | bytes 786440 | tf_op jit(solution)/shard_map/ppermute | solution.py:33
  132.0 2.9 %collective-permute-start.28 = (f32[128,1024]{1,0:T(8,128)S(1)}, f32[128,1024]{1,0:T(8,128)S(1)}, u32[]{:S(2)}, u32[]{:S(2)}) collective-permute-start(f32[128,1024]{1,0:T(8,128)S(1)} %shard_map.57), channel_id=1, source_target_pairs={{0,4},{1,5},{2,6},{3,7},{4,0},{5,1},{6,2},{7,3},{8,12},{9,13},{10,... | collective-permute-start | bytes 1572872 | tf_op jit(solution)/shard_map/ppermute | solution.py:29

commit v7 on v6

--- a/solution.py
+++ b/solution.py
@@ -231,10 +231,13 @@
     return total
 
 
-def early_square(where, own, other, near, far0, far1, far2, far3, early, mine, its):
-    chips = [(near, i * ROWS, i, 0) for i in range(4)]
-    chips += [(ref, 0, i, 2) for i, ref in enumerate((far0, far1, far2, far3))]
-    early[...] = chips_times(where, own, other, chips, mine, its)
+def square_near(where, own, other, near, early, mine, its):
+    early[...] = chips_times(where, own, other, [(near, i * ROWS, i, 0) for i in range(4)], mine, its)
+
+
+def square_far(where, own, other, far0, far1, far2, far3, early, _, __, out, mine, its):
+    chips = [(ref, 0, i, 2) for i, ref in enumerate((far0, far1, far2, far3))]
+    out[...] = early[...] + chips_times(where, own, other, chips, mine, its)
 
 
 def second_square(where, keep_s, own, other, one, three, early, _, __, square, low, mine, its):
@@ -362,8 +365,11 @@
     far = gather(far, from_first)
     half_shape = jax.ShapeDtypeStruct((N // 2, COLS), jnp.bfloat16)
     early, mine, its = call(
-        early_square, 1, [where, own, other, near, *far], [full_block, half_shape, half_shape],
-        [], block_flops // 2, 10 * MIB)
+        square_near, 1, [where, own, other, near], [full_block, half_shape, half_shape],
+        [], block_flops // 4, 6 * MIB)
+    early, mine, its = call(
+        square_far, 1, [where, own, other, *far, early, mine, its], [full_block, half_shape, half_shape],
+        [], block_flops // 4, 6 * MIB, {8: 1, 9: 2})
     square, low, mine, its = call(
         second_square, 2, [where, keep_square, own, other, one, three, early, mine, its],
         [full_block, low_block, half_shape, half_shape],

time: 137 us -> 136 us (level)
  waiting for transfers between devices: 47.5 us -> 44.9 us
  starting transfers between devices: 39.4 us -> 40.8 us
    ppermute x9, waiting for transfers between devices: 21.6 us -> 17.3 us  [from_first(): lax.ppermute(a, AXES, pairs(lambda x, y, core, z: (x - d, y, core, z) if...]
    pallas_call x13 -> x14, Pallas kernels: 47.4 us -> 48 us  [call(): pl.pallas_call(kernel, in_specs=[SMEM] * n_smem + [VMEM] * (len(ins) - n_...]
  transfers between devices with their start and end apart: 29 -> 29, of which waited for: 12 -> 13; matrix products, arithmetic and copies ran while one was open for 1% -> 1% of each run, Pallas kernels for 25% -> 26%
where the time goes in v7:
time: 136 us
  Pallas kernels  48 us (35%)
  waiting for transfers between devices  44.9 us (33%)
  starting transfers between devices  40.8 us (30%)
    pallas_call x14, Pallas kernels, call(): pl.pallas_call(kernel, in_specs=[SMEM] * n_smem + [VMEM] * (len(ins) - n_...  48 us
    ppermute x9, waiting for transfers between devices, from_first(): lax.ppermute(a, AXES, pairs(lambda x, y, core, z: (x - d, y, core, z) if...  17.3 us
    ppermute x6, waiting for transfers between devices, from_z(): lax.ppermute(a, AXES, pairs(lambda x, y, core, z: (x, y, core, z - d)))  14.7 us
    ppermute x9, starting transfers between devices, from_first(): lax.ppermute(a, AXES, pairs(lambda x, y, core, z: (x - d, y, core, z) if...  12.8 us
    ppermute x6, starting transfers between devices, from_second(): lax.ppermute(a, AXES, pairs(lambda x, y, core, z: (x, y - d, core, z) if...  11.1 us
    ppermute x6, waiting for transfers between devices, from_second(): lax.ppermute(a, AXES, pairs(lambda x, y, core, z: (x, y - d, core, z) if...  11 us
    ppermute x6, starting transfers between devices, from_z(): lax.ppermute(a, AXES, pairs(lambda x, y, core, z: (x, y, core, z - d)))  8.58 us
    ppermute x8, starting transfers between devices, other_core(): lax.ppermute(a, AXES, pairs(lambda x, y, core, z: (x, y, 1 - core, z)))  8.35 us
  transfers between devices with their start and end apart: 29, of which 13 were waited for; matrix products, arithmetic and copies ran while one was open for 1% of the time, Pallas kernels for 26%

profile of v7, /device:TPU:1, one launch (start us, length us, event | category | flops | bytes accessed | tf_op | source)
XLA Modules:
  0.0 135.9 jit_solution(10383778982642496704)
XLA Ops:
  0.0 4.4 %collective-permute-start.1 = (bf16[128,256]{1,0:T(8,128)(2,1)}, bf16[128,256]{1,0:T(8,128)(2,1)S(1)}, u32[]{:S(2)}, u32[]{:S(2)}) collective-permute-start(bf16[128,256]{1,0:T(8,128)(2,1)} %param.4), channel_id=1, source_target_pairs={{0,2},{1,3},{2,0},{3,1},{4,6},{5,7},{6,4},{7,5},{8,10},{9,11},{10,... | collective-permute-start | bytes 196616 | tf_op jit(solution)/shard_map/ppermute | solution.py:33
  4.9 1.0 collective-permute-start.2
  6.7 1.4 %collective-permute-done = bf16[128,256]{1,0:T(8,128)(2,1)S(1)} collective-permute-done((bf16[128,256]{1,0:T(8,128)(2,1)}, bf16[128,256]{1,0:T(8,128)(2,1)S(1)}, u32[]{:S(2)}, u32[]{:S(2)}) %collective-permute-start) | collective-permute-done | bytes 65568 | tf_op jit(solution)/shard_map/ppermute | solution.py:33
  8.1 1.3 collective-permute-done.2
  9.4 0.9 maximum_multiply_fusion
  10.3 1.4 %collective-permute-start.5 = (bf16[128,1024]{1,0:T(8,128)(2,1)S(1)}, bf16[128,1024]{1,0:T(8,128)(2,1)S(1)}, u32[]{:S(2)}, u32[]{:S(2)}) collective-permute-start(bf16[128,1024]{1,0:T(8,128)(2,1)S(1)} %maximum_multiply_fusion), channel_id=1, source_target_pairs={{0,32},{1,33},{2,34},{3,35},{4,12},{5,13},{6,14},{7,15},{8,40},{9,... | collective-permute-start | bytes 786440 | tf_op jit(solution)/shard_map/ppermute | solution.py:37
  11.7 2.6 %collective-permute-start.4 = (bf16[128,1024]{1,0:T(8,128)(2,1)S(1)}, bf16[128,1024]{1,0:T(8,128)(2,1)S(1)}, u32[]{:S(2)}, u32[]{:S(2)}) collective-permute-start(bf16[128,1024]{1,0:T(8,128)(2,1)S(1)} %maximum_multiply_fusion), channel_id=1, source_target_pairs={{0,64},{1,65},{2,66},{3,67},{4,20},{5,21},{6,22},{7,23},{8,72},{9,... | collective-permute-start | bytes 786440 | tf_op jit(solution)/shard_map/ppermute | solution.py:37
  14.3 1.1 collective-permute-start.3
  15.4 1.8 %collective-permute-done.5 = bf16[128,1024]{1,0:T(8,128)(2,1)S(1)} collective-permute-done((bf16[128,1024]{1,0:T(8,128)(2,1)S(1)}, bf16[128,1024]{1,0:T(8,128)(2,1)S(1)}, u32[]{:S(2)}, u32[]{:S(2)}) %collective-permute-start.5) | collective-permute-done | bytes 262176 | tf_op jit(solution)/shard_map/ppermute | solution.py:37
  17.2 4.0 %collective-permute-done.4 = bf16[128,1024]{1,0:T(8,128)(2,1)S(1)} collective-permute-done((bf16[128,1024]{1,0:T(8,128)(2,1)S(1)}, bf16[128,1024]{1,0:T(8,128)(2,1)S(1)}, u32[]{:S(2)}, u32[]{:S(2)}) %collective-permute-start.4) | collective-permute-done | bytes 262176 | tf_op jit(solution)/shard_map/ppermute | solution.py:37
  21.2 3.1 %collective-permute-start.6 = (bf16[512,1024]{1,0:T(8,128)(2,1)S(1)}, bf16[512,1024]{1,0:T(8,128)(2,1)}, u32[]{:S(2)}, u32[]{:S(2)}) collective-permute-start(bf16[512,1024]{1,0:T(8,128)(2,1)S(1)} %pad_maximum_fusion.own0), channel_id=1, source_target_pairs={{0,4},{1,5},{2,6},{3,7},{4,0},{5,1},{6,2},{7,3},{8,12},{9,13},{10,... | collective-permute-start | bytes 3145736 | tf_op jit(solution)/shard_map/ppermute | solution.py:29
  24.3 1.6 %collective-permute-start.8 = (bf16[512,1024]{1,0:T(8,128)(2,1)S(1)}, bf16[512,1024]{1,0:T(8,128)(2,1)S(1)}, u32[]{:S(2)}, u32[]{:S(2)}) collective-permute-start(bf16[512,1024]{1,0:T(8,128)(2,1)S(1)} %pad_maximum_fusion.own0), channel_id=1, source_target_pairs={{0,8},{1,9},{2,10},{3,11},{4,36},{5,37},{6,38},{7,39},{8,16},{9,17... | collective-permute-start | bytes 3145736 | tf_op jit(solution)/shard_map/ppermute | solution.py:42
  25.9 1.1 collective-permute-start.7
  27.0 3.1 %shard_map.46 = (bf16[4096,2048]{1,0:T(8,128)(2,1)S(1)}, bf16[256,4096]{1,0:T(8,128)(2,1)S(1)}, bf16[256,1024]{1,0:T(8,128)(2,1)S(1)}) custom-call(s32[4]{0:T(128)S(1)} %pad_add_fusion.1.where, s32[2,32,32]{2,1,0:T(8,128)S(1)} %copy-done.1, bf16[512,1024]{1,0:T(8,128)(2,1)S(1)} %pad_maximum_fusion.own0, bf16[512,1024]{1,0:T(8,128)(2,1)} %collective-permute-done.6.other0), custom_call_target="tpu_custom_call" | custom-call | flops 67108864 | bytes 1048576 | tf_op jit(solution)/shard_map/pallas_call | solution.py:294
  30.1 9.3 %collective-permute-done.8.own3 = bf16[512,1024]{1,0:T(8,128)(2,1)S(1)} collective-permute-done((bf16[512,1024]{1,0:T(8,128)(2,1)S(1)}, bf16[512,1024]{1,0:T(8,128)(2,1)S(1)}, u32[]{:S(2)}, u32[]{:S(2)}) %collective-permute-start.8) | collective-permute-done | bytes 1048608 | tf_op jit(solution)/shard_map/ppermute | solution.py:42
  39.8 0.9 collective-permute-start.9
  40.7 2.7 %collective-permute-start.11 = (bf16[512,1024]{1,0:T(8,128)(2,1)S(1)}, bf16[512,1024]{1,0:T(8,128)(2,1)S(1)}, u32[]{:S(2)}, u32[]{:S(2)}) collective-permute-start(bf16[512,1024]{1,0:T(8,128)(2,1)S(1)} %pad_maximum_fusion.own0), channel_id=1, source_target_pairs={{0,16},{1,17},{2,18},{3,19},{4,68},{5,69},{6,70},{7,71},{8,24},{9,... | collective-permute-start | bytes 3145736 | tf_op jit(solution)/shard_map/ppermute | solution.py:42
  43.4 5.9 %shard_map.47 = (bf16[4096,2048]{1,0:T(8,128)(2,1)S(1)}, bf16[256,4096]{1,0:T(8,128)(2,1)S(1)}) custom-call(s32[4]{0:T(128)S(1)} %pad_add_fusion.1.where, s32[2,32,32]{2,1,0:T(8,128)S(1)} %copy-done.1, bf16[512,1024]{1,0:T(8,128)(2,1)S(1)} %pad_maximum_fusion.own0, ...), custom_call_target="tpu_custom_call", output_to_operand_aliasing={{0}: (7, {}), {1}: (8, {})} | custom-call | flops 5905580032 | bytes 8388608 | tf_op jit(solution)/shard_map/pallas_call | solution.py:294
  49.4 8.0 %shard_map.48 = (bf16[4096,2048]{1,0:T(8,128)(2,1)S(1)}, bf16[256,4096]{1,0:T(8,128)(2,1)S(1)}, f32[256,2048]{1,0:T(8,128)S(1)}) custom-call(s32[4]{0:T(128)S(1)} %pad_add_fusion.1.where, s32[2,32,32]{2,1,0:T(8,128)S(1)} %copy-done.1, bf16[512,1024]{1,0:T(8,128)(2,1)S(1)} %pad_maximum_fusion.own0, ...), custom_call_target="tpu_custom_call", output_to_operand_aliasing={{0}: (8, {}), {1}: (9, {})} | custom-call | flops 5905580032 | bytes 8388608 | tf_op jit(solution)/shard_map/pallas_call | solution.py:294
  57.4 1.0 collective-permute-start.12
  58.5 5.7 %shard_map.49 = (bf16[4096,2048]{1,0:T(8,128)(2,1)S(1)}, bf16[256,4096]{1,0:T(8,128)(2,1)S(1)}) custom-call(s32[4]{0:T(128)S(1)} %pad_add_fusion.1.where, s32[2,32,32]{2,1,0:T(8,128)S(1)} %copy-done.1, bf16[512,1024]{1,0:T(8,128)(2,1)S(1)} %pad_maximum_fusion.own0, ...), custom_call_target="tpu_custom_call", output_to_operand_aliasing={{0}: (10, {}), {1}: (11, {})} | custom-call | flops 5368709120 | bytes 8388608 | tf_op jit(solution)/shard_map/pallas_call | solution.py:294
  64.2 7.0 %shard_map.50 = (bf16[4096,2048]{1,0:T(8,128)(2,1)S(1)}, bf16[256,4096]{1,0:T(8,128)(2,1)S(1)}, bf16[256,2048]{1,0:T(8,128)(2,1)S(1)}, f32[256,2048]{1,0:T(8,128)S(1)}) custom-call(s32[4]{0:T(128)S(1)} %pad_add_fusion.1.where, s32[2,32,32]{2,1,0:T(8,128)S(1)} %copy-done.1, ...), custom_call_target="tpu_custom_call", output_to_operand_aliasing={{0}: (10, {}), {1}: (11, {})} | custom-call | flops 4294967296 | bytes 20971520 | tf_op jit(solution)/shard_map/pallas_call | solution.py:294
  71.3 2.3 %shard_map.52 = (f32[256,512]{1,0:T(8,128)S(1)}, bf16[4096,512]{1,0:T(8,128)(2,1)S(1)}) custom-call(s32[4]{0:T(128)S(1)} %pad_add_fusion.1.where, bf16[256,2048]{1,0:T(8,128)(2,1)S(1)} %get-tuple-element.63.low, bf16[4096,2048]{1,0:T(8,128)(2,1)S(1)} %get-tuple-element.64.panel), custom_call_target="tpu_custom_call" | custom-call | flops 536870912 | bytes 12582912 | tf_op jit(solution)/shard_map/pallas_call | solution.py:294
  74.0 1.8 %shard_map.53 = bf16[256,512]{1,0:T(8,128)(2,1)S(1)} custom-call(s32[4]{0:T(128)S(1)} %pad_add_fusion.1.where, s32[2,32,32]{2,1,0:T(8,128)S(1)} %copy-done.1, bf16[256,2048]{1,0:T(8,128)(2,1)S(1)} %collective-permute-done.13.its, bf16[4096,512]{1,0:T(8,128)(2,1)S(1)} %get-tuple-element.66.columns, f32[256,512]{1,0:T(8,128)S(1)} %get-tuple-element.67.early, ...), custom_call_target="tpu_custom_call" | custom-call | flops 536870912 | bytes 4194304 | tf_op jit(solution)/shard_map/pallas_call | solution.py:294
  75.8 2.7 %collective-permute-start.18 = (bf16[256,512]{1,0:T(8,128)(2,1)S(1)}, bf16[256,512]{1,0:T(8,128)(2,1)S(1)}, u32[]{:S(2)}, u32[]{:S(2)}) collective-permute-start(bf16[256,512]{1,0:T(8,128)(2,1)S(1)} %shard_map.53), channel_id=1, source_target_pairs={{0,16},{1,17},{2,18},{3,19},{4,68},{5,69},{6,70},{7,71},{8,24},{9,... | collective-permute-start | bytes 786440 | tf_op jit(solution)/shard_map/ppermute | solution.py:42
  78.5 1.7 %collective-permute-start.17 = (bf16[256,512]{1,0:T(8,128)(2,1)S(1)}, bf16[256,512]{1,0:T(8,128)(2,1)S(1)}, u32[]{:S(2)}, u32[]{:S(2)}) collective-permute-start(bf16[256,512]{1,0:T(8,128)(2,1)S(1)} %shard_map.53), channel_id=1, source_target_pairs={{0,64},{1,65},{2,66},{3,67},{4,20},{5,21},{6,22},{7,23},{8,72},{9,... | collective-permute-start | bytes 786440 | tf_op jit(solution)/shard_map/ppermute | solution.py:37
  80.2 0.5 collective-permute-start.16
  80.8 2.1 %collective-permute-start.15 = (bf16[256,512]{1,0:T(8,128)(2,1)S(1)}, bf16[256,512]{1,0:T(8,128)(2,1)S(1)}, u32[]{:S(2)}, u32[]{:S(2)}) collective-permute-start(bf16[256,512]{1,0:T(8,128)(2,1)S(1)} %shard_map.53), channel_id=1, source_target_pairs={{0,96},{1,97},{2,98},{3,99},{4,28},{5,29},{6,30},{7,31},{8,104},{9... | collective-permute-start | bytes 786440 | tf_op jit(solution)/shard_map/ppermute | solution.py:37
  82.9 6.3 %shard_map.51.own = bf16[256,2048]{1,0:T(8,128)(2,1)S(1)} custom-call(s32[4]{0:T(128)S(1)} %pad_add_fusion.1.where, s32[2,32,32]{2,1,0:T(8,128)S(1)} %copy-done.1, bf16[256,2048]{1,0:T(8,128)(2,1)S(1)} %get-tuple-element.63.low, bf16[256,2048]{1,0:T(8,128)(2,1)S(1)} %collective-permute-done.13.its, bf16[4096,2048]{1,0:T(8,128)(2,1)S(1)} %get-tuple-element.64.panel, ...), custom_call_target="tpu_custom_call" | custom-call | flops 4294967296 | bytes 23068672 | tf_op jit(solution)/shard_map/pallas_call | solution.py:294
  89.2 1.3 collective-permute-start.14
  91.0 2.7 %collective-permute-start.19 = (bf16[1024,512]{1,0:T(8,128)(2,1)S(1)}, bf16[1024,512]{1,0:T(8,128)(2,1)S(1)}, u32[]{:S(2)}, u32[]{:S(2)}) collective-permute-start(bf16[1024,512]{1,0:T(8,128)(2,1)S(1)} %constant_dynamic-update-slice_fusion.near), channel_id=1, source_target_pairs={{0,24},{1,25},{2,26},{3,27},{4,100},{5,101},{6,102},{7,103},{8,0},... | collective-permute-start | bytes 3145736 | tf_op jit(solution)/shard_map/ppermute | solution.py:42
  94.2 1.9 %collective-permute-start.22 = (bf16[256,512]{1,0:T(8,128)(2,1)S(1)}, bf16[256,512]{1,0:T(8,128)(2,1)S(1)}, u32[]{:S(2)}, u32[]{:S(2)}) collective-permute-start(bf16[256,512]{1,0:T(8,128)(2,1)S(1)} %collective-permute-done.18.far0), channel_id=1, source_target_pairs={{0,64},{1,65},{2,66},{3,67},{4,20},{5,21},{6,22},{7,23},{8,72},{9,... | collective-permute-start | bytes 786440 | tf_op jit(solution)/shard_map/ppermute | solution.py:37
  96.1 0.9 collective-permute-start.21
  97.0 1.0 shard_map.54
  98.0 5.5 %collective-permute-done.23.far3 = bf16[256,512]{1,0:T(8,128)(2,1)S(1)} collective-permute-done((bf16[256,512]{1,0:T(8,128)(2,1)S(1)}, bf16[256,512]{1,0:T(8,128)(2,1)S(1)}, u32[]{:S(2)}, u32[]{:S(2)}) %collective-permute-start.23) | collective-permute-done | bytes 262176 | tf_op jit(solution)/shard_map/ppermute | solution.py:37
  103.5 5.1 %collective-permute-done.22.far2 = bf16[256,512]{1,0:T(8,128)(2,1)S(1)} collective-permute-done((bf16[256,512]{1,0:T(8,128)(2,1)S(1)}, bf16[256,512]{1,0:T(8,128)(2,1)S(1)}, u32[]{:S(2)}, u32[]{:S(2)}) %collective-permute-start.22) | collective-permute-done | bytes 262176 | tf_op jit(solution)/shard_map/ppermute | solution.py:37
  108.6 0.8 collective-permute-done.21.far1
  109.5 1.0 shard_map.55
  110.5 1.3 collective-permute-done.20.three
  111.8 1.9 %shard_map.56 = (f32[256,512]{1,0:T(8,128)S(1)}, bf16[256,512]{1,0:T(8,128)(2,1)S(1)}, bf16[2048,512]{1,0:T(8,128)(2,1)S(1)}, bf16[2048,512]{1,0:T(8,128)(2,1)S(1)}) custom-call(s32[4]{0:T(128)S(1)} %pad_add_fusion.1.where, s32[2,32,32]{2,1,0:T(8,128)S(1)} %copy-done.2, ...), custom_call_target="tpu_custom_call", output_to_operand_aliasing={{2}: (7, {}), {3}: (8, {})} | custom-call | flops 536870912 | bytes 8388608 | tf_op jit(solution)/shard_map/pallas_call | solution.py:294
  113.7 1.0 collective-permute-start.26
  114.7 2.7 %collective-permute-start.24 = (bf16[256,512]{1,0:T(8,128)(2,1)S(1)}, bf16[256,512]{1,0:T(8,128)(2,1)S(1)}, u32[]{:S(2)}, u32[]{:S(2)}) collective-permute-start(bf16[256,512]{1,0:T(8,128)(2,1)S(1)} %get-tuple-element.79.own0), channel_id=1, source_target_pairs={{0,3},{1,0},{2,1},{3,2},{4,7},{5,4},{6,5},{7,6},{8,11},{9,8},{10,9... | collective-permute-start | bytes 786440 | tf_op jit(solution)/shard_map/ppermute | solution.py:33
  117.3 12.0 %collective-permute-done.25.own3 = bf16[256,512]{1,0:T(8,128)(2,1)S(1)} collective-permute-done((bf16[256,512]{1,0:T(8,128)(2,1)S(1)}, bf16[256,512]{1,0:T(8,128)(2,1)S(1)}, u32[]{:S(2)}, u32[]{:S(2)}) %collective-permute-start.25) | collective-permute-done | bytes 262176 | tf_op jit(solution)/shard_map/ppermute | solution.py:33
  129.4 1.5 %shard_map.57.early = f32[256,1024]{1,0:T(8,128)S(1)} custom-call(s32[4]{0:T(128)S(1)} %pad_add_fusion.1.where, bf16[256,512]{1,0:T(8,128)(2,1)S(1)} %get-tuple-element.79.own0, bf16[256,512]{1,0:T(8,128)(2,1)S(1)} %collective-permute-done.24.own1, bf16[256,512]{1,0:T(8,128)(2,1)S(1)} %collective-permute-done.25.own3, ...), custom_call_target="tpu_custom_call" | custom-call | flops 805306368 | bytes 4194304 | tf_op jit(solution)/shard_map/pallas_call | solution.py:294
  130.9 0.9 shard_map.58
  131.8 0.9 collective-permute-start.28
  132.7 1.5 %collective-permute-done.28.share = f32[128,1024]{1,0:T(8,128)S(1)} collective-permute-done((f32[128,1024]{1,0:T(8,128)S(1)}, f32[128,1024]{1,0:T(8,128)S(1)}, u32[]{:S(2)}, u32[]{:S(2)}) %collective-permute-start.28) | collective-permute-done | bytes 524320 | tf_op jit(solution)/shard_map/ppermute | solution.py:29
  134.2 1.7 %shard_map.59 = f32[128,1024]{1,0:T(8,128)} custom-call(s32[4]{0:T(128)S(1)} %pad_add_fusion.1.where, bf16[256,512]{1,0:T(8,128)(2,1)S(1)} %collective-permute-done.27.own2, f32[256,1024]{1,0:T(8,128)S(1)} %shard_map.57.early, f32[256,512]{1,0:T(8,128)S(1)} %get-tuple-element.84.square, bf16[2048,512]{1,0:T(8,128)(2,1)S(1)} %get-tuple-element.80.mine, ...), custom_call_target="tpu_custom_call" | custom-call | flops 134217728 | bytes 3145728 | tf_op jit(solution)/shard_map/pallas_call | solution.py:294
  (45 shorter events, 3.3 us)
Async XLA Ops:
  0.0 5.9 %copy-start = (s32[32,8]{0,1:T(8,128)S(1)}, s32[32,8]{0,1:T(8,128)}, u32[]{:S(2)}) copy-start(s32[32,8]{0,1:T(8,128)} %param.5) | copy-start | bytes 3076
  0.0 27.0 %copy-start.1 = (s32[2,32,32]{2,1,0:T(8,128)S(1)}, s32[2,32,32]{2,1,0:T(8,128)}, u32[]{:S(2)}) copy-start(s32[2,32,32]{2,1,0:T(8,128)} %keep_d.13) | copy-start | bytes 24580
  0.0 6.7 %collective-permute-start.1 = (bf16[128,256]{1,0:T(8,128)(2,1)}, bf16[128,256]{1,0:T(8,128)(2,1)S(1)}, u32[]{:S(2)}, u32[]{:S(2)}) collective-permute-start(bf16[128,256]{1,0:T(8,128)(2,1)} %param.4), channel_id=1, source_target_pairs={{0,2},{1,3},{2,0},{3,1},{4,6},{5,7},{6,4},{7,5},{8,10},{9,11},{10,... | collective-permute-start | bytes 196616 | tf_op jit(solution)/shard_map/ppermute | solution.py:33
  4.4 3.7 %collective-permute-start = (bf16[128,256]{1,0:T(8,128)(2,1)}, bf16[128,256]{1,0:T(8,128)(2,1)S(1)}, u32[]{:S(2)}, u32[]{:S(2)}) collective-permute-start(bf16[128,256]{1,0:T(8,128)(2,1)} %param.4), channel_id=1, source_target_pairs={{0,3},{1,0},{2,1},{3,2},{4,7},{5,4},{6,5},{7,6},{8,11},{9,8},{10,9... | collective-permute-start | bytes 196616 | tf_op jit(solution)/shard_map/ppermute | solution.py:33
  4.9 4.5 %collective-permute-start.2 = (bf16[128,256]{1,0:T(8,128)(2,1)}, bf16[128,256]{1,0:T(8,128)(2,1)S(1)}, u32[]{:S(2)}, u32[]{:S(2)}) collective-permute-start(bf16[128,256]{1,0:T(8,128)(2,1)} %param.4), channel_id=1, source_target_pairs={{0,1},{1,2},{2,3},{3,0},{4,5},{5,6},{6,7},{7,4},{8,9},{9,10},{10,1... | collective-permute-start | bytes 196616 | tf_op jit(solution)/shard_map/ppermute | solution.py:33
  10.3 6.9 %collective-permute-start.5 = (bf16[128,1024]{1,0:T(8,128)(2,1)S(1)}, bf16[128,1024]{1,0:T(8,128)(2,1)S(1)}, u32[]{:S(2)}, u32[]{:S(2)}) collective-permute-start(bf16[128,1024]{1,0:T(8,128)(2,1)S(1)} %maximum_multiply_fusion), channel_id=1, source_target_pairs={{0,32},{1,33},{2,34},{3,35},{4,12},{5,13},{6,14},{7,15},{8,40},{9,... | collective-permute-start | bytes 786440 | tf_op jit(solution)/shard_map/ppermute | solution.py:37
  11.7 9.5 %collective-permute-start.4 = (bf16[128,1024]{1,0:T(8,128)(2,1)S(1)}, bf16[128,1024]{1,0:T(8,128)(2,1)S(1)}, u32[]{:S(2)}, u32[]{:S(2)}) collective-permute-start(bf16[128,1024]{1,0:T(8,128)(2,1)S(1)} %maximum_multiply_fusion), channel_id=1, source_target_pairs={{0,64},{1,65},{2,66},{3,67},{4,20},{5,21},{6,22},{7,23},{8,72},{9,... | collective-permute-start | bytes 786440 | tf_op jit(solution)/shard_map/ppermute | solution.py:37
  14.3 6.9 %collective-permute-start.3 = (bf16[128,1024]{1,0:T(8,128)(2,1)S(1)}, bf16[128,1024]{1,0:T(8,128)(2,1)S(1)}, u32[]{:S(2)}, u32[]{:S(2)}) collective-permute-start(bf16[128,1024]{1,0:T(8,128)(2,1)S(1)} %maximum_multiply_fusion), channel_id=1, source_target_pairs={{0,96},{1,97},{2,98},{3,99},{4,28},{5,29},{6,30},{7,31},{8,104},{9... | collective-permute-start | bytes 786440 | tf_op jit(solution)/shard_map/ppermute | solution.py:37
  21.2 5.8 %collective-permute-start.6 = (bf16[512,1024]{1,0:T(8,128)(2,1)S(1)}, bf16[512,1024]{1,0:T(8,128)(2,1)}, u32[]{:S(2)}, u32[]{:S(2)}) collective-permute-start(bf16[512,1024]{1,0:T(8,128)(2,1)S(1)} %pad_maximum_fusion.own0), channel_id=1, source_target_pairs={{0,4},{1,5},{2,6},{3,7},{4,0},{5,1},{6,2},{7,3},{8,12},{9,13},{10,... | collective-permute-start | bytes 3145736 | tf_op jit(solution)/shard_map/ppermute | solution.py:29
  24.3 15.2 %collective-permute-start.8 = (bf16[512,1024]{1,0:T(8,128)(2,1)S(1)}, bf16[512,1024]{1,0:T(8,128)(2,1)S(1)}, u32[]{:S(2)}, u32[]{:S(2)}) collective-permute-start(bf16[512,1024]{1,0:T(8,128)(2,1)S(1)} %pad_maximum_fusion.own0), channel_id=1, source_target_pairs={{0,8},{1,9},{2,10},{3,11},{4,36},{5,37},{6,38},{7,39},{8,16},{9,17... | collective-permute-start | bytes 3145736 | tf_op jit(solution)/shard_map/ppermute | solution.py:42
  25.9 13.9 %collective-permute-start.7 = (bf16[512,1024]{1,0:T(8,128)(2,1)S(1)}, bf16[512,1024]{1,0:T(8,128)(2,1)S(1)}, u32[]{:S(2)}, u32[]{:S(2)}) collective-permute-start(bf16[512,1024]{1,0:T(8,128)(2,1)S(1)} %pad_maximum_fusion.own0), channel_id=1, source_target_pairs={{0,24},{1,25},{2,26},{3,27},{4,100},{5,101},{6,102},{7,103},{8,0},... | collective-permute-start | bytes 3145736 | tf_op jit(solution)/shard_map/ppermute | solution.py:42
  39.8 9.5 %collective-permute-start.9 = (bf16[512,1024]{1,0:T(8,128)(2,1)S(1)}, bf16[512,1024]{1,0:T(8,128)(2,1)S(1)}, u32[]{:S(2)}, u32[]{:S(2)}) collective-permute-start(bf16[512,1024]{1,0:T(8,128)(2,1)S(1)} %collective-permute-done.7.own1), channel_id=1, source_target_pairs={{0,4},{1,5},{2,6},{3,7},{4,0},{5,1},{6,2},{7,3},{8,12},{9,13},{10,... | collective-permute-start | bytes 3145736 | tf_op jit(solution)/shard_map/ppermute | solution.py:29
  40.7 8.6 %collective-permute-start.10 = (bf16[512,1024]{1,0:T(8,128)(2,1)S(1)}, bf16[512,1024]{1,0:T(8,128)(2,1)S(1)}, u32[]{:S(2)}, u32[]{:S(2)}) collective-permute-start(bf16[512,1024]{1,0:T(8,128)(2,1)S(1)} %collective-permute-done.8.own3), channel_id=1, source_target_pairs={{0,4},{1,5},{2,6},{3,7},{4,0},{5,1},{6,2},{7,3},{8,12},{9,13},{10,... | collective-permute-start | bytes 3145736 | tf_op jit(solution)/shard_map/ppermute | solution.py:29
  40.7 16.7 %collective-permute-start.11 = (bf16[512,1024]{1,0:T(8,128)(2,1)S(1)}, bf16[512,1024]{1,0:T(8,128)(2,1)S(1)}, u32[]{:S(2)}, u32[]{:S(2)}) collective-permute-start(bf16[512,1024]{1,0:T(8,128)(2,1)S(1)} %pad_maximum_fusion.own0), channel_id=1, source_target_pairs={{0,16},{1,17},{2,18},{3,19},{4,68},{5,69},{6,70},{7,71},{8,24},{9,... | collective-permute-start | bytes 3145736 | tf_op jit(solution)/shard_map/ppermute | solution.py:42
  57.4 6.7 %copy-start.2 = (s32[2,32,32]{2,1,0:T(8,128)S(1)}, s32[2,32,32]{2,1,0:T(8,128)}, u32[]{:S(2)}) copy-start(s32[2,32,32]{2,1,0:T(8,128)} %keep_s.3) | copy-start | bytes 24580
  57.4 6.7 %collective-permute-start.12 = (bf16[512,1024]{1,0:T(8,128)(2,1)S(1)}, bf16[512,1024]{1,0:T(8,128)(2,1)S(1)}, u32[]{:S(2)}, u32[]{:S(2)}) collective-permute-start(bf16[512,1024]{1,0:T(8,128)(2,1)S(1)} %collective-permute-done.11.own2), channel_id=1, source_target_pairs={{0,4},{1,5},{2,6},{3,7},{4,0},{5,1},{6,2},{7,3},{8,12},{9,13},{10,... | collective-permute-start | bytes 3145736 | tf_op jit(solution)/shard_map/ppermute | solution.py:29
  71.2 2.7 %collective-permute-start.13 = (bf16[256,2048]{1,0:T(8,128)(2,1)S(1)}, bf16[256,2048]{1,0:T(8,128)(2,1)S(1)}, u32[]{:S(2)}, u32[]{:S(2)}) collective-permute-start(bf16[256,2048]{1,0:T(8,128)(2,1)S(1)} %get-tuple-element.63.low), channel_id=1, source_target_pairs={{0,4},{1,5},{2,6},{3,7},{4,0},{5,1},{6,2},{7,3},{8,12},{9,13},{10,... | collective-permute-start | bytes 3145736 | tf_op jit(solution)/shard_map/ppermute | solution.py:29
  75.8 14.8 %collective-permute-start.18 = (bf16[256,512]{1,0:T(8,128)(2,1)S(1)}, bf16[256,512]{1,0:T(8,128)(2,1)S(1)}, u32[]{:S(2)}, u32[]{:S(2)}) collective-permute-start(bf16[256,512]{1,0:T(8,128)(2,1)S(1)} %shard_map.53), channel_id=1, source_target_pairs={{0,16},{1,17},{2,18},{3,19},{4,68},{5,69},{6,70},{7,71},{8,24},{9,... | collective-permute-start | bytes 786440 | tf_op jit(solution)/shard_map/ppermute | solution.py:42
  78.5 12.0 %collective-permute-start.17 = (bf16[256,512]{1,0:T(8,128)(2,1)S(1)}, bf16[256,512]{1,0:T(8,128)(2,1)S(1)}, u32[]{:S(2)}, u32[]{:S(2)}) collective-permute-start(bf16[256,512]{1,0:T(8,128)(2,1)S(1)} %shard_map.53), channel_id=1, source_target_pairs={{0,64},{1,65},{2,66},{3,67},{4,20},{5,21},{6,22},{7,23},{8,72},{9,... | collective-permute-start | bytes 786440 | tf_op jit(solution)/shard_map/ppermute | solution.py:37
  80.2 10.3 %collective-permute-start.16 = (bf16[256,512]{1,0:T(8,128)(2,1)S(1)}, bf16[256,512]{1,0:T(8,128)(2,1)S(1)}, u32[]{:S(2)}, u32[]{:S(2)}) collective-permute-start(bf16[256,512]{1,0:T(8,128)(2,1)S(1)} %shard_map.53), channel_id=1, source_target_pairs={{0,32},{1,33},{2,34},{3,35},{4,12},{5,13},{6,14},{7,15},{8,40},{9,... | collective-permute-start | bytes 786440 | tf_op jit(solution)/shard_map/ppermute | solution.py:37
  80.8 9.8 %collective-permute-start.15 = (bf16[256,512]{1,0:T(8,128)(2,1)S(1)}, bf16[256,512]{1,0:T(8,128)(2,1)S(1)}, u32[]{:S(2)}, u32[]{:S(2)}) collective-permute-start(bf16[256,512]{1,0:T(8,128)(2,1)S(1)} %shard_map.53), channel_id=1, source_target_pairs={{0,96},{1,97},{2,98},{3,99},{4,28},{5,29},{6,30},{7,31},{8,104},{9... | collective-permute-start | bytes 786440 | tf_op jit(solution)/shard_map/ppermute | solution.py:37
  89.2 6.9 %collective-permute-start.14 = (bf16[256,2048]{1,0:T(8,128)(2,1)S(1)}, bf16[256,2048]{1,0:T(8,128)(2,1)S(1)}, u32[]{:S(2)}, u32[]{:S(2)}) collective-permute-start(bf16[256,2048]{1,0:T(8,128)(2,1)S(1)} %shard_map.51.own), channel_id=1, source_target_pairs={{0,4},{1,5},{2,6},{3,7},{4,0},{5,1},{6,2},{7,3},{8,12},{9,13},{10,... | collective-permute-start | bytes 3145736 | tf_op jit(solution)/shard_map/ppermute | solution.py:29
  90.7 21.1 %collective-permute-start.20 = (bf16[1024,512]{1,0:T(8,128)(2,1)S(1)}, bf16[1024,512]{1,0:T(8,128)(2,1)S(1)}, u32[]{:S(2)}, u32[]{:S(2)}) collective-permute-start(bf16[1024,512]{1,0:T(8,128)(2,1)S(1)} %constant_dynamic-update-slice_fusion.near), channel_id=1, source_target_pairs={{0,8},{1,9},{2,10},{3,11},{4,36},{5,37},{6,38},{7,39},{8,16},{9,17... | collective-permute-start | bytes 3145736 | tf_op jit(solution)/shard_map/ppermute | solution.py:42
  91.0 20.8 %collective-permute-start.19 = (bf16[1024,512]{1,0:T(8,128)(2,1)S(1)}, bf16[1024,512]{1,0:T(8,128)(2,1)S(1)}, u32[]{:S(2)}, u32[]{:S(2)}) collective-permute-start(bf16[1024,512]{1,0:T(8,128)(2,1)S(1)} %constant_dynamic-update-slice_fusion.near), channel_id=1, source_target_pairs={{0,24},{1,25},{2,26},{3,27},{4,100},{5,101},{6,102},{7,103},{8,0},... | collective-permute-start | bytes 3145736 | tf_op jit(solution)/shard_map/ppermute | solution.py:42
  93.7 9.9 %collective-permute-start.23 = (bf16[256,512]{1,0:T(8,128)(2,1)S(1)}, bf16[256,512]{1,0:T(8,128)(2,1)S(1)}, u32[]{:S(2)}, u32[]{:S(2)}) collective-permute-start(bf16[256,512]{1,0:T(8,128)(2,1)S(1)} %collective-permute-done.18.far0), channel_id=1, source_target_pairs={{0,32},{1,33},{2,34},{3,35},{4,12},{5,13},{6,14},{7,15},{8,40},{9,... | collective-permute-start | bytes 786440 | tf_op jit(solution)/shard_map/ppermute | solution.py:37
  94.2 14.4 %collective-permute-start.22 = (bf16[256,512]{1,0:T(8,128)(2,1)S(1)}, bf16[256,512]{1,0:T(8,128)(2,1)S(1)}, u32[]{:S(2)}, u32[]{:S(2)}) collective-permute-start(bf16[256,512]{1,0:T(8,128)(2,1)S(1)} %collective-permute-done.18.far0), channel_id=1, source_target_pairs={{0,64},{1,65},{2,66},{3,67},{4,20},{5,21},{6,22},{7,23},{8,72},{9,... | collective-permute-start | bytes 786440 | tf_op jit(solution)/shard_map/ppermute | solution.py:37
  96.1 13.4 %collective-permute-start.21 = (bf16[256,512]{1,0:T(8,128)(2,1)S(1)}, bf16[256,512]{1,0:T(8,128)(2,1)S(1)}, u32[]{:S(2)}, u32[]{:S(2)}) collective-permute-start(bf16[256,512]{1,0:T(8,128)(2,1)S(1)} %collective-permute-done.18.far0), channel_id=1, source_target_pairs={{0,96},{1,97},{2,98},{3,99},{4,28},{5,29},{6,30},{7,31},{8,104},{9... | collective-permute-start | bytes 786440 | tf_op jit(solution)/shard_map/ppermute | solution.py:37
  113.7 15.7 %collective-permute-start.26 = (bf16[2048,512]{1,0:T(8,128)(2,1)S(1)}, bf16[2048,512]{1,0:T(8,128)(2,1)S(1)}, u32[]{:S(2)}, u32[]{:S(2)}) collective-permute-start(bf16[2048,512]{1,0:T(8,128)(2,1)S(1)} %get-tuple-element.81), channel_id=1, source_target_pairs={{0,4},{1,5},{2,6},{3,7},{4,0},{5,1},{6,2},{7,3},{8,12},{9,13},{10,... | collective-permute-start | bytes 6291464 | tf_op jit(solution)/shard_map/ppermute | solution.py:29
  114.7 14.7 %collective-permute-start.25 = (bf16[256,512]{1,0:T(8,128)(2,1)S(1)}, bf16[256,512]{1,0:T(8,128)(2,1)S(1)}, u32[]{:S(2)}, u32[]{:S(2)}) collective-permute-start(bf16[256,512]{1,0:T(8,128)(2,1)S(1)} %get-tuple-element.79.own0), channel_id=1, source_target_pairs={{0,1},{1,2},{2,3},{3,0},{4,5},{5,6},{6,7},{7,4},{8,9},{9,10},{10,1... | collective-permute-start | bytes 786440 | tf_op jit(solution)/shard_map/ppermute | solution.py:33
  114.7 14.7 %collective-permute-start.24 = (bf16[256,512]{1,0:T(8,128)(2,1)S(1)}, bf16[256,512]{1,0:T(8,128)(2,1)S(1)}, u32[]{:S(2)}, u32[]{:S(2)}) collective-permute-start(bf16[256,512]{1,0:T(8,128)(2,1)S(1)} %get-tuple-element.79.own0), channel_id=1, source_target_pairs={{0,3},{1,0},{2,1},{3,2},{4,7},{5,4},{6,5},{7,6},{8,11},{9,8},{10,9... | collective-permute-start | bytes 786440 | tf_op jit(solution)/shard_map/ppermute | solution.py:33
  117.3 13.5 %collective-permute-start.27 = (bf16[256,512]{1,0:T(8,128)(2,1)S(1)}, bf16[256,512]{1,0:T(8,128)(2,1)S(1)}, u32[]{:S(2)}, u32[]{:S(2)}) collective-permute-start(bf16[256,512]{1,0:T(8,128)(2,1)S(1)} %get-tuple-element.79.own0), channel_id=1, source_target_pairs={{0,2},{1,3},{2,0},{3,1},{4,6},{5,7},{6,4},{7,5},{8,10},{9,11},{10,... | collective-permute-start | bytes 786440 | tf_op jit(solution)/shard_map/ppermute | solution.py:33
  131.8 2.5 %collective-permute-start.28 = (f32[128,1024]{1,0:T(8,128)S(1)}, f32[128,1024]{1,0:T(8,128)S(1)}, u32[]{:S(2)}, u32[]{:S(2)}) collective-permute-start(f32[128,1024]{1,0:T(8,128)S(1)} %shard_map.58), channel_id=1, source_target_pairs={{0,4},{1,5},{2,6},{3,7},{4,0},{5,1},{6,2},{7,3},{8,12},{9,13},{10,... | collective-permute-start | bytes 1572872 | tf_op jit(solution)/shard_map/ppermute | solution.py:29

commit v8 on v7

--- a/solution.py
+++ b/solution.py
@@ -1,3 +1,5 @@
+import functools
+
 import jax
 import jax.numpy as jnp
 from jax import lax
@@ -252,38 +254,33 @@
             low[t * B:(t + 1) * B, u * B:(u + 1) * B] = piece.astype(jnp.bfloat16)
 
 
-def parts_times_panel(parts, z, mine, come):
-    total = [None, None]
+def parts_times_panel(parts, z, panel):
+    total = None
     for value, d in parts:
-        for n, panel in enumerate((mine, come)):
-            term = dot(value, panel[aligned((z + d) & 3, 512), :])
-            total[n] = term if total[n] is None else total[n] + term
+        term = dot(value, panel[aligned((z + d) & 3, 512), :])
+        total = term if total is None else total + term
     return total
 
 
-def early_cube(where, own0, own1, own3, mine, come, out):
-    parts = [(own0[...], 0), (own1[...], 1), (own3[...], 3)]
-    out[:, :COLS], out[:, COLS:] = parts_times_panel(parts, where[3], mine, come)
-
-
-def density_share(where, at, own2, early, square, mine, come):
-    first, second = parts_times_panel([(own2[at, :], 2)], where[3], mine, come)
-    return 3.0 * square[at, :] - 2.0 * (early[at, :COLS] + first), -2.0 * (early[at, COLS:] + second)
-
-
-def leaving_density(where, own2, early, square, mine, come, out):
-    at = aligned(1 - where[2], B)
-    out[:, :COLS], out[:, COLS:] = density_share(where, at, own2, early, square, mine, come)
-
-
-def second_density(where, own2, early, square, mine, come, share, out):
-    own, other = density_share(where, aligned(where[2], B), own2, early, square, mine, come)
-    own, other = own + share[:, COLS:], other + share[:, :COLS]
+def early_cube(where, own0, mine, out):
+    out[...] = parts_times_panel([(own0[...], 0)], where[3], mine)
+
+
+def density_share(leave, where, own0, own1, own2, own3, early, square, mine, come, out):
+    core, z = where[2], where[3]
+    at = aligned(1 - core if leave else core, B)
+    parts = [(own1[at, :], 1), (own3[at, :], 3), (own2[at, :], 2)]
+    out[:, :COLS] = 3.0 * square[at, :] - 2.0 * (early[at, :] + parts_times_panel(parts, z, mine))
+    out[:, COLS:] = -2.0 * parts_times_panel([(own0[at, :], 0)] + parts, z, come)
+
+
+def join(where, stay, share, out):
     first = where[2] == 0
     for t in range(4):
-        one, two = own[:, t * B:(t + 1) * B], other[:, t * B:(t + 1) * B]
-        out[:, 2 * t * B:(2 * t + 1) * B] = jnp.where(first, one, two)
-        out[:, (2 * t + 1) * B:(2 * t + 2) * B] = jnp.where(first, two, one)
+        at, far = slice(t * B, (t + 1) * B), slice(COLS + t * B, COLS + (t + 1) * B)
+        own, other = stay[:, at] + share[:, far], stay[:, far] + share[:, at]
+        out[:, 2 * t * B:(2 * t + 1) * B] = jnp.where(first, own, other)
+        out[:, (2 * t + 1) * B:(2 * t + 2) * B] = jnp.where(first, other, own)
 
 
 SMEM = pl.BlockSpec(memory_space=pltpu.SMEM)
@@ -378,15 +375,13 @@
     own0, own1, own2, own3 = gather(low, from_z)
     come = other_core(its)
     (early,) = call(
-        early_cube, 1, [where, own0, own1, own3, mine, come],
-        [jax.ShapeDtypeStruct((ROWS, 2 * COLS), jnp.float32)], [], block_flops * 3 // 4, 4 * MIB)
-    early, own2 = lax.optimization_barrier((early, own2))
+        early_cube, 1, [where, own0, mine], [full_block], [], block_flops // 8, 2 * MIB)
     half = jax.ShapeDtypeStruct((B, 2 * COLS), jnp.float32)
-    (leave,) = call(
-        leaving_density, 1, [where, own2, early, square, mine, come], [half], [], block_flops // 8, 3 * MIB)
-    (out,) = call(
-        second_density, 1, [where, own2, early, square, mine, come, other_core(leave)], [half], [],
-        block_flops // 8, 3 * MIB)
+    last = [where, own0, own1, own2, own3, early, square, mine, come]
+    (leave,) = call(functools.partial(density_share, True), 1, last, [half], [], block_flops * 3 // 8, 5 * MIB)
+    share = other_core(leave)
+    (stay,) = call(functools.partial(density_share, False), 1, last, [half], [], block_flops * 3 // 8, 5 * MIB)
+    (out,) = call(join, 1, [where, stay, share], [half], [], 0, 2 * MIB)
     return out
 
 

time: 136 us -> 135 us (level)
  waiting for transfers between devices: 44.9 us -> 42.9 us
    pallas_call x14 -> x15, Pallas kernels: 48 us -> 48.6 us  [call(): pl.pallas_call(kernel, in_specs=[SMEM] * n_smem + [VMEM] * (len(ins) - n_...]
  transfers between devices with their start and end apart: 29 -> 29, of which waited for: 13 -> 14; matrix products, arithmetic and copies ran while one was open for 1% -> 1% of each run, Pallas kernels for 26% -> 26%
where the time goes in v8:
time: 135 us
  Pallas kernels  48.6 us (36%)
  waiting for transfers between devices  42.9 us (32%)
  starting transfers between devices  41.4 us (31%)
    pallas_call x15, Pallas kernels, call(): pl.pallas_call(kernel, in_specs=[SMEM] * n_smem + [VMEM] * (len(ins) - n_...  48.6 us
    ppermute x9, waiting for transfers between devices, from_first(): lax.ppermute(a, AXES, pairs(lambda x, y, core, z: (x - d, y, core, z) if...  17.3 us
    ppermute x6, waiting for transfers between devices, from_z(): lax.ppermute(a, AXES, pairs(lambda x, y, core, z: (x, y, core, z - d)))  13.9 us
    ppermute x9, starting transfers between devices, from_first(): lax.ppermute(a, AXES, pairs(lambda x, y, core, z: (x - d, y, core, z) if...  12.8 us
    ppermute x6, starting transfers between devices, from_second(): lax.ppermute(a, AXES, pairs(lambda x, y, core, z: (x, y - d, core, z) if...  11.1 us
    ppermute x6, waiting for transfers between devices, from_second(): lax.ppermute(a, AXES, pairs(lambda x, y, core, z: (x, y - d, core, z) if...  11 us
    ppermute x6, starting transfers between devices, from_z(): lax.ppermute(a, AXES, pairs(lambda x, y, core, z: (x, y, core, z - d)))  8.86 us
    ppermute x8, starting transfers between devices, other_core(): lax.ppermute(a, AXES, pairs(lambda x, y, core, z: (x, y, 1 - core, z)))  8.68 us
  transfers between devices with their start and end apart: 29, of which 14 were waited for; matrix products, arithmetic and copies ran while one was open for 1% of the time, Pallas kernels for 26%

profile of v8, /device:TPU:1, one launch (start us, length us, event | category | flops | bytes accessed | tf_op | source)
XLA Modules:
  0.0 135.1 jit_solution(9664632621785875106)
XLA Ops:
  0.0 4.4 %collective-permute-start.1 = (bf16[128,256]{1,0:T(8,128)(2,1)}, bf16[128,256]{1,0:T(8,128)(2,1)S(1)}, u32[]{:S(2)}, u32[]{:S(2)}) collective-permute-start(bf16[128,256]{1,0:T(8,128)(2,1)} %param.4), channel_id=1, source_target_pairs={{0,2},{1,3},{2,0},{3,1},{4,6},{5,7},{6,4},{7,5},{8,10},{9,11},{10,... | collective-permute-start | bytes 196616 | tf_op jit(solution)/shard_map/ppermute | solution.py:35
  4.9 1.0 collective-permute-start.2
  6.7 1.4 %collective-permute-done = bf16[128,256]{1,0:T(8,128)(2,1)S(1)} collective-permute-done((bf16[128,256]{1,0:T(8,128)(2,1)}, bf16[128,256]{1,0:T(8,128)(2,1)S(1)}, u32[]{:S(2)}, u32[]{:S(2)}) %collective-permute-start) | collective-permute-done | bytes 65568 | tf_op jit(solution)/shard_map/ppermute | solution.py:35
  8.1 1.3 collective-permute-done.2
  9.4 0.9 maximum_multiply_fusion
  10.3 1.4 %collective-permute-start.5 = (bf16[128,1024]{1,0:T(8,128)(2,1)S(1)}, bf16[128,1024]{1,0:T(8,128)(2,1)S(1)}, u32[]{:S(2)}, u32[]{:S(2)}) collective-permute-start(bf16[128,1024]{1,0:T(8,128)(2,1)S(1)} %maximum_multiply_fusion), channel_id=1, source_target_pairs={{0,32},{1,33},{2,34},{3,35},{4,12},{5,13},{6,14},{7,15},{8,40},{9,... | collective-permute-start | bytes 786440 | tf_op jit(solution)/shard_map/ppermute | solution.py:39
  11.7 2.6 %collective-permute-start.4 = (bf16[128,1024]{1,0:T(8,128)(2,1)S(1)}, bf16[128,1024]{1,0:T(8,128)(2,1)S(1)}, u32[]{:S(2)}, u32[]{:S(2)}) collective-permute-start(bf16[128,1024]{1,0:T(8,128)(2,1)S(1)} %maximum_multiply_fusion), channel_id=1, source_target_pairs={{0,64},{1,65},{2,66},{3,67},{4,20},{5,21},{6,22},{7,23},{8,72},{9,... | collective-permute-start | bytes 786440 | tf_op jit(solution)/shard_map/ppermute | solution.py:39
  14.3 1.1 collective-permute-start.3
  15.4 1.8 %collective-permute-done.5 = bf16[128,1024]{1,0:T(8,128)(2,1)S(1)} collective-permute-done((bf16[128,1024]{1,0:T(8,128)(2,1)S(1)}, bf16[128,1024]{1,0:T(8,128)(2,1)S(1)}, u32[]{:S(2)}, u32[]{:S(2)}) %collective-permute-start.5) | collective-permute-done | bytes 262176 | tf_op jit(solution)/shard_map/ppermute | solution.py:39
  17.2 4.0 %collective-permute-done.4 = bf16[128,1024]{1,0:T(8,128)(2,1)S(1)} collective-permute-done((bf16[128,1024]{1,0:T(8,128)(2,1)S(1)}, bf16[128,1024]{1,0:T(8,128)(2,1)S(1)}, u32[]{:S(2)}, u32[]{:S(2)}) %collective-permute-start.4) | collective-permute-done | bytes 262176 | tf_op jit(solution)/shard_map/ppermute | solution.py:39
  21.2 3.1 %collective-permute-start.6 = (bf16[512,1024]{1,0:T(8,128)(2,1)S(1)}, bf16[512,1024]{1,0:T(8,128)(2,1)}, u32[]{:S(2)}, u32[]{:S(2)}) collective-permute-start(bf16[512,1024]{1,0:T(8,128)(2,1)S(1)} %pad_maximum_fusion.own0), channel_id=1, source_target_pairs={{0,4},{1,5},{2,6},{3,7},{4,0},{5,1},{6,2},{7,3},{8,12},{9,13},{10,... | collective-permute-start | bytes 3145736 | tf_op jit(solution)/shard_map/ppermute | solution.py:31
  24.3 1.6 %collective-permute-start.8 = (bf16[512,1024]{1,0:T(8,128)(2,1)S(1)}, bf16[512,1024]{1,0:T(8,128)(2,1)S(1)}, u32[]{:S(2)}, u32[]{:S(2)}) collective-permute-start(bf16[512,1024]{1,0:T(8,128)(2,1)S(1)} %pad_maximum_fusion.own0), channel_id=1, source_target_pairs={{0,8},{1,9},{2,10},{3,11},{4,36},{5,37},{6,38},{7,39},{8,16},{9,17... | collective-permute-start | bytes 3145736 | tf_op jit(solution)/shard_map/ppermute | solution.py:44
  25.9 1.1 collective-permute-start.7
  27.0 3.1 %shard_map.46 = (bf16[4096,2048]{1,0:T(8,128)(2,1)S(1)}, bf16[256,4096]{1,0:T(8,128)(2,1)S(1)}, bf16[256,1024]{1,0:T(8,128)(2,1)S(1)}) custom-call(s32[4]{0:T(128)S(1)} %pad_add_fusion.1.where, s32[2,32,32]{2,1,0:T(8,128)S(1)} %copy-done.1, bf16[512,1024]{1,0:T(8,128)(2,1)S(1)} %pad_maximum_fusion.own0, bf16[512,1024]{1,0:T(8,128)(2,1)} %collective-permute-done.6.other0), custom_call_target="tpu_custom_call" | custom-call | flops 67108864 | bytes 1048576 | tf_op jit(solution)/shard_map/pallas_call | solution.py:291
  30.1 9.3 %collective-permute-done.8.own3 = bf16[512,1024]{1,0:T(8,128)(2,1)S(1)} collective-permute-done((bf16[512,1024]{1,0:T(8,128)(2,1)S(1)}, bf16[512,1024]{1,0:T(8,128)(2,1)S(1)}, u32[]{:S(2)}, u32[]{:S(2)}) %collective-permute-start.8) | collective-permute-done | bytes 1048608 | tf_op jit(solution)/shard_map/ppermute | solution.py:44
  39.8 0.9 collective-permute-start.9
  40.7 2.7 %collective-permute-start.11 = (bf16[512,1024]{1,0:T(8,128)(2,1)S(1)}, bf16[512,1024]{1,0:T(8,128)(2,1)S(1)}, u32[]{:S(2)}, u32[]{:S(2)}) collective-permute-start(bf16[512,1024]{1,0:T(8,128)(2,1)S(1)} %pad_maximum_fusion.own0), channel_id=1, source_target_pairs={{0,16},{1,17},{2,18},{3,19},{4,68},{5,69},{6,70},{7,71},{8,24},{9,... | collective-permute-start | bytes 3145736 | tf_op jit(solution)/shard_map/ppermute | solution.py:44
  43.4 5.9 %shard_map.47 = (bf16[4096,2048]{1,0:T(8,128)(2,1)S(1)}, bf16[256,4096]{1,0:T(8,128)(2,1)S(1)}) custom-call(s32[4]{0:T(128)S(1)} %pad_add_fusion.1.where, s32[2,32,32]{2,1,0:T(8,128)S(1)} %copy-done.1, bf16[512,1024]{1,0:T(8,128)(2,1)S(1)} %pad_maximum_fusion.own0, ...), custom_call_target="tpu_custom_call", output_to_operand_aliasing={{0}: (7, {}), {1}: (8, {})} | custom-call | flops 5905580032 | bytes 8388608 | tf_op jit(solution)/shard_map/pallas_call | solution.py:291
  49.4 8.0 %shard_map.48 = (bf16[4096,2048]{1,0:T(8,128)(2,1)S(1)}, bf16[256,4096]{1,0:T(8,128)(2,1)S(1)}, f32[256,2048]{1,0:T(8,128)S(1)}) custom-call(s32[4]{0:T(128)S(1)} %pad_add_fusion.1.where, s32[2,32,32]{2,1,0:T(8,128)S(1)} %copy-done.1, bf16[512,1024]{1,0:T(8,128)(2,1)S(1)} %pad_maximum_fusion.own0, ...), custom_call_target="tpu_custom_call", output_to_operand_aliasing={{0}: (8, {}), {1}: (9, {})} | custom-call | flops 5905580032 | bytes 8388608 | tf_op jit(solution)/shard_map/pallas_call | solution.py:291
  57.4 1.0 collective-permute-start.12
  58.5 5.7 %shard_map.49 = (bf16[4096,2048]{1,0:T(8,128)(2,1)S(1)}, bf16[256,4096]{1,0:T(8,128)(2,1)S(1)}) custom-call(s32[4]{0:T(128)S(1)} %pad_add_fusion.1.where, s32[2,32,32]{2,1,0:T(8,128)S(1)} %copy-done.1, bf16[512,1024]{1,0:T(8,128)(2,1)S(1)} %pad_maximum_fusion.own0, ...), custom_call_target="tpu_custom_call", output_to_operand_aliasing={{0}: (10, {}), {1}: (11, {})} | custom-call | flops 5368709120 | bytes 8388608 | tf_op jit(solution)/shard_map/pallas_call | solution.py:291
  64.2 7.0 %shard_map.50 = (bf16[4096,2048]{1,0:T(8,128)(2,1)S(1)}, bf16[256,4096]{1,0:T(8,128)(2,1)S(1)}, bf16[256,2048]{1,0:T(8,128)(2,1)S(1)}, f32[256,2048]{1,0:T(8,128)S(1)}) custom-call(s32[4]{0:T(128)S(1)} %pad_add_fusion.1.where, s32[2,32,32]{2,1,0:T(8,128)S(1)} %copy-done.1, ...), custom_call_target="tpu_custom_call", output_to_operand_aliasing={{0}: (10, {}), {1}: (11, {})} | custom-call | flops 4294967296 | bytes 20971520 | tf_op jit(solution)/shard_map/pallas_call | solution.py:291
  71.3 2.3 %shard_map.52 = (f32[256,512]{1,0:T(8,128)S(1)}, bf16[4096,512]{1,0:T(8,128)(2,1)S(1)}) custom-call(s32[4]{0:T(128)S(1)} %pad_add_fusion.1.where, bf16[256,2048]{1,0:T(8,128)(2,1)S(1)} %get-tuple-element.61.low, bf16[4096,2048]{1,0:T(8,128)(2,1)S(1)} %get-tuple-element.62.panel), custom_call_target="tpu_custom_call" | custom-call | flops 536870912 | bytes 12582912 | tf_op jit(solution)/shard_map/pallas_call | solution.py:291
  74.0 1.8 %shard_map.53 = bf16[256,512]{1,0:T(8,128)(2,1)S(1)} custom-call(s32[4]{0:T(128)S(1)} %pad_add_fusion.1.where, s32[2,32,32]{2,1,0:T(8,128)S(1)} %copy-done.1, bf16[256,2048]{1,0:T(8,128)(2,1)S(1)} %collective-permute-done.13.its, bf16[4096,512]{1,0:T(8,128)(2,1)S(1)} %get-tuple-element.64.columns, f32[256,512]{1,0:T(8,128)S(1)} %get-tuple-element.65.early, ...), custom_call_target="tpu_custom_call" | custom-call | flops 536870912 | bytes 4194304 | tf_op jit(solution)/shard_map/pallas_call | solution.py:291
  75.8 2.7 %collective-permute-start.18 = (bf16[256,512]{1,0:T(8,128)(2,1)S(1)}, bf16[256,512]{1,0:T(8,128)(2,1)S(1)}, u32[]{:S(2)}, u32[]{:S(2)}) collective-permute-start(bf16[256,512]{1,0:T(8,128)(2,1)S(1)} %shard_map.53), channel_id=1, source_target_pairs={{0,16},{1,17},{2,18},{3,19},{4,68},{5,69},{6,70},{7,71},{8,24},{9,... | collective-permute-start | bytes 786440 | tf_op jit(solution)/shard_map/ppermute | solution.py:44
  78.5 1.7 %collective-permute-start.17 = (bf16[256,512]{1,0:T(8,128)(2,1)S(1)}, bf16[256,512]{1,0:T(8,128)(2,1)S(1)}, u32[]{:S(2)}, u32[]{:S(2)}) collective-permute-start(bf16[256,512]{1,0:T(8,128)(2,1)S(1)} %shard_map.53), channel_id=1, source_target_pairs={{0,64},{1,65},{2,66},{3,67},{4,20},{5,21},{6,22},{7,23},{8,72},{9,... | collective-permute-start | bytes 786440 | tf_op jit(solution)/shard_map/ppermute | solution.py:39
  80.8 2.1 %collective-permute-start.15 = (bf16[256,512]{1,0:T(8,128)(2,1)S(1)}, bf16[256,512]{1,0:T(8,128)(2,1)S(1)}, u32[]{:S(2)}, u32[]{:S(2)}) collective-permute-start(bf16[256,512]{1,0:T(8,128)(2,1)S(1)} %shard_map.53), channel_id=1, source_target_pairs={{0,96},{1,97},{2,98},{3,99},{4,28},{5,29},{6,30},{7,31},{8,104},{9... | collective-permute-start | bytes 786440 | tf_op jit(solution)/shard_map/ppermute | solution.py:39
  82.9 6.3 %shard_map.51.own = bf16[256,2048]{1,0:T(8,128)(2,1)S(1)} custom-call(s32[4]{0:T(128)S(1)} %pad_add_fusion.1.where, s32[2,32,32]{2,1,0:T(8,128)S(1)} %copy-done.1, bf16[256,2048]{1,0:T(8,128)(2,1)S(1)} %get-tuple-element.61.low, bf16[256,2048]{1,0:T(8,128)(2,1)S(1)} %collective-permute-done.13.its, bf16[4096,2048]{1,0:T(8,128)(2,1)S(1)} %get-tuple-element.62.panel, ...), custom_call_target="tpu_custom_call" | custom-call | flops 4294967296 | bytes 23068672 | tf_op jit(solution)/shard_map/pallas_call | solution.py:291
  89.2 1.3 collective-permute-start.14
  91.0 2.7 %collective-permute-start.19 = (bf16[1024,512]{1,0:T(8,128)(2,1)S(1)}, bf16[1024,512]{1,0:T(8,128)(2,1)S(1)}, u32[]{:S(2)}, u32[]{:S(2)}) collective-permute-start(bf16[1024,512]{1,0:T(8,128)(2,1)S(1)} %constant_dynamic-update-slice_fusion.near), channel_id=1, source_target_pairs={{0,24},{1,25},{2,26},{3,27},{4,100},{5,101},{6,102},{7,103},{8,0},... | collective-permute-start | bytes 3145736 | tf_op jit(solution)/shard_map/ppermute | solution.py:44
  94.2 1.9 %collective-permute-start.22 = (bf16[256,512]{1,0:T(8,128)(2,1)S(1)}, bf16[256,512]{1,0:T(8,128)(2,1)S(1)}, u32[]{:S(2)}, u32[]{:S(2)}) collective-permute-start(bf16[256,512]{1,0:T(8,128)(2,1)S(1)} %collective-permute-done.18.far0), channel_id=1, source_target_pairs={{0,64},{1,65},{2,66},{3,67},{4,20},{5,21},{6,22},{7,23},{8,72},{9,... | collective-permute-start | bytes 786440 | tf_op jit(solution)/shard_map/ppermute | solution.py:39
  96.1 0.9 collective-permute-start.21
  97.0 1.0 shard_map.54
  98.0 5.5 %collective-permute-done.23.far3 = bf16[256,512]{1,0:T(8,128)(2,1)S(1)} collective-permute-done((bf16[256,512]{1,0:T(8,128)(2,1)S(1)}, bf16[256,512]{1,0:T(8,128)(2,1)S(1)}, u32[]{:S(2)}, u32[]{:S(2)}) %collective-permute-start.23) | collective-permute-done | bytes 262176 | tf_op jit(solution)/shard_map/ppermute | solution.py:39
  103.5 5.1 %collective-permute-done.22.far2 = bf16[256,512]{1,0:T(8,128)(2,1)S(1)} collective-permute-done((bf16[256,512]{1,0:T(8,128)(2,1)S(1)}, bf16[256,512]{1,0:T(8,128)(2,1)S(1)}, u32[]{:S(2)}, u32[]{:S(2)}) %collective-permute-start.22) | collective-permute-done | bytes 262176 | tf_op jit(solution)/shard_map/ppermute | solution.py:39
  108.6 0.8 collective-permute-done.21.far1
  109.5 1.0 shard_map.55
  110.5 1.3 collective-permute-done.20.three
  111.8 1.9 %shard_map.56 = (f32[256,512]{1,0:T(8,128)S(1)}, bf16[256,512]{1,0:T(8,128)(2,1)S(1)}, bf16[2048,512]{1,0:T(8,128)(2,1)S(1)}, bf16[2048,512]{1,0:T(8,128)(2,1)S(1)}) custom-call(s32[4]{0:T(128)S(1)} %pad_add_fusion.1.where, s32[2,32,32]{2,1,0:T(8,128)S(1)} %copy-done.2, ...), custom_call_target="tpu_custom_call", output_to_operand_aliasing={{2}: (7, {}), {3}: (8, {})} | custom-call | flops 536870912 | bytes 8388608 | tf_op jit(solution)/shard_map/pallas_call | solution.py:291
  113.7 1.0 collective-permute-start.27
  114.7 1.6 %collective-permute-start.25 = (bf16[256,512]{1,0:T(8,128)(2,1)S(1)}, bf16[256,512]{1,0:T(8,128)(2,1)S(1)}, u32[]{:S(2)}, u32[]{:S(2)}) collective-permute-start(bf16[256,512]{1,0:T(8,128)(2,1)S(1)} %get-tuple-element.77.own0), channel_id=1, source_target_pairs={{0,2},{1,3},{2,0},{3,1},{4,6},{5,7},{6,4},{7,5},{8,10},{9,11},{10,... | collective-permute-start | bytes 786440 | tf_op jit(solution)/shard_map/ppermute | solution.py:35
  116.3 1.4 %collective-permute-start.24 = (bf16[256,512]{1,0:T(8,128)(2,1)S(1)}, bf16[256,512]{1,0:T(8,128)(2,1)S(1)}, u32[]{:S(2)}, u32[]{:S(2)}) collective-permute-start(bf16[256,512]{1,0:T(8,128)(2,1)S(1)} %get-tuple-element.77.own0), channel_id=1, source_target_pairs={{0,3},{1,0},{2,1},{3,2},{4,7},{5,4},{6,5},{7,6},{8,11},{9,8},{10,9... | collective-permute-start | bytes 786440 | tf_op jit(solution)/shard_map/ppermute | solution.py:35
  117.6 0.8 shard_map.57.early
  118.5 10.9 %collective-permute-done.26.own3 = bf16[256,512]{1,0:T(8,128)(2,1)S(1)} collective-permute-done((bf16[256,512]{1,0:T(8,128)(2,1)S(1)}, bf16[256,512]{1,0:T(8,128)(2,1)S(1)}, u32[]{:S(2)}, u32[]{:S(2)}) %collective-permute-start.26) | collective-permute-done | bytes 262176 | tf_op jit(solution)/shard_map/ppermute | solution.py:35
  129.7 1.2 shard_map.59
  130.9 1.3 collective-permute-start.28
  132.1 1.2 shard_map.58.stay
  133.7 1.4 %shard_map.60 = f32[128,1024]{1,0:T(8,128)} custom-call(s32[4]{0:T(128)S(1)} %pad_add_fusion.1.where, f32[128,1024]{1,0:T(8,128)S(1)} %shard_map.58.stay, f32[128,1024]{1,0:T(8,128)S(1)} %collective-permute-done.28.share), custom_call_target="tpu_custom_call" | custom-call | bytes 2097152 | tf_op jit(solution)/shard_map/pallas_call | solution.py:291
  (46 shorter events, 4.4 us)
Async XLA Ops:
  0.0 5.9 %copy-start = (s32[32,8]{0,1:T(8,128)S(1)}, s32[32,8]{0,1:T(8,128)}, u32[]{:S(2)}) copy-start(s32[32,8]{0,1:T(8,128)} %param.5) | copy-start | bytes 3076
  0.0 27.0 %copy-start.1 = (s32[2,32,32]{2,1,0:T(8,128)S(1)}, s32[2,32,32]{2,1,0:T(8,128)}, u32[]{:S(2)}) copy-start(s32[2,32,32]{2,1,0:T(8,128)} %keep_d.13) | copy-start | bytes 24580
  0.0 6.7 %collective-permute-start.1 = (bf16[128,256]{1,0:T(8,128)(2,1)}, bf16[128,256]{1,0:T(8,128)(2,1)S(1)}, u32[]{:S(2)}, u32[]{:S(2)}) collective-permute-start(bf16[128,256]{1,0:T(8,128)(2,1)} %param.4), channel_id=1, source_target_pairs={{0,2},{1,3},{2,0},{3,1},{4,6},{5,7},{6,4},{7,5},{8,10},{9,11},{10,... | collective-permute-start | bytes 196616 | tf_op jit(solution)/shard_map/ppermute | solution.py:35
  4.4 3.7 %collective-permute-start = (bf16[128,256]{1,0:T(8,128)(2,1)}, bf16[128,256]{1,0:T(8,128)(2,1)S(1)}, u32[]{:S(2)}, u32[]{:S(2)}) collective-permute-start(bf16[128,256]{1,0:T(8,128)(2,1)} %param.4), channel_id=1, source_target_pairs={{0,3},{1,0},{2,1},{3,2},{4,7},{5,4},{6,5},{7,6},{8,11},{9,8},{10,9... | collective-permute-start | bytes 196616 | tf_op jit(solution)/shard_map/ppermute | solution.py:35
  4.9 4.5 %collective-permute-start.2 = (bf16[128,256]{1,0:T(8,128)(2,1)}, bf16[128,256]{1,0:T(8,128)(2,1)S(1)}, u32[]{:S(2)}, u32[]{:S(2)}) collective-permute-start(bf16[128,256]{1,0:T(8,128)(2,1)} %param.4), channel_id=1, source_target_pairs={{0,1},{1,2},{2,3},{3,0},{4,5},{5,6},{6,7},{7,4},{8,9},{9,10},{10,1... | collective-permute-start | bytes 196616 | tf_op jit(solution)/shard_map/ppermute | solution.py:35
  10.3 6.9 %collective-permute-start.5 = (bf16[128,1024]{1,0:T(8,128)(2,1)S(1)}, bf16[128,1024]{1,0:T(8,128)(2,1)S(1)}, u32[]{:S(2)}, u32[]{:S(2)}) collective-permute-start(bf16[128,1024]{1,0:T(8,128)(2,1)S(1)} %maximum_multiply_fusion), channel_id=1, source_target_pairs={{0,32},{1,33},{2,34},{3,35},{4,12},{5,13},{6,14},{7,15},{8,40},{9,... | collective-permute-start | bytes 786440 | tf_op jit(solution)/shard_map/ppermute | solution.py:39
  11.7 9.5 %collective-permute-start.4 = (bf16[128,1024]{1,0:T(8,128)(2,1)S(1)}, bf16[128,1024]{1,0:T(8,128)(2,1)S(1)}, u32[]{:S(2)}, u32[]{:S(2)}) collective-permute-start(bf16[128,1024]{1,0:T(8,128)(2,1)S(1)} %maximum_multiply_fusion), channel_id=1, source_target_pairs={{0,64},{1,65},{2,66},{3,67},{4,20},{5,21},{6,22},{7,23},{8,72},{9,... | collective-permute-start | bytes 786440 | tf_op jit(solution)/shard_map/ppermute | solution.py:39
  14.3 6.9 %collective-permute-start.3 = (bf16[128,1024]{1,0:T(8,128)(2,1)S(1)}, bf16[128,1024]{1,0:T(8,128)(2,1)S(1)}, u32[]{:S(2)}, u32[]{:S(2)}) collective-permute-start(bf16[128,1024]{1,0:T(8,128)(2,1)S(1)} %maximum_multiply_fusion), channel_id=1, source_target_pairs={{0,96},{1,97},{2,98},{3,99},{4,28},{5,29},{6,30},{7,31},{8,104},{9... | collective-permute-start | bytes 786440 | tf_op jit(solution)/shard_map/ppermute | solution.py:39
  21.2 5.8 %collective-permute-start.6 = (bf16[512,1024]{1,0:T(8,128)(2,1)S(1)}, bf16[512,1024]{1,0:T(8,128)(2,1)}, u32[]{:S(2)}, u32[]{:S(2)}) collective-permute-start(bf16[512,1024]{1,0:T(8,128)(2,1)S(1)} %pad_maximum_fusion.own0), channel_id=1, source_target_pairs={{0,4},{1,5},{2,6},{3,7},{4,0},{5,1},{6,2},{7,3},{8,12},{9,13},{10,... | collective-permute-start | bytes 3145736 | tf_op jit(solution)/shard_map/ppermute | solution.py:31
  24.3 15.2 %collective-permute-start.8 = (bf16[512,1024]{1,0:T(8,128)(2,1)S(1)}, bf16[512,1024]{1,0:T(8,128)(2,1)S(1)}, u32[]{:S(2)}, u32[]{:S(2)}) collective-permute-start(bf16[512,1024]{1,0:T(8,128)(2,1)S(1)} %pad_maximum_fusion.own0), channel_id=1, source_target_pairs={{0,8},{1,9},{2,10},{3,11},{4,36},{5,37},{6,38},{7,39},{8,16},{9,17... | collective-permute-start | bytes 3145736 | tf_op jit(solution)/shard_map/ppermute | solution.py:44
  25.9 13.9 %collective-permute-start.7 = (bf16[512,1024]{1,0:T(8,128)(2,1)S(1)}, bf16[512,1024]{1,0:T(8,128)(2,1)S(1)}, u32[]{:S(2)}, u32[]{:S(2)}) collective-permute-start(bf16[512,1024]{1,0:T(8,128)(2,1)S(1)} %pad_maximum_fusion.own0), channel_id=1, source_target_pairs={{0,24},{1,25},{2,26},{3,27},{4,100},{5,101},{6,102},{7,103},{8,0},... | collective-permute-start | bytes 3145736 | tf_op jit(solution)/shard_map/ppermute | solution.py:44
  39.8 9.5 %collective-permute-start.9 = (bf16[512,1024]{1,0:T(8,128)(2,1)S(1)}, bf16[512,1024]{1,0:T(8,128)(2,1)S(1)}, u32[]{:S(2)}, u32[]{:S(2)}) collective-permute-start(bf16[512,1024]{1,0:T(8,128)(2,1)S(1)} %collective-permute-done.7.own1), channel_id=1, source_target_pairs={{0,4},{1,5},{2,6},{3,7},{4,0},{5,1},{6,2},{7,3},{8,12},{9,13},{10,... | collective-permute-start | bytes 3145736 | tf_op jit(solution)/shard_map/ppermute | solution.py:31
  40.7 8.6 %collective-permute-start.10 = (bf16[512,1024]{1,0:T(8,128)(2,1)S(1)}, bf16[512,1024]{1,0:T(8,128)(2,1)S(1)}, u32[]{:S(2)}, u32[]{:S(2)}) collective-permute-start(bf16[512,1024]{1,0:T(8,128)(2,1)S(1)} %collective-permute-done.8.own3), channel_id=1, source_target_pairs={{0,4},{1,5},{2,6},{3,7},{4,0},{5,1},{6,2},{7,3},{8,12},{9,13},{10,... | collective-permute-start | bytes 3145736 | tf_op jit(solution)/shard_map/ppermute | solution.py:31
  40.7 16.7 %collective-permute-start.11 = (bf16[512,1024]{1,0:T(8,128)(2,1)S(1)}, bf16[512,1024]{1,0:T(8,128)(2,1)S(1)}, u32[]{:S(2)}, u32[]{:S(2)}) collective-permute-start(bf16[512,1024]{1,0:T(8,128)(2,1)S(1)} %pad_maximum_fusion.own0), channel_id=1, source_target_pairs={{0,16},{1,17},{2,18},{3,19},{4,68},{5,69},{6,70},{7,71},{8,24},{9,... | collective-permute-start | bytes 3145736 | tf_op jit(solution)/shard_map/ppermute | solution.py:44
  57.4 6.7 %copy-start.2 = (s32[2,32,32]{2,1,0:T(8,128)S(1)}, s32[2,32,32]{2,1,0:T(8,128)}, u32[]{:S(2)}) copy-start(s32[2,32,32]{2,1,0:T(8,128)} %keep_s.3) | copy-start | bytes 24580
  57.4 6.7 %collective-permute-start.12 = (bf16[512,1024]{1,0:T(8,128)(2,1)S(1)}, bf16[512,1024]{1,0:T(8,128)(2,1)S(1)}, u32[]{:S(2)}, u32[]{:S(2)}) collective-permute-start(bf16[512,1024]{1,0:T(8,128)(2,1)S(1)} %collective-permute-done.11.own2), channel_id=1, source_target_pairs={{0,4},{1,5},{2,6},{3,7},{4,0},{5,1},{6,2},{7,3},{8,12},{9,13},{10,... | collective-permute-start | bytes 3145736 | tf_op jit(solution)/shard_map/ppermute | solution.py:31
  71.2 2.7 %collective-permute-start.13 = (bf16[256,2048]{1,0:T(8,128)(2,1)S(1)}, bf16[256,2048]{1,0:T(8,128)(2,1)S(1)}, u32[]{:S(2)}, u32[]{:S(2)}) collective-permute-start(bf16[256,2048]{1,0:T(8,128)(2,1)S(1)} %get-tuple-element.61.low), channel_id=1, source_target_pairs={{0,4},{1,5},{2,6},{3,7},{4,0},{5,1},{6,2},{7,3},{8,12},{9,13},{10,... | collective-permute-start | bytes 3145736 | tf_op jit(solution)/shard_map/ppermute | solution.py:31
  75.8 14.8 %collective-permute-start.18 = (bf16[256,512]{1,0:T(8,128)(2,1)S(1)}, bf16[256,512]{1,0:T(8,128)(2,1)S(1)}, u32[]{:S(2)}, u32[]{:S(2)}) collective-permute-start(bf16[256,512]{1,0:T(8,128)(2,1)S(1)} %shard_map.53), channel_id=1, source_target_pairs={{0,16},{1,17},{2,18},{3,19},{4,68},{5,69},{6,70},{7,71},{8,24},{9,... | collective-permute-start | bytes 786440 | tf_op jit(solution)/shard_map/ppermute | solution.py:44
  78.5 12.0 %collective-permute-start.17 = (bf16[256,512]{1,0:T(8,128)(2,1)S(1)}, bf16[256,512]{1,0:T(8,128)(2,1)S(1)}, u32[]{:S(2)}, u32[]{:S(2)}) collective-permute-start(bf16[256,512]{1,0:T(8,128)(2,1)S(1)} %shard_map.53), channel_id=1, source_target_pairs={{0,64},{1,65},{2,66},{3,67},{4,20},{5,21},{6,22},{7,23},{8,72},{9,... | collective-permute-start | bytes 786440 | tf_op jit(solution)/shard_map/ppermute | solution.py:39
  80.2 10.3 %collective-permute-start.16 = (bf16[256,512]{1,0:T(8,128)(2,1)S(1)}, bf16[256,512]{1,0:T(8,128)(2,1)S(1)}, u32[]{:S(2)}, u32[]{:S(2)}) collective-permute-start(bf16[256,512]{1,0:T(8,128)(2,1)S(1)} %shard_map.53), channel_id=1, source_target_pairs={{0,32},{1,33},{2,34},{3,35},{4,12},{5,13},{6,14},{7,15},{8,40},{9,... | collective-permute-start | bytes 786440 | tf_op jit(solution)/shard_map/ppermute | solution.py:39
  80.8 9.8 %collective-permute-start.15 = (bf16[256,512]{1,0:T(8,128)(2,1)S(1)}, bf16[256,512]{1,0:T(8,128)(2,1)S(1)}, u32[]{:S(2)}, u32[]{:S(2)}) collective-permute-start(bf16[256,512]{1,0:T(8,128)(2,1)S(1)} %shard_map.53), channel_id=1, source_target_pairs={{0,96},{1,97},{2,98},{3,99},{4,28},{5,29},{6,30},{7,31},{8,104},{9... | collective-permute-start | bytes 786440 | tf_op jit(solution)/shard_map/ppermute | solution.py:39
  89.2 6.9 %collective-permute-start.14 = (bf16[256,2048]{1,0:T(8,128)(2,1)S(1)}, bf16[256,2048]{1,0:T(8,128)(2,1)S(1)}, u32[]{:S(2)}, u32[]{:S(2)}) collective-permute-start(bf16[256,2048]{1,0:T(8,128)(2,1)S(1)} %shard_map.51.own), channel_id=1, source_target_pairs={{0,4},{1,5},{2,6},{3,7},{4,0},{5,1},{6,2},{7,3},{8,12},{9,13},{10,... | collective-permute-start | bytes 3145736 | tf_op jit(solution)/shard_map/ppermute | solution.py:31
  90.7 21.1 %collective-permute-start.20 = (bf16[1024,512]{1,0:T(8,128)(2,1)S(1)}, bf16[1024,512]{1,0:T(8,128)(2,1)S(1)}, u32[]{:S(2)}, u32[]{:S(2)}) collective-permute-start(bf16[1024,512]{1,0:T(8,128)(2,1)S(1)} %constant_dynamic-update-slice_fusion.near), channel_id=1, source_target_pairs={{0,8},{1,9},{2,10},{3,11},{4,36},{5,37},{6,38},{7,39},{8,16},{9,17... | collective-permute-start | bytes 3145736 | tf_op jit(solution)/shard_map/ppermute | solution.py:44
  91.0 20.8 %collective-permute-start.19 = (bf16[1024,512]{1,0:T(8,128)(2,1)S(1)}, bf16[1024,512]{1,0:T(8,128)(2,1)S(1)}, u32[]{:S(2)}, u32[]{:S(2)}) collective-permute-start(bf16[1024,512]{1,0:T(8,128)(2,1)S(1)} %constant_dynamic-update-slice_fusion.near), channel_id=1, source_target_pairs={{0,24},{1,25},{2,26},{3,27},{4,100},{5,101},{6,102},{7,103},{8,0},... | collective-permute-start | bytes 3145736 | tf_op jit(solution)/shard_map/ppermute | solution.py:44
  93.7 9.9 %collective-permute-start.23 = (bf16[256,512]{1,0:T(8,128)(2,1)S(1)}, bf16[256,512]{1,0:T(8,128)(2,1)S(1)}, u32[]{:S(2)}, u32[]{:S(2)}) collective-permute-start(bf16[256,512]{1,0:T(8,128)(2,1)S(1)} %collective-permute-done.18.far0), channel_id=1, source_target_pairs={{0,32},{1,33},{2,34},{3,35},{4,12},{5,13},{6,14},{7,15},{8,40},{9,... | collective-permute-start | bytes 786440 | tf_op jit(solution)/shard_map/ppermute | solution.py:39
  94.2 14.4 %collective-permute-start.22 = (bf16[256,512]{1,0:T(8,128)(2,1)S(1)}, bf16[256,512]{1,0:T(8,128)(2,1)S(1)}, u32[]{:S(2)}, u32[]{:S(2)}) collective-permute-start(bf16[256,512]{1,0:T(8,128)(2,1)S(1)} %collective-permute-done.18.far0), channel_id=1, source_target_pairs={{0,64},{1,65},{2,66},{3,67},{4,20},{5,21},{6,22},{7,23},{8,72},{9,... | collective-permute-start | bytes 786440 | tf_op jit(solution)/shard_map/ppermute | solution.py:39
  96.1 13.4 %collective-permute-start.21 = (bf16[256,512]{1,0:T(8,128)(2,1)S(1)}, bf16[256,512]{1,0:T(8,128)(2,1)S(1)}, u32[]{:S(2)}, u32[]{:S(2)}) collective-permute-start(bf16[256,512]{1,0:T(8,128)(2,1)S(1)} %collective-permute-done.18.far0), channel_id=1, source_target_pairs={{0,96},{1,97},{2,98},{3,99},{4,28},{5,29},{6,30},{7,31},{8,104},{9... | collective-permute-start | bytes 786440 | tf_op jit(solution)/shard_map/ppermute | solution.py:39
  113.7 16.0 %collective-permute-start.27 = (bf16[2048,512]{1,0:T(8,128)(2,1)S(1)}, bf16[2048,512]{1,0:T(8,128)(2,1)S(1)}, u32[]{:S(2)}, u32[]{:S(2)}) collective-permute-start(bf16[2048,512]{1,0:T(8,128)(2,1)S(1)} %get-tuple-element.80), channel_id=1, source_target_pairs={{0,4},{1,5},{2,6},{3,7},{4,0},{5,1},{6,2},{7,3},{8,12},{9,13},{10,... | collective-permute-start | bytes 6291464 | tf_op jit(solution)/shard_map/ppermute | solution.py:31
  114.7 14.7 %collective-permute-start.26 = (bf16[256,512]{1,0:T(8,128)(2,1)S(1)}, bf16[256,512]{1,0:T(8,128)(2,1)S(1)}, u32[]{:S(2)}, u32[]{:S(2)}) collective-permute-start(bf16[256,512]{1,0:T(8,128)(2,1)S(1)} %get-tuple-element.77.own0), channel_id=1, source_target_pairs={{0,1},{1,2},{2,3},{3,0},{4,5},{5,6},{6,7},{7,4},{8,9},{9,10},{10,1... | collective-permute-start | bytes 786440 | tf_op jit(solution)/shard_map/ppermute | solution.py:35
  114.7 14.7 %collective-permute-start.25 = (bf16[256,512]{1,0:T(8,128)(2,1)S(1)}, bf16[256,512]{1,0:T(8,128)(2,1)S(1)}, u32[]{:S(2)}, u32[]{:S(2)}) collective-permute-start(bf16[256,512]{1,0:T(8,128)(2,1)S(1)} %get-tuple-element.77.own0), channel_id=1, source_target_pairs={{0,2},{1,3},{2,0},{3,1},{4,6},{5,7},{6,4},{7,5},{8,10},{9,11},{10,... | collective-permute-start | bytes 786440 | tf_op jit(solution)/shard_map/ppermute | solution.py:35
  116.3 13.4 %collective-permute-start.24 = (bf16[256,512]{1,0:T(8,128)(2,1)S(1)}, bf16[256,512]{1,0:T(8,128)(2,1)S(1)}, u32[]{:S(2)}, u32[]{:S(2)}) collective-permute-start(bf16[256,512]{1,0:T(8,128)(2,1)S(1)} %get-tuple-element.77.own0), channel_id=1, source_target_pairs={{0,3},{1,0},{2,1},{3,2},{4,7},{5,4},{6,5},{7,6},{8,11},{9,8},{10,9... | collective-permute-start | bytes 786440 | tf_op jit(solution)/shard_map/ppermute | solution.py:35
  130.9 2.8 %collective-permute-start.28 = (f32[128,1024]{1,0:T(8,128)S(1)}, f32[128,1024]{1,0:T(8,128)S(1)}, u32[]{:S(2)}, u32[]{:S(2)}) collective-permute-start(f32[128,1024]{1,0:T(8,128)S(1)} %shard_map.59), channel_id=1, source_target_pairs={{0,4},{1,5},{2,6},{3,7},{4,0},{5,1},{6,2},{7,3},{8,12},{9,13},{10,... | collective-permute-start | bytes 1572872 | tf_op jit(solution)/shard_map/ppermute | solution.py:31
